TPU v7x, 32 devices: a whole 2x2x4 slice. The times are simulated.
32 devices in a mesh: fsdp: 4 (over x, core), ctx: 2 (over y), tp: 4 (over z).
Axes of the slice: x: 2, y: 2, z: 4, core: 2. Of those that a mesh axis runs over, the one named last changes fastest.
Arguments:
- tokens: bfloat16 [8192, 2048], P(('fsdp', 'ctx'), 'tp'), may hold values from -6 to 6
- segments: int32 [8192], replicated, may hold values from 0 to 11, as said below
- query_weight: bfloat16 [2048, 2048], P(('fsdp', 'ctx'), 'tp'), may hold values from -0.125 to 0.125
- key_weight: bfloat16 [2048, 2048], P(('fsdp', 'ctx'), 'tp'), may hold values from -0.125 to 0.125
- value_weight: bfloat16 [2048, 2048], P(('fsdp', 'ctx'), 'tp'), may hold values from -0.125 to 0.125
- output_weight: bfloat16 [2048, 2048], P(('fsdp', 'ctx'), 'tp'), may hold values from -3 to 3
- expand_weight: bfloat16 [2048, 8192], P(('fsdp', 'ctx'), 'tp'), may hold values from -0.125 to 0.125
- shrink_weight: bfloat16 [2048, 8192], P(('fsdp', 'ctx'), 'tp'), may hold values from -0.0625 to 0.0625
- query_bias: bfloat16 [2048], P('tp'), may hold values from -3 to 3
- value_bias: bfloat16 [2048], P('tp'), may hold values from -0.1796875 to 0.1796875
- hidden_bias: bfloat16 [8192], P('tp'), may hold values from -3 to 3
- norm_gains: bfloat16 [2, 2048], P(None, 'tp'), may hold values from 0.25 to 1.75
- row_biases: bfloat16 [4, 2048], P(None, 'tp'), may hold values from -1.796875 to 1.796875
- out_grad: bfloat16 [8192, 2048], P(('fsdp', 'ctx'), 'tp'), may hold values from -6 to 6
Outputs:
- mixed: bfloat16 [8192, 2048], P(('fsdp', 'ctx'), 'tp')
- input_grad: bfloat16 [8192, 2048], P(('fsdp', 'ctx'), 'tp')
- query_weight_grad: float32 [2048, 2048], P(('fsdp', 'ctx'), 'tp')
- key_weight_grad: float32 [2048, 2048], P(('fsdp', 'ctx'), 'tp')
- value_weight_grad: float32 [2048, 2048], P(('fsdp', 'ctx'), 'tp')
- output_weight_grad: float32 [2048, 2048], P(('fsdp', 'ctx'), 'tp')
- expand_weight_grad: float32 [2048, 8192], P(('fsdp', 'ctx'), 'tp')
- shrink_weight_grad: float32 [2048, 8192], P(('fsdp', 'ctx'), 'tp')
- query_bias_grad: float32 [2048], P('tp')
- value_bias_grad: float32 [2048], P('tp')
- hidden_bias_grad: float32 [8192], P('tp')
- norm_gains_grad: float32 [2, 2048], P(None, 'tp')
- row_biases_grad: float32 [4, 2048], P(None, 'tp')
Inputs may be any that keep to these rules, and one draw needn't show every extreme that they name: `segments`: the tokens form 4 runs of 2048 tokens; run s holds three documents with ids 3 s, 3 s + 1 and 3 s + 2 in this order, the middle one starting within the run's first 1024 tokens and ending within its last 1024.
All inputs are finite; a program needn't handle non-finite values.
Results may differ from a plain program's by a relative error of at most 0.015.
Values may be sent and summed in bfloat16 or wider, within the bound.
A program may use at most 320 MiB of HBM per device.

v0:
```python
import math

import jax
import jax.numpy as jnp
from jax import lax
from jax.sharding import PartitionSpec as P

HD = 128
WIN = 1024
QB = 512


epsilon = 1e-06
masked_value = -1000000000.0


def padded(block, sides, width):
    for axis, dim in sides:
        count = lax.axis_size(axis)
        forward = [(i, i + 1) for i in range(count - 1)]
        backward = [(target, source) for source, target in forward]
        low = lax.ppermute(
            lax.slice_in_dim(block, block.shape[dim] - width, None, axis=dim), axis, forward
        )
        high = lax.ppermute(lax.slice_in_dim(block, 0, width, axis=dim), axis, backward)
        block = jnp.concatenate([low, block, high], axis=dim)
    return block


def own_slice(values):
    quarter = values.shape[-1] // lax.axis_size("tp")
    return lax.dynamic_slice_in_dim(
        values, lax.axis_index("tp") * quarter, quarter, values.ndim - 1
    )


def to_own(values):
    return own_slice(values)


def reduce_rows(partial_value):
    return lax.psum(partial_value, "tp")


def row_means(first, second):
    return (jnp.mean(first, axis=-1, keepdims=True), jnp.mean(second, axis=-1, keepdims=True))


def from_own(rows):
    return lax.all_gather(rows, "tp", axis=1, tiled=True)


def norm_back(upstream, normed, inverse, gain):
    scaled = upstream * gain
    first_mean, second_mean = row_means(scaled, scaled * normed)
    return inverse * (scaled - first_mean - normed * second_mean)


def gelu_tanh(values):
    return jax.nn.gelu(values, approximate=True)


def dot_plain(left, right):
    return jnp.dot(left, right, preferred_element_type=jnp.float32)


def dot_rows(left, right):
    return lax.dot_general(
        left, right, (((0,), (0,)), ((), ())), preferred_element_type=jnp.float32
    )


def dot_cols(left, right):
    return lax.dot_general(
        left, right, (((1,), (1,)), ((), ())), preferred_element_type=jnp.float32
    )


def body(
    tokens,
    segments,
    query_weight,
    key_weight,
    value_weight,
    output_weight,
    expand_weight,
    shrink_weight,
    query_bias,
    value_bias,
    hidden_bias,
    norm_gains,
    row_biases,
    out_grad,
):
    block_rows = tokens.shape[0]
    head_cols = query_weight.shape[1]
    head_count = head_cols // HD
    score_scale = 1.0 / math.sqrt(HD)
    span = QB + 2 * WIN
    block_count = block_rows // QB
    weights_local = (
        query_weight,
        key_weight,
        value_weight,
        output_weight,
        expand_weight,
        shrink_weight,
    )
    gathered = (
        lax.all_gather(weights_local[0], ("fsdp", "ctx"), axis=0, tiled=True),
        lax.all_gather(weights_local[1], ("fsdp", "ctx"), axis=0, tiled=True),
        lax.all_gather(weights_local[2], ("fsdp", "ctx"), axis=0, tiled=True),
        lax.all_gather(weights_local[3], ("fsdp", "ctx"), axis=0, tiled=True),
        lax.all_gather(weights_local[4], ("fsdp", "ctx"), axis=0, tiled=True),
        lax.all_gather(weights_local[5], ("fsdp", "ctx"), axis=0, tiled=True),
    )
    full_query, full_key, full_value, full_output, full_expand, full_shrink = gathered
    wide_tokens, wide_gains, wide_biases = (
        lax.all_gather(tokens, "tp", axis=1, tiled=True),
        lax.all_gather(norm_gains, "tp", axis=1, tiled=True),
        lax.all_gather(row_biases, "tp", axis=1, tiled=True),
    )
    gains_float = wide_gains.astype(jnp.float32)
    biases_float = wide_biases.astype(jnp.float32)
    first_token = (
        lax.axis_index("fsdp") * lax.axis_size("ctx") + lax.axis_index("ctx")
    ) * block_rows
    id_pad = jnp.pad(segments, (WIN, WIN), constant_values=-1)
    key_ids = lax.dynamic_slice_in_dim(id_pad, first_token, block_rows + 2 * WIN, 0)
    own_ids = key_ids[WIN : WIN + block_rows]
    distance = (
        jnp.arange(span, dtype=jnp.int32)[None, :] - WIN - jnp.arange(QB, dtype=jnp.int32)[:, None]
    )
    in_reach = jnp.abs(distance) <= WIN
    queries = (dot_plain(wide_tokens, full_query) + query_bias.astype(jnp.float32)).astype(
        jnp.bfloat16
    )
    keys_own = dot_plain(wide_tokens, full_key).astype(jnp.bfloat16)
    values_own = (dot_plain(wide_tokens, full_value) + value_bias.astype(jnp.float32)).astype(
        jnp.bfloat16
    )
    key_value = jnp.concatenate([keys_own, values_own], axis=1)
    key_value_ext = padded(key_value, (("ctx", 0),), WIN)

    def window_at(offset):
        query_rows = lax.dynamic_slice_in_dim(queries, offset, QB, 0).reshape(QB, head_count, HD)
        pair_rows = lax.dynamic_slice_in_dim(key_value_ext, offset, span, 0)
        key_rows = pair_rows[:, :head_cols].reshape(span, head_count, HD)
        value_rows = pair_rows[:, head_cols:].reshape(span, head_count, HD)
        query_ids = lax.dynamic_slice_in_dim(own_ids, offset, QB, 0)
        window_ids = lax.dynamic_slice_in_dim(key_ids, offset, span, 0)
        visible = in_reach & (query_ids[:, None] == window_ids[None, :])
        scores = (
            jnp.einsum("qhd,khd->hqk", query_rows, key_rows, preferred_element_type=jnp.float32)
            * score_scale
        )
        scores = jnp.where(visible[None], scores, masked_value)
        return (query_rows, key_rows, value_rows, scores)

    def forward_block(offset):
        query_rows, key_rows, value_rows, scores = window_at(offset)
        highest = jnp.max(scores, axis=-1, keepdims=True)
        powers = jnp.exp(scores - highest)
        totals = jnp.sum(powers, axis=-1, keepdims=True)
        attn_probs = (powers / totals).astype(jnp.bfloat16)
        attended_rows = jnp.einsum(
            "hqk,khd->qhd", attn_probs, value_rows, preferred_element_type=jnp.float32
        )
        return (
            attended_rows.astype(jnp.bfloat16).reshape(QB, head_cols),
            (highest + jnp.log(totals))[:, :, 0],
        )

    offsets = jnp.arange(block_count, dtype=jnp.int32) * QB
    attended_blocks, log_totals = lax.map(forward_block, offsets)
    attended = attended_blocks.reshape(block_rows, head_cols)
    first_sum = (
        wide_tokens.astype(jnp.float32)
        + reduce_rows(dot_cols(attended, full_output))
        + biases_float[0]
    )
    mean_one, square_one = row_means(first_sum, first_sum * first_sum)
    inverse_one = lax.rsqrt(square_one - mean_one * mean_one + epsilon)
    normed_one = (first_sum - mean_one) * inverse_one
    first_norm = normed_one * gains_float[0] + biases_float[1]
    norm_low = first_norm.astype(jnp.bfloat16)
    hidden = dot_plain(norm_low, full_expand) + hidden_bias.astype(jnp.float32)
    activated = gelu_tanh(hidden).astype(jnp.bfloat16)
    second_sum = first_norm + reduce_rows(dot_cols(activated, full_shrink)) + biases_float[2]
    mean_two, square_two = row_means(second_sum, second_sum * second_sum)
    inverse_two = lax.rsqrt(square_two - mean_two * mean_two + epsilon)
    normed_two = (second_sum - mean_two) * inverse_two
    mixed = to_own(normed_two * gains_float[1] + biases_float[3]).astype(jnp.bfloat16)
    back_query, back_key, back_value, back_output, back_expand, back_shrink = (
        lax.all_gather(weights_local[0], ("fsdp", "ctx"), axis=0, tiled=True),
        lax.all_gather(weights_local[1], ("fsdp", "ctx"), axis=0, tiled=True),
        lax.all_gather(weights_local[2], ("fsdp", "ctx"), axis=0, tiled=True),
        lax.all_gather(weights_local[3], ("fsdp", "ctx"), axis=0, tiled=True),
        lax.all_gather(weights_local[4], ("fsdp", "ctx"), axis=0, tiled=True),
        lax.all_gather(weights_local[5], ("fsdp", "ctx"), axis=0, tiled=True),
    )
    upstream = from_own(out_grad).astype(jnp.float32)
    grad_second = norm_back(upstream, normed_two, inverse_two, gains_float[1])
    gain_two_grad = jnp.sum(upstream * normed_two, axis=0)
    shift_two_grad = jnp.sum(upstream, axis=0)
    ffn_low = grad_second.astype(jnp.bfloat16)
    ffn_bias_grad = jnp.sum(ffn_low.astype(jnp.float32), axis=0)
    shrink_grad = dot_rows(ffn_low, activated)
    gelu_value, gelu_pull = jax.vjp(gelu_tanh, hidden)
    hidden_low = gelu_pull(dot_plain(ffn_low, back_shrink))[0].astype(jnp.bfloat16)
    expand_grad = dot_rows(norm_low, hidden_low)
    hidden_bias_grad = jnp.sum(hidden_low.astype(jnp.float32), axis=0)
    grad_first = grad_second + reduce_rows(dot_cols(hidden_low, back_expand))
    gain_one_grad = jnp.sum(grad_first * normed_one, axis=0)
    shift_one_grad = jnp.sum(grad_first, axis=0)
    grad_inner = norm_back(grad_first, normed_one, inverse_one, gains_float[0])
    branch_low = grad_inner.astype(jnp.bfloat16)
    branch_bias_grad = jnp.sum(branch_low.astype(jnp.float32), axis=0)
    output_grad = dot_rows(branch_low, attended)
    attended_grad = dot_plain(branch_low, back_output).astype(jnp.bfloat16)

    def backward_block(number, carry):
        query_grad, pair_grad = carry
        offset = number * QB
        query_rows, key_rows, value_rows, scores = window_at(offset)
        block_totals = lax.dynamic_index_in_dim(log_totals, number, 0, keepdims=False)
        attn_probs = jnp.exp(scores - block_totals[:, :, None])
        probs_low = attn_probs.astype(jnp.bfloat16)
        upstream_rows = lax.dynamic_slice_in_dim(attended_grad, offset, QB, 0).reshape(
            QB, head_count, HD
        )
        value_part = jnp.einsum(
            "hqk,qhd->khd", probs_low, upstream_rows, preferred_element_type=jnp.float32
        )
        prob_grad = jnp.einsum(
            "qhd,khd->hqk", upstream_rows, value_rows, preferred_element_type=jnp.float32
        )
        row_delta = jnp.sum(attn_probs * prob_grad, axis=-1, keepdims=True)
        score_grad = (attn_probs * (prob_grad - row_delta)).astype(jnp.bfloat16)
        query_part = (
            jnp.einsum("hqk,khd->qhd", score_grad, key_rows, preferred_element_type=jnp.float32)
            * score_scale
        )
        key_part = (
            jnp.einsum("hqk,qhd->khd", score_grad, query_rows, preferred_element_type=jnp.float32)
            * score_scale
        )
        window_grad = jnp.concatenate(
            [key_part.reshape(span, head_cols), value_part.reshape(span, head_cols)], axis=1
        )
        pair_grad = lax.dynamic_update_slice_in_dim(
            pair_grad, lax.dynamic_slice_in_dim(pair_grad, offset, span, 0) + window_grad, offset, 0
        )
        query_grad = lax.dynamic_update_slice_in_dim(
            query_grad, query_part.reshape(QB, head_cols), offset, 0
        )
        return (query_grad, pair_grad)

    query_start = jnp.zeros((block_rows, head_cols), jnp.float32)
    pair_start = jnp.zeros((block_rows + 2 * WIN, 2 * head_cols), jnp.float32)
    query_grad, pair_grad = lax.fori_loop(0, block_count, backward_block, (query_start, pair_start))
    edges = jnp.concatenate([pair_grad[:WIN], pair_grad[WIN + block_rows :]], axis=0)
    edge_ext = padded(edges, (("ctx", 0),), WIN)
    pair_own = pair_grad[WIN : WIN + block_rows]
    pair_own = pair_own.at[:WIN].add(edge_ext[:WIN]).at[block_rows - WIN :].add(edge_ext[3 * WIN :])
    query_low = query_grad.astype(jnp.bfloat16)
    key_low = pair_own[:, :head_cols].astype(jnp.bfloat16)
    value_low = pair_own[:, head_cols:].astype(jnp.bfloat16)
    query_w_grad = dot_rows(wide_tokens, query_low)
    key_w_grad = dot_rows(wide_tokens, key_low)
    value_w_grad = dot_rows(wide_tokens, value_low)
    input_partial = (
        dot_cols(query_low, back_query)
        + dot_cols(key_low, back_key)
        + dot_cols(value_low, back_value)
    )
    input_grad = (
        lax.psum_scatter(input_partial, "tp", scatter_dimension=1, tiled=True) + to_own(grad_inner)
    ).astype(jnp.bfloat16)
    weight_grads = (
        lax.psum_scatter(query_w_grad, ("fsdp", "ctx"), scatter_dimension=0, tiled=True),
        lax.psum_scatter(key_w_grad, ("fsdp", "ctx"), scatter_dimension=0, tiled=True),
        lax.psum_scatter(value_w_grad, ("fsdp", "ctx"), scatter_dimension=0, tiled=True),
        lax.psum_scatter(output_grad, ("fsdp", "ctx"), scatter_dimension=0, tiled=True),
        lax.psum_scatter(expand_grad, ("fsdp", "ctx"), scatter_dimension=0, tiled=True),
        lax.psum_scatter(shrink_grad, ("fsdp", "ctx"), scatter_dimension=0, tiled=True),
    )
    gains_grad = jnp.stack([to_own(gain_one_grad), to_own(gain_two_grad)])
    biases_grad = jnp.stack(
        [
            to_own(branch_bias_grad),
            to_own(shift_one_grad),
            to_own(ffn_bias_grad),
            to_own(shift_two_grad),
        ]
    )
    vector_grads = lax.psum(
        (
            jnp.sum(query_low.astype(jnp.float32), axis=0),
            jnp.sum(value_low.astype(jnp.float32), axis=0),
            hidden_bias_grad,
            gains_grad,
            biases_grad,
        ),
        ("fsdp", "ctx"),
    )
    return (
        mixed,
        input_grad,
        weight_grads[0],
        weight_grads[1],
        weight_grads[2],
        weight_grads[3],
        weight_grads[4],
        weight_grads[5],
        vector_grads[0],
        vector_grads[1],
        vector_grads[2],
        vector_grads[3],
        vector_grads[4],
    )


def solution(mesh):
    placed = (
        P(("fsdp", "ctx"), "tp"),
        P(),
        P(("fsdp", "ctx"), "tp"),
        P(("fsdp", "ctx"), "tp"),
        P(("fsdp", "ctx"), "tp"),
        P(("fsdp", "ctx"), "tp"),
        P(("fsdp", "ctx"), "tp"),
        P(("fsdp", "ctx"), "tp"),
        P("tp"),
        P("tp"),
        P("tp"),
        P(None, "tp"),
        P(None, "tp"),
        P(("fsdp", "ctx"), "tp"),
    )
    return jax.shard_map(
        body,
        mesh=mesh,
        in_specs=placed,
        out_specs=(
            P(("fsdp", "ctx"), "tp"),
            P(("fsdp", "ctx"), "tp"),
            P(("fsdp", "ctx"), "tp"),
            P(("fsdp", "ctx"), "tp"),
            P(("fsdp", "ctx"), "tp"),
            P(("fsdp", "ctx"), "tp"),
            P(("fsdp", "ctx"), "tp"),
            P(("fsdp", "ctx"), "tp"),
            P("tp"),
            P("tp"),
            P("tp"),
            P(None, "tp"),
            P(None, "tp"),
        ),
        check_vma=False,
    )
```

profile of v0, /device:TPU:8, one launch (start us, length us, event | category | flops | bytes accessed | tf_op | source)
XLA Modules:
  0.0 2354.0 jit_solution(13496302368244385018)
XLA Ops:
  10.7 28.3 %all-gather.11.cloned.1.call-done = bf16[2048,512]{1,0:T(8,128)(2,1)} async-done(((bf16[256,512]{1,0:T(8,128)(2,1)}), bf16[2048,512]{1,0:T(8,128)(2,1)}) %all-gather.11.cloned.1.call-update) | async-done | bytes 2097168 | tf_op jit(solution)/shard_map/all_gather | solution.py:111
  39.0 79.7 %all-gather.9.cloned.1.call-done = bf16[1024,2048]{1,0:T(8,128)(2,1)} async-done(((bf16[1024,512]{1,0:T(8,128)(2,1)}), bf16[1024,2048]{1,0:T(8,128)(2,1)}) %all-gather.9.cloned.1.call-update) | async-done | bytes 4194320 | tf_op jit(solution)/shard_map/all_gather | solution.py:119
  123.9 25.8 %all-gather.13.cloned.1.call-done = bf16[2048,512]{1,0:T(8,128)(2,1)} async-done(((bf16[256,512]{1,0:T(8,128)(2,1)}), bf16[2048,512]{1,0:T(8,128)(2,1)}) %all-gather.13.cloned.1.call-update) | async-done | bytes 2097168 | tf_op jit(solution)/shard_map/all_gather | solution.py:112
  165.3 22.6 all-gather.15.cloned.1.call-done
  194.4 27.7 %collective-permute-done.1 = bf16[1024,1024]{0,1:T(8,128)(2,1)} collective-permute-done((bf16[1024,1024]{0,1:T(8,128)(2,1)}, bf16[1024,1024]{0,1:T(8,128)(2,1)}, u32[]{:S(2)}, u32[]{:S(2)}) %collective-permute-start.1) | collective-permute-done | bytes 2097184 | tf_op jit(solution)/shard_map/ppermute | solution.py:25
  223.0 19.0 pad_maximum_fusion
  242.0 95.1 %while.33 = (s32[]{:T(128)}, bf16[2,512,512]{2,1,0:T(8,128)(2,1)}, f32[2,4,512]{2,1,0:T(4,128)S(1)}, s32[2]{0:T(128)S(1)}, bf16[3072,1024]{0,1:T(8,128)(2,1)}, /...) while((s32[]{:T(128)}, bf16[2,512,512]{2,1,0:T(8,128)(2,1)}, ...), condition=%wide.region_3.4_spmd.clone, body=%wide.region_0.3_spmd.clone.sunk | while | flops 2754082816 | bytes 172079392 | solution.py:175
  250.5 7.8 constant_dynamic-slice_fusion.9
  277.7 10.7 fusion.133
  297.8 7.7 constant_dynamic-slice_fusion.9
  324.9 10.8 fusion.133
  337.2 7.5 fusion.66
  346.3 12.0 all_gather.42
  358.4 13.9 all_gather.41
  372.9 262.9 %all-reduce.6.cloned.1.call-done = f32[1024,2048]{1,0:T(8,128)} async-done(((f32[1024,2048]{1,0:T(8,128)}), f32[1024,2048]{1,0:T(8,128)}) %all-reduce.6.cloned.1.call-update) | async-done | bytes 8388624 | tf_op jit(solution)/shard_map/psum | solution.py:42
  635.8 7.5 fusion.59
  643.4 49.9 %all-gather.19.cloned.1.call-done = bf16[2048,2048]{1,0:T(8,128)(2,1)} async-done(((bf16[256,2048]{1,0:T(8,128)(2,1)}), bf16[2048,2048]{1,0:T(8,128)(2,1)}) %all-gather.19.cloned.1.call-update) | async-done | bytes 8388624 | tf_op jit(solution)/shard_map/all_gather | solution.py:114
  693.3 15.8 fusion.56
  709.1 40.5 %all-gather.21.cloned.1.call-done = bf16[2048,2048]{1,0:T(8,128)(2,1)} async-done(((bf16[256,2048]{1,0:T(8,128)(2,1)}), bf16[2048,2048]{1,0:T(8,128)(2,1)}) %all-gather.21.cloned.1.call-update) | async-done | bytes 8388624 | tf_op jit(solution)/shard_map/all_gather | solution.py:115
  749.6 17.4 fusion.53
  767.7 288.2 %all-reduce.8.cloned.1.call-done = f32[1024,2048]{1,0:T(8,128)} async-done(((f32[1024,2048]{1,0:T(8,128)}), f32[1024,2048]{1,0:T(8,128)}) %all-reduce.8.cloned.1.call-update) | async-done | bytes 8388624 | tf_op jit(solution)/shard_map/psum | solution.py:42
  1055.9 9.4 fusion.58
  1065.3 71.2 %all-gather.23.cloned.1.call-done = bf16[1024,2048]{1,0:T(8,128)(2,1)} async-done(((bf16[1024,512]{1,0:T(8,128)(2,1)}), bf16[1024,2048]{1,0:T(8,128)(2,1)}) %all-gather.23.cloned.1.call-update) | async-done | bytes 4194320 | tf_op jit(solution)/shard_map/all_gather | solution.py:50
  1136.6 7.6 fusion.32
  1147.5 21.0 convert_reduce_fusion.3
  1170.5 13.8 fusion.67
  1184.4 290.0 %all-reduce.10.cloned.1.call-done = f32[1024,2048]{1,0:T(8,128)} async-done(((f32[1024,2048]{1,0:T(8,128)}), f32[1024,2048]{1,0:T(8,128)}) %all-reduce.10.cloned.1.call-update) | async-done | bytes 8388624 | tf_op jit(solution)/shard_map/psum | solution.py:42
  1474.4 11.6 multiply_reduce_fusion.1
  1502.7 160.3 %while.34 = (s32[]{:T(128)}, bf16[1024,512]{0,1:T(8,128)(2,1)}, f32[3072,1024]{0,1:T(8,128)}, bf16[3072,1024]{0,1:T(8,128)(2,1)}, s32[1024]{0:T(1024)S(1)}, /*in...) while((s32[]{:T(128)}, bf16[1024,512]{0,1:T(8,128)(2,1)}, ...), condition=%wide.region_17.18_spmd.clone, body=%wide.region_15.17_spmd.clone.sunk | while | flops 6803159040 | bytes 238131536 | solution.py:261
  1512.0 8.5 fusion.145
  1520.5 12.7 fusion.147
  1533.2 16.1 multiply_reduce_fusion.7
  1549.3 15.8 multiply_convert_fusion.5
  1570.3 12.6 fusion.148
  1591.9 8.5 fusion.145
  1600.4 12.7 fusion.147
  1613.2 16.1 multiply_reduce_fusion.7
  1629.2 15.8 multiply_convert_fusion.5
  1650.2 12.5 fusion.148
  1679.8 105.1 %collective-permute-done.2 = f32[1024,1024]{0,1:T(8,128)S(1)} collective-permute-done((f32[1024,1024]{0,1:T(8,128)S(1)}, f32[1024,1024]{0,1:T(8,128)S(1)}, u32[]{:S(2)}, u32[]{:S(2)}) %collective-permute-start.2) | collective-permute-done | bytes 4194336 | tf_op jit(solution)/shard_map/ppermute | solution.py:22
  1816.3 8.1 fusion.44
  1824.6 17.5 fusion.47
  1842.9 16.6 fusion.54
  1869.1 23.6 %all-reduce.1 = (f32[512]{0:T(512)}, f32[512]{0:T(512)}, f32[2048]{0:T(1024)}, f32[2,512]{1,0:T(2,128)}, f32[4,512]{1,0:T(4,128)}) all-reduce(f32[512]{0:T(512)S(1)} %convert_reduce_fusion.5, f32[512]{0:T(512)S(1)} %convert_reduce_fusion.4, f32[2048]{0:T(1024)S(1)} %copy-done.20, ...), channel_id=1, replica_groups=mesh['fsdp'=4,'ctx'=2,'tp'=4] {'fsdp','ctx'}, use_global_device_ids=true, to_apply=%region_26.27 | all-reduce | flops 6144 | bytes 49152 | tf_op jit(solution)/shard_map/psum | solution.py:297
  1905.9 144.5 %reduce-scatter.8.cloned.1.call-done = f32[1024,512]{1,0:T(8,128)} async-done(((f32[1024,2048]{1,0:T(8,128)}), f32[1024,512]{1,0:T(8,128)}) %reduce-scatter.8.cloned.1.call-update) | async-done | bytes 2097168 | tf_op jit(solution)/shard_map/reduce_scatter | solution.py:278
  2054.0 53.0 %reduce-scatter.16.cloned.1.call-done = f32[256,512]{1,0:T(8,128)} async-done(((f32[2048,512]{1,0:T(8,128)}), f32[256,512]{1,0:T(8,128)}) %reduce-scatter.16.cloned.1.call-update) | async-done | bytes 524304 | tf_op jit(solution)/shard_map/reduce_scatter | solution.py:284
  2107.0 120.0 %reduce-scatter.20.cloned.1.call-done = f32[256,2048]{1,0:T(8,128)} async-done(((f32[2048,2048]{1,0:T(8,128)}), f32[256,2048]{1,0:T(8,128)}) %reduce-scatter.20.cloned.1.call-update) | async-done | bytes 2097168 | tf_op jit(solution)/shard_map/reduce_scatter | solution.py:286
  2227.0 120.0 %reduce-scatter.18.cloned.1.call-done = f32[256,2048]{1,0:T(8,128)} async-done(((f32[2048,2048]{1,0:T(8,128)}), f32[256,2048]{1,0:T(8,128)}) %reduce-scatter.18.cloned.1.call-update) | async-done | bytes 2097168 | tf_op jit(solution)/shard_map/reduce_scatter | solution.py:285
  (205 shorter events, 211.1 us)
Async XLA Ops:
  7.2 31.8 %all-gather.11.cloned.1.call-start = ((), (), s32[]{:S(2)}) async-start(), calls=%async_computation.8 | async-start | bytes 2359296 | tf_op jit(solution)/shard_map/all_gather | solution.py:111
  7.9 110.8 %all-gather.9.cloned.1.call-start = ((), (), s32[]{:S(2)}) async-start(), calls=%async_computation.7 | async-start | bytes 5242880 | tf_op jit(solution)/shard_map/all_gather | solution.py:119
  8.7 141.0 %all-gather.13.cloned.1.call-start = ((), (), s32[]{:S(2)}) async-start(), calls=%async_computation.9 | async-start | bytes 2359296 | tf_op jit(solution)/shard_map/all_gather | solution.py:112
  9.4 178.5 %all-gather.15.cloned.1.call-start = ((), (), s32[]{:S(2)}) async-start(), calls=%async_computation.10 | async-start | bytes 2359296 | tf_op jit(solution)/shard_map/all_gather | solution.py:110
  10.0 327.2 %all-gather.17.cloned.1.call-start = ((), (), s32[]{:S(2)}) async-start(), calls=%async_computation.11 | async-start | bytes 2359296 | tf_op jit(solution)/shard_map/all_gather | solution.py:113
  123.9 41.3 %copy-start.26 = (bf16[512]{0:T(512)(128)(2,1)S(1)}, bf16[512]{0:T(512)(128)(2,1)}, u32[]{:S(2)}) copy-start(bf16[512]{0:T(512)(128)(2,1)} %param.34) | copy-start | bytes 3076
  123.9 41.3 %copy-start.10 = (s32[8192]{0:T(1024)S(1)}, s32[8192]{0:T(1024)}, u32[]{:S(2)}) copy-start(s32[8192]{0:T(1024)} %param.27) | copy-start | bytes 98308
  156.4 65.7 %collective-permute-start.1 = (bf16[1024,1024]{0,1:T(8,128)(2,1)}, bf16[1024,1024]{0,1:T(8,128)(2,1)}, u32[]{:S(2)}, u32[]{:S(2)}) collective-permute-start(bf16[1024,1024]{0,1:T(8,128)(2,1)} %pad_maximum_fusion.1), channel_id=1, source_target_pairs={{4,0},{5,1},{6,2},{7,3},{12,8},{13,9},{14,10},{15,11},{20,16},{21,... | collective-permute-start | bytes 6291464 | tf_op jit(solution)/shard_map/ppermute | solution.py:25
  157.7 65.3 %collective-permute-start = (bf16[1024,1024]{0,1:T(8,128)(2,1)}, bf16[1024,1024]{0,1:T(8,128)(2,1)}, u32[]{:S(2)}, u32[]{:S(2)}) collective-permute-start(bf16[1024,1024]{0,1:T(8,128)(2,1)} %pad_maximum_fusion.1), channel_id=1, source_target_pairs={{0,4},{1,5},{2,6},{3,7},{8,12},{9,13},{10,14},{11,15},{16,20},{17,... | collective-permute-start | bytes 6291464 | tf_op jit(solution)/shard_map/ppermute | solution.py:22
  165.0 470.9 %all-reduce.6.cloned.1.call-start = ((), (), s32[]{:S(2)}) async-start(), calls=%async_computation.12 | async-start | bytes 16777216 | tf_op jit(solution)/shard_map/psum | solution.py:42
  264.6 7.0 copy-start
  311.8 7.0 copy-start
  337.2 9.2 copy-start.23
  337.2 9.2 copy-start.25
  337.2 21.2 copy-start.24
  344.8 348.5 %all-gather.19.cloned.1.call-start = ((), (), s32[]{:S(2)}) async-start(), calls=%async_computation.13 | async-start | bytes 9437184 | tf_op jit(solution)/shard_map/all_gather | solution.py:114
  345.5 404.1 %all-gather.21.cloned.1.call-start = ((), (), s32[]{:S(2)}) async-start(), calls=%async_computation.14 | async-start | bytes 9437184 | tf_op jit(solution)/shard_map/all_gather | solution.py:115
  346.3 709.6 %all-reduce.8.cloned.1.call-start = ((), (), s32[]{:S(2)}) async-start(), calls=%async_computation.15 | async-start | bytes 16777216 | tf_op jit(solution)/shard_map/psum | solution.py:42
  346.3 801.2 %copy-start.21 = (f32[2048]{0:T(1024)}, f32[2048]{0:T(1024)S(1)}, u32[]{:S(2)}) copy-start(f32[2048]{0:T(1024)S(1)} %convert_element_type.106) | copy-start | bytes 24580
  372.3 771.9 %copy-start.13 = (f32[1,2048]{1,0:T(1,128)}, f32[1,2048]{1,0:T(1,128)S(1)}, u32[]{:S(2)}) copy-start(f32[1,2048]{1,0:T(1,128)S(1)} %get-tuple-element.452) | copy-start | bytes 24580
  372.3 1113.7 %copy-start.11 = (f32[1,2048]{1,0:T(1,128)}, f32[1,2048]{1,0:T(1,128)S(1)}, u32[]{:S(2)}) copy-start(f32[1,2048]{1,0:T(1,128)S(1)} %get-tuple-element.451) | copy-start | bytes 24580
  372.9 682.9 %copy-start.18 = (f32[1,2048]{1,0:T(1,128)}, f32[1,2048]{1,0:T(1,128)S(1)}, u32[]{:S(2)}) copy-start(f32[1,2048]{1,0:T(1,128)S(1)} %get-tuple-element.449) | copy-start | bytes 24580
  643.4 842.7 %copy-start.14 = (f32[1024]{0:T(1024)}, f32[1024]{0:T(1024)S(1)}, u32[]{:S(2)}) copy-start(f32[1024]{0:T(1024)S(1)} %get-tuple-element.455) | copy-start | bytes 12292
  643.4 842.7 %copy-start.16 = (f32[1024]{0:T(1024)}, f32[1024]{0:T(1024)S(1)}, u32[]{:S(2)}) copy-start(f32[1024]{0:T(1024)S(1)} %get-tuple-element.456) | copy-start | bytes 12292
  767.0 369.5 %all-gather.23.cloned.1.call-start = ((), (), s32[]{:S(2)}) async-start(), calls=%async_computation.16 | async-start | bytes 5242880 | tf_op jit(solution)/shard_map/all_gather | solution.py:50
  767.6 706.8 %all-reduce.10.cloned.1.call-start = ((), (), s32[]{:S(2)}) async-start(), calls=%async_computation.17 | async-start | bytes 16777216 | tf_op jit(solution)/shard_map/psum | solution.py:42
  1136.6 7.6 copy-start.3
  1144.2 3.4 copy-start.1
  1147.5 21.0 copy-start.2
  1184.4 708.4 %reduce-scatter.10.cloned.1.call-start = ((), (), s32[]{:S(2)}) async-start(), calls=%async_computation.19 | async-start | bytes 4718592 | tf_op jit(solution)/shard_map/reduce_scatter | solution.py:281
  1486.0 5.8 copy-start.28
  1491.8 3.7 copy-start.4
  1570.2 12.6 copy-start.6
  1650.2 12.5 copy-start.6
  1669.9 224.9 %reduce-scatter.12.cloned.1.call-start = ((), (), s32[]{:S(2)}) async-start(), calls=%async_computation.20 | async-start | bytes 4718592 | tf_op jit(solution)/shard_map/reduce_scatter | solution.py:282
  1674.3 118.4 %copy-start.8 = (bf16[1024,2048]{1,0:T(8,128)(2,1)S(1)}, bf16[1024,2048]{1,0:T(8,128)(2,1)}, u32[]{:S(2)}) copy-start(bf16[1024,2048]{1,0:T(8,128)(2,1)} %all-gather.9.cloned.1.call-done) | copy-start | bytes 12582916
  1674.3 110.5 %collective-permute-start.2 = (f32[1024,1024]{0,1:T(8,128)S(1)}, f32[1024,1024]{0,1:T(8,128)S(1)}, u32[]{:S(2)}, u32[]{:S(2)}) collective-permute-start(f32[1024,1024]{0,1:T(8,128)S(1)} %get-tuple-element.445), channel_id=1, source_target_pairs={{0,4},{1,5},{2,6},{3,7},{8,12},{9,13},{10,14},{11,15},{16,20},{17,... | collective-permute-start | bytes 12582920 | tf_op jit(solution)/shard_map/ppermute | solution.py:22
  1678.5 110.7 %collective-permute-start.3 = (f32[1024,1024]{0,1:T(8,128)S(1)}, f32[1024,1024]{0,1:T(8,128)S(1)}, u32[]{:S(2)}, u32[]{:S(2)}) collective-permute-start(f32[1024,1024]{0,1:T(8,128)S(1)} %get-tuple-element.446), channel_id=1, source_target_pairs={{4,0},{5,1},{6,2},{7,3},{12,8},{13,9},{14,10},{15,11},{20,16},{21,... | collective-permute-start | bytes 12582920 | tf_op jit(solution)/shard_map/ppermute | solution.py:25
  1797.0 6.7 copy-start.7
  1797.1 106.8 %reduce-scatter.14.cloned.1.call-start = ((), (), s32[]{:S(2)}) async-start(), calls=%async_computation.21 | async-start | bytes 4718592 | tf_op jit(solution)/shard_map/reduce_scatter | solution.py:283
  1803.7 246.8 %reduce-scatter.8.cloned.1.call-start = ((), (), s32[]{:S(2)}) async-start(), calls=%async_computation.18 | async-start | bytes 10485760 | tf_op jit(solution)/shard_map/reduce_scatter | solution.py:278
  1803.7 4.3 copy-start.27
  1808.1 2.4 copy-start.9
  1816.2 8.4 copy-start.22
  1816.2 290.7 %reduce-scatter.16.cloned.1.call-start = ((), (), s32[]{:S(2)}) async-start(), calls=%async_computation.22 | async-start | bytes 4718592 | tf_op jit(solution)/shard_map/reduce_scatter | solution.py:284
  1824.4 402.6 %reduce-scatter.20.cloned.1.call-start = ((), (), s32[]{:S(2)}) async-start(), calls=%async_computation.24 | async-start | bytes 18874368 | tf_op jit(solution)/shard_map/reduce_scatter | solution.py:286
  1842.2 504.7 %reduce-scatter.18.cloned.1.call-start = ((), (), s32[]{:S(2)}) async-start(), calls=%async_computation.23 | async-start | bytes 18874368 | tf_op jit(solution)/shard_map/reduce_scatter | solution.py:285
  1859.5 9.6 copy-start.20
  (7 other events, 8.0 us)
Sparse Core Ops, SparseCore 0:
  9.9 29.0 all-gather.10
  40.6 78.0 all-gather.8
  120.6 29.0 all-gather.12
  151.4 36.4 all-gather.14
  189.7 35.0 all-gather.16
  344.9 290.8 all-reduce.5
  637.7 55.5 all-gather.18
  695.2 54.3 all-gather.20
  767.2 288.6 all-reduce.7
  1057.3 79.2 all-gather.22
  1184.5 289.8 all-reduce.9
  1670.0 69.4 reduce-scatter.9
  1797.2 51.4 reduce-scatter.11
  1851.9 51.9 reduce-scatter.13
  1906.2 144.1 reduce-scatter.7
  2054.6 52.3 reduce-scatter.15
  2111.0 115.9 reduce-scatter.19
  2231.0 115.9 reduce-scatter.17
where the time goes:
time: 2360 us; the launch traced here: 2350 us
  waiting for transfers between devices  1750 us (74%)
  matrix products  286 us (12%)
  other arithmetic  155 us (7%)
  local copies, waits for them, and re-layouts  79.7 us (3%)
  blocking collectives  49.5 us (2%)
    psum x3, waiting for transfers between devices, reduce_rows(): return lax.psum(partial_value, 'tp')  841 us
    reduce_scatter x1, waiting for transfers between devices, body(): lax.psum_scatter(input_partial, 'tp', scatter_dimension=1, tiled=True)  144 us
    reduce_scatter x1, waiting for transfers between devices, body(): lax.psum_scatter(shrink_grad, ('fsdp', 'ctx'), scatter_dimension=0, tiled...  120 us
    reduce_scatter x1, waiting for transfers between devices, body(): lax.psum_scatter(expand_grad, ('fsdp', 'ctx'), scatter_dimension=0, tiled...  120 us
    ppermute x2, waiting for transfers between devices, padded(): lax.ppermute(lax.slice_in_dim(block, block.shape[dim] - width, None, axis...  106 us
    all_gather x1, waiting for transfers between devices, body(): lax.all_gather(tokens, 'tp', axis=1, tiled=True)  79.7 us
    all_gather x1, waiting for transfers between devices, from_own(): return lax.all_gather(rows, 'tp', axis=1, tiled=True)  71.2 us
    dot_general x6, matrix products, dot_rows(): lax.dot_general(left, right, (((0,), (0,)), ((), ())), preferred_element_...  59.9 us
  transfers between devices with their start and end apart: 22, of which 19 were waited for; matrix products, arithmetic and copies ran while one was open for 10% of the time, Pallas kernels for 0%

commit v1 on v0

v1 whole, which is shorter than its diff:
```python
import functools
import math

import jax
import jax.numpy as jnp
from jax import lax
from jax.experimental import pallas as pl
from jax.experimental.pallas import tpu as pltpu
from jax.sharding import PartitionSpec as P

HD = 128
WIN = 1024
QB = 512
KB = 512

epsilon = 1e-06
hidden_floor = -1e30
score_scale = 1.0 / math.sqrt(HD)
log2_e = 1.0 / math.log(2.0)


def dot_plain(left, right):
    return jnp.dot(left, right, preferred_element_type=jnp.float32)


def dot_rows(left, right):
    return lax.dot_general(
        left, right, (((0,), (0,)), ((), ())), preferred_element_type=jnp.float32
    )


def dot_cols(left, right):
    return lax.dot_general(
        left, right, (((1,), (1,)), ((), ())), preferred_element_type=jnp.float32
    )


def attend_kernel(first, last, q_ref, k_ref, v_ref, low_ref, high_ref, out_ref, lse_ref, vt):
    block = pl.program_id(1)
    rows = q_ref.shape[0]

    @pl.when(block == 0)
    def _():
        vt[...] = v_ref[...].T

    queries = q_ref[...]
    low, high = low_ref[...], high_ref[...]
    places = lax.broadcasted_iota(jnp.int32, (KB, rows), 0)

    def step(number, carry):
        top, total, mixed = carry
        start = pl.multiple_of(number * KB, KB)
        scores = dot_cols(k_ref[pl.ds(start, KB), :], queries) * (score_scale * log2_e)
        keep = (places >= low - start) & (places <= high - start)
        scores = jnp.where(keep, scores, hidden_floor)
        new_top = jnp.maximum(top, jnp.max(scores, axis=0, keepdims=True))
        shrink = jnp.exp2(top - new_top)
        powers = jnp.exp2(scores - new_top)
        total = total * shrink + jnp.sum(powers, axis=0, keepdims=True)
        mixed = mixed * shrink + dot_plain(vt[:, pl.ds(start, KB)], powers.astype(jnp.bfloat16))
        return new_top, total, mixed

    top, total, mixed = lax.fori_loop(
        first[block],
        last[block],
        step,
        (
            jnp.full((1, rows), hidden_floor, jnp.float32),
            jnp.zeros((1, rows), jnp.float32),
            jnp.zeros((HD, rows), jnp.float32),
        ),
    )
    out_ref[...] = (mixed / total).T.astype(out_ref.dtype)
    lse_ref[...] = (top + jnp.log2(total))[None]


def attend(queries, keys, values, low, high, first, last):
    rows, width = queries.shape
    span = keys.shape[0]
    heads = width // HD
    return pl.pallas_call(
        attend_kernel,
        out_shape=(
            jax.ShapeDtypeStruct((rows, width), jnp.bfloat16),
            jax.ShapeDtypeStruct((heads, 1, rows), jnp.float32),
        ),
        grid_spec=pltpu.PrefetchScalarGridSpec(
            num_scalar_prefetch=2,
            grid=(heads, rows // QB),
            in_specs=[
                pl.BlockSpec((QB, HD), lambda h, i, *_: (i, h)),
                pl.BlockSpec((span, HD), lambda h, i, *_: (0, h)),
                pl.BlockSpec((span, HD), lambda h, i, *_: (0, h)),
                pl.BlockSpec((1, QB), lambda h, i, *_: (0, i)),
                pl.BlockSpec((1, QB), lambda h, i, *_: (0, i)),
            ],
            out_specs=[
                pl.BlockSpec((QB, HD), lambda h, i, *_: (i, h)),
                pl.BlockSpec((1, 1, QB), lambda h, i, *_: (h, 0, i)),
            ],
            scratch_shapes=[pltpu.VMEM((HD, span), jnp.bfloat16)],
        ),
        compiler_params=pltpu.CompilerParams(vmem_limit_bytes=32 << 20),
        cost_estimate=pl.CostEstimate(
            flops=3 * rows * span * width,
            bytes_accessed=2 * (2 * rows + 2 * span) * width,
            transcendentals=rows * span * heads,
        ),
        name="attend",
    )(first, last, queries, keys, values, low, high)


def attend_back_kernel(
    first, last, q_ref, k_ref, v_ref, o_ref, g_ref, lse_ref, low_ref, high_ref,
    dq_ref, dk_ref, dv_ref, kt, dk_sum, dv_sum,
):
    block = pl.program_id(1)
    rows = q_ref.shape[0]

    @pl.when(block == 0)
    def _():
        kt[...] = k_ref[...].T
        dk_sum[...] = jnp.zeros_like(dk_sum)
        dv_sum[...] = jnp.zeros_like(dv_sum)

    queries = q_ref[...]
    upstream = g_ref[...]
    lse = lse_ref[0]
    low, high = low_ref[...], high_ref[...]
    places = lax.broadcasted_iota(jnp.int32, (KB, rows), 0)
    product = upstream.astype(jnp.float32) * o_ref[...].astype(jnp.float32)
    delta = jnp.sum(product.T, axis=0, keepdims=True)

    def step(number, dq):
        start = pl.multiple_of(number * KB, KB)
        window = pl.ds(start, KB)
        scores = dot_cols(k_ref[window, :], queries) * (score_scale * log2_e)
        keep = (places >= low - start) & (places <= high - start)
        probs = jnp.exp2(jnp.where(keep, scores - lse, hidden_floor))
        prob_grad = dot_cols(v_ref[window, :], upstream)
        score_grad = (probs * (prob_grad - delta)).astype(jnp.bfloat16)
        dv_sum[window, :] += dot_plain(probs.astype(jnp.bfloat16), upstream)
        dk_sum[window, :] += dot_plain(score_grad, queries)
        return dq + dot_plain(kt[:, window], score_grad)

    dq = lax.fori_loop(
        first[block], last[block], step, jnp.zeros((HD, rows), jnp.float32)
    )
    dq_ref[...] = (dq * score_scale).T.astype(dq_ref.dtype)

    @pl.when(block == pl.num_programs(1) - 1)
    def _():
        dk_ref[...] = (dk_sum[...] * score_scale).astype(dk_ref.dtype)
        dv_ref[...] = dv_sum[...].astype(dv_ref.dtype)


def attend_back(queries, keys, values, out, upstream, lse, low, high, first, last, kind):
    rows, width = queries.shape
    span = keys.shape[0]
    heads = width // HD
    row_spec = pl.BlockSpec((QB, HD), lambda h, i, *_: (i, h))
    key_spec = pl.BlockSpec((span, HD), lambda h, i, *_: (0, h))
    mark_spec = pl.BlockSpec((1, QB), lambda h, i, *_: (0, i))
    return pl.pallas_call(
        attend_back_kernel,
        out_shape=(
            jax.ShapeDtypeStruct((rows, width), jnp.bfloat16),
            jax.ShapeDtypeStruct((span, width), kind),
            jax.ShapeDtypeStruct((span, width), kind),
        ),
        grid_spec=pltpu.PrefetchScalarGridSpec(
            num_scalar_prefetch=2,
            grid=(heads, rows // QB),
            in_specs=[
                row_spec, key_spec, key_spec, row_spec, row_spec,
                pl.BlockSpec((1, 1, QB), lambda h, i, *_: (h, 0, i)),
                mark_spec, mark_spec,
            ],
            out_specs=[row_spec, key_spec, key_spec],
            scratch_shapes=[
                pltpu.VMEM((HD, span), jnp.bfloat16),
                pltpu.VMEM((span, HD), jnp.float32),
                pltpu.VMEM((span, HD), jnp.float32),
            ],
        ),
        compiler_params=pltpu.CompilerParams(vmem_limit_bytes=32 << 20),
        cost_estimate=pl.CostEstimate(
            flops=8 * rows * span * width,
            bytes_accessed=2 * (4 * rows + 4 * span) * width,
            transcendentals=rows * span * heads,
        ),
        name="attend_back",
    )(first, last, queries, keys, values, out, upstream, lse, low, high)


def key_bounds(query_ids, key_ids, offset):
    rows, span = query_ids.shape[0], key_ids.shape[0]
    start = jnp.sum(key_ids[:, None] < query_ids[None, :], axis=0, dtype=jnp.int32)
    stop = jnp.sum(key_ids[:, None] <= query_ids[None, :], axis=0, dtype=jnp.int32)
    places = jnp.arange(rows, dtype=jnp.int32) + offset
    low = jnp.maximum(start, places - WIN)
    high = jnp.minimum(stop - 1, places + WIN)
    first = jnp.min(low.reshape(-1, QB), axis=1) // KB
    last = jnp.max(high.reshape(-1, QB), axis=1) // KB + 1
    return low[None], high[None], first, last


def padded(block, width):
    count = lax.axis_size("ctx")
    forward = [(i, i + 1) for i in range(count - 1)]
    backward = [(target, source) for source, target in forward]
    below = lax.ppermute(block[block.shape[0] - width :], "ctx", forward)
    above = lax.ppermute(block[:width], "ctx", backward)
    return jnp.concatenate([below, block, above], axis=0)


def swap_halves(own, other):
    got = lax.ppermute(other, "ctx", [(0, 1), (1, 0)])
    here = lax.axis_index("ctx") == 0
    return jnp.where(here, own, got), jnp.where(here, got, own)


def heads_in(block):
    half = block.shape[1] // 2
    here = lax.axis_index("ctx") == 0
    left, right = block[:, :half], block[:, half:]
    pair = swap_halves(jnp.where(here, left, right), jnp.where(here, right, left))
    return jnp.concatenate(pair, axis=0)


def heads_out(block):
    half = block.shape[0] // 2
    here = lax.axis_index("ctx") == 0
    top, bottom = block[:half], block[half:]
    pair = swap_halves(jnp.where(here, top, bottom), jnp.where(here, bottom, top))
    return jnp.concatenate(pair, axis=1)


def norm_parts(rows):
    mean = jnp.mean(rows, axis=-1, keepdims=True)
    square = jnp.mean(rows * rows, axis=-1, keepdims=True)
    inverse = lax.rsqrt(square - mean * mean + epsilon)
    return (rows - mean) * inverse, inverse


def norm_back(upstream, normed, inverse, gain):
    scaled = upstream * gain
    first_mean = jnp.mean(scaled, axis=-1, keepdims=True)
    second_mean = jnp.mean(scaled * normed, axis=-1, keepdims=True)
    return inverse * (scaled - first_mean - normed * second_mean)


def gelu_tanh(values):
    return jax.nn.gelu(values, approximate=True)


def gather_rows(rows):
    return lax.all_gather(rows, "tp", axis=0, tiled=True)


def scatter_rows(partial_rows):
    low = partial_rows.astype(jnp.bfloat16)
    return lax.psum_scatter(low, "tp", scatter_dimension=0, tiled=True).astype(jnp.float32)


def spread(block):
    return lax.all_to_all(block, "tp", split_axis=0, concat_axis=1, tiled=True)


def unspread(block):
    return lax.all_to_all(block, "tp", split_axis=1, concat_axis=0, tiled=True)


def body(
    tokens,
    segments,
    query_weight,
    key_weight,
    value_weight,
    output_weight,
    expand_weight,
    shrink_weight,
    query_bias,
    value_bias,
    hidden_bias,
    norm_gains,
    row_biases,
    out_grad,
):
    rows = tokens.shape[0]
    head_cols = query_weight.shape[1]
    plane = ("fsdp", "ctx")
    ctx_size = lax.axis_size("ctx")
    own_rows = rows // lax.axis_size("tp")
    by_heads = ctx_size == 2 and (head_cols // HD) % 2 == 0

    def weight_rows(weight):
        return lax.all_gather(weight, plane, axis=0, tiled=True)

    wide_qkv = weight_rows(jnp.concatenate([query_weight, key_weight, value_weight], axis=1))
    wide_tokens = lax.all_gather(tokens, "tp", axis=1, tiled=True)
    full_output = weight_rows(output_weight)
    full_expand = weight_rows(expand_weight)
    full_shrink = weight_rows(shrink_weight)
    gains = lax.all_gather(norm_gains, "tp", axis=1, tiled=True).astype(jnp.float32)
    biases = lax.all_gather(row_biases, "tp", axis=1, tiled=True).astype(jnp.float32)
    upstream = spread(out_grad).astype(jnp.float32)

    qkv_bias = jnp.concatenate([query_bias, jnp.zeros_like(query_bias), value_bias])
    qkv = (dot_plain(wide_tokens, wide_qkv) + qkv_bias.astype(jnp.float32)).astype(jnp.bfloat16)
    queries, keys, values = (
        qkv[:, i * head_cols : (i + 1) * head_cols] for i in range(3)
    )
    block_index = lax.axis_index("fsdp") * ctx_size + lax.axis_index("ctx")
    if by_heads:
        queries, keys, values = heads_in(queries), heads_in(keys), heads_in(values)
        stream_ids = lax.dynamic_slice_in_dim(
            segments, lax.axis_index("fsdp") * ctx_size * rows, ctx_size * rows, 0
        )
        bounds = key_bounds(stream_ids, stream_ids, 0)
    else:
        keys, values = padded(keys, WIN), padded(values, WIN)
        ids = jnp.concatenate(
            [
                jnp.full((WIN,), -1, jnp.int32),
                segments,
                jnp.full((WIN,), jnp.iinfo(jnp.int32).max, jnp.int32),
            ]
        )
        key_ids = lax.dynamic_slice_in_dim(ids, block_index * rows, rows + 2 * WIN, 0)
        bounds = key_bounds(key_ids[WIN : WIN + rows], key_ids, WIN)
    attended_heads, lse = attend(queries, keys, values, *bounds)
    attended = heads_out(attended_heads) if by_heads else attended_heads

    own_start = lax.axis_index("tp") * own_rows
    own_tokens = lax.dynamic_slice_in_dim(wide_tokens, own_start, own_rows, 0)
    branch = scatter_rows(dot_cols(attended, full_output)) + biases[0]
    normed_one, inverse_one = norm_parts(own_tokens.astype(jnp.float32) + branch)
    first_norm = normed_one * gains[0] + biases[1]
    norm_low = gather_rows(first_norm.astype(jnp.bfloat16))
    hidden = dot_plain(norm_low, full_expand) + hidden_bias.astype(jnp.float32)
    activated = gelu_tanh(hidden).astype(jnp.bfloat16)
    second_sum = first_norm + scatter_rows(dot_cols(activated, full_shrink)) + biases[2]
    normed_two, inverse_two = norm_parts(second_sum)
    mixed = unspread((normed_two * gains[1] + biases[3]).astype(jnp.bfloat16))

    grad_second = norm_back(upstream, normed_two, inverse_two, gains[1])
    gain_two_grad = jnp.sum(upstream * normed_two, axis=0)
    shift_two_grad = jnp.sum(upstream, axis=0)
    ffn_own = grad_second.astype(jnp.bfloat16)
    ffn_bias_grad = jnp.sum(ffn_own.astype(jnp.float32), axis=0)
    ffn_low = gather_rows(ffn_own)

    def owner_sum(grad):
        return lax.psum_scatter(
            grad.astype(jnp.bfloat16), plane, scatter_dimension=0, tiled=True
        ).astype(jnp.float32)

    shrink_grad = owner_sum(dot_rows(ffn_low, activated))
    _, gelu_pull = jax.vjp(gelu_tanh, hidden)
    hidden_low = gelu_pull(dot_plain(ffn_low, full_shrink))[0].astype(jnp.bfloat16)
    hidden_bias_grad = jnp.sum(hidden_low.astype(jnp.float32), axis=0)
    grad_first = grad_second + scatter_rows(dot_cols(hidden_low, full_expand))
    expand_grad = owner_sum(dot_rows(norm_low, hidden_low))
    gain_one_grad = jnp.sum(grad_first * normed_one, axis=0)
    shift_one_grad = jnp.sum(grad_first, axis=0)
    grad_inner = norm_back(grad_first, normed_one, inverse_one, gains[0])
    branch_own = grad_inner.astype(jnp.bfloat16)
    branch_bias_grad = jnp.sum(branch_own.astype(jnp.float32), axis=0)
    branch_low = gather_rows(branch_own)
    output_grad = owner_sum(dot_rows(branch_low, attended))
    attended_grad = dot_plain(branch_low, full_output).astype(jnp.bfloat16)

    if by_heads:
        grads = attend_back(
            queries, keys, values, attended_heads, heads_in(attended_grad), lse, *bounds,
            jnp.bfloat16,
        )
        query_low, key_low, value_low = (heads_out(grad) for grad in grads)
    else:
        query_low, key_ext, value_ext = attend_back(
            queries, keys, values, attended_heads, attended_grad, lse, *bounds, jnp.float32
        )

        def fold(ext):
            edges = jnp.concatenate([ext[:WIN], ext[WIN + rows :]], axis=0)
            around = padded(edges, WIN)
            own = ext[WIN : WIN + rows]
            own = own.at[:WIN].add(around[:WIN]).at[rows - WIN :].add(around[3 * WIN :])
            return own.astype(jnp.bfloat16)

        key_low, value_low = fold(key_ext), fold(value_ext)
    qkv_low = jnp.concatenate([query_low, key_low, value_low], axis=1)
    qkv_grad = owner_sum(dot_rows(wide_tokens, qkv_low))
    input_partial = dot_cols(qkv_low, wide_qkv)
    own_part = lax.dynamic_slice_in_dim(input_partial, own_start, own_rows, 0) + grad_inner
    input_partial = lax.dynamic_update_slice_in_dim(input_partial, own_part, own_start, 0)
    input_grad = lax.psum_scatter(
        input_partial.astype(jnp.bfloat16), "tp", scatter_dimension=1, tiled=True
    )
    row_vectors = jnp.stack(
        [
            gain_one_grad, gain_two_grad,
            branch_bias_grad, shift_one_grad, ffn_bias_grad, shift_two_grad,
        ]
    )
    own_vectors = lax.psum_scatter(row_vectors, "tp", scatter_dimension=1, tiled=True)
    qkv_sums = jnp.sum(qkv_low.astype(jnp.float32), axis=0)
    own_vectors, qkv_sums, hidden_bias_grad = lax.psum(
        (own_vectors, qkv_sums, hidden_bias_grad), plane
    )
    return (
        mixed,
        input_grad,
        qkv_grad[:, :head_cols],
        qkv_grad[:, head_cols : 2 * head_cols],
        qkv_grad[:, 2 * head_cols :],
        output_grad,
        expand_grad,
        shrink_grad,
        qkv_sums[:head_cols],
        qkv_sums[2 * head_cols :],
        hidden_bias_grad,
        own_vectors[:2],
        own_vectors[2:],
    )


def solution(mesh):
    rows, whole, cols = P(("fsdp", "ctx"), "tp"), P(), P("tp")
    wide = P(None, "tp")
    return jax.shard_map(
        body,
        mesh=mesh,
        in_specs=(rows, whole) + (rows,) * 6 + (cols,) * 3 + (wide,) * 2 + (rows,),
        out_specs=(rows,) * 8 + (cols,) * 3 + (wide,) * 2,
        check_vma=False,
    )
```

time: 2360 us -> 1290 us (0.55)
  waiting for transfers between devices: 1750 us -> 922 us
  matrix products: 286 us -> 136 us
  other arithmetic: 155 us -> 42.2 us
  local copies, waits for them, and re-layouts: 79.7 us -> 22.6 us
  Pallas kernels: 0 us -> 52.8 us
  blocking collectives: 49.5 us -> 79.1 us
    psum x3 -> x0, waiting for transfers between devices: 841 us -> none  [reduce_rows(): return lax.psum(partial_value, 'tp')]
    dot_general x14 -> x0, matrix products: 119 us -> none  [the longest x2 32.2 us: backward_block(): jnp.einsum('qhd,khd->hqk', upstream_rows, value_rows, preferred_element_t...]
    all_gather x8, waiting for transfers between devices: 318 us -> 421 us  [the longest x3 205 us: gather_rows(): return lax.all_gather(rows, 'tp', axis=0, tiled=True)]
    reduce_scatter x7 -> x9, waiting for transfers between devices: 444 us -> 345 us  [the longest x3 171 us: scatter_rows(): lax.psum_scatter(low, 'tp', scatter_dimension=0, tiled=True)]
    pallas_call x0 -> x2, Pallas kernels: none -> 52.8 us  [the longest x1 29.7 us: attend_back(): pl.pallas_call(attend_back_kernel, out_shape=(jax.ShapeDtypeStruct((rows,...]
    all_to_all x0 -> x1, waiting for transfers between devices: none -> 48.1 us  [spread(): return lax.all_to_all(block, 'tp', split_axis=0, concat_axis=1, tiled=True)]
    ppermute x4 -> x8, waiting for transfers between devices: 138 us -> 105 us  [swap_halves(): got = lax.ppermute(other, 'ctx', [(0, 1), (1, 0)])]
    all_to_all x0 -> x1, blocking collectives: none -> 29.8 us  [unspread(): return lax.all_to_all(block, 'tp', split_axis=1, concat_axis=0, tiled=True)]
  transfers between devices with their start and end apart: 22 -> 26, of which waited for: 19 -> 22; matrix products, arithmetic and copies ran while one was open for 10% -> 9% of each run, Pallas kernels for 0% -> 4%
where the time goes in v1:
time: 1290 us
  waiting for transfers between devices  922 us (71%)
  matrix products  136 us (11%)
  blocking collectives  79.1 us (6%)
  Pallas kernels  52.8 us (4%)
  other arithmetic  42.2 us (3%)
  local copies, waits for them, and re-layouts  22.6 us (2%)
  starting transfers between devices  15.8 us (1%)
  between operations  15.1 us (1%)
    all_gather x3, waiting for transfers between devices, gather_rows(): return lax.all_gather(rows, 'tp', axis=0, tiled=True)  205 us
    reduce_scatter x3, waiting for transfers between devices, scatter_rows(): lax.psum_scatter(low, 'tp', scatter_dimension=0, tiled=True)  171 us
    all_gather x4, waiting for transfers between devices, weight_rows(): return lax.all_gather(weight, plane, axis=0, tiled=True)  143 us
    ppermute x8, waiting for transfers between devices, swap_halves(): got = lax.ppermute(other, 'ctx', [(0, 1), (1, 0)])  105 us
    reduce_scatter x4, waiting for transfers between devices, owner_sum(): lax.psum_scatter(grad.astype(jnp.bfloat16), plane, scatter_dimension=0, t...  83.2 us
    reduce_scatter x1, waiting for transfers between devices, body(): lax.psum_scatter(input_partial.astype(jnp.bfloat16), 'tp', scatter_dimens...  75.2 us
    all_gather x1, waiting for transfers between devices, body(): wide_tokens = lax.all_gather(tokens, 'tp', axis=1, tiled=True)  73.3 us
    dot_general x4, matrix products, dot_plain(): return jnp.dot(left, right, preferred_element_type=jnp.float32)  48.3 us
  transfers between devices with their start and end apart: 26, of which 22 were waited for; matrix products, arithmetic and copies ran while one was open for 9% of the time, Pallas kernels for 4%

profile of v1, /device:TPU:8, one launch (start us, length us, event | category | flops | bytes accessed | tf_op | source)
XLA Modules:
  0.0 1286.0 jit_solution(8033347940832402007)
XLA Ops:
  11.5 4.0 convert_reduce_fusion
  15.6 73.3 %all-gather.9.cloned.1.call-done = bf16[1024,2048]{1,0:T(8,128)(2,1)} async-done(((bf16[1024,512]{1,0:T(8,128)(2,1)}), bf16[1024,2048]{1,0:T(8,128)(2,1)}) %all-gather.9.cloned.1.call-update) | async-done | bytes 4194320 | tf_op jit(solution)/shard_map/all_gather | solution.py:301
  88.9 49.2 %all-gather.11.cloned.1.call-done = bf16[2048,1536]{1,0:T(8,128)(2,1)} async-done(((bf16[256,1536]{1,0:T(8,128)(2,1)}), bf16[2048,1536]{1,0:T(8,128)(2,1)}) %all-gather.11.cloned.1.call-update) | async-done | bytes 6291472 | tf_op jit(solution)/shard_map/all_gather | solution.py:298
  138.1 10.0 fusion.8
  150.5 15.6 %collective-permute-done.2 = bf16[1024,256]{1,0:T(8,128)(2,1)S(1)} collective-permute-done((bf16[1024,256]{1,0:T(8,128)(2,1)S(1)}, bf16[1024,256]{1,0:T(8,128)(2,1)S(1)}, u32[]{:S(2)}, u32[]{:S(2)}) %collective-permute-start.2) | collective-permute-done | bytes 524320 | tf_op jit(solution)/shard_map/ppermute | solution.py:218
  166.1 15.0 %collective-permute-done = bf16[1024,256]{1,0:T(8,128)(2,1)S(1)} collective-permute-done((bf16[1024,256]{1,0:T(8,128)(2,1)S(1)}, bf16[1024,256]{1,0:T(8,128)(2,1)S(1)}, u32[]{:S(2)}, u32[]{:S(2)}) %collective-permute-start) | collective-permute-done | bytes 524320 | tf_op jit(solution)/shard_map/ppermute | solution.py:218
  182.4 12.8 collective-permute-done.1
  195.4 23.1 %attend.1 = (bf16[2048,256]{1,0:T(8,128)(2,1)S(1)}, f32[2,1,2048]{2,1,0:T(1,128)S(1)}) custom-call(s32[4]{0:T(128)S(1)} %get-tuple-element.119.first, s32[4]{0:T(128)S(1)} %get-tuple-element.120.last, bf16[2048,256]{1,0:T(8,128)(2,1)S(1)} %get-tuple-element.121.q_ref, bf16[2048,256]{1,0:T(8,128)(2,1)S(1)} %pad_maximum_fusion.1.k_ref, ...), custom_call_target="tpu_custom_call" | custom-call | flops 3221225472 | bytes 4194304 | tf_op jit(solution)/shard_map/attend/pallas_call | solution.py:81
  219.2 12.9 %collective-permute-done.3 = bf16[1024,256]{1,0:T(8,128)(2,1)S(1)} collective-permute-done((bf16[1024,256]{1,0:T(8,128)(2,1)S(1)}, bf16[1024,256]{1,0:T(8,128)(2,1)S(1)}, u32[]{:S(2)}, u32[]{:S(2)}) %collective-permute-start.3) | collective-permute-done | bytes 524320 | tf_op jit(solution)/shard_map/ppermute | solution.py:218
  232.2 6.3 convolution_convert_fusion.5
  239.2 12.1 all_gather.34
  251.4 13.3 %all_gather.33 = bf16[4,2048]{1,0:T(4,128)(2,1)S(1)} all-gather(bf16[4,512]{1,0:T(4,128)(2,1)S(1)} %copy-done.31), channel_id=1, replica_groups=mesh['fsdp'=4,'ctx'=2,'tp'=4] {'tp'}, dimensions={1}, use_global_device_ids=true | all-gather | bytes 20480 | tf_op jit(solution)/shard_map/all_gather | solution.py:306
  264.7 51.1 %reduce-scatter.10.cloned.1.call-done = bf16[256,2048]{1,0:T(8,128)(2,1)} async-done(((bf16[1024,2048]{1,0:T(8,128)(2,1)}), bf16[256,2048]{1,0:T(8,128)(2,1)}) %reduce-scatter.10.cloned.1.call-update) | async-done | bytes 1048592 | tf_op jit(solution)/shard_map/reduce_scatter | solution.py:263
  318.0 3.2 fusion.12
  322.2 50.3 %all-gather.17.cloned.1.call-done = bf16[2048,2048]{1,0:T(8,128)(2,1)} async-done(((bf16[256,2048]{1,0:T(8,128)(2,1)}), bf16[2048,2048]{1,0:T(8,128)(2,1)}) %all-gather.17.cloned.1.call-update) | async-done | bytes 8388624 | tf_op jit(solution)/shard_map/all_gather | solution.py:298
  372.5 80.2 %all-gather.15.cloned.1.call-done = bf16[1024,2048]{1,0:T(8,128)(2,1)} async-done(((bf16[256,2048]{1,0:T(8,128)(2,1)}), bf16[1024,2048]{1,0:T(8,128)(2,1)}) %all-gather.15.cloned.1.call-update) | async-done | bytes 4194320 | tf_op jit(solution)/shard_map/all_gather | solution.py:258
  452.7 14.5 %fusion.24 = f32[1024,2048]{1,0:T(8,128)} fusion(bf16[1024,2048]{1,0:T(8,128)(2,1)} %all-gather.15.cloned.1.call-done, bf16[2048,2048]{1,0:T(8,128)(2,1)} %all-gather.17.cloned.1.call-done), kind=kOutput, calls=%fused_computation.123 | convolution fusion | flops 8589934592 | bytes 20971520 | tf_op jit(solution)/shard_map/dot_general | solution.py:23
  467.3 43.1 %all-gather.19.cloned.1.call-done = bf16[2048,2048]{1,0:T(8,128)(2,1)} async-done(((bf16[256,2048]{1,0:T(8,128)(2,1)}), bf16[2048,2048]{1,0:T(8,128)(2,1)}) %all-gather.19.cloned.1.call-update) | async-done | bytes 8388624 | tf_op jit(solution)/shard_map/all_gather | solution.py:298
  510.4 16.8 %convolution_convert_fusion.4 = bf16[1024,2048]{1,0:T(8,128)(2,1)} fusion(bf16[2048,2048]{1,0:T(8,128)(2,1)} %all-gather.19.cloned.1.call-done, f32[1024,2048]{1,0:T(8,128)} %fusion.24, f32[2048]{0:T(1024)S(1)} %convert_element_type.137), kind=kOutput, calls=%fused_computation.20 | convolution fusion | flops 8613003264 | bytes 20979712 | tf_op jit(solution)/shard_map/dot_general | solution.py:33
  527.2 5.1 all-to-all-start.1
  532.5 48.1 %all-to-all-done.1 = bf16[4,256,512]{2,1,0:T(8,128)(2,1)S(1)} async-done(((bf16[4,256,512]{2,1,0:T(8,128)(2,1)}), bf16[4,256,512]{2,1,0:T(8,128)(2,1)S(1)}, u32[]{:S(2)}, u32[]{:S(2)}) %all-to-all-start.1) | async-done | bytes 1048608 | tf_op jit(solution)/shard_map/all_to_all | solution.py:267
  583.5 42.3 %reduce-scatter.12.cloned.1.call-done = bf16[256,2048]{1,0:T(8,128)(2,1)} async-done(((bf16[1024,2048]{1,0:T(8,128)(2,1)}), bf16[256,2048]{1,0:T(8,128)(2,1)}) %reduce-scatter.12.cloned.1.call-update) | async-done | bytes 1048592 | tf_op jit(solution)/shard_map/reduce_scatter | solution.py:263
  629.2 3.9 convert_reduce_fusion.4
  633.6 76.0 %all-gather.21.cloned.1.call-done = bf16[1024,2048]{1,0:T(8,128)(2,1)} async-done(((bf16[256,2048]{1,0:T(8,128)(2,1)}), bf16[1024,2048]{1,0:T(8,128)(2,1)}) %all-gather.21.cloned.1.call-update) | async-done | bytes 4194320 | tf_op jit(solution)/shard_map/all_gather | solution.py:258
  709.6 18.5 %convert_reduce_fusion.2 = (f32[2048]{0:T(1024)S(1)}, bf16[1024,2048]{1,0:T(8,128)(2,1)S(1)}) fusion(f32[1024,2048]{1,0:T(8,128)} %fusion.24, f32[2048]{0:T(1024)S(1)} %convert_element_type.137, bf16[1024,2048]{1,0:T(8,128)(2,1)} %all-gather.21.cloned.1.call-done, bf16[2048,2048]{1,0:T(8,128)(2,1)} %all-gather.19.cloned.1.call-done), kind=kOutput, calls=%fused_computation.11 | convolution fusion | flops 8638167040 | bytes 25182208 | tf_op jit(solution)/shard_map/dot_general | solution.py:23
  730.1 12.6 convolution_convert_fusion.3
  743.0 77.9 %reduce-scatter.14.cloned.1.call-done = bf16[256,2048]{1,0:T(8,128)(2,1)} async-done(((bf16[1024,2048]{1,0:T(8,128)(2,1)}), bf16[256,2048]{1,0:T(8,128)(2,1)}) %reduce-scatter.14.cloned.1.call-update) | async-done | bytes 1048592 | tf_op jit(solution)/shard_map/reduce_scatter | solution.py:263
  820.9 2.9 multiply_reduce_fusion.1
  823.8 4.0 convert_reduce_fusion.5
  827.9 15.1 %convolution_convert_fusion = bf16[2048,2048]{1,0:T(8,128)(2,1)} fusion(bf16[1024,2048]{1,0:T(8,128)(2,1)} %all-gather.21.cloned.1.call-done, f32[1024,2048]{1,0:T(8,128)} %fusion.24, f32[2048]{0:T(1024)S(1)} %convert_element_type.137), kind=kOutput, calls=%fused_computation.13 | convolution fusion | flops 8615100416 | bytes 20979712 | tf_op jit(solution)/shard_map/dot_general | solution.py:27
  843.3 14.1 %convolution_convert_fusion.1 = bf16[2048,2048]{1,0:T(8,128)(2,1)} fusion(bf16[1024,2048]{1,0:T(8,128)(2,1)} %all-gather.15.cloned.1.call-done, bf16[1024,2048]{1,0:T(8,128)(2,1)} %copy-done.37), kind=kOutput, calls=%fused_computation.14 | convolution fusion | flops 8594128896 | bytes 16777216 | tf_op jit(solution)/shard_map/dot_general | solution.py:27
  857.5 49.2 %all-gather.23.cloned.1.call-done = bf16[1024,2048]{1,0:T(8,128)(2,1)} async-done(((bf16[256,2048]{1,0:T(8,128)(2,1)}), bf16[1024,2048]{1,0:T(8,128)(2,1)}) %all-gather.23.cloned.1.call-update) | async-done | bytes 4194320 | tf_op jit(solution)/shard_map/all_gather | solution.py:258
  906.7 5.2 convolution_convert_fusion.7
  914.5 11.3 collective-permute-done.4
  931.2 29.7 %attend_back.1 = (bf16[2048,256]{1,0:T(8,128)(2,1)S(1)}, bf16[2048,256]{1,0:T(8,128)(2,1)S(1)}, bf16[2048,256]{1,0:T(8,128)(2,1)S(1)}) custom-call(s32[4]{0:T(128)S(1)} %copy-done.13, s32[4]{0:T(128)S(1)} %copy-done.15, bf16[2048,256]{1,0:T(8,128)(2,1)S(1)} %copy-done.5, bf16[2048,256]{1,0:T(8,128)(2,1)S(1)} %copy-done.3, bf16[2048,256]{1,0:T(8,128)(2,1)S(1)} %copy-done.7, ...), custom_call_target="tpu_custom_call" | custom-call | flops 8589934592 | bytes 8388608 | tf_op jit(solution)/shard_map/attend_back/pallas_call | solution.py:164
  963.4 3.7 convolution_convert_fusion.6
  969.7 9.4 collective-permute-done.5
  980.6 27.5 %collective-permute-done.6 = bf16[1024,256]{1,0:T(8,128)(2,1)S(1)} collective-permute-done((bf16[1024,256]{1,0:T(8,128)(2,1)S(1)}, bf16[1024,256]{1,0:T(8,128)(2,1)S(1)}, u32[]{:S(2)}, u32[]{:S(2)}) %collective-permute-start.6) | collective-permute-done | bytes 524320 | tf_op jit(solution)/shard_map/ppermute | solution.py:218
  1012.4 8.8 fusion.7
  1021.3 10.6 fusion.25
  1036.4 29.8 %all_to_all.32 = bf16[256,4,512]{2,0,1:T(8,128)(2,1)} all-to-all(bf16[256,4,512]{2,0,1:T(8,128)(2,1)S(1)} %bitcast.63), channel_id=1, replica_groups=mesh['fsdp'=4,'ctx'=2,'tp'=4] {'tp'}, dimensions={1} | all-to-all | bytes 2097152 | tf_op jit(solution)/shard_map/all_to_all | solution.py:271
  1066.2 2.9 convert_element_type.161
  1069.1 2.8 convert_element_type.159
  1072.4 15.4 %reduce-scatter.26.cloned.1.call-done = f32[6,512]{1,0:T(8,128)} async-done(((f32[6,2048]{1,0:T(8,128)}), f32[6,512]{1,0:T(8,128)}) %reduce-scatter.26.cloned.1.call-update) | async-done | bytes 12304 | tf_op jit(solution)/shard_map/reduce_scatter | solution.py:407
  1087.8 24.0 %all-reduce = (f32[1536]{0:T(1024)S(1)}, f32[2048]{0:T(1024)}, f32[6,512]{1,0:T(8,128)S(1)}) all-reduce(f32[1536]{0:T(1024)S(1)} %convert_reduce_fusion.3, f32[2048]{0:T(1024)S(1)} %get-tuple-element.85, f32[6,512]{1,0:T(8,128)} %reduce-scatter.26.cloned.1.call-done), channel_id=1, replica_groups=mesh['fsdp'=4,'ctx'=2,'tp'=4] {'fsdp','ctx'}, use_global_device_ids=true, to_apply=%region_21.22 | all-reduce | flops 6656 | bytes 53248 | tf_op jit(solution)/shard_map/psum | solution.py:409
  1113.5 19.6 %reduce-scatter.20.cloned.1.call-done = bf16[256,512]{1,0:T(8,128)(2,1)} async-done(((bf16[2048,512]{1,0:T(8,128)(2,1)}), bf16[256,512]{1,0:T(8,128)(2,1)}) %reduce-scatter.20.cloned.1.call-update) | async-done | bytes 262160 | tf_op jit(solution)/shard_map/reduce_scatter | solution.py:355
  1135.0 63.6 %reduce-scatter.18.cloned.1.call-done = bf16[256,1536]{0,1:T(8,128)(2,1)} async-done(((bf16[2048,1536]{0,1:T(8,128)(2,1)}), bf16[256,1536]{0,1:T(8,128)(2,1)}) %reduce-scatter.18.cloned.1.call-update) | async-done | bytes 786448 | tf_op jit(solution)/shard_map/reduce_scatter | solution.py:355
  1202.8 75.2 %reduce-scatter.16.cloned.1.call-done = bf16[1024,512]{1,0:T(8,128)(2,1)} async-done(((bf16[1024,2048]{1,0:T(8,128)(2,1)}), bf16[1024,512]{1,0:T(8,128)(2,1)}) %reduce-scatter.16.cloned.1.call-update) | async-done | bytes 1048592 | tf_op jit(solution)/shard_map/reduce_scatter | solution.py:398
  (185 shorter events, 54.7 us)
Async XLA Ops:
  7.2 8.4 copy-start.34
  7.2 8.4 copy-start.35
  7.2 81.7 %all-gather.9.cloned.1.call-start = ((), (), s32[]{:S(2)}) async-start(), calls=%async_computation.11 | async-start | bytes 5242880 | tf_op jit(solution)/shard_map/all_gather | solution.py:301
  7.9 130.2 %all-gather.11.cloned.1.call-start = ((), (), s32[]{:S(2)}) async-start(), calls=%async_computation.12 | async-start | bytes 7077888 | tf_op jit(solution)/shard_map/all_gather | solution.py:298
  10.0 222.2 %all-gather.13.cloned.1.call-start = ((), (), s32[]{:S(2)}) async-start(), calls=%async_computation.13 | async-start | bytes 2359296 | tf_op jit(solution)/shard_map/all_gather | solution.py:298
  10.8 305.0 %reduce-scatter.10.cloned.1.call-start = ((), (), s32[]{:S(2)}) async-start(), calls=%async_computation.14 | async-start | bytes 5242880 | tf_op jit(solution)/shard_map/reduce_scatter | solution.py:263
  148.2 17.9 %collective-permute-start.2 = (bf16[1024,256]{1,0:T(8,128)(2,1)S(1)}, bf16[1024,256]{1,0:T(8,128)(2,1)S(1)}, u32[]{:S(2)}, u32[]{:S(2)}) collective-permute-start(bf16[1024,256]{1,0:T(8,128)(2,1)S(1)} %get-tuple-element.97), channel_id=1, source_target_pairs={{0,4},{4,0},{1,5},{5,1},{2,6},{6,2},{3,7},{7,3},{8,12},{12,8},{9,1... | collective-permute-start | bytes 1572872 | tf_op jit(solution)/shard_map/ppermute | solution.py:218
  149.5 31.6 %collective-permute-start = (bf16[1024,256]{1,0:T(8,128)(2,1)S(1)}, bf16[1024,256]{1,0:T(8,128)(2,1)S(1)}, u32[]{:S(2)}, u32[]{:S(2)}) collective-permute-start(bf16[1024,256]{1,0:T(8,128)(2,1)S(1)} %get-tuple-element.98), channel_id=1, source_target_pairs={{0,4},{4,0},{1,5},{5,1},{2,6},{6,2},{3,7},{7,3},{8,12},{12,8},{9,1... | collective-permute-start | bytes 1572872 | tf_op jit(solution)/shard_map/ppermute | solution.py:218
  150.5 44.9 %copy-start.8 = (s32[1,2048]{1,0:T(1,128)}, s32[1,2048]{1,0:T(1,128)S(1)}, u32[]{:S(2)}) copy-start(s32[1,2048]{1,0:T(1,128)S(1)} %get-tuple-element.123.high_ref) | copy-start | bytes 24580
  150.5 44.9 %copy-start.10 = (s32[1,2048]{1,0:T(1,128)}, s32[1,2048]{1,0:T(1,128)S(1)}, u32[]{:S(2)}) copy-start(s32[1,2048]{1,0:T(1,128)S(1)} %get-tuple-element.124.low_ref) | copy-start | bytes 24580
  181.4 13.7 %collective-permute-start.1 = (bf16[1024,256]{1,0:T(8,128)(2,1)S(1)}, bf16[1024,256]{1,0:T(8,128)(2,1)S(1)}, u32[]{:S(2)}, u32[]{:S(2)}) collective-permute-start(bf16[1024,256]{1,0:T(8,128)(2,1)S(1)} %get-tuple-element.96), channel_id=1, source_target_pairs={{0,4},{4,0},{1,5},{5,1},{2,6},{6,2},{3,7},{7,3},{8,12},{12,8},{9,1... | collective-permute-start | bytes 1572872 | tf_op jit(solution)/shard_map/ppermute | solution.py:218
  182.2 13.2 %copy-start.12 = (s32[4]{0:T(128)}, s32[4]{0:T(128)S(1)}, u32[]{:S(2)}) copy-start(s32[4]{0:T(128)S(1)} %get-tuple-element.119.first) | copy-start | bytes 52
  182.2 13.2 %copy-start.14 = (s32[4]{0:T(128)}, s32[4]{0:T(128)S(1)}, u32[]{:S(2)}) copy-start(s32[4]{0:T(128)S(1)} %get-tuple-element.120.last) | copy-start | bytes 52
  182.3 36.1 %copy-start.4 = (bf16[2048,256]{1,0:T(8,128)(2,1)}, bf16[2048,256]{1,0:T(8,128)(2,1)S(1)}, u32[]{:S(2)}) copy-start(bf16[2048,256]{1,0:T(8,128)(2,1)S(1)} %get-tuple-element.121.q_ref) | copy-start | bytes 3145732
  182.4 36.1 %copy-start.6 = (bf16[2048,256]{1,0:T(8,128)(2,1)}, bf16[2048,256]{1,0:T(8,128)(2,1)S(1)}, u32[]{:S(2)}) copy-start(bf16[2048,256]{1,0:T(8,128)(2,1)S(1)} %get-tuple-element.122.v_ref) | copy-start | bytes 3145732
  195.3 23.2 %copy-start.2 = (bf16[2048,256]{1,0:T(8,128)(2,1)}, bf16[2048,256]{1,0:T(8,128)(2,1)S(1)}, u32[]{:S(2)}) copy-start(bf16[2048,256]{1,0:T(8,128)(2,1)S(1)} %pad_maximum_fusion.1.k_ref) | copy-start | bytes 3145732
  218.5 13.6 %copy-start = (bf16[2048,256]{1,0:T(8,128)(2,1)}, bf16[2048,256]{1,0:T(8,128)(2,1)S(1)}, u32[]{:S(2)}) copy-start(bf16[2048,256]{1,0:T(8,128)(2,1)S(1)} %get-tuple-element.18.o_ref) | copy-start | bytes 3145732
  218.6 13.5 %collective-permute-start.3 = (bf16[1024,256]{1,0:T(8,128)(2,1)S(1)}, bf16[1024,256]{1,0:T(8,128)(2,1)S(1)}, u32[]{:S(2)}, u32[]{:S(2)}) collective-permute-start(bf16[1024,256]{1,0:T(8,128)(2,1)S(1)} %broadcast_select_fusion.12), channel_id=1, source_target_pairs={{0,4},{4,0},{1,5},{5,1},{2,6},{6,2},{3,7},{7,3},{8,12},{12,8},{9,1... | collective-permute-start | bytes 1572872 | tf_op jit(solution)/shard_map/ppermute | solution.py:218
  238.6 12.8 copy-start.31
  238.6 133.9 %all-gather.17.cloned.1.call-start = ((), (), s32[]{:S(2)}) async-start(), calls=%async_computation.16 | async-start | bytes 9437184 | tf_op jit(solution)/shard_map/all_gather | solution.py:298
  239.2 213.6 %all-gather.15.cloned.1.call-start = ((), (), s32[]{:S(2)}) async-start(), calls=%async_computation.15 | async-start | bytes 5242880 | tf_op jit(solution)/shard_map/all_gather | solution.py:258
  321.2 189.2 %all-gather.19.cloned.1.call-start = ((), (), s32[]{:S(2)}) async-start(), calls=%async_computation.17 | async-start | bytes 9437184 | tf_op jit(solution)/shard_map/all_gather | solution.py:298
  321.9 303.9 %reduce-scatter.12.cloned.1.call-start = ((), (), s32[]{:S(2)}) async-start(), calls=%async_computation.18 | async-start | bytes 5242880 | tf_op jit(solution)/shard_map/reduce_scatter | solution.py:263
  527.2 53.3 %all-to-all-start.1 = ((bf16[4,256,512]{2,1,0:T(8,128)(2,1)}), bf16[4,256,512]{2,1,0:T(8,128)(2,1)S(1)}, u32[]{:S(2)}, u32[]{:S(2)}) async-start(bf16[4,256,512]{2,1,0:T(8,128)(2,1)} %bitcast.11), calls=%async_computation.3 | async-start | bytes 2097152 | tf_op jit(solution)/shard_map/all_to_all | solution.py:267
  532.4 177.2 %all-gather.21.cloned.1.call-start = ((), (), s32[]{:S(2)}) async-start(), calls=%async_computation.19 | async-start | bytes 5242880 | tf_op jit(solution)/shard_map/all_gather | solution.py:258
  581.8 44.0 %copy-start.16 = (bf16[256,2048]{1,0:T(8,128)(2,1)S(1)}, bf16[256,2048]{1,0:T(8,128)(2,1)}, u32[]{:S(2)}) copy-start(bf16[256,2048]{1,0:T(8,128)(2,1)} %reduce-scatter.10.cloned.1.call-done) | copy-start | bytes 3145732
  583.0 45.5 %copy-start.17 = (f32[4,32,8,512]{3,2,0,1:T(8,128)}, f32[4,32,8,512]{3,2,0,1:T(8,128)S(1)}, u32[]{:S(2)}) copy-start(f32[4,32,8,512]{3,2,0,1:T(8,128)S(1)} %copy.43) | copy-start | bytes 6291460
  633.1 187.7 %reduce-scatter.14.cloned.1.call-start = ((), (), s32[]{:S(2)}) async-start(), calls=%async_computation.20 | async-start | bytes 5242880 | tf_op jit(solution)/shard_map/reduce_scatter | solution.py:263
  742.8 163.9 %all-gather.23.cloned.1.call-start = ((), (), s32[]{:S(2)}) async-start(), calls=%async_computation.21 | async-start | bytes 5242880 | tf_op jit(solution)/shard_map/all_gather | solution.py:258
  827.9 238.3 %reduce-scatter.24.cloned.1.call-start = ((), (), s32[]{:S(2)}) async-start(), calls=%async_computation.26 | async-start | bytes 9437184 | tf_op jit(solution)/shard_map/reduce_scatter | solution.py:355
  843.0 226.1 %reduce-scatter.22.cloned.1.call-start = ((), (), s32[]{:S(2)}) async-start(), calls=%async_computation.25 | async-start | bytes 9437184 | tf_op jit(solution)/shard_map/reduce_scatter | solution.py:355
  857.4 230.4 %reduce-scatter.26.cloned.1.call-start = ((), (), s32[]{:S(2)}) async-start(), calls=%async_computation.27 | async-start | bytes 81920 | tf_op jit(solution)/shard_map/reduce_scatter | solution.py:407
  911.9 14.1 %copy-start.9 = (s32[1,2048]{1,0:T(1,128)S(1)}, s32[1,2048]{1,0:T(1,128)}, u32[]{:S(2)}) copy-start(s32[1,2048]{1,0:T(1,128)} %copy-done.8) | copy-start | bytes 24580
  911.9 14.1 %copy-start.11 = (s32[1,2048]{1,0:T(1,128)S(1)}, s32[1,2048]{1,0:T(1,128)}, u32[]{:S(2)}) copy-start(s32[1,2048]{1,0:T(1,128)} %copy-done.10) | copy-start | bytes 24580
  911.9 14.1 %copy-start.13 = (s32[4]{0:T(128)S(1)}, s32[4]{0:T(128)}, u32[]{:S(2)}) copy-start(s32[4]{0:T(128)} %copy-done.12) | copy-start | bytes 52
  911.9 14.1 %copy-start.15 = (s32[4]{0:T(128)S(1)}, s32[4]{0:T(128)}, u32[]{:S(2)}) copy-start(s32[4]{0:T(128)} %copy-done.14) | copy-start | bytes 52
  912.0 13.8 %collective-permute-start.4 = (bf16[1024,256]{1,0:T(8,128)(2,1)S(1)}, bf16[1024,256]{1,0:T(8,128)(2,1)S(1)}, u32[]{:S(2)}, u32[]{:S(2)}) collective-permute-start(bf16[1024,256]{1,0:T(8,128)(2,1)S(1)} %broadcast_select_fusion.8), channel_id=1, source_target_pairs={{0,4},{4,0},{1,5},{5,1},{2,6},{6,2},{3,7},{7,3},{8,12},{12,8},{9,1... | collective-permute-start | bytes 1572872 | tf_op jit(solution)/shard_map/ppermute | solution.py:218
  914.4 218.7 %reduce-scatter.20.cloned.1.call-start = ((), (), s32[]{:S(2)}) async-start(), calls=%async_computation.24 | async-start | bytes 2359296 | tf_op jit(solution)/shard_map/reduce_scatter | solution.py:355
  931.2 32.1 %copy-start.28 = (bf16[1024,256]{1,0:T(8,128)(2,1)S(1)}, bf16[1024,256]{1,0:T(8,128)(2,1)}, u32[]{:S(2)}) copy-start(bf16[1024,256]{1,0:T(8,128)(2,1)} %copy-done.27) | copy-start | bytes 1572868
  931.2 32.1 %copy-start.30 = (bf16[1024,256]{1,0:T(8,128)(2,1)S(1)}, bf16[1024,256]{1,0:T(8,128)(2,1)}, u32[]{:S(2)}) copy-start(bf16[1024,256]{1,0:T(8,128)(2,1)} %copy-done.29) | copy-start | bytes 1572868
  931.2 32.1 %copy-start.36 = (bf16[1024,2048]{1,0:T(8,128)(2,1)S(1)}, bf16[1024,2048]{1,0:T(8,128)(2,1)}, u32[]{:S(2)}) copy-start(bf16[1024,2048]{1,0:T(8,128)(2,1)} %all-gather.23.cloned.1.call-done) | copy-start | bytes 12582916
  961.8 17.3 %collective-permute-start.5 = (bf16[1024,256]{1,0:T(8,128)(2,1)}, bf16[1024,256]{1,0:T(8,128)(2,1)}, u32[]{:S(2)}, u32[]{:S(2)}) collective-permute-start(bf16[1024,256]{1,0:T(8,128)(2,1)} %broadcast_select_fusion.4), channel_id=1, source_target_pairs={{0,4},{4,0},{1,5},{5,1},{2,6},{6,2},{3,7},{7,3},{8,12},{12,8},{9,1... | collective-permute-start | bytes 1572872 | tf_op jit(solution)/shard_map/ppermute | solution.py:218
  967.1 231.5 %reduce-scatter.18.cloned.1.call-start = ((), (), s32[]{:S(2)}) async-start(), calls=%async_computation.23 | async-start | bytes 7077888 | tf_op jit(solution)/shard_map/reduce_scatter | solution.py:355
  967.4 41.1 %collective-permute-start.7 = (bf16[1024,256]{1,0:T(8,128)(2,1)S(1)}, bf16[1024,256]{1,0:T(8,128)(2,1)S(1)}, u32[]{:S(2)}, u32[]{:S(2)}) collective-permute-start(bf16[1024,256]{1,0:T(8,128)(2,1)S(1)} %broadcast_select_fusion), channel_id=1, source_target_pairs={{0,4},{4,0},{1,5},{5,1},{2,6},{6,2},{3,7},{7,3},{8,12},{12,8},{9,1... | collective-permute-start | bytes 1572872 | tf_op jit(solution)/shard_map/ppermute | solution.py:218
  968.0 40.1 %collective-permute-start.6 = (bf16[1024,256]{1,0:T(8,128)(2,1)S(1)}, bf16[1024,256]{1,0:T(8,128)(2,1)S(1)}, u32[]{:S(2)}, u32[]{:S(2)}) collective-permute-start(bf16[1024,256]{1,0:T(8,128)(2,1)S(1)} %broadcast_select_fusion.2), channel_id=1, source_target_pairs={{0,4},{4,0},{1,5},{5,1},{2,6},{6,2},{3,7},{7,3},{8,12},{12,8},{9,1... | collective-permute-start | bytes 1572872 | tf_op jit(solution)/shard_map/ppermute | solution.py:218
  1021.2 10.7 copy-start.20
  1021.2 256.8 %reduce-scatter.16.cloned.1.call-start = ((), (), s32[]{:S(2)}) async-start(), calls=%async_computation.22 | async-start | bytes 5242880 | tf_op jit(solution)/shard_map/reduce_scatter | solution.py:398
  1135.0 143.1 %copy-start.25 = (bf16[256,4,512]{2,0,1:T(8,128)(2,1)S(1)}, bf16[256,4,512]{2,0,1:T(8,128)(2,1)}, u32[]{:S(2)}) copy-start(bf16[256,4,512]{2,0,1:T(8,128)(2,1)} %all_to_all.32) | copy-start | bytes 3145732
  (16 other events, 42.8 us)
Sparse Core Ops, SparseCore 0:
  9.6 79.2 all-gather.8
  91.3 46.7 all-gather.10
  140.0 35.7 all-gather.12
  238.7 77.0 reduce-scatter.9
  317.7 54.7 all-gather.16
  374.6 78.1 all-gather.14
  454.8 55.5 all-gather.18
  527.4 98.4 reduce-scatter.11
  633.2 76.2 all-gather.20
  742.9 77.9 reduce-scatter.13
  828.0 78.6 all-gather.22
  910.4 83.7 reduce-scatter.23
  997.6 71.1 reduce-scatter.21
  1071.6 16.1 reduce-scatter.25
  1090.9 42.1 reduce-scatter.19
  1136.8 61.7 reduce-scatter.17
  1201.3 76.6 reduce-scatter.15

commit v2 on v1

--- a/solution.py
+++ b/solution.py
@@ -254,21 +254,525 @@
     return jax.nn.gelu(values, approximate=True)
 
 
-def gather_rows(rows):
-    return lax.all_gather(rows, "tp", axis=0, tiled=True)
-
-
-def scatter_rows(partial_rows):
-    low = partial_rows.astype(jnp.bfloat16)
-    return lax.psum_scatter(low, "tp", scatter_dimension=0, tiled=True).astype(jnp.float32)
-
-
-def spread(block):
-    return lax.all_to_all(block, "tp", split_axis=0, concat_axis=1, tiled=True)
-
-
-def unspread(block):
-    return lax.all_to_all(block, "tp", split_axis=1, concat_axis=0, tiled=True)
+MESH = pl.DeviceIdType.MESH
+PIECES = 4
+TILE = 512
+
+
+def greet(me, count):
+    barrier = pltpu.get_barrier_semaphore()
+
+    @pl.when(me > 0)
+    def _():
+        pl.semaphore_signal(barrier, inc=1, device_id={"tp": me - 1}, device_id_type=MESH)
+
+    @pl.when(me < count - 1)
+    def _():
+        pl.semaphore_signal(barrier, inc=1, device_id={"tp": me + 1}, device_id_type=MESH)
+
+    @pl.when((me == 0) | (me == count - 1))
+    def _():
+        pl.semaphore_wait(barrier, 1)
+
+    @pl.when((me > 0) & (me < count - 1))
+    def _():
+        pl.semaphore_wait(barrier, 2)
+
+
+def at_distance(me, count, distance, action):
+    for index in (me - distance, me + distance):
+
+        @pl.when((index >= 0) & (index < count))
+        def _(index=index):
+            action(index)
+
+
+class Line:
+    def __init__(self, me, count, sum_slots, sum_sent, sum_got, spread_view, spread_sent, spread_got):
+        self.me, self.count = me, count
+        self.sum_slots, self.sum_sent, self.sum_got = sum_slots, sum_sent, sum_got
+        self.spread_view, self.spread_sent, self.spread_got = spread_view, spread_sent, spread_got
+
+    def sum_copy(self, piece, owner):
+        onward = jnp.where(owner > self.me, self.me + 1, self.me - 1)
+        place = jnp.where((owner < self.me) & (owner == self.me - 1), self.count, owner)
+        return pltpu.make_async_remote_copy(
+            src_ref=self.sum_slots.at[piece, owner],
+            dst_ref=self.sum_slots.at[piece, place],
+            send_sem=self.sum_sent.at[piece, owner],
+            recv_sem=self.sum_got.at[piece, place],
+            device_id={"tp": onward},
+            device_id_type=MESH,
+        )
+
+    def sum_arrival(self, piece, place):
+        pltpu.make_async_copy(
+            self.sum_slots.at[piece, place],
+            self.sum_slots.at[piece, place],
+            self.sum_got.at[piece, place],
+        ).wait()
+
+    def sum_start(self, piece, term):
+        me, count = self.me, self.count
+
+        @pl.when((me == 0) | (me == count - 1))
+        def _():
+            for k in range(count - 1):
+                owner = jnp.where(me == 0, count - 1 - k, k)
+                self.sum_slots[piece, owner] = term(owner).astype(jnp.bfloat16)
+                self.sum_copy(piece, owner).start()
+
+    def sum_onward(self, piece, term):
+        me, count = self.me, self.count
+
+        @pl.when((me > 0) & (me < count - 1))
+        def _():
+            for distance in range(count - 2, 0, -1):
+
+                def pass_on(owner):
+                    self.sum_arrival(piece, owner)
+                    total = self.sum_slots[piece, owner].astype(jnp.float32) + term(owner)
+                    self.sum_slots[piece, owner] = total.astype(jnp.bfloat16)
+                    self.sum_copy(piece, owner).start()
+
+                at_distance(me, count, distance, pass_on)
+
+    def sum_end(self, piece, total):
+        me, count = self.me, self.count
+
+        @pl.when(me > 0)
+        def _():
+            self.sum_arrival(piece, me)
+            total[...] += self.sum_slots[piece, me].astype(jnp.float32)
+
+        @pl.when(me < count - 1)
+        def _():
+            self.sum_arrival(piece, count)
+            total[...] += self.sum_slots[piece, count].astype(jnp.float32)
+
+    def sum_finish(self, pieces):
+        @pl.loop(0, pieces)
+        def _(piece):
+            for distance in range(1, self.count):
+                at_distance(
+                    self.me, self.count, distance,
+                    lambda owner: self.sum_copy(piece, owner).wait_send(),
+                )
+
+    def spread_copy(self, piece, owner, to, sent, source=None):
+        return pltpu.make_async_remote_copy(
+            src_ref=self.spread_view(piece, owner) if source is None else source,
+            dst_ref=self.spread_view(piece, owner),
+            send_sem=self.spread_sent.at[piece, sent],
+            recv_sem=self.spread_got.at[piece, owner],
+            device_id={"tp": to},
+            device_id_type=MESH,
+        )
+
+    def own_copies(self, piece, action, source=None):
+        me, count = self.me, self.count
+
+        @pl.when(me > 0)
+        def _():
+            action(self.spread_copy(piece, me, me - 1, count, source))
+
+        @pl.when(me < count - 1)
+        def _():
+            action(self.spread_copy(piece, me, me + 1, me, source))
+
+    def spread_start(self, piece, source=None):
+        self.own_copies(piece, lambda copy: copy.start(), source)
+
+    def onward_copy(self, piece, owner, action):
+        me, count = self.me, self.count
+
+        @pl.when((owner < me) & (me < count - 1))
+        def _():
+            action(self.spread_copy(piece, owner, me + 1, owner))
+
+        @pl.when((owner > me) & (me > 0))
+        def _():
+            action(self.spread_copy(piece, owner, me - 1, owner))
+
+    def spread_onward(self, piece, distance):
+        def pass_on(owner):
+            view = self.spread_view(piece, owner)
+            pltpu.make_async_copy(view, view, self.spread_got.at[piece, owner]).wait()
+            self.onward_copy(piece, owner, lambda copy: copy.start())
+
+        at_distance(self.me, self.count, distance, pass_on)
+
+    def spread_finish(self, pieces, source=None):
+        @pl.loop(0, pieces)
+        def _(piece):
+            self.own_copies(
+                piece, lambda copy: copy.wait_send(), None if source is None else source(piece)
+            )
+            for distance in range(1, self.count):
+                at_distance(
+                    self.me, self.count, distance,
+                    lambda owner: self.onward_copy(piece, owner, lambda copy: copy.wait_send()),
+                )
+
+
+def line_semaphores(count, pieces):
+    return [
+        pltpu.SemaphoreType.DMA((pieces, count)),
+        pltpu.SemaphoreType.DMA((pieces, count + 1)),
+    ], [
+        pltpu.SemaphoreType.DMA((pieces, count + 1)),
+        pltpu.SemaphoreType.DMA((pieces, count)),
+    ]
+
+
+def gather_kernel(count, x_ref, out_ref, sent, got):
+    me = lax.axis_index("tp")
+    height = x_ref.shape[0] // PIECES
+    width = x_ref.shape[1]
+
+    def view(piece, owner):
+        return out_ref.at[
+            pl.ds(pl.multiple_of(piece * height, height), height),
+            pl.ds(pl.multiple_of(owner * width, width), width),
+        ]
+
+    def source(piece):
+        return x_ref.at[pl.ds(pl.multiple_of(piece * height, height), height)]
+
+    line = Line(me, count, None, None, None, view, sent, got)
+    greet(me, count)
+
+    @pl.loop(0, PIECES)
+    def _(piece):
+        line.spread_start(piece, source(piece))
+
+    out_ref[:, pl.ds(pl.multiple_of(me * width, width), width)] = x_ref[...]
+    for distance in range(1, count):
+
+        @pl.loop(0, PIECES)
+        def _(piece, distance=distance):
+            line.spread_onward(piece, distance)
+
+    line.spread_finish(PIECES, source)
+
+
+def gather_features(x, collective_id):
+    count = lax.axis_size("tp")
+    rows, width = x.shape
+    return pl.pallas_call(
+        functools.partial(gather_kernel, count),
+        out_shape=jax.ShapeDtypeStruct((rows, count * width), x.dtype),
+        in_specs=[pl.BlockSpec(memory_space=pltpu.VMEM)],
+        out_specs=pl.BlockSpec(memory_space=pltpu.VMEM),
+        scratch_shapes=line_semaphores(count, PIECES)[1],
+        compiler_params=pltpu.CompilerParams(
+            collective_id=collective_id, has_side_effects=True, vmem_limit_bytes=16 << 20
+        ),
+        cost_estimate=pl.CostEstimate(
+            flops=0, bytes_accessed=64 * rows * count * width, transcendentals=0
+        ),
+        name="gather_features",
+    )(x)
+
+
+def relay_kernel(count, row_step, use_step, sizes, *refs):
+    row_in, use_in, row_out, use_out, shared = sizes
+    refs = list(refs)
+
+    def take(number):
+        taken = refs[:number]
+        del refs[:number]
+        return taken
+
+    x_ref, sum_weight = take(2)
+    use_weight = sum_weight if shared else take(1)[0]
+    row_inputs, use_inputs = take(row_in), take(use_in)
+    (gathered,) = take(1)
+    row_outputs, use_outputs = take(row_out), take(use_out)
+    terms, total, slots, sum_sent, sum_got, spread_sent, spread_got = refs
+    me = lax.axis_index("tp")
+    height = x_ref.shape[0] // PIECES
+    own = height // count
+    width = sum_weight.shape[0]
+
+    def view(piece, owner):
+        return gathered.at[pl.ds(pl.multiple_of(piece * height + owner * own, own), own)]
+
+    line = Line(me, count, slots, sum_sent, sum_got, view, spread_sent, spread_got)
+    greet(me, count)
+
+    def piece_rows(piece):
+        return pl.ds(pl.multiple_of(piece * height, height), height)
+
+    @pl.loop(0, PIECES + 2)
+    def _(step):
+        odd = lax.rem(step, 2)
+
+        def term(owner):
+            return terms[odd, pl.ds(pl.multiple_of(owner * own, own), own), :]
+
+        @pl.when(step < PIECES)
+        def _():
+            x = x_ref[piece_rows(step), :]
+
+            @pl.loop(0, width // TILE)
+            def _(tile):
+                part = pl.ds(pl.multiple_of(tile * TILE, TILE), TILE)
+                terms[odd, :, part] = dot_cols(x, sum_weight[part, :])
+
+            line.sum_start(step, term)
+
+        @pl.when((step >= 1) & (step <= PIECES))
+        def _():
+            piece = step - 1
+            total[...] = terms[1 - odd, pl.ds(pl.multiple_of(me * own, own), own), :]
+            line.sum_end(piece, total)
+            view(piece, me)[...] = row_step(piece, total, row_inputs, row_outputs)
+            line.spread_start(piece)
+
+        @pl.when(step >= 2)
+        def _():
+            for distance in range(2, count):
+                line.spread_onward(step - 2, distance)
+
+        @pl.when(step < PIECES)
+        def _():
+            line.sum_onward(step, term)
+
+        @pl.when((step >= 1) & (step <= PIECES))
+        def _():
+            line.spread_onward(step - 1, 1)
+
+        @pl.when(step >= 2)
+        def _():
+            rows = piece_rows(step - 2)
+            use_step(rows, gathered[rows, :], use_weight, use_inputs, use_outputs)
+
+    line.sum_finish(PIECES)
+    line.spread_finish(PIECES)
+
+
+def relay(
+    x, sum_weight, use_weight, row_inputs, row_step, row_shapes, use_inputs, use_step, use_shapes,
+    collective_id, name,
+):
+    count = lax.axis_size("tp")
+    rows = x.shape[0]
+    width = sum_weight.shape[0]
+    height = rows // PIECES
+    own = height // count
+    shared = use_weight is None
+    operands = [x, sum_weight, *([] if shared else [use_weight]), *row_inputs, *use_inputs]
+    shapes = [jax.ShapeDtypeStruct((rows, width), jnp.bfloat16), *row_shapes, *use_shapes]
+    sums, spreads = line_semaphores(count, PIECES)
+    sizes = (len(row_inputs), len(use_inputs), len(row_shapes), len(use_shapes), shared)
+    return pl.pallas_call(
+        functools.partial(relay_kernel, count, row_step, use_step, sizes),
+        out_shape=shapes,
+        in_specs=[pl.BlockSpec(memory_space=pltpu.VMEM)] * len(operands),
+        out_specs=[pl.BlockSpec(memory_space=pltpu.VMEM)] * len(shapes),
+        scratch_shapes=[
+            pltpu.VMEM((2, height, width), jnp.float32),
+            pltpu.VMEM((own, width), jnp.float32),
+            pltpu.VMEM((PIECES, count + 1, own, width), jnp.bfloat16),
+            *sums,
+            *spreads,
+        ],
+        compiler_params=pltpu.CompilerParams(
+            collective_id=collective_id, has_side_effects=True, vmem_limit_bytes=60 << 20
+        ),
+        cost_estimate=pl.CostEstimate(
+            flops=100_000_000_000, bytes_accessed=64 * rows * width, transcendentals=0
+        ),
+        name=name,
+    )(*operands)
+
+
+def own_rows_of(piece, like):
+    own = like.shape[0] // PIECES
+    return pl.ds(pl.multiple_of(piece * own, own), own)
+
+
+def first_norm_step(piece, total, inputs, outputs):
+    tokens, gains, biases = inputs
+    first_norm, normed_one, inverse_one = outputs
+    part = own_rows_of(piece, tokens)
+    summed = tokens[part, :].astype(jnp.float32) + (total[...] + biases[0:1, :])
+    normed, inverse = norm_parts(summed)
+    result = normed * gains[0:1, :] + biases[1:2, :]
+    first_norm[part, :] = result
+    normed_one[part, :] = normed
+    inverse_one[part, :] = jnp.broadcast_to(inverse, (inverse.shape[0], 128))
+    return result.astype(jnp.bfloat16)
+
+
+def expand_step(rows, chunk, weight, inputs, outputs):
+    (bias,) = inputs
+    hidden, activated = outputs
+
+    @pl.loop(0, hidden.shape[1] // TILE)
+    def _(tile):
+        part = pl.ds(pl.multiple_of(tile * TILE, TILE), TILE)
+        values = dot_plain(chunk, weight[:, part]) + bias[:, part]
+        hidden[rows, part] = values
+        activated[rows, part] = gelu_tanh(values).astype(jnp.bfloat16)
+
+
+def add_sums(piece, sums, *values):
+    @pl.when(piece == 0)
+    def _():
+        sums[...] = jnp.zeros_like(sums)
+
+    for i, value in enumerate(values):
+        sums[i : i + 1, :] += jnp.sum(value, axis=0, keepdims=True)
+
+
+def second_norm_step(piece, total, inputs, outputs):
+    first_norm, out_grad, gains, biases = inputs
+    mixed, grad_second, sums = outputs
+    part = own_rows_of(piece, first_norm)
+    normed, inverse = norm_parts(first_norm[part, :] + total[...] + biases[2:3, :])
+    mixed[part, :] = (normed * gains[1:2, :] + biases[3:4, :]).astype(jnp.bfloat16)
+    upstream = out_grad[part, :].astype(jnp.float32)
+    grad = norm_back(upstream, normed, inverse, gains[1:2, :])
+    grad_second[part, :] = grad
+    low = grad.astype(jnp.bfloat16)
+    add_sums(piece, sums, upstream * normed, upstream, low.astype(jnp.float32))
+    return low
+
+
+def gelu_slope(values):
+    scale = math.sqrt(2.0 / math.pi)
+    square = values * values
+    bend = jnp.tanh(scale * values * (1.0 + 0.044715 * square))
+    inner = scale * (1.0 + 3 * 0.044715 * square)
+    return 0.5 * (1.0 + bend) + 0.5 * values * (1.0 - bend * bend) * inner
+
+
+def shrink_step(rows, chunk, weight, inputs, outputs):
+    (hidden,) = inputs
+    hidden_low, sums = outputs
+
+    @pl.when(rows.start == 0)
+    def _():
+        sums[...] = jnp.zeros_like(sums)
+
+    @pl.loop(0, hidden.shape[1] // TILE)
+    def _(tile):
+        part = pl.ds(pl.multiple_of(tile * TILE, TILE), TILE)
+        grad = dot_plain(chunk, weight[:, part]) * gelu_slope(hidden[rows, part])
+        low = grad.astype(jnp.bfloat16)
+        hidden_low[rows, part] = low
+        sums[0:1, part] += jnp.sum(low.astype(jnp.float32), axis=0, keepdims=True)
+
+
+def first_back_step(piece, total, inputs, outputs):
+    grad_second, normed_one, inverse_one, gains = inputs
+    grad_inner, sums = outputs
+    part = own_rows_of(piece, grad_second)
+    normed = normed_one[part, :]
+    grad_first = grad_second[part, :] + total[...]
+    grad = norm_back(grad_first, normed, inverse_one[part, 0:1], gains[0:1, :])
+    grad_inner[part, :] = grad
+    low = grad.astype(jnp.bfloat16)
+    add_sums(piece, sums, grad_first * normed, grad_first, low.astype(jnp.float32))
+    return low
+
+
+def attended_step(rows, chunk, weight, inputs, outputs):
+    (attended_grad,) = outputs
+    attended_grad[rows, :] = dot_plain(chunk, weight[...]).astype(jnp.bfloat16)
+
+
+def input_kernel(
+    count, x_ref, weight, inner_ref, out_ref, term_ref, total, slots, sum_sent, sum_got
+):
+    me = lax.axis_index("tp")
+    height = x_ref.shape[0] // PIECES
+    own = height // count
+    width = out_ref.shape[1]
+    line = Line(me, count, slots, sum_sent, sum_got, None, None, None)
+    greet(me, count)
+
+    def terms(piece):
+        def term(owner):
+            features = pl.ds(pl.multiple_of(owner * width, width), width)
+            term_ref[...] = dot_cols(
+                x_ref[pl.ds(pl.multiple_of(piece * height, height), height), :],
+                weight[features, :],
+            )
+            inner = inner_ref[pl.ds(pl.multiple_of(piece * own, own), own), features]
+            term_ref[pl.ds(pl.multiple_of(me * own, own), own), :] += inner
+            return term_ref[...]
+
+        return term
+
+    @pl.loop(0, PIECES + 1)
+    def _(step):
+        @pl.when(step < PIECES)
+        def _():
+            line.sum_start(step, terms(step))
+            line.sum_onward(step, terms(step))
+
+        @pl.when(step >= 1)
+        def _():
+            piece = step - 1
+            total[...] = terms(piece)(me)
+            line.sum_end(piece, total)
+            rows = pl.ds(pl.multiple_of(piece * height, height), height)
+            out_ref[rows, :] = total[...].astype(out_ref.dtype)
+
+    line.sum_finish(PIECES)
+
+
+def input_sum(x, weight, inner, collective_id):
+    count = lax.axis_size("tp")
+    rows = x.shape[0]
+    width = weight.shape[0] // count
+    height = rows // PIECES
+    return pl.pallas_call(
+        functools.partial(input_kernel, count),
+        out_shape=jax.ShapeDtypeStruct((rows, width), jnp.bfloat16),
+        in_specs=[pl.BlockSpec(memory_space=pltpu.VMEM)] * 3,
+        out_specs=pl.BlockSpec(memory_space=pltpu.VMEM),
+        scratch_shapes=[
+            pltpu.VMEM((height, width), jnp.float32),
+            pltpu.VMEM((height, width), jnp.float32),
+            pltpu.VMEM((PIECES, count + 1, height, width), jnp.bfloat16),
+            *line_semaphores(count, PIECES)[0],
+        ],
+        compiler_params=pltpu.CompilerParams(
+            collective_id=collective_id, has_side_effects=True, vmem_limit_bytes=40 << 20
+        ),
+        cost_estimate=pl.CostEstimate(
+            flops=60_000_000_000, bytes_accessed=64 * rows * width, transcendentals=0
+        ),
+        name="input_sum",
+    )(x, weight, inner)
+
+
+def to_own_rows(wide):
+    count = lax.axis_size("tp")
+    parts = wide.reshape(PIECES, count, -1, wide.shape[1])
+    return lax.dynamic_index_in_dim(parts, lax.axis_index("tp"), 1, keepdims=False).reshape(
+        -1, wide.shape[1]
+    )
+
+
+def spread_own(block):
+    count = lax.axis_size("tp")
+    rows, width = block.shape
+    parts = block.reshape(PIECES, count, -1, width)
+    got = lax.all_to_all(parts, "tp", split_axis=1, concat_axis=1, tiled=True)
+    return got.transpose(0, 2, 1, 3).reshape(rows // count, count * width)
+
+
+def unspread_own(block):
+    count = lax.axis_size("tp")
+    rows, width = block.shape
+    parts = block.reshape(PIECES, -1, count, width // count).transpose(0, 2, 1, 3)
+    got = lax.all_to_all(parts, "tp", split_axis=1, concat_axis=1, tiled=True)
+    return got.reshape(rows * count, width // count)
 
 
 def body(
@@ -291,20 +795,19 @@
     head_cols = query_weight.shape[1]
     plane = ("fsdp", "ctx")
     ctx_size = lax.axis_size("ctx")
-    own_rows = rows // lax.axis_size("tp")
     by_heads = ctx_size == 2 and (head_cols // HD) % 2 == 0
 
     def weight_rows(weight):
         return lax.all_gather(weight, plane, axis=0, tiled=True)
 
     wide_qkv = weight_rows(jnp.concatenate([query_weight, key_weight, value_weight], axis=1))
-    wide_tokens = lax.all_gather(tokens, "tp", axis=1, tiled=True)
+    wide_tokens = gather_features(tokens, 0)
     full_output = weight_rows(output_weight)
     full_expand = weight_rows(expand_weight)
     full_shrink = weight_rows(shrink_weight)
     gains = lax.all_gather(norm_gains, "tp", axis=1, tiled=True).astype(jnp.float32)
     biases = lax.all_gather(row_biases, "tp", axis=1, tiled=True).astype(jnp.float32)
-    upstream = spread(out_grad).astype(jnp.float32)
+    upstream = spread_own(out_grad)
 
     qkv_bias = jnp.concatenate([query_bias, jnp.zeros_like(query_bias), value_bias])
     qkv = (dot_plain(wide_tokens, wide_qkv) + qkv_bias.astype(jnp.float32)).astype(jnp.bfloat16)
@@ -332,24 +835,31 @@
     attended_heads, lse = attend(queries, keys, values, *bounds)
     attended = heads_out(attended_heads) if by_heads else attended_heads
 
-    own_start = lax.axis_index("tp") * own_rows
-    own_tokens = lax.dynamic_slice_in_dim(wide_tokens, own_start, own_rows, 0)
-    branch = scatter_rows(dot_cols(attended, full_output)) + biases[0]
-    normed_one, inverse_one = norm_parts(own_tokens.astype(jnp.float32) + branch)
-    first_norm = normed_one * gains[0] + biases[1]
-    norm_low = gather_rows(first_norm.astype(jnp.bfloat16))
-    hidden = dot_plain(norm_low, full_expand) + hidden_bias.astype(jnp.float32)
-    activated = gelu_tanh(hidden).astype(jnp.bfloat16)
-    second_sum = first_norm + scatter_rows(dot_cols(activated, full_shrink)) + biases[2]
-    normed_two, inverse_two = norm_parts(second_sum)
-    mixed = unspread((normed_two * gains[1] + biases[3]).astype(jnp.bfloat16))
-
-    grad_second = norm_back(upstream, normed_two, inverse_two, gains[1])
-    gain_two_grad = jnp.sum(upstream * normed_two, axis=0)
-    shift_two_grad = jnp.sum(upstream, axis=0)
-    ffn_own = grad_second.astype(jnp.bfloat16)
-    ffn_bias_grad = jnp.sum(ffn_own.astype(jnp.float32), axis=0)
-    ffn_low = gather_rows(ffn_own)
+    own_tokens = to_own_rows(wide_tokens)
+    own_rows, features = own_tokens.shape
+    hidden_cols = expand_weight.shape[1]
+
+    def shape(extent, kind=jnp.float32):
+        return jax.ShapeDtypeStruct(extent, kind)
+
+    own_shape = shape((own_rows, features))
+    norm_low, first_norm, normed_one, inverse_one, hidden, activated = relay(
+        attended, full_output, full_expand,
+        [own_tokens, gains, biases], first_norm_step,
+        [own_shape, own_shape, shape((own_rows, 128))],
+        [hidden_bias.astype(jnp.float32)[None]], expand_step,
+        [shape((rows, hidden_cols)), shape((rows, hidden_cols), jnp.bfloat16)],
+        1, "first_norm",
+    )
+    ffn_low, mixed_own, grad_second, second_sums, hidden_low, hidden_sums = relay(
+        activated, full_shrink, None,
+        [first_norm, upstream, gains, biases], second_norm_step,
+        [shape((own_rows, features), jnp.bfloat16), own_shape, shape((8, features))],
+        [hidden], shrink_step,
+        [shape((rows, hidden_cols), jnp.bfloat16), shape((8, hidden_cols))],
+        2, "second_norm",
+    )
+    mixed = unspread_own(mixed_own)
 
     def owner_sum(grad):
         return lax.psum_scatter(
@@ -357,19 +867,16 @@
         ).astype(jnp.float32)
 
     shrink_grad = owner_sum(dot_rows(ffn_low, activated))
-    _, gelu_pull = jax.vjp(gelu_tanh, hidden)
-    hidden_low = gelu_pull(dot_plain(ffn_low, full_shrink))[0].astype(jnp.bfloat16)
-    hidden_bias_grad = jnp.sum(hidden_low.astype(jnp.float32), axis=0)
-    grad_first = grad_second + scatter_rows(dot_cols(hidden_low, full_expand))
+    branch_low, grad_inner, first_sums, attended_grad = relay(
+        hidden_low, full_expand, full_output,
+        [grad_second, normed_one, inverse_one, gains], first_back_step,
+        [own_shape, shape((8, features))],
+        [], attended_step,
+        [shape((rows, head_cols), jnp.bfloat16)],
+        3, "first_back",
+    )
     expand_grad = owner_sum(dot_rows(norm_low, hidden_low))
-    gain_one_grad = jnp.sum(grad_first * normed_one, axis=0)
-    shift_one_grad = jnp.sum(grad_first, axis=0)
-    grad_inner = norm_back(grad_first, normed_one, inverse_one, gains[0])
-    branch_own = grad_inner.astype(jnp.bfloat16)
-    branch_bias_grad = jnp.sum(branch_own.astype(jnp.float32), axis=0)
-    branch_low = gather_rows(branch_own)
     output_grad = owner_sum(dot_rows(branch_low, attended))
-    attended_grad = dot_plain(branch_low, full_output).astype(jnp.bfloat16)
 
     if by_heads:
         grads = attend_back(
@@ -392,12 +899,9 @@
         key_low, value_low = fold(key_ext), fold(value_ext)
     qkv_low = jnp.concatenate([query_low, key_low, value_low], axis=1)
     qkv_grad = owner_sum(dot_rows(wide_tokens, qkv_low))
-    input_partial = dot_cols(qkv_low, wide_qkv)
-    own_part = lax.dynamic_slice_in_dim(input_partial, own_start, own_rows, 0) + grad_inner
-    input_partial = lax.dynamic_update_slice_in_dim(input_partial, own_part, own_start, 0)
-    input_grad = lax.psum_scatter(
-        input_partial.astype(jnp.bfloat16), "tp", scatter_dimension=1, tiled=True
-    )
+    input_grad = input_sum(qkv_low, wide_qkv, grad_inner, 4)
+    gain_one_grad, shift_one_grad, branch_bias_grad = first_sums[:3]
+    gain_two_grad, shift_two_grad, ffn_bias_grad = second_sums[:3]
     row_vectors = jnp.stack(
         [
             gain_one_grad, gain_two_grad,
@@ -407,7 +911,7 @@
     own_vectors = lax.psum_scatter(row_vectors, "tp", scatter_dimension=1, tiled=True)
     qkv_sums = jnp.sum(qkv_low.astype(jnp.float32), axis=0)
     own_vectors, qkv_sums, hidden_bias_grad = lax.psum(
-        (own_vectors, qkv_sums, hidden_bias_grad), plane
+        (own_vectors, qkv_sums, hidden_sums[0]), plane
     )
     return (
         mixed,

time: 1290 us -> 947 us (0.73)
  waiting for transfers between devices: 922 us -> 135 us
  Pallas kernels: 52.8 us -> 600 us
  matrix products: 136 us -> 50.8 us
  blocking collectives: 79.1 us -> 49.3 us
  other arithmetic: 42.2 us -> 24 us
  local copies, waits for them, and re-layouts: 22.6 us -> 40.8 us
    pallas_call x0 -> x5, Pallas kernels: none -> 555 us  [the longest x3 392 us: relay(): pl.pallas_call(functools.partial(relay_kernel, count, row_step, use_step,...]
    all_gather x4 -> x0, waiting for transfers between devices: 279 us -> none  [the longest x3 205 us: gather_rows(): return lax.all_gather(rows, 'tp', axis=0, tiled=True)]
    reduce_scatter x4 -> x0, waiting for transfers between devices: 247 us -> none  [the longest x3 171 us: scatter_rows(): lax.psum_scatter(low, 'tp', scatter_dimension=0, tiled=True)]
    all_gather x4, waiting for transfers between devices: 143 us -> 0.05 us  [weight_rows(): return lax.all_gather(weight, plane, axis=0, tiled=True)]
    all_to_all x1 -> x2, waiting for transfers between devices: 48.1 us -> 0.01 us  [the longest x1 0.01 us: spread_own(): got = lax.all_to_all(parts, 'tp', split_axis=1, concat_axis=1, tiled=True)]
    dot_general x4 -> x0, matrix products: 46.4 us -> none  [dot_cols(): lax.dot_general(left, right, (((1,), (1,)), ((), ())), preferred_element_...]
    reduce_scatter x4, waiting for transfers between devices: 83.2 us -> 42.1 us  [owner_sum(): lax.psum_scatter(grad.astype(jnp.bfloat16), plane, scatter_dimension=0, t...]
    dot_general x4 -> x1, matrix products: 48.3 us -> 10 us  [dot_plain(): return jnp.dot(left, right, preferred_element_type=jnp.float32)]
  transfers between devices with their start and end apart: 26 -> 19, of which waited for: 22 -> 7; matrix products, arithmetic and copies ran while one was open for 9% -> 10% of each run, Pallas kernels for 4% -> 36%
where the time goes in v2:
time: 947 us; the launch traced here: 938 us
  Pallas kernels  600 us (63%)
  waiting for transfers between devices  135 us (14%)
  matrix products  50.8 us (5%)
  blocking collectives  49.3 us (5%)
  local copies, waits for them, and re-layouts  40.8 us (4%)
  other arithmetic  24 us (3%)
  starting transfers between devices  22.7 us (2%)
  between operations  14.9 us (2%)
    pallas_call x3, Pallas kernels, relay(): pl.pallas_call(functools.partial(relay_kernel, count, row_step, use_step,...  392 us
    ppermute x8, waiting for transfers between devices, swap_halves(): got = lax.ppermute(other, 'ctx', [(0, 1), (1, 0)])  90.7 us
    pallas_call x1, Pallas kernels, input_sum(): pl.pallas_call(functools.partial(input_kernel, count), out_shape=jax.Shap...  83.9 us
    pallas_call x1, Pallas kernels, gather_features(): pl.pallas_call(functools.partial(gather_kernel, count), out_shape=jax.Sha...  79.1 us
    reduce_scatter x4, waiting for transfers between devices, owner_sum(): lax.psum_scatter(grad.astype(jnp.bfloat16), plane, scatter_dimension=0, t...  42.1 us
    dot_general x4, matrix products, dot_rows(): lax.dot_general(left, right, (((0,), (0,)), ((), ())), preferred_element_...  40.8 us
    pallas_call x1, Pallas kernels, attend_back(): pl.pallas_call(attend_back_kernel, out_shape=(jax.ShapeDtypeStruct((rows,...  25.6 us
    psum x1, blocking collectives, body(): lax.psum((own_vectors, qkv_sums, hidden_sums[0]), plane)  23.4 us
  transfers between devices with their start and end apart: 19, of which 7 were waited for; matrix products, arithmetic and copies ran while one was open for 10% of the time, Pallas kernels for 36%

profile of v2, /device:TPU:8, one launch (start us, length us, event | category | flops | bytes accessed | tf_op | source)
XLA Modules:
  0.0 937.5 jit_solution(6605897588920088689)
XLA Ops:
  7.2 2.1 pad_maximum_fusion.5
  12.0 5.3 all-to-all-start
  18.6 4.0 convert_reduce_fusion
  22.6 79.1 %gather_features.1 = bf16[1024,2048]{1,0:T(8,128)(2,1)S(1)} custom-call(bf16[1024,512]{1,0:T(8,128)(2,1)S(1)} %copy-done.6), custom_call_target="tpu_custom_call" | custom-call | bytes 134217728 | tf_op jit(solution)/shard_map/gather_features/pallas_call | solution.py:462
  101.8 2.0 copy-done
  103.8 10.0 %fusion.1 = bf16[1024,1536]{1,0:T(8,128)(2,1)S(1)} fusion(bf16[1024,2048]{1,0:T(8,128)(2,1)} %copy-done, bf16[2048,1536]{1,0:T(8,128)(2,1)} %all-gather.5.cloned.1.call-done.weight, f32[1536]{0:T(1024)S(1)} %maximum_convert_fusion), kind=kOutput, calls=%fused_computation.8 | convolution fusion | flops 6445596672 | bytes 13637632 | tf_op jit(solution)/shard_map/dot_general | solution.py:23
  113.9 1.6 collective-permute-start.2
  116.2 22.7 %collective-permute-done.2 = bf16[1024,256]{1,0:T(8,128)(2,1)S(1)} collective-permute-done((bf16[1024,256]{1,0:T(8,128)(2,1)S(1)}, bf16[1024,256]{1,0:T(8,128)(2,1)S(1)}, u32[]{:S(2)}, u32[]{:S(2)}) %collective-permute-start.2) | collective-permute-done | bytes 524320 | tf_op jit(solution)/shard_map/ppermute | solution.py:218
  138.9 21.4 %collective-permute-done = bf16[1024,256]{1,0:T(8,128)(2,1)S(1)} collective-permute-done((bf16[1024,256]{1,0:T(8,128)(2,1)S(1)}, bf16[1024,256]{1,0:T(8,128)(2,1)S(1)}, u32[]{:S(2)}, u32[]{:S(2)}) %collective-permute-start) | collective-permute-done | bytes 524320 | tf_op jit(solution)/shard_map/ppermute | solution.py:218
  160.6 2.5 collective-permute-start.1
  163.5 7.9 collective-permute-done.1
  171.7 19.8 %attend.1 = (bf16[2048,256]{1,0:T(8,128)(2,1)S(1)}, f32[2,1,2048]{2,1,0:T(1,128)S(1)}) custom-call(s32[4]{0:T(128)S(1)} %get-tuple-element.142.first, s32[4]{0:T(128)S(1)} %get-tuple-element.143.last, bf16[2048,256]{1,0:T(8,128)(2,1)S(1)} %get-tuple-element.138.q_ref, bf16[2048,256]{1,0:T(8,128)(2,1)S(1)} %pad_maximum_fusion.1.k_ref, ...), custom_call_target="tpu_custom_call" | custom-call | flops 3221225472 | bytes 4194304 | tf_op jit(solution)/shard_map/attend/pallas_call | solution.py:81
  191.6 1.6 collective-permute-start.3
  193.8 14.0 %all_gather.21 = bf16[2,2048]{1,0:T(2,128)(2,1)S(1)} all-gather(bf16[2,512]{1,0:T(2,128)(2,1)S(1)} %copy-done.32), channel_id=1, replica_groups=mesh['fsdp'=4,'ctx'=2,'tp'=4] {'tp'}, dimensions={1}, use_global_device_ids=true | all-gather | bytes 10240 | tf_op jit(solution)/shard_map/all_gather | solution.py:808
  208.3 11.9 %all_gather.22 = bf16[4,2048]{1,0:T(4,128)(2,1)S(1)} all-gather(bf16[4,512]{1,0:T(4,128)(2,1)S(1)} %copy-done.31), channel_id=1, replica_groups=mesh['fsdp'=4,'ctx'=2,'tp'=4] {'tp'}, dimensions={1}, use_global_device_ids=true | all-gather | bytes 20480 | tf_op jit(solution)/shard_map/all_gather | solution.py:809
  220.8 2.3 constant_dynamic-slice_fusion
  224.0 1.2 copy.56
  227.4 131.5 %first_norm.1 = (bf16[1024,2048]{1,0:T(8,128)(2,1)}, f32[256,2048]{1,0:T(8,128)}, f32[256,2048]{1,0:T(8,128)}, f32[256,128]{1,0:T(8,128)}, f32[1024,2048]{1,0:T(8,128)}, /*index=5*/bf16[1024,2048]{1,0:T(8,128)(2,1)}) custom-call(bf16[1024,512]{1,0:T(8,128)(2,1)} %pad_maximum_fusion.3.refs_0_, bf16[2048,512]{1,0:T(8,128)(2,1)} %all-gather.7.cloned.1.call-done.refs_1_.refs_2_, ...), custom_call_target="tpu_custom_call" | custom-call | flops 99999997952 | bytes 134217728 | tf_op jit(solution)/shard_map/first_norm/pallas_call | solution.py:569
  358.9 133.9 %second_norm.1 = (bf16[1024,2048]{1,0:T(8,128)(2,1)}, bf16[256,2048]{1,0:T(8,128)(2,1)}, f32[256,2048]{1,0:T(8,128)}, f32[8,2048]{1,0:T(8,128)}, bf16[1024,2048]{1,0:T(8,128)(2,1)}, /*index=5*/f32[8,2048]{1,0:T(8,128)}) custom-call(bf16[1024,2048]{1,0:T(8,128)(2,1)} %get-tuple-element.35.refs_0_, bf16[2048,2048]{1,0:T(8,128)(2,1)} %all-gather.11.cloned.1.call-done.refs_1_, ...), custom_call_target="tpu_custom_call" | custom-call | flops 99999997952 | bytes 134217728 | tf_op jit(solution)/shard_map/second_norm/pallas_call | solution.py:569
  492.8 126.4 %first_back.1 = (bf16[1024,2048]{1,0:T(8,128)(2,1)}, f32[256,2048]{1,0:T(8,128)}, f32[8,2048]{1,0:T(8,128)}, bf16[1024,512]{1,0:T(8,128)(2,1)}) custom-call(bf16[1024,2048]{1,0:T(8,128)(2,1)} %get-tuple-element.39.refs_0_, bf16[2048,2048]{1,0:T(8,128)(2,1)} %all-gather.9.cloned.1.call-done.refs_2_.refs_1_, ...), custom_call_target="tpu_custom_call" | custom-call | flops 99999997952 | bytes 134217728 | tf_op jit(solution)/shard_map/first_back/pallas_call | solution.py:569
  619.3 1.3 broadcast_select_fusion.8
  623.4 6.4 collective-permute-done.4
  629.8 1.3 broadcast_select_fusion.7
  633.7 1.2 copy-done.12
  636.1 25.6 %attend_back.1 = (bf16[2048,256]{1,0:T(8,128)(2,1)S(1)}, bf16[2048,256]{1,0:T(8,128)(2,1)S(1)}, bf16[2048,256]{1,0:T(8,128)(2,1)S(1)}) custom-call(s32[4]{0:T(128)S(1)} %copy-done.20, s32[4]{0:T(128)S(1)} %copy-done.22, bf16[2048,256]{1,0:T(8,128)(2,1)S(1)} %copy-done.12, bf16[2048,256]{1,0:T(8,128)(2,1)S(1)} %copy-done.8, bf16[2048,256]{1,0:T(8,128)(2,1)S(1)} %copy-done.14, ...), custom_call_target="tpu_custom_call" | custom-call | flops 8589934592 | bytes 8388608 | tf_op jit(solution)/shard_map/attend_back/pallas_call | solution.py:164
  662.7 3.7 convolution_convert_fusion.3
  666.7 2.1 collective-permute-start.7
  668.9 8.9 collective-permute-done.5
  678.0 1.3 select_dynamic-update-slice_fusion.4
  679.3 23.3 %collective-permute-done.6 = bf16[1024,256]{1,0:T(8,128)(2,1)S(1)} collective-permute-done((bf16[1024,256]{1,0:T(8,128)(2,1)S(1)}, bf16[1024,256]{1,0:T(8,128)(2,1)S(1)}, u32[]{:S(2)}, u32[]{:S(2)}) %collective-permute-start.6) | collective-permute-done | bytes 524320 | tf_op jit(solution)/shard_map/ppermute | solution.py:218
  703.5 1.5 copy-done.1
  705.0 8.8 fusion
  713.8 1.6 copy-done.2
  715.6 14.1 %convolution_convert_fusion = bf16[2048,2048]{1,0:T(8,128)(2,1)} fusion(bf16[1024,2048]{1,0:T(8,128)(2,1)} %get-tuple-element.51, bf16[1024,2048]{1,0:T(8,128)(2,1)} %get-tuple-element.35.refs_0_), kind=kOutput, calls=%fused_computation.2 | convolution fusion | flops 8594128896 | bytes 16777216 | tf_op jit(solution)/shard_map/dot_general | solution.py:27
  730.0 14.2 %convolution_convert_fusion.1 = bf16[2048,2048]{1,0:T(8,128)(2,1)} fusion(bf16[1024,2048]{1,0:T(8,128)(2,1)} %get-tuple-element.50, bf16[1024,2048]{1,0:T(8,128)(2,1)} %get-tuple-element.39.refs_0_), kind=kOutput, calls=%fused_computation.3 | convolution fusion | flops 8594128896 | bytes 16777216 | tf_op jit(solution)/shard_map/dot_general | solution.py:27
  744.3 2.8 reshape.111
  747.0 2.4 copy.58
  750.3 8.1 all-to-all-start.1
  758.4 2.9 copy-done.23
  761.3 1.6 copy-done.24
  762.9 83.9 %input_sum.1 = bf16[1024,512]{1,0:T(8,128)(2,1)S(1)} custom-call(bf16[1024,1536]{1,0:T(8,128)(2,1)S(1)} %copy-done.3, bf16[2048,1536]{1,0:T(8,128)(2,1)S(1)} %copy-done.23, f32[256,2048]{1,0:T(8,128)S(1)} %copy-done.24), custom_call_target="tpu_custom_call" | custom-call | flops 60000002048 | bytes 33554432 | tf_op jit(solution)/shard_map/input_sum/pallas_call | solution.py:733
  848.2 23.4 %all-reduce = (f32[1536]{0:T(1024)S(1)}, f32[2048]{0:T(1024)}, f32[6,512]{1,0:T(8,128)S(1)}) all-reduce(f32[1536]{0:T(1024)S(1)} %convert_reduce_fusion.2, f32[2048]{0:T(1024)S(1)} %bitcast.40, f32[6,512]{1,0:T(8,128)} %reduce-scatter.14.cloned.1.call-done), channel_id=1, replica_groups=mesh['fsdp'=4,'ctx'=2,'tp'=4] {'fsdp','ctx'}, use_global_device_ids=true, to_apply=%region_9.10 | all-reduce | flops 6656 | bytes 53248 | tf_op jit(solution)/shard_map/psum | solution.py:913
  873.5 2.3 copy.51
  875.8 1.8 convert_element_type.67
  877.6 1.2 fusion.3
  881.8 2.9 convert_element_type.71
  884.7 42.1 %reduce-scatter.10.cloned.1.call-done = bf16[256,2048]{1,0:T(8,128)(2,1)} async-done(((bf16[2048,2048]{1,0:T(8,128)(2,1)}), bf16[256,2048]{1,0:T(8,128)(2,1)}) %reduce-scatter.10.cloned.1.call-update) | async-done | bytes 1048592 | tf_op jit(solution)/shard_map/reduce_scatter | solution.py:865
  926.8 2.8 convert_element_type.69
  (144 shorter events, 27.7 us)
Async XLA Ops:
  7.2 3.7 copy-start.29
  7.2 96.6 %all-gather.5.cloned.1.call-start = ((), (), s32[]{:S(2)}) async-start(), calls=%async_computation.7 | async-start | bytes 7077888 | tf_op jit(solution)/shard_map/all_gather | solution.py:801
  9.4 218.0 %all-gather.7.cloned.1.call-start = ((), (), s32[]{:S(2)}) async-start(), calls=%async_computation.8 | async-start | bytes 2359296 | tf_op jit(solution)/shard_map/all_gather | solution.py:801
  10.1 12.5 %copy-start.6 = (bf16[1024,512]{1,0:T(8,128)(2,1)S(1)}, bf16[1024,512]{1,0:T(8,128)(2,1)}, u32[]{:S(2)}) copy-start(bf16[1024,512]{1,0:T(8,128)(2,1)} %x_ref.1) | copy-start | bytes 3145732
  10.1 217.2 %all-gather.9.cloned.1.call-start = ((), (), s32[]{:S(2)}) async-start(), calls=%async_computation.9 | async-start | bytes 9437184 | tf_op jit(solution)/shard_map/all_gather | solution.py:801
  12.0 211.2 %all-to-all-start = ((bf16[4,4,64,512]{3,2,0,1:T(8,128)(2,1)}), bf16[4,4,64,512]{3,2,0,1:T(8,128)(2,1)S(1)}, u32[]{:S(2)}, u32[]{:S(2)}) async-start(bf16[4,4,64,512]{3,2,0,1:T(8,128)(2,1)} %copy.48), calls=%async_computation | async-start | bytes 2097152 | tf_op jit(solution)/shard_map/all_to_all | solution.py:766
  17.3 86.5 %copy-start.33 = (bf16[512]{0:T(512)(128)(2,1)S(1)}, bf16[512]{0:T(512)(128)(2,1)}, u32[]{:S(2)}) copy-start(bf16[512]{0:T(512)(128)(2,1)} %param.23) | copy-start | bytes 3076
  17.3 86.5 %copy-start.34 = (bf16[512]{0:T(512)(128)(2,1)S(1)}, bf16[512]{0:T(512)(128)(2,1)}, u32[]{:S(2)}) copy-start(bf16[512]{0:T(512)(128)(2,1)} %param.22) | copy-start | bytes 3076
  17.3 341.6 %all-gather.11.cloned.1.call-start = ((), (), s32[]{:S(2)}) async-start(), calls=%async_computation.10 | async-start | bytes 9437184 | tf_op jit(solution)/shard_map/all_gather | solution.py:801
  17.8 830.4 %reduce-scatter.14.cloned.1.call-start = ((), (), s32[]{:S(2)}) async-start(), calls=%async_computation.15 | async-start | bytes 81920 | tf_op jit(solution)/shard_map/reduce_scatter | solution.py:911
  101.7 2.0 copy-start
  113.9 25.0 %collective-permute-start.2 = (bf16[1024,256]{1,0:T(8,128)(2,1)S(1)}, bf16[1024,256]{1,0:T(8,128)(2,1)S(1)}, u32[]{:S(2)}, u32[]{:S(2)}) collective-permute-start(bf16[1024,256]{1,0:T(8,128)(2,1)S(1)} %get-tuple-element.121), channel_id=1, source_target_pairs={{0,4},{4,0},{1,5},{5,1},{2,6},{6,2},{3,7},{7,3},{8,12},{12,8},{9,1... | collective-permute-start | bytes 1572872 | tf_op jit(solution)/shard_map/ppermute | solution.py:218
  115.5 44.8 %collective-permute-start = (bf16[1024,256]{1,0:T(8,128)(2,1)S(1)}, bf16[1024,256]{1,0:T(8,128)(2,1)S(1)}, u32[]{:S(2)}, u32[]{:S(2)}) collective-permute-start(bf16[1024,256]{1,0:T(8,128)(2,1)S(1)} %get-tuple-element.122), channel_id=1, source_target_pairs={{0,4},{4,0},{1,5},{5,1},{2,6},{6,2},{3,7},{7,3},{8,12},{12,8},{9,1... | collective-permute-start | bytes 1572872 | tf_op jit(solution)/shard_map/ppermute | solution.py:218
  116.2 55.5 %copy-start.15 = (s32[1,2048]{1,0:T(1,128)}, s32[1,2048]{1,0:T(1,128)S(1)}, u32[]{:S(2)}) copy-start(s32[1,2048]{1,0:T(1,128)S(1)} %get-tuple-element.140.high_ref) | copy-start | bytes 24580
  116.2 55.5 %copy-start.17 = (s32[1,2048]{1,0:T(1,128)}, s32[1,2048]{1,0:T(1,128)S(1)}, u32[]{:S(2)}) copy-start(s32[1,2048]{1,0:T(1,128)S(1)} %get-tuple-element.141.low_ref) | copy-start | bytes 24580
  160.6 10.8 %collective-permute-start.1 = (bf16[1024,256]{1,0:T(8,128)(2,1)S(1)}, bf16[1024,256]{1,0:T(8,128)(2,1)S(1)}, u32[]{:S(2)}, u32[]{:S(2)}) collective-permute-start(bf16[1024,256]{1,0:T(8,128)(2,1)S(1)} %get-tuple-element.120), channel_id=1, source_target_pairs={{0,4},{4,0},{1,5},{5,1},{2,6},{6,2},{3,7},{7,3},{8,12},{12,8},{9,1... | collective-permute-start | bytes 1572872 | tf_op jit(solution)/shard_map/ppermute | solution.py:218
  163.3 8.4 copy-start.19
  163.3 8.4 copy-start.21
  163.4 28.0 %copy-start.11 = (bf16[2048,256]{1,0:T(8,128)(2,1)}, bf16[2048,256]{1,0:T(8,128)(2,1)S(1)}, u32[]{:S(2)}) copy-start(bf16[2048,256]{1,0:T(8,128)(2,1)S(1)} %get-tuple-element.138.q_ref) | copy-start | bytes 3145732
  163.5 28.0 %copy-start.13 = (bf16[2048,256]{1,0:T(8,128)(2,1)}, bf16[2048,256]{1,0:T(8,128)(2,1)S(1)}, u32[]{:S(2)}) copy-start(bf16[2048,256]{1,0:T(8,128)(2,1)S(1)} %get-tuple-element.139.v_ref) | copy-start | bytes 3145732
  171.6 19.9 %copy-start.7 = (bf16[2048,256]{1,0:T(8,128)(2,1)}, bf16[2048,256]{1,0:T(8,128)(2,1)S(1)}, u32[]{:S(2)}) copy-start(bf16[2048,256]{1,0:T(8,128)(2,1)S(1)} %pad_maximum_fusion.1.k_ref) | copy-start | bytes 3145732
  171.7 21.5 %copy-start.30 = (bf16[2048]{0:T(1024)(128)(2,1)S(1)}, bf16[2048]{0:T(1024)(128)(2,1)}, u32[]{:S(2)}) copy-start(bf16[2048]{0:T(1024)(128)(2,1)} %param.24) | copy-start | bytes 12292
  171.7 22.1 %copy-start.32 = (bf16[2,512]{1,0:T(2,128)(2,1)S(1)}, bf16[2,512]{1,0:T(2,128)(2,1)}, u32[]{:S(2)}) copy-start(bf16[2,512]{1,0:T(2,128)(2,1)} %param.25) | copy-start | bytes 6148
  171.7 36.7 %copy-start.31 = (bf16[4,512]{1,0:T(4,128)(2,1)S(1)}, bf16[4,512]{1,0:T(4,128)(2,1)}, u32[]{:S(2)}) copy-start(bf16[4,512]{1,0:T(4,128)(2,1)} %param.26) | copy-start | bytes 12292
  191.5 33.7 %copy-start.4 = (bf16[2048,256]{1,0:T(8,128)(2,1)}, bf16[2048,256]{1,0:T(8,128)(2,1)S(1)}, u32[]{:S(2)}) copy-start(bf16[2048,256]{1,0:T(8,128)(2,1)S(1)} %get-tuple-element.34.o_ref) | copy-start | bytes 3145732
  191.6 33.7 %collective-permute-start.3 = (bf16[1024,256]{1,0:T(8,128)(2,1)S(1)}, bf16[1024,256]{1,0:T(8,128)(2,1)S(1)}, u32[]{:S(2)}, u32[]{:S(2)}) collective-permute-start(bf16[1024,256]{1,0:T(8,128)(2,1)S(1)} %broadcast_select_fusion.12), channel_id=1, source_target_pairs={{0,4},{4,0},{1,5},{5,1},{2,6},{6,2},{3,7},{7,3},{8,12},{12,8},{9,1... | collective-permute-start | bytes 1572872 | tf_op jit(solution)/shard_map/ppermute | solution.py:218
  619.2 12.0 %copy-start.16 = (s32[1,2048]{1,0:T(1,128)S(1)}, s32[1,2048]{1,0:T(1,128)}, u32[]{:S(2)}) copy-start(s32[1,2048]{1,0:T(1,128)} %copy-done.15) | copy-start | bytes 24580
  619.2 12.0 %copy-start.18 = (s32[1,2048]{1,0:T(1,128)S(1)}, s32[1,2048]{1,0:T(1,128)}, u32[]{:S(2)}) copy-start(s32[1,2048]{1,0:T(1,128)} %copy-done.17) | copy-start | bytes 24580
  619.2 12.0 %copy-start.20 = (s32[4]{0:T(128)S(1)}, s32[4]{0:T(128)}, u32[]{:S(2)}) copy-start(s32[4]{0:T(128)} %copy-done.19) | copy-start | bytes 52
  619.3 12.0 %copy-start.22 = (s32[4]{0:T(128)S(1)}, s32[4]{0:T(128)}, u32[]{:S(2)}) copy-start(s32[4]{0:T(128)} %copy-done.21) | copy-start | bytes 52
  620.5 9.2 collective-permute-start.4
  623.3 252.5 %reduce-scatter.8.cloned.1.call-start = ((), (), s32[]{:S(2)}) async-start(), calls=%async_computation.12 | async-start | bytes 2359296 | tf_op jit(solution)/shard_map/reduce_scatter | solution.py:865
  636.1 26.5 %copy-start.26 = (bf16[1024,256]{1,0:T(8,128)(2,1)S(1)}, bf16[1024,256]{1,0:T(8,128)(2,1)}, u32[]{:S(2)}) copy-start(bf16[1024,256]{1,0:T(8,128)(2,1)} %copy-done.25) | copy-start | bytes 1572868
  636.1 26.5 %copy-start.28 = (bf16[1024,256]{1,0:T(8,128)(2,1)S(1)}, bf16[1024,256]{1,0:T(8,128)(2,1)}, u32[]{:S(2)}) copy-start(bf16[1024,256]{1,0:T(8,128)(2,1)} %copy-done.27) | copy-start | bytes 1572868
  636.1 26.5 %copy-start.35 = (bf16[1024,2048]{1,0:T(8,128)(2,1)S(1)}, bf16[1024,2048]{1,0:T(8,128)(2,1)}, u32[]{:S(2)}) copy-start(bf16[1024,2048]{1,0:T(8,128)(2,1)} %get-tuple-element.49) | copy-start | bytes 12582916
  662.6 15.2 %collective-permute-start.5 = (bf16[1024,256]{1,0:T(8,128)(2,1)}, bf16[1024,256]{1,0:T(8,128)(2,1)}, u32[]{:S(2)}, u32[]{:S(2)}) collective-permute-start(bf16[1024,256]{1,0:T(8,128)(2,1)} %broadcast_select_fusion.4), channel_id=1, source_target_pairs={{0,4},{4,0},{1,5},{5,1},{2,6},{6,2},{3,7},{7,3},{8,12},{12,8},{9,1... | collective-permute-start | bytes 1572872 | tf_op jit(solution)/shard_map/ppermute | solution.py:218
  666.4 211.2 %reduce-scatter.6.cloned.1.call-start = ((), (), s32[]{:S(2)}) async-start(), calls=%async_computation.11 | async-start | bytes 7077888 | tf_op jit(solution)/shard_map/reduce_scatter | solution.py:865
  666.7 36.4 %collective-permute-start.7 = (bf16[1024,256]{1,0:T(8,128)(2,1)S(1)}, bf16[1024,256]{1,0:T(8,128)(2,1)S(1)}, u32[]{:S(2)}, u32[]{:S(2)}) collective-permute-start(bf16[1024,256]{1,0:T(8,128)(2,1)S(1)} %broadcast_select_fusion), channel_id=1, source_target_pairs={{0,4},{4,0},{1,5},{5,1},{2,6},{6,2},{3,7},{7,3},{8,12},{12,8},{9,1... | collective-permute-start | bytes 1572872 | tf_op jit(solution)/shard_map/ppermute | solution.py:218
  668.8 33.8 %collective-permute-start.6 = (bf16[1024,256]{1,0:T(8,128)(2,1)S(1)}, bf16[1024,256]{1,0:T(8,128)(2,1)S(1)}, u32[]{:S(2)}, u32[]{:S(2)}) collective-permute-start(bf16[1024,256]{1,0:T(8,128)(2,1)S(1)} %broadcast_select_fusion.2), channel_id=1, source_target_pairs={{0,4},{4,0},{1,5},{5,1},{2,6},{6,2},{3,7},{7,3},{8,12},{12,8},{9,1... | collective-permute-start | bytes 1572872 | tf_op jit(solution)/shard_map/ppermute | solution.py:218
  702.8 2.2 copy-start.1
  713.8 1.6 copy-start.2
  715.5 166.3 %reduce-scatter.12.cloned.1.call-start = ((), (), s32[]{:S(2)}) async-start(), calls=%async_computation.14 | async-start | bytes 9437184 | tf_op jit(solution)/shard_map/reduce_scatter | solution.py:865
  729.7 197.1 %reduce-scatter.10.cloned.1.call-start = ((), (), s32[]{:S(2)}) async-start(), calls=%async_computation.13 | async-start | bytes 9437184 | tf_op jit(solution)/shard_map/reduce_scatter | solution.py:865
  744.2 14.1 %copy-start.3 = (bf16[1024,1536]{1,0:T(8,128)(2,1)S(1)}, bf16[1024,1536]{1,0:T(8,128)(2,1)}, u32[]{:S(2)}) copy-start(bf16[1024,1536]{1,0:T(8,128)(2,1)} %copy-done.2) | copy-start | bytes 9437188
  750.3 123.2 %all-to-all-start.1 = ((bf16[4,4,64,512]{3,2,0,1:T(8,128)(2,1)}), bf16[4,4,64,512]{3,2,0,1:T(8,128)(2,1)}, u32[]{:S(2)}, u32[]{:S(2)}) async-start(bf16[4,4,64,512]{3,2,0,1:T(8,128)(2,1)} %bitcast.32), calls=%async_computation.1 | async-start | bytes 2097152 | tf_op jit(solution)/shard_map/all_to_all | solution.py:774
  758.4 2.9 copy-start.23
  761.3 1.6 copy-start.24
  881.8 47.8 %copy-start.10 = (bf16[1024,512]{1,0:T(8,128)(2,1)S(1)}, bf16[1024,512]{1,0:T(8,128)(2,1)}, u32[]{:S(2)}) copy-start(bf16[1024,512]{1,0:T(8,128)(2,1)} %copy-done.9) | copy-start | bytes 3145732
  (7 other events, 7.6 us)
Sparse Core Ops, SparseCore 0:
  10.5 46.6 all-gather.4
  59.1 27.8 all-gather.6
  88.9 74.9 all-gather.8
  165.6 65.2 all-gather.10
  623.4 17.2 reduce-scatter.13
  666.5 44.9 reduce-scatter.7
  715.6 61.1 reduce-scatter.5
  780.6 71.3 reduce-scatter.11
  855.5 71.2 reduce-scatter.9

commit v3 on v2

--- a/solution.py
+++ b/solution.py
@@ -279,6 +279,46 @@
         pl.semaphore_wait(barrier, 2)
 
 
+def peers_along_tp(me, count):
+    return [{"tp": lax.rem(me + i, count)} for i in range(1, count)]
+
+
+def greet_peers(peers):
+    barrier = pltpu.get_barrier_semaphore()
+    for peer in peers:
+        pl.semaphore_signal(barrier, inc=1, device_id=peer, device_id_type=MESH)
+    pl.semaphore_wait(barrier, len(peers))
+
+
+class Exchange:
+    def __init__(self, peers, sent, got, source, place):
+        self.peers, self.sent, self.got = peers, sent, got
+        self.source, self.place = source, place
+
+    def copies(self):
+        for i, peer in enumerate(self.peers):
+            yield pltpu.make_async_remote_copy(
+                src_ref=self.source(i + 1),
+                dst_ref=self.place(i),
+                send_sem=self.sent.at[i],
+                recv_sem=self.got.at[i],
+                device_id=peer,
+                device_id_type=MESH,
+            )
+
+    def start(self):
+        for copy in self.copies():
+            copy.start()
+
+    def wait_arrivals(self):
+        for copy in self.copies():
+            copy.wait_recv()
+
+    def wait_sent(self):
+        for copy in self.copies():
+            copy.wait_send()
+
+
 def at_distance(me, count, distance, action):
     for index in (me - distance, me + distance):
 
@@ -425,7 +465,9 @@
     ]
 
 
-def gather_kernel(count, x_ref, out_ref, sent, got):
+def gather_kernel(
+    count, x_ref, marks_ref, out_ref, marks_out, slots, sent, got, marks_sent, marks_got
+):
     me = lax.axis_index("tp")
     height = x_ref.shape[0] // PIECES
     width = x_ref.shape[1]
@@ -440,31 +482,51 @@
         return x_ref.at[pl.ds(pl.multiple_of(piece * height, height), height)]
 
     line = Line(me, count, None, None, None, view, sent, got)
-    greet(me, count)
+    peers = peers_along_tp(me, count)
+    greet_peers(peers)
 
     @pl.loop(0, PIECES)
     def _(piece):
         line.spread_start(piece, source(piece))
 
-    out_ref[:, pl.ds(pl.multiple_of(me * width, width), width)] = x_ref[...]
+    marks = Exchange(
+        peers, marks_sent, marks_got, lambda _: marks_ref, lambda i: slots.at[i]
+    )
+    marks.start()
+    own = pl.ds(pl.multiple_of(me * width, width), width)
+    out_ref[:, own] = x_ref[...]
+    marks_out[:, own] = marks_ref[...]
     for distance in range(1, count):
 
         @pl.loop(0, PIECES)
         def _(piece, distance=distance):
             line.spread_onward(piece, distance)
 
+    marks.wait_arrivals()
+    for i in range(1, count):
+        owner = lax.rem(me - i + count, count)
+        marks_out[:, pl.ds(pl.multiple_of(owner * width, width), width)] = slots[i - 1]
+    marks.wait_sent()
     line.spread_finish(PIECES, source)
 
 
-def gather_features(x, collective_id):
+def gather_features(x, marks, collective_id):
     count = lax.axis_size("tp")
     rows, width = x.shape
     return pl.pallas_call(
         functools.partial(gather_kernel, count),
-        out_shape=jax.ShapeDtypeStruct((rows, count * width), x.dtype),
-        in_specs=[pl.BlockSpec(memory_space=pltpu.VMEM)],
-        out_specs=pl.BlockSpec(memory_space=pltpu.VMEM),
-        scratch_shapes=line_semaphores(count, PIECES)[1],
+        out_shape=[
+            jax.ShapeDtypeStruct((rows, count * width), x.dtype),
+            jax.ShapeDtypeStruct((marks.shape[0], count * width), marks.dtype),
+        ],
+        in_specs=[pl.BlockSpec(memory_space=pltpu.VMEM)] * 2,
+        out_specs=[pl.BlockSpec(memory_space=pltpu.VMEM)] * 2,
+        scratch_shapes=[
+            pltpu.VMEM((count - 1, *marks.shape), marks.dtype),
+            *line_semaphores(count, PIECES)[1],
+            pltpu.SemaphoreType.DMA((count - 1,)),
+            pltpu.SemaphoreType.DMA((count - 1,)),
+        ],
         compiler_params=pltpu.CompilerParams(
             collective_id=collective_id, has_side_effects=True, vmem_limit_bytes=16 << 20
         ),
@@ -472,7 +534,7 @@
             flops=0, bytes_accessed=64 * rows * count * width, transcendentals=0
         ),
         name="gather_features",
-    )(x)
+    )(x, marks)
 
 
 def relay_kernel(count, row_step, use_step, sizes, *refs):
@@ -684,15 +746,41 @@
     attended_grad[rows, :] = dot_plain(chunk, weight[...]).astype(jnp.bfloat16)
 
 
+def peers_in_plane(sizes):
+    fsdp, ctx = lax.axis_index("fsdp"), lax.axis_index("ctx")
+    return [
+        {"fsdp": lax.rem(fsdp + i, sizes[0]), "ctx": lax.rem(ctx + j, sizes[1])}
+        for i in range(sizes[0])
+        for j in range(sizes[1])
+        if i or j
+    ]
+
+
 def input_kernel(
-    count, x_ref, weight, inner_ref, out_ref, term_ref, total, slots, sum_sent, sum_got
+    sizes, x_ref, weight, inner_ref, rows_ref, hidden_ref, out_ref, vectors_ref,
+    term_ref, total, slots, own_vectors, tp_slots, plane_slots,
+    sum_sent, sum_got, tp_sent, tp_got, plane_sent, plane_got,
 ):
+    count = sizes[2]
     me = lax.axis_index("tp")
     height = x_ref.shape[0] // PIECES
     own = height // count
     width = out_ref.shape[1]
     line = Line(me, count, slots, sum_sent, sum_got, None, None, None)
-    greet(me, count)
+    tp_peers, plane_peers = peers_along_tp(me, count), peers_in_plane(sizes)
+    greet_peers(tp_peers + plane_peers)
+
+    def own_part(index):
+        return rows_ref.at[:, pl.ds(pl.multiple_of(index * width, width), width)]
+
+    over_tp = Exchange(
+        tp_peers, tp_sent, tp_got,
+        lambda i: own_part(lax.rem(me + i, count)), lambda i: tp_slots.at[i],
+    )
+    over_plane = Exchange(
+        plane_peers, plane_sent, plane_got, lambda _: own_vectors, lambda i: plane_slots.at[i]
+    )
+    over_tp.start()
 
     def terms(piece):
         def term(owner):
@@ -707,12 +795,29 @@
 
         return term
 
+    def pack():
+        over_tp.wait_arrivals()
+        own_vectors[0:8, :] = own_part(me)[...]
+        for i in range(count - 1):
+            own_vectors[0:8, :] += tp_slots[i]
+        own_vectors[8:, :] = jnp.zeros_like(own_vectors[8:, :])
+        hidden_rows = hidden_ref.shape[1] // width
+        for i in range(hidden_rows):
+            own_vectors[8 + i : 9 + i, :] = hidden_ref[0:1, i * width : (i + 1) * width]
+        for i in range(x_ref.shape[1] // width):
+            part = x_ref[:, i * width : (i + 1) * width].astype(jnp.float32)
+            place = 8 + hidden_rows + i
+            own_vectors[place : place + 1, :] = jnp.sum(part, axis=0, keepdims=True)
+        over_plane.start()
+
     @pl.loop(0, PIECES + 1)
     def _(step):
         @pl.when(step < PIECES)
         def _():
             line.sum_start(step, terms(step))
             line.sum_onward(step, terms(step))
+
+        pl.when(step == 1)(pack)
 
         @pl.when(step >= 1)
         def _():
@@ -722,24 +827,43 @@
             rows = pl.ds(pl.multiple_of(piece * height, height), height)
             out_ref[rows, :] = total[...].astype(out_ref.dtype)
 
+    over_plane.wait_arrivals()
+    vectors_ref[...] = own_vectors[...]
+    for i in range(len(plane_peers)):
+        vectors_ref[...] += plane_slots[i]
+    over_tp.wait_sent()
+    over_plane.wait_sent()
     line.sum_finish(PIECES)
 
 
-def input_sum(x, weight, inner, collective_id):
-    count = lax.axis_size("tp")
+def input_sum(x, weight, inner, row_sums, hidden_sums, collective_id):
+    sizes = tuple(lax.axis_size(axis) for axis in ("fsdp", "ctx", "tp"))
+    count = sizes[2]
+    others = sizes[0] * sizes[1] - 1
     rows = x.shape[0]
     width = weight.shape[0] // count
     height = rows // PIECES
+    packed = 8 + -(-(hidden_sums.shape[1] + x.shape[1]) // (8 * width)) * 8
     return pl.pallas_call(
-        functools.partial(input_kernel, count),
-        out_shape=jax.ShapeDtypeStruct((rows, width), jnp.bfloat16),
-        in_specs=[pl.BlockSpec(memory_space=pltpu.VMEM)] * 3,
-        out_specs=pl.BlockSpec(memory_space=pltpu.VMEM),
+        functools.partial(input_kernel, sizes),
+        out_shape=[
+            jax.ShapeDtypeStruct((rows, width), jnp.bfloat16),
+            jax.ShapeDtypeStruct((packed, width), jnp.float32),
+        ],
+        in_specs=[pl.BlockSpec(memory_space=pltpu.VMEM)] * 5,
+        out_specs=[pl.BlockSpec(memory_space=pltpu.VMEM)] * 2,
         scratch_shapes=[
             pltpu.VMEM((height, width), jnp.float32),
             pltpu.VMEM((height, width), jnp.float32),
             pltpu.VMEM((PIECES, count + 1, height, width), jnp.bfloat16),
+            pltpu.VMEM((packed, width), jnp.float32),
+            pltpu.VMEM((count - 1, 8, width), jnp.float32),
+            pltpu.VMEM((others, packed, width), jnp.float32),
             *line_semaphores(count, PIECES)[0],
+            pltpu.SemaphoreType.DMA((count - 1,)),
+            pltpu.SemaphoreType.DMA((count - 1,)),
+            pltpu.SemaphoreType.DMA((others,)),
+            pltpu.SemaphoreType.DMA((others,)),
         ],
         compiler_params=pltpu.CompilerParams(
             collective_id=collective_id, has_side_effects=True, vmem_limit_bytes=40 << 20
@@ -748,7 +872,7 @@
             flops=60_000_000_000, bytes_accessed=64 * rows * width, transcendentals=0
         ),
         name="input_sum",
-    )(x, weight, inner)
+    )(x, weight, inner, row_sums, hidden_sums)
 
 
 def to_own_rows(wide):
@@ -801,12 +925,15 @@
         return lax.all_gather(weight, plane, axis=0, tiled=True)
 
     wide_qkv = weight_rows(jnp.concatenate([query_weight, key_weight, value_weight], axis=1))
-    wide_tokens = gather_features(tokens, 0)
+    marks = jnp.concatenate(
+        [norm_gains, row_biases, jnp.zeros((10, norm_gains.shape[1]), norm_gains.dtype)]
+    )
+    wide_tokens, wide_marks = gather_features(tokens, marks, 0)
+    gains = wide_marks[:2].astype(jnp.float32)
+    biases = wide_marks[2:6].astype(jnp.float32)
     full_output = weight_rows(output_weight)
     full_expand = weight_rows(expand_weight)
     full_shrink = weight_rows(shrink_weight)
-    gains = lax.all_gather(norm_gains, "tp", axis=1, tiled=True).astype(jnp.float32)
-    biases = lax.all_gather(row_biases, "tp", axis=1, tiled=True).astype(jnp.float32)
     upstream = spread_own(out_grad)
 
     qkv_bias = jnp.concatenate([query_bias, jnp.zeros_like(query_bias), value_bias])
@@ -863,10 +990,13 @@
 
     def owner_sum(grad):
         return lax.psum_scatter(
-            grad.astype(jnp.bfloat16), plane, scatter_dimension=0, tiled=True
+            grad, plane, scatter_dimension=0, tiled=True
         ).astype(jnp.float32)
 
-    shrink_grad = owner_sum(dot_rows(ffn_low, activated))
+    hidden_low, shrink_part = lax.optimization_barrier(
+        (hidden_low, dot_rows(ffn_low, activated).astype(jnp.bfloat16))
+    )
+    shrink_grad = owner_sum(shrink_part)
     branch_low, grad_inner, first_sums, attended_grad = relay(
         hidden_low, full_expand, full_output,
         [grad_second, normed_one, inverse_one, gains], first_back_step,
@@ -875,8 +1005,15 @@
         [shape((rows, head_cols), jnp.bfloat16)],
         3, "first_back",
     )
-    expand_grad = owner_sum(dot_rows(norm_low, hidden_low))
-    output_grad = owner_sum(dot_rows(branch_low, attended))
+    attended_grad, expand_part, output_part = lax.optimization_barrier(
+        (
+            attended_grad,
+            dot_rows(norm_low, hidden_low).astype(jnp.bfloat16),
+            dot_rows(branch_low, attended).astype(jnp.bfloat16),
+        )
+    )
+    expand_grad = owner_sum(expand_part)
+    output_grad = owner_sum(output_part)
 
     if by_heads:
         grads = attend_back(
@@ -898,21 +1035,20 @@
 
         key_low, value_low = fold(key_ext), fold(value_ext)
     qkv_low = jnp.concatenate([query_low, key_low, value_low], axis=1)
-    qkv_grad = owner_sum(dot_rows(wide_tokens, qkv_low))
-    input_grad = input_sum(qkv_low, wide_qkv, grad_inner, 4)
-    gain_one_grad, shift_one_grad, branch_bias_grad = first_sums[:3]
-    gain_two_grad, shift_two_grad, ffn_bias_grad = second_sums[:3]
-    row_vectors = jnp.stack(
+    qkv_low, qkv_part = lax.optimization_barrier(
+        (qkv_low, dot_rows(wide_tokens, qkv_low).astype(jnp.bfloat16))
+    )
+    qkv_grad = owner_sum(qkv_part)
+    row_sums = jnp.concatenate(
         [
-            gain_one_grad, gain_two_grad,
-            branch_bias_grad, shift_one_grad, ffn_bias_grad, shift_two_grad,
+            first_sums[0:1], second_sums[0:1],
+            first_sums[2:3], first_sums[1:2], second_sums[2:3], second_sums[1:2],
+            jnp.zeros_like(first_sums[:2]),
         ]
     )
-    own_vectors = lax.psum_scatter(row_vectors, "tp", scatter_dimension=1, tiled=True)
-    qkv_sums = jnp.sum(qkv_low.astype(jnp.float32), axis=0)
-    own_vectors, qkv_sums, hidden_bias_grad = lax.psum(
-        (own_vectors, qkv_sums, hidden_sums[0]), plane
-    )
+    input_grad, vectors = input_sum(qkv_low, wide_qkv, grad_inner, row_sums, hidden_sums[:1], 4)
+    hidden_rows = hidden_cols // head_cols
+    query_place = 8 + hidden_rows
     return (
         mixed,
         input_grad,
@@ -922,11 +1058,11 @@
         output_grad,
         expand_grad,
         shrink_grad,
-        qkv_sums[:head_cols],
-        qkv_sums[2 * head_cols :],
-        hidden_bias_grad,
-        own_vectors[:2],
-        own_vectors[2:],
+        vectors[query_place],
+        vectors[query_place + 2],
+        vectors[8:query_place].reshape(-1),
+        vectors[:2],
+        vectors[2:6],
     )
 
 

time: 947 us -> 983 us (1.038)
  waiting for transfers between devices: 135 us -> 197 us
  blocking collectives: 49.3 us -> 0 us
  Pallas kernels: 600 us -> 621 us
  local copies, waits for them, and re-layouts: 40.8 us -> 30.9 us
    reduce_scatter x5 -> x4, waiting for transfers between devices: 42.1 us -> 111 us  [owner_sum(): lax.psum_scatter(grad, plane, scatter_dimension=0, tiled=True)]
    all_gather x2 -> x0, blocking collectives: 25.8 us -> none  [the longest x1 14 us: body(): lax.all_gather(norm_gains, 'tp', axis=1, tiled=True).astype(jnp.float32)]
    pallas_call x2, Pallas kernels: 163 us -> 187 us  [the longest x1 106 us: input_sum(): pl.pallas_call(functools.partial(input_kernel, sizes), out_shape=[jax.Sha...]
    psum x1 -> x0, blocking collectives: 23.4 us -> none  [body(): lax.psum((own_vectors, qkv_sums, hidden_sums[0]), plane)]
    pallas_call x3, Pallas kernels: 392 us -> 375 us  [relay(): pl.pallas_call(functools.partial(relay_kernel, count, row_step, use_step,...]
    unnamed x77 -> x71, local copies, waits for them, and re-layouts: 21.8 us -> 12.2 us
  transfers between devices with their start and end apart: 19 -> 18, of which waited for: 7 -> 10; matrix products, arithmetic and copies ran while one was open for 10% -> 6% of each run, Pallas kernels for 36% -> 36%
where the time goes in v3:
time: 983 us; the launch traced here: 970 us
  Pallas kernels  621 us (63%)
  waiting for transfers between devices  197 us (20%)
  matrix products  53 us (5%)
  local copies, waits for them, and re-layouts  30.9 us (3%)
  starting transfers between devices  26.8 us (3%)
  other arithmetic  24.9 us (3%)
  between operations  15.3 us (2%)
    pallas_call x3, Pallas kernels, relay(): pl.pallas_call(functools.partial(relay_kernel, count, row_step, use_step,...  375 us
    reduce_scatter x4, waiting for transfers between devices, owner_sum(): lax.psum_scatter(grad, plane, scatter_dimension=0, tiled=True)  111 us
    pallas_call x1, Pallas kernels, input_sum(): pl.pallas_call(functools.partial(input_kernel, sizes), out_shape=[jax.Sha...  106 us
    ppermute x8, waiting for transfers between devices, swap_halves(): got = lax.ppermute(other, 'ctx', [(0, 1), (1, 0)])  82.9 us
    pallas_call x1, Pallas kernels, gather_features(): pl.pallas_call(functools.partial(gather_kernel, count), out_shape=[jax.Sh...  80.1 us
    dot_general x4, matrix products, dot_rows(): lax.dot_general(left, right, (((0,), (0,)), ((), ())), preferred_element_...  43 us
    pallas_call x1, Pallas kernels, attend_back(): pl.pallas_call(attend_back_kernel, out_shape=(jax.ShapeDtypeStruct((rows,...  33.7 us
    pallas_call x1, Pallas kernels, attend(): pl.pallas_call(attend_kernel, out_shape=(jax.ShapeDtypeStruct((rows, widt...  26.4 us
  transfers between devices with their start and end apart: 18, of which 10 were waited for; matrix products, arithmetic and copies ran while one was open for 6% of the time, Pallas kernels for 36%

profile of v3, /device:TPU:8, one launch (start us, length us, event | category | flops | bytes accessed | tf_op | source)
XLA Modules:
  0.0 969.5 jit_solution(7918773025752986005)
XLA Ops:
  7.2 2.1 pad_maximum_fusion.5
  12.0 5.3 all-to-all-start
  18.6 4.0 convert_reduce_fusion
  22.8 80.1 %gather_features.1 = (bf16[1024,2048]{1,0:T(8,128)(2,1)S(1)}, bf16[16,2048]{1,0:T(8,128)(2,1)S(1)}) custom-call(bf16[1024,512]{1,0:T(8,128)(2,1)S(1)} %copy-done.2, bf16[16,512]{1,0:T(8,128)(2,1)S(1)} %maximum_maximum_fusion.marks_ref), custom_call_target="tpu_custom_call" | custom-call | bytes 134217728 | tf_op jit(solution)/shard_map/gather_features/pallas_call | solution.py:516
  102.9 2.0 copy-done.9
  105.0 10.0 %add_convert_fusion = bf16[1024,1536]{1,0:T(8,128)(2,1)S(1)} fusion(bf16[1024,2048]{1,0:T(8,128)(2,1)} %copy-done.9, bf16[2048,1536]{1,0:T(8,128)(2,1)} %all-gather.5.cloned.1.call-done.weight, f32[1536]{0:T(1024)S(1)} %maximum_convert_fusion), kind=kOutput, calls=%fused_computation.5 | convolution fusion | flops 6445596672 | bytes 13637632 | tf_op jit(solution)/shard_map/dot_general | solution.py:23
  115.1 1.6 collective-permute-start
  117.9 23.3 %collective-permute-done = bf16[1024,256]{1,0:T(8,128)(2,1)S(1)} collective-permute-done((bf16[1024,256]{1,0:T(8,128)(2,1)S(1)}, bf16[1024,256]{1,0:T(8,128)(2,1)S(1)}, u32[]{:S(2)}, u32[]{:S(2)}) %collective-permute-start) | collective-permute-done | bytes 524320 | tf_op jit(solution)/shard_map/ppermute | solution.py:218
  141.3 20.1 %collective-permute-done.2 = bf16[1024,256]{1,0:T(8,128)(2,1)S(1)} collective-permute-done((bf16[1024,256]{1,0:T(8,128)(2,1)S(1)}, bf16[1024,256]{1,0:T(8,128)(2,1)S(1)}, u32[]{:S(2)}, u32[]{:S(2)}) %collective-permute-start.2) | collective-permute-done | bytes 524320 | tf_op jit(solution)/shard_map/ppermute | solution.py:218
  161.4 1.7 broadcast_select_fusion.15
  163.1 1.5 collective-permute-start.1
  164.8 1.7 pad_maximum_fusion
  166.4 6.3 collective-permute-done.1
  174.0 26.4 %attend.1 = (bf16[2048,256]{1,0:T(8,128)(2,1)S(1)}, f32[2,1,2048]{2,1,0:T(1,128)S(1)}) custom-call(s32[4]{0:T(128)S(1)} %get-tuple-element.111.first, s32[4]{0:T(128)S(1)} %get-tuple-element.112.last, bf16[2048,256]{1,0:T(8,128)(2,1)S(1)} %get-tuple-element.107.q_ref, bf16[2048,256]{1,0:T(8,128)(2,1)S(1)} %pad_maximum_fusion.1.k_ref, ...), custom_call_target="tpu_custom_call" | custom-call | flops 3221225472 | bytes 4194304 | tf_op jit(solution)/shard_map/attend/pallas_call | solution.py:81
  200.6 1.7 collective-permute-start.3
  202.3 2.3 constant_dynamic-slice_fusion
  205.8 2.0 copy.40
  207.9 1.2 copy.44
  209.1 11.9 %collective-permute-done.3 = bf16[1024,256]{1,0:T(8,128)(2,1)S(1)} collective-permute-done((bf16[1024,256]{1,0:T(8,128)(2,1)S(1)}, bf16[1024,256]{1,0:T(8,128)(2,1)S(1)}, u32[]{:S(2)}, u32[]{:S(2)}) %collective-permute-start.3) | collective-permute-done | bytes 524320 | tf_op jit(solution)/shard_map/ppermute | solution.py:218
  223.1 131.5 %first_norm.1 = (bf16[1024,2048]{1,0:T(8,128)(2,1)}, f32[256,2048]{1,0:T(8,128)}, f32[256,2048]{1,0:T(8,128)}, f32[256,128]{1,0:T(8,128)}, f32[1024,2048]{1,0:T(8,128)}, /*index=5*/bf16[1024,2048]{1,0:T(8,128)(2,1)}) custom-call(bf16[1024,512]{1,0:T(8,128)(2,1)} %pad_maximum_fusion.3.refs_0_, bf16[2048,512]{1,0:T(8,128)(2,1)} %all-gather.7.cloned.1.call-done.refs_1_.refs_2_, ...), custom_call_target="tpu_custom_call" | custom-call | flops 99999997952 | bytes 134217728 | tf_op jit(solution)/shard_map/first_norm/pallas_call | solution.py:631
  354.6 125.5 %second_norm.1 = (bf16[1024,2048]{1,0:T(8,128)(2,1)}, bf16[256,2048]{1,0:T(8,128)(2,1)}, f32[256,2048]{1,0:T(8,128)}, f32[8,2048]{1,0:T(8,128)}, bf16[1024,2048]{1,0:T(8,128)(2,1)}, /*index=5*/f32[8,2048]{1,0:T(8,128)}) custom-call(bf16[1024,2048]{1,0:T(8,128)(2,1)} %get-tuple-element.48.refs_0_, bf16[2048,2048]{1,0:T(8,128)(2,1)} %all-gather.11.cloned.1.call-done.refs_1_, ...), custom_call_target="tpu_custom_call" | custom-call | flops 99999997952 | bytes 134217728 | tf_op jit(solution)/shard_map/second_norm/pallas_call | solution.py:631
  480.1 14.1 %convolution_convert_fusion.2 = bf16[2048,2048]{1,0:T(8,128)(2,1)} fusion(bf16[1024,2048]{1,0:T(8,128)(2,1)} %get-tuple-element.53, bf16[1024,2048]{1,0:T(8,128)(2,1)} %get-tuple-element.48.refs_0_), kind=kOutput, calls=%fused_computation.4 | convolution fusion | flops 8594128896 | bytes 16777216 | tf_op jit(solution)/shard_map/dot_general | solution.py:27
  494.3 117.7 %first_back.1 = (bf16[1024,2048]{1,0:T(8,128)(2,1)}, f32[256,2048]{1,0:T(8,128)}, f32[8,2048]{1,0:T(8,128)}, bf16[1024,512]{1,0:T(8,128)(2,1)}) custom-call(bf16[1024,2048]{1,0:T(8,128)(2,1)} %get-tuple-element.54.refs_0_, bf16[2048,2048]{1,0:T(8,128)(2,1)} %all-gather.9.cloned.1.call-done.refs_2_.refs_1_, ...), custom_call_target="tpu_custom_call" | custom-call | flops 99999997952 | bytes 134217728 | tf_op jit(solution)/shard_map/first_back/pallas_call | solution.py:631
  612.0 5.9 convolution_convert_fusion.3
  617.9 14.1 %convolution_convert_fusion.1 = bf16[2048,2048]{1,0:T(8,128)(2,1)} fusion(bf16[1024,2048]{1,0:T(8,128)(2,1)} %get-tuple-element.59, bf16[1024,2048]{1,0:T(8,128)(2,1)} %get-tuple-element.54.refs_0_), kind=kOutput, calls=%fused_computation.3 | convolution fusion | flops 8594128896 | bytes 16777216 | tf_op jit(solution)/shard_map/dot_general | solution.py:27
  632.1 3.8 collective-permute-start.4
  635.9 7.2 collective-permute-done.4
  643.3 33.7 %attend_back.1 = (bf16[2048,256]{1,0:T(8,128)(2,1)S(1)}, bf16[2048,256]{1,0:T(8,128)(2,1)S(1)}, bf16[2048,256]{1,0:T(8,128)(2,1)S(1)}) custom-call(s32[4]{0:T(128)S(1)} %copy-done.18, s32[4]{0:T(128)S(1)} %copy-done.20, bf16[2048,256]{1,0:T(8,128)(2,1)S(1)} %copy-done.6, bf16[2048,256]{1,0:T(8,128)(2,1)S(1)} %copy-done.4, bf16[2048,256]{1,0:T(8,128)(2,1)S(1)} %copy-done.8, ...), custom_call_target="tpu_custom_call" | custom-call | flops 8589934592 | bytes 8388608 | tf_op jit(solution)/shard_map/attend_back/pallas_call | solution.py:164
  677.9 2.0 collective-permute-start.5
  680.5 2.1 collective-permute-start.7
  682.5 4.9 collective-permute-done.5
  687.6 1.2 select_dynamic-update-slice_fusion.4
  688.8 4.1 collective-permute-done.6
  693.3 5.2 collective-permute-done.7
  698.9 8.8 convolution_convert_fusion
  707.7 1.7 copy-done.11
  711.8 2.0 reshape.114
  715.0 7.7 all-to-all-start.1
  724.7 1.9 copy-done.12
  726.6 2.8 copy-done.21
  729.4 106.4 %input_sum.1 = (bf16[1024,512]{1,0:T(8,128)(2,1)S(1)}, f32[16,512]{1,0:T(8,128)S(1)}) custom-call(bf16[1024,1536]{1,0:T(8,128)(2,1)S(1)} %copy-done.12, bf16[2048,1536]{1,0:T(8,128)(2,1)S(1)} %copy-done.21, f32[256,2048]{1,0:T(8,128)S(1)} %copy-done.22, f32[8,2048]{1,0:T(8,128)S(1)} %concatenate.43.rows_ref, f32[1,2048]{1,0:T(1,128)S(1)} %slice.132.hidden_ref), custom_call_target="tpu_custom_call" | custom-call | flops 60000002048 | bytes 33554432 | tf_op jit(solution)/shard_map/input_sum/pallas_call | solution.py:847
  838.2 2.3 copy.42
  840.5 1.8 convert_element_type.58
  842.3 2.3 fusion.1
  844.6 38.7 %reduce-scatter.9.cloned.1.call-done = bf16[256,2048]{1,0:T(8,128)(2,1)} async-done(((bf16[2048,2048]{1,0:T(8,128)(2,1)}), bf16[256,2048]{1,0:T(8,128)(2,1)}) %reduce-scatter.9.cloned.1.call-update) | async-done | bytes 1048592 | tf_op jit(solution)/shard_map/reduce_scatter | solution.py:992
  883.3 2.8 convert_element_type.59
  886.1 72.4 %reduce-scatter.11.cloned.1.call-done = bf16[256,2048]{1,0:T(8,128)(2,1)} async-done(((bf16[2048,2048]{1,0:T(8,128)(2,1)}), bf16[256,2048]{1,0:T(8,128)(2,1)}) %reduce-scatter.11.cloned.1.call-update) | async-done | bytes 1048592 | tf_op jit(solution)/shard_map/reduce_scatter | solution.py:992
  958.5 2.8 convert_element_type.60
  (135 shorter events, 21.8 us)
Async XLA Ops:
  7.2 3.7 copy-start.28
  7.2 97.8 %all-gather.5.cloned.1.call-start = ((), (), s32[]{:S(2)}) async-start(), calls=%async_computation.6 | async-start | bytes 7077888 | tf_op jit(solution)/shard_map/all_gather | solution.py:925
  9.4 213.8 %all-gather.7.cloned.1.call-start = ((), (), s32[]{:S(2)}) async-start(), calls=%async_computation.7 | async-start | bytes 2359296 | tf_op jit(solution)/shard_map/all_gather | solution.py:925
  10.1 12.6 %copy-start.30 = (bf16[4,512]{1,0:T(4,128)(2,1)S(1)}, bf16[4,512]{1,0:T(4,128)(2,1)}, u32[]{:S(2)}) copy-start(bf16[4,512]{1,0:T(4,128)(2,1)} %param.26) | copy-start | bytes 12292
  10.1 12.6 %copy-start.31 = (bf16[2,512]{1,0:T(2,128)(2,1)S(1)}, bf16[2,512]{1,0:T(2,128)(2,1)}, u32[]{:S(2)}) copy-start(bf16[2,512]{1,0:T(2,128)(2,1)} %param.25) | copy-start | bytes 6148
  10.2 12.7 %copy-start.2 = (bf16[1024,512]{1,0:T(8,128)(2,1)S(1)}, bf16[1024,512]{1,0:T(8,128)(2,1)}, u32[]{:S(2)}) copy-start(bf16[1024,512]{1,0:T(8,128)(2,1)} %x_ref.1) | copy-start | bytes 3145732
  10.2 213.0 %all-gather.9.cloned.1.call-start = ((), (), s32[]{:S(2)}) async-start(), calls=%async_computation.8 | async-start | bytes 9437184 | tf_op jit(solution)/shard_map/all_gather | solution.py:925
  10.9 94.0 %copy-start.32 = (bf16[512]{0:T(512)(128)(2,1)S(1)}, bf16[512]{0:T(512)(128)(2,1)}, u32[]{:S(2)}) copy-start(bf16[512]{0:T(512)(128)(2,1)} %param.23) | copy-start | bytes 3076
  10.9 94.0 %copy-start.33 = (bf16[512]{0:T(512)(128)(2,1)S(1)}, bf16[512]{0:T(512)(128)(2,1)}, u32[]{:S(2)}) copy-start(bf16[512]{0:T(512)(128)(2,1)} %param.22) | copy-start | bytes 3076
  12.0 193.8 %all-to-all-start = ((bf16[4,4,64,512]{3,2,0,1:T(8,128)(2,1)}), bf16[4,4,64,512]{3,2,0,1:T(8,128)(2,1)}, u32[]{:S(2)}, u32[]{:S(2)}) async-start(bf16[4,4,64,512]{3,2,0,1:T(8,128)(2,1)} %copy.39), calls=%async_computation | async-start | bytes 2097152 | tf_op jit(solution)/shard_map/all_to_all | solution.py:890
  17.3 337.3 %all-gather.11.cloned.1.call-start = ((), (), s32[]{:S(2)}) async-start(), calls=%async_computation.9 | async-start | bytes 9437184 | tf_op jit(solution)/shard_map/all_gather | solution.py:925
  17.9 822.6 %reduce-scatter.7.cloned.1.call-start = ((), (), s32[]{:S(2)}) async-start(), calls=%async_computation.11 | async-start | bytes 2359296 | tf_op jit(solution)/shard_map/reduce_scatter | solution.py:992
  102.9 2.0 copy-start.9
  104.9 69.1 %copy-start.13 = (s32[1,2048]{1,0:T(1,128)}, s32[1,2048]{1,0:T(1,128)S(1)}, u32[]{:S(2)}) copy-start(s32[1,2048]{1,0:T(1,128)S(1)} %get-tuple-element.109.high_ref) | copy-start | bytes 24580
  104.9 69.1 %copy-start.15 = (s32[1,2048]{1,0:T(1,128)}, s32[1,2048]{1,0:T(1,128)S(1)}, u32[]{:S(2)}) copy-start(s32[1,2048]{1,0:T(1,128)S(1)} %get-tuple-element.110.low_ref) | copy-start | bytes 24580
  115.1 26.1 %collective-permute-start = (bf16[1024,256]{1,0:T(8,128)(2,1)S(1)}, bf16[1024,256]{1,0:T(8,128)(2,1)S(1)}, u32[]{:S(2)}, u32[]{:S(2)}) collective-permute-start(bf16[1024,256]{1,0:T(8,128)(2,1)S(1)} %get-tuple-element.89), channel_id=1, source_target_pairs={{0,4},{4,0},{1,5},{5,1},{2,6},{6,2},{3,7},{7,3},{8,12},{12,8},{9,1... | collective-permute-start | bytes 1572872 | tf_op jit(solution)/shard_map/ppermute | solution.py:218
  116.7 44.7 %collective-permute-start.2 = (bf16[1024,256]{1,0:T(8,128)(2,1)S(1)}, bf16[1024,256]{1,0:T(8,128)(2,1)S(1)}, u32[]{:S(2)}, u32[]{:S(2)}) collective-permute-start(bf16[1024,256]{1,0:T(8,128)(2,1)S(1)} %get-tuple-element.88), channel_id=1, source_target_pairs={{0,4},{4,0},{1,5},{5,1},{2,6},{6,2},{3,7},{7,3},{8,12},{12,8},{9,1... | collective-permute-start | bytes 1572872 | tf_op jit(solution)/shard_map/ppermute | solution.py:218
  163.1 9.6 collective-permute-start.1
  164.7 9.3 copy-start.17
  164.7 9.3 copy-start.19
  166.4 34.0 %copy-start.5 = (bf16[2048,256]{1,0:T(8,128)(2,1)}, bf16[2048,256]{1,0:T(8,128)(2,1)S(1)}, u32[]{:S(2)}) copy-start(bf16[2048,256]{1,0:T(8,128)(2,1)S(1)} %get-tuple-element.107.q_ref) | copy-start | bytes 3145732
  166.4 34.0 %copy-start.7 = (bf16[2048,256]{1,0:T(8,128)(2,1)}, bf16[2048,256]{1,0:T(8,128)(2,1)S(1)}, u32[]{:S(2)}) copy-start(bf16[2048,256]{1,0:T(8,128)(2,1)S(1)} %get-tuple-element.108.v_ref) | copy-start | bytes 3145732
  174.0 26.5 %copy-start.3 = (bf16[2048,256]{1,0:T(8,128)(2,1)}, bf16[2048,256]{1,0:T(8,128)(2,1)S(1)}, u32[]{:S(2)}) copy-start(bf16[2048,256]{1,0:T(8,128)(2,1)S(1)} %pad_maximum_fusion.1.k_ref) | copy-start | bytes 3145732
  200.5 20.5 %copy-start = (bf16[2048,256]{1,0:T(8,128)(2,1)}, bf16[2048,256]{1,0:T(8,128)(2,1)S(1)}, u32[]{:S(2)}) copy-start(bf16[2048,256]{1,0:T(8,128)(2,1)S(1)} %get-tuple-element.46.o_ref) | copy-start | bytes 3145732
  200.5 4.1 copy-start.29
  200.6 20.5 %collective-permute-start.3 = (bf16[1024,256]{1,0:T(8,128)(2,1)S(1)}, bf16[1024,256]{1,0:T(8,128)(2,1)S(1)}, u32[]{:S(2)}, u32[]{:S(2)}) collective-permute-start(bf16[1024,256]{1,0:T(8,128)(2,1)S(1)} %broadcast_select_fusion.12), channel_id=1, source_target_pairs={{0,4},{4,0},{1,5},{5,1},{2,6},{6,2},{3,7},{7,3},{8,12},{12,8},{9,1... | collective-permute-start | bytes 1572872 | tf_op jit(solution)/shard_map/ppermute | solution.py:218
  494.3 117.7 %copy-start.25 = (bf16[1024,256]{1,0:T(8,128)(2,1)S(1)}, bf16[1024,256]{1,0:T(8,128)(2,1)}, u32[]{:S(2)}) copy-start(bf16[1024,256]{1,0:T(8,128)(2,1)} %copy-done.24) | copy-start | bytes 1572868
  494.3 117.7 %copy-start.27 = (bf16[1024,256]{1,0:T(8,128)(2,1)S(1)}, bf16[1024,256]{1,0:T(8,128)(2,1)}, u32[]{:S(2)}) copy-start(bf16[1024,256]{1,0:T(8,128)(2,1)} %copy-done.26) | copy-start | bytes 1572868
  617.9 14.1 %copy-start.23 = (bf16[1024,512]{1,0:T(8,128)(2,1)S(1)}, bf16[1024,512]{1,0:T(8,128)(2,1)}, u32[]{:S(2)}) copy-start(bf16[1024,512]{1,0:T(8,128)(2,1)} %get-tuple-element.61) | copy-start | bytes 3145732
  632.0 11.2 %copy-start.1 = (bf16[2048,256]{1,0:T(8,128)(2,1)S(1)}, bf16[2048,256]{1,0:T(8,128)(2,1)}, u32[]{:S(2)}) copy-start(bf16[2048,256]{1,0:T(8,128)(2,1)} %copy-done) | copy-start | bytes 3145732
  632.0 11.3 %copy-start.4 = (bf16[2048,256]{1,0:T(8,128)(2,1)S(1)}, bf16[2048,256]{1,0:T(8,128)(2,1)}, u32[]{:S(2)}) copy-start(bf16[2048,256]{1,0:T(8,128)(2,1)} %copy-done.3) | copy-start | bytes 3145732
  632.0 11.3 %copy-start.6 = (bf16[2048,256]{1,0:T(8,128)(2,1)S(1)}, bf16[2048,256]{1,0:T(8,128)(2,1)}, u32[]{:S(2)}) copy-start(bf16[2048,256]{1,0:T(8,128)(2,1)} %copy-done.5) | copy-start | bytes 3145732
  632.0 11.3 %copy-start.8 = (bf16[2048,256]{1,0:T(8,128)(2,1)S(1)}, bf16[2048,256]{1,0:T(8,128)(2,1)}, u32[]{:S(2)}) copy-start(bf16[2048,256]{1,0:T(8,128)(2,1)} %copy-done.7) | copy-start | bytes 3145732
  632.0 11.3 %copy-start.14 = (s32[1,2048]{1,0:T(1,128)S(1)}, s32[1,2048]{1,0:T(1,128)}, u32[]{:S(2)}) copy-start(s32[1,2048]{1,0:T(1,128)} %copy-done.13) | copy-start | bytes 24580
  632.0 11.3 %copy-start.16 = (s32[1,2048]{1,0:T(1,128)S(1)}, s32[1,2048]{1,0:T(1,128)}, u32[]{:S(2)}) copy-start(s32[1,2048]{1,0:T(1,128)} %copy-done.15) | copy-start | bytes 24580
  632.0 11.3 %copy-start.18 = (s32[4]{0:T(128)S(1)}, s32[4]{0:T(128)}, u32[]{:S(2)}) copy-start(s32[4]{0:T(128)} %copy-done.17) | copy-start | bytes 52
  632.0 11.3 %copy-start.20 = (s32[4]{0:T(128)S(1)}, s32[4]{0:T(128)}, u32[]{:S(2)}) copy-start(s32[4]{0:T(128)} %copy-done.19) | copy-start | bytes 52
  632.1 10.9 %collective-permute-start.4 = (bf16[1024,256]{1,0:T(8,128)(2,1)S(1)}, bf16[1024,256]{1,0:T(8,128)(2,1)S(1)}, u32[]{:S(2)}, u32[]{:S(2)}) collective-permute-start(bf16[1024,256]{1,0:T(8,128)(2,1)S(1)} %broadcast_select_fusion.8), channel_id=1, source_target_pairs={{0,4},{4,0},{1,5},{5,1},{2,6},{6,2},{3,7},{7,3},{8,12},{12,8},{9,1... | collective-permute-start | bytes 1572872 | tf_op jit(solution)/shard_map/ppermute | solution.py:218
  677.9 9.5 collective-permute-start.5
  679.9 162.4 %reduce-scatter.5.cloned.1.call-start = ((), (), s32[]{:S(2)}) async-start(), calls=%async_computation.10 | async-start | bytes 7077888 | tf_op jit(solution)/shard_map/reduce_scatter | solution.py:992
  680.3 12.6 %collective-permute-start.6 = (bf16[1024,256]{1,0:T(8,128)(2,1)S(1)}, bf16[1024,256]{1,0:T(8,128)(2,1)S(1)}, u32[]{:S(2)}, u32[]{:S(2)}) collective-permute-start(bf16[1024,256]{1,0:T(8,128)(2,1)S(1)} %broadcast_select_fusion.2), channel_id=1, source_target_pairs={{0,4},{4,0},{1,5},{5,1},{2,6},{6,2},{3,7},{7,3},{8,12},{12,8},{9,1... | collective-permute-start | bytes 1572872 | tf_op jit(solution)/shard_map/ppermute | solution.py:218
  680.5 18.1 %collective-permute-start.7 = (bf16[1024,256]{1,0:T(8,128)(2,1)S(1)}, bf16[1024,256]{1,0:T(8,128)(2,1)S(1)}, u32[]{:S(2)}, u32[]{:S(2)}) collective-permute-start(bf16[1024,256]{1,0:T(8,128)(2,1)S(1)} %broadcast_select_fusion), channel_id=1, source_target_pairs={{0,4},{4,0},{1,5},{5,1},{2,6},{6,2},{3,7},{7,3},{8,12},{12,8},{9,1... | collective-permute-start | bytes 1572872 | tf_op jit(solution)/shard_map/ppermute | solution.py:218
  693.1 5.8 copy-start.10
  709.4 173.9 %reduce-scatter.9.cloned.1.call-start = ((), (), s32[]{:S(2)}) async-start(), calls=%async_computation.12 | async-start | bytes 9437184 | tf_op jit(solution)/shard_map/reduce_scatter | solution.py:992
  710.2 248.3 %reduce-scatter.11.cloned.1.call-start = ((), (), s32[]{:S(2)}) async-start(), calls=%async_computation.13 | async-start | bytes 9437184 | tf_op jit(solution)/shard_map/reduce_scatter | solution.py:992
  711.8 12.9 %copy-start.22 = (f32[256,2048]{1,0:T(8,128)S(1)}, f32[256,2048]{1,0:T(8,128)}, u32[]{:S(2)}) copy-start(f32[256,2048]{1,0:T(8,128)} %get-tuple-element.67.inner_ref) | copy-start | bytes 6291460
  715.0 123.3 %all-to-all-start.1 = ((bf16[4,4,64,512]{3,2,0,1:T(8,128)(2,1)}), bf16[4,4,64,512]{3,2,0,1:T(8,128)(2,1)}, u32[]{:S(2)}, u32[]{:S(2)}) async-start(bf16[4,4,64,512]{3,2,0,1:T(8,128)(2,1)} %bitcast.29), calls=%async_computation.1 | async-start | bytes 2097152 | tf_op jit(solution)/shard_map/all_to_all | solution.py:898
  726.6 2.8 copy-start.21
  (4 other events, 5.3 us)
Sparse Core Ops, SparseCore 0:
  10.5 46.6 all-gather.4
  59.1 27.8 all-gather.6
  88.9 74.4 all-gather.8
  165.2 62.8 all-gather.10
  680.1 59.4 reduce-scatter.6
  743.2 67.1 reduce-scatter.4
  813.9 69.3 reduce-scatter.8
  887.1 71.2 reduce-scatter.10

commit v4 on v3

--- a/solution.py
+++ b/solution.py
@@ -991,7 +991,7 @@
     def owner_sum(grad):
         return lax.psum_scatter(
             grad, plane, scatter_dimension=0, tiled=True
-        ).astype(jnp.float32)
+        )
 
     hidden_low, shrink_part = lax.optimization_barrier(
         (hidden_low, dot_rows(ffn_low, activated).astype(jnp.bfloat16))
@@ -1005,9 +1005,10 @@
         [shape((rows, head_cols), jnp.bfloat16)],
         3, "first_back",
     )
-    attended_grad, expand_part, output_part = lax.optimization_barrier(
+    attended_grad, shrink_grad, expand_part, output_part = lax.optimization_barrier(
         (
             attended_grad,
+            shrink_grad,
             dot_rows(norm_low, hidden_low).astype(jnp.bfloat16),
             dot_rows(branch_low, attended).astype(jnp.bfloat16),
         )
@@ -1035,8 +1036,8 @@
 
         key_low, value_low = fold(key_ext), fold(value_ext)
     qkv_low = jnp.concatenate([query_low, key_low, value_low], axis=1)
-    qkv_low, qkv_part = lax.optimization_barrier(
-        (qkv_low, dot_rows(wide_tokens, qkv_low).astype(jnp.bfloat16))
+    qkv_low, expand_grad, qkv_part = lax.optimization_barrier(
+        (qkv_low, expand_grad, dot_rows(wide_tokens, qkv_low).astype(jnp.bfloat16))
     )
     qkv_grad = owner_sum(qkv_part)
     row_sums = jnp.concatenate(
@@ -1052,12 +1053,12 @@
     return (
         mixed,
         input_grad,
-        qkv_grad[:, :head_cols],
-        qkv_grad[:, head_cols : 2 * head_cols],
-        qkv_grad[:, 2 * head_cols :],
-        output_grad,
-        expand_grad,
-        shrink_grad,
+        qkv_grad[:, :head_cols].astype(jnp.float32),
+        qkv_grad[:, head_cols : 2 * head_cols].astype(jnp.float32),
+        qkv_grad[:, 2 * head_cols :].astype(jnp.float32),
+        output_grad.astype(jnp.float32),
+        expand_grad.astype(jnp.float32),
+        shrink_grad.astype(jnp.float32),
         vectors[query_place],
         vectors[query_place + 2],
         vectors[8:query_place].reshape(-1),

time: 983 us -> 902 us (0.918)
  waiting for transfers between devices: 197 us -> 143 us
  Pallas kernels: 621 us -> 609 us
    reduce_scatter x4, waiting for transfers between devices: 111 us -> 0.01 us  [owner_sum(): return lax.psum_scatter(grad, plane, scatter_dimension=0, tiled=True)]
    ppermute x8, waiting for transfers between devices: 82.9 us -> 124 us  [swap_halves(): got = lax.ppermute(other, 'ctx', [(0, 1), (1, 0)])]
    pallas_call x1, Pallas kernels: 106 us -> 77.3 us  [input_sum(): pl.pallas_call(functools.partial(input_kernel, sizes), out_shape=[jax.Sha...]
    pallas_call x3, Pallas kernels: 375 us -> 399 us  [relay(): pl.pallas_call(functools.partial(relay_kernel, count, row_step, use_step,...]
    all_to_all x1, waiting for transfers between devices: 0.01 us -> 17.3 us  [unspread_own(): got = lax.all_to_all(parts, 'tp', split_axis=1, concat_axis=1, tiled=True)]
  transfers between devices with their start and end apart: 18 -> 18, of which waited for: 10 -> 9; matrix products, arithmetic and copies ran while one was open for 6% -> 9% of each run, Pallas kernels for 36% -> 53%
where the time goes in v4:
time: 902 us; the launch traced here: 893 us
  Pallas kernels  609 us (68%)
  waiting for transfers between devices  143 us (16%)
  matrix products  52.8 us (6%)
  local copies, waits for them, and re-layouts  27.6 us (3%)
  other arithmetic  26.2 us (3%)
  starting transfers between devices  19 us (2%)
  between operations  15.3 us (2%)
    pallas_call x3, Pallas kernels, relay(): pl.pallas_call(functools.partial(relay_kernel, count, row_step, use_step,...  399 us
    ppermute x8, waiting for transfers between devices, swap_halves(): got = lax.ppermute(other, 'ctx', [(0, 1), (1, 0)])  124 us
    pallas_call x1, Pallas kernels, gather_features(): pl.pallas_call(functools.partial(gather_kernel, count), out_shape=[jax.Sh...  80.1 us
    pallas_call x1, Pallas kernels, input_sum(): pl.pallas_call(functools.partial(input_kernel, sizes), out_shape=[jax.Sha...  77.3 us
    dot_general x4, matrix products, dot_rows(): lax.dot_general(left, right, (((0,), (0,)), ((), ())), preferred_element_...  42.8 us
    pallas_call x1, Pallas kernels, attend_back(): pl.pallas_call(attend_back_kernel, out_shape=(jax.ShapeDtypeStruct((rows,...  29.7 us
    pallas_call x1, Pallas kernels, attend(): pl.pallas_call(attend_kernel, out_shape=(jax.ShapeDtypeStruct((rows, widt...  23.1 us
  transfers between devices with their start and end apart: 18, of which 9 were waited for; matrix products, arithmetic and copies ran while one was open for 9% of the time, Pallas kernels for 53%

profile of v4, /device:TPU:8, one launch (start us, length us, event | category | flops | bytes accessed | tf_op | source)
XLA Modules:
  0.0 893.5 jit_solution(12843045521533297211)
XLA Ops:
  7.2 2.1 pad_maximum_fusion.5
  12.0 5.3 all-to-all-start
  18.6 4.0 convert_reduce_fusion
  22.8 80.1 %gather_features.1 = (bf16[1024,2048]{1,0:T(8,128)(2,1)S(1)}, bf16[16,2048]{1,0:T(8,128)(2,1)S(1)}) custom-call(bf16[1024,512]{1,0:T(8,128)(2,1)S(1)} %copy-done.2, bf16[16,512]{1,0:T(8,128)(2,1)S(1)} %maximum_maximum_fusion.marks_ref), custom_call_target="tpu_custom_call" | custom-call | bytes 134217728 | tf_op jit(solution)/shard_map/gather_features/pallas_call | solution.py:516
  102.9 2.0 copy-done.9
  105.0 10.0 %add_convert_fusion = bf16[1024,1536]{1,0:T(8,128)(2,1)S(1)} fusion(bf16[1024,2048]{1,0:T(8,128)(2,1)} %copy-done.9, bf16[2048,1536]{1,0:T(8,128)(2,1)} %all-gather.5.cloned.1.call-done.weight, f32[1536]{0:T(1024)S(1)} %maximum_convert_fusion), kind=kOutput, calls=%fused_computation.5 | convolution fusion | flops 6445596672 | bytes 13637632 | tf_op jit(solution)/shard_map/dot_general | solution.py:23
  115.1 1.6 collective-permute-start
  118.0 23.3 %collective-permute-done = bf16[1024,256]{1,0:T(8,128)(2,1)S(1)} collective-permute-done((bf16[1024,256]{1,0:T(8,128)(2,1)S(1)}, bf16[1024,256]{1,0:T(8,128)(2,1)S(1)}, u32[]{:S(2)}, u32[]{:S(2)}) %collective-permute-start) | collective-permute-done | bytes 524320 | tf_op jit(solution)/shard_map/ppermute | solution.py:218
  141.3 20.1 %collective-permute-done.2 = bf16[1024,256]{1,0:T(8,128)(2,1)S(1)} collective-permute-done((bf16[1024,256]{1,0:T(8,128)(2,1)S(1)}, bf16[1024,256]{1,0:T(8,128)(2,1)S(1)}, u32[]{:S(2)}, u32[]{:S(2)}) %collective-permute-start.2) | collective-permute-done | bytes 524320 | tf_op jit(solution)/shard_map/ppermute | solution.py:218
  161.4 1.7 broadcast_select_fusion.15
  163.1 1.5 collective-permute-start.1
  164.8 1.7 pad_maximum_fusion
  166.4 6.3 collective-permute-done.1
  172.7 1.2 broadcast_select_fusion.19
  174.0 23.1 %attend.1 = (bf16[2048,256]{1,0:T(8,128)(2,1)S(1)}, f32[2,1,2048]{2,1,0:T(1,128)S(1)}) custom-call(s32[4]{0:T(128)S(1)} %get-tuple-element.115.first, s32[4]{0:T(128)S(1)} %get-tuple-element.116.last, bf16[2048,256]{1,0:T(8,128)(2,1)S(1)} %get-tuple-element.111.q_ref, bf16[2048,256]{1,0:T(8,128)(2,1)S(1)} %pad_maximum_fusion.1.k_ref, ...), custom_call_target="tpu_custom_call" | custom-call | flops 3221225472 | bytes 4194304 | tf_op jit(solution)/shard_map/attend/pallas_call | solution.py:81
  197.3 1.8 collective-permute-start.3
  199.0 2.3 constant_dynamic-slice_fusion
  202.6 2.0 copy.40
  204.6 1.2 copy.44
  205.8 16.4 %collective-permute-done.3 = bf16[1024,256]{1,0:T(8,128)(2,1)S(1)} collective-permute-done((bf16[1024,256]{1,0:T(8,128)(2,1)S(1)}, bf16[1024,256]{1,0:T(8,128)(2,1)S(1)}, u32[]{:S(2)}, u32[]{:S(2)}) %collective-permute-start.3) | collective-permute-done | bytes 524320 | tf_op jit(solution)/shard_map/ppermute | solution.py:218
  222.4 1.2 pad_maximum_fusion.3.refs_0_
  223.5 137.7 %first_norm.1 = (bf16[1024,2048]{1,0:T(8,128)(2,1)}, f32[256,2048]{1,0:T(8,128)}, f32[256,2048]{1,0:T(8,128)}, f32[256,128]{1,0:T(8,128)}, f32[1024,2048]{1,0:T(8,128)}, /*index=5*/bf16[1024,2048]{1,0:T(8,128)(2,1)}) custom-call(bf16[1024,512]{1,0:T(8,128)(2,1)} %pad_maximum_fusion.3.refs_0_, bf16[2048,512]{1,0:T(8,128)(2,1)} %all-gather.7.cloned.1.call-done.refs_1_.refs_2_, ...), custom_call_target="tpu_custom_call" | custom-call | flops 99999997952 | bytes 134217728 | tf_op jit(solution)/shard_map/first_norm/pallas_call | solution.py:631
  361.3 132.7 %second_norm.1 = (bf16[1024,2048]{1,0:T(8,128)(2,1)}, bf16[256,2048]{1,0:T(8,128)(2,1)}, f32[256,2048]{1,0:T(8,128)}, f32[8,2048]{1,0:T(8,128)}, bf16[1024,2048]{1,0:T(8,128)(2,1)}, /*index=5*/f32[8,2048]{1,0:T(8,128)}) custom-call(bf16[1024,2048]{1,0:T(8,128)(2,1)} %get-tuple-element.50.refs_0_, bf16[2048,2048]{1,0:T(8,128)(2,1)} %all-gather.11.cloned.1.call-done.refs_1_, ...), custom_call_target="tpu_custom_call" | custom-call | flops 99999997952 | bytes 134217728 | tf_op jit(solution)/shard_map/second_norm/pallas_call | solution.py:631
  494.0 14.0 %convolution_convert_fusion.2 = bf16[2048,2048]{1,0:T(8,128)(2,1)} fusion(bf16[1024,2048]{1,0:T(8,128)(2,1)} %get-tuple-element.55, bf16[1024,2048]{1,0:T(8,128)(2,1)} %get-tuple-element.50.refs_0_), kind=kOutput, calls=%fused_computation.4 | convolution fusion | flops 8594128896 | bytes 16777216 | tf_op jit(solution)/shard_map/dot_general | solution.py:27
  508.1 128.6 %first_back.1 = (bf16[1024,2048]{1,0:T(8,128)(2,1)}, f32[256,2048]{1,0:T(8,128)}, f32[8,2048]{1,0:T(8,128)}, bf16[1024,512]{1,0:T(8,128)(2,1)}) custom-call(bf16[1024,2048]{1,0:T(8,128)(2,1)} %get-tuple-element.56.refs_0_, bf16[2048,2048]{1,0:T(8,128)(2,1)} %all-gather.9.cloned.1.call-done.refs_2_.refs_1_, ...), custom_call_target="tpu_custom_call" | custom-call | flops 99999997952 | bytes 134217728 | tf_op jit(solution)/shard_map/first_back/pallas_call | solution.py:631
  636.7 5.9 convolution_convert_fusion.3
  642.6 14.1 %convolution_convert_fusion.1 = bf16[2048,2048]{1,0:T(8,128)(2,1)} fusion(bf16[1024,2048]{1,0:T(8,128)(2,1)} %get-tuple-element.62, bf16[1024,2048]{1,0:T(8,128)(2,1)} %get-tuple-element.56.refs_0_), kind=kOutput, calls=%fused_computation.3 | convolution fusion | flops 8594128896 | bytes 16777216 | tf_op jit(solution)/shard_map/dot_general | solution.py:27
  656.8 1.1 copy-done.23
  658.3 9.0 %collective-permute-done.4 = bf16[1024,256]{1,0:T(8,128)(2,1)S(1)} collective-permute-done((bf16[1024,256]{1,0:T(8,128)(2,1)S(1)}, bf16[1024,256]{1,0:T(8,128)(2,1)S(1)}, u32[]{:S(2)}, u32[]{:S(2)}) %collective-permute-start.4) | collective-permute-done | bytes 524320 | tf_op jit(solution)/shard_map/ppermute | solution.py:218
  667.5 29.7 %attend_back.1 = (bf16[2048,256]{1,0:T(8,128)(2,1)S(1)}, bf16[2048,256]{1,0:T(8,128)(2,1)S(1)}, bf16[2048,256]{1,0:T(8,128)(2,1)S(1)}) custom-call(s32[4]{0:T(128)S(1)} %copy-done.18, s32[4]{0:T(128)S(1)} %copy-done.20, bf16[2048,256]{1,0:T(8,128)(2,1)S(1)} %copy-done.6, bf16[2048,256]{1,0:T(8,128)(2,1)S(1)} %copy-done.4, bf16[2048,256]{1,0:T(8,128)(2,1)S(1)} %copy-done.8, ...), custom_call_target="tpu_custom_call" | custom-call | flops 8589934592 | bytes 8388608 | tf_op jit(solution)/shard_map/attend_back/pallas_call | solution.py:164
  698.7 1.9 collective-permute-start.6
  700.9 18.8 %collective-permute-done.5 = bf16[1024,256]{1,0:T(8,128)(2,1)} collective-permute-done((bf16[1024,256]{1,0:T(8,128)(2,1)}, bf16[1024,256]{1,0:T(8,128)(2,1)}, u32[]{:S(2)}, u32[]{:S(2)}) %collective-permute-start.5) | collective-permute-done | bytes 524320 | tf_op jit(solution)/shard_map/ppermute | solution.py:218
  719.9 1.2 select_dynamic-update-slice_fusion.4
  721.2 13.6 %collective-permute-done.6 = bf16[1024,256]{1,0:T(8,128)(2,1)S(1)} collective-permute-done((bf16[1024,256]{1,0:T(8,128)(2,1)S(1)}, bf16[1024,256]{1,0:T(8,128)(2,1)S(1)}, u32[]{:S(2)}, u32[]{:S(2)}) %collective-permute-start.6) | collective-permute-done | bytes 524320 | tf_op jit(solution)/shard_map/ppermute | solution.py:218
  735.2 16.6 %collective-permute-done.7 = bf16[1024,256]{1,0:T(8,128)(2,1)S(1)} collective-permute-done((bf16[1024,256]{1,0:T(8,128)(2,1)S(1)}, bf16[1024,256]{1,0:T(8,128)(2,1)S(1)}, u32[]{:S(2)}, u32[]{:S(2)}) %collective-permute-start.7) | collective-permute-done | bytes 524320 | tf_op jit(solution)/shard_map/ppermute | solution.py:218
  752.1 8.8 convolution_convert_fusion
  760.9 1.6 copy-done.11
  762.6 1.3 copy-done.30
  764.6 1.2 copy.47
  765.8 5.1 all-to-all-start.1
  774.0 17.3 %all-to-all-done.1 = bf16[4,4,64,512]{3,2,0,1:T(8,128)(2,1)S(1)} async-done(((bf16[4,4,64,512]{3,2,0,1:T(8,128)(2,1)}), bf16[4,4,64,512]{3,2,0,1:T(8,128)(2,1)S(1)}, u32[]{:S(2)}, u32[]{:S(2)}) %all-to-all-start.1) | async-done | bytes 1048608 | tf_op jit(solution)/shard_map/all_to_all | solution.py:898
  792.3 2.8 convert_element_type.68
  795.1 1.8 convert_element_type.66
  796.9 1.9 copy-done.12
  798.8 2.8 copy-done.21
  801.6 77.3 %input_sum.1 = (bf16[1024,512]{1,0:T(8,128)(2,1)S(1)}, f32[16,512]{1,0:T(8,128)S(1)}) custom-call(bf16[1024,1536]{1,0:T(8,128)(2,1)S(1)} %copy-done.12, bf16[2048,1536]{1,0:T(8,128)(2,1)S(1)} %copy-done.21, f32[256,2048]{1,0:T(8,128)S(1)} %copy-done.22, f32[8,2048]{1,0:T(8,128)S(1)} %concatenate.43.rows_ref, f32[1,2048]{1,0:T(1,128)S(1)} %slice.132.hidden_ref), custom_call_target="tpu_custom_call" | custom-call | flops 60000002048 | bytes 33554432 | tf_op jit(solution)/shard_map/input_sum/pallas_call | solution.py:847
  879.0 1.6 convert_element_type.67
  882.9 2.3 slice_convert_fusion
  (139 shorter events, 18.8 us)
Async XLA Ops:
  7.2 3.7 copy-start.29
  7.2 97.8 %all-gather.5.cloned.1.call-start = ((), (), s32[]{:S(2)}) async-start(), calls=%async_computation.6 | async-start | bytes 7077888 | tf_op jit(solution)/shard_map/all_gather | solution.py:925
  9.4 214.1 %all-gather.7.cloned.1.call-start = ((), (), s32[]{:S(2)}) async-start(), calls=%async_computation.7 | async-start | bytes 2359296 | tf_op jit(solution)/shard_map/all_gather | solution.py:925
  10.1 12.6 %copy-start.32 = (bf16[4,512]{1,0:T(4,128)(2,1)S(1)}, bf16[4,512]{1,0:T(4,128)(2,1)}, u32[]{:S(2)}) copy-start(bf16[4,512]{1,0:T(4,128)(2,1)} %param.26) | copy-start | bytes 12292
  10.1 12.6 %copy-start.33 = (bf16[2,512]{1,0:T(2,128)(2,1)S(1)}, bf16[2,512]{1,0:T(2,128)(2,1)}, u32[]{:S(2)}) copy-start(bf16[2,512]{1,0:T(2,128)(2,1)} %param.25) | copy-start | bytes 6148
  10.2 12.7 %copy-start.2 = (bf16[1024,512]{1,0:T(8,128)(2,1)S(1)}, bf16[1024,512]{1,0:T(8,128)(2,1)}, u32[]{:S(2)}) copy-start(bf16[1024,512]{1,0:T(8,128)(2,1)} %x_ref.1) | copy-start | bytes 3145732
  10.2 213.4 %all-gather.9.cloned.1.call-start = ((), (), s32[]{:S(2)}) async-start(), calls=%async_computation.8 | async-start | bytes 9437184 | tf_op jit(solution)/shard_map/all_gather | solution.py:925
  10.9 94.0 %copy-start.34 = (bf16[512]{0:T(512)(128)(2,1)S(1)}, bf16[512]{0:T(512)(128)(2,1)}, u32[]{:S(2)}) copy-start(bf16[512]{0:T(512)(128)(2,1)} %param.23) | copy-start | bytes 3076
  10.9 94.0 %copy-start.35 = (bf16[512]{0:T(512)(128)(2,1)S(1)}, bf16[512]{0:T(512)(128)(2,1)}, u32[]{:S(2)}) copy-start(bf16[512]{0:T(512)(128)(2,1)} %param.22) | copy-start | bytes 3076
  12.0 190.6 %all-to-all-start = ((bf16[4,4,64,512]{3,2,0,1:T(8,128)(2,1)}), bf16[4,4,64,512]{3,2,0,1:T(8,128)(2,1)}, u32[]{:S(2)}, u32[]{:S(2)}) async-start(bf16[4,4,64,512]{3,2,0,1:T(8,128)(2,1)} %copy.39), calls=%async_computation | async-start | bytes 2097152 | tf_op jit(solution)/shard_map/all_to_all | solution.py:890
  17.3 343.9 %all-gather.11.cloned.1.call-start = ((), (), s32[]{:S(2)}) async-start(), calls=%async_computation.9 | async-start | bytes 9437184 | tf_op jit(solution)/shard_map/all_gather | solution.py:925
  17.9 638.8 %reduce-scatter.5.cloned.1.call-start = ((), (), s32[]{:S(2)}) async-start(), calls=%async_computation.10 | async-start | bytes 9437184 | tf_op jit(solution)/shard_map/reduce_scatter | solution.py:992
  104.9 69.1 %copy-start.13 = (s32[1,2048]{1,0:T(1,128)}, s32[1,2048]{1,0:T(1,128)S(1)}, u32[]{:S(2)}) copy-start(s32[1,2048]{1,0:T(1,128)S(1)} %get-tuple-element.113.high_ref) | copy-start | bytes 24580
  104.9 69.1 %copy-start.15 = (s32[1,2048]{1,0:T(1,128)}, s32[1,2048]{1,0:T(1,128)S(1)}, u32[]{:S(2)}) copy-start(s32[1,2048]{1,0:T(1,128)S(1)} %get-tuple-element.114.low_ref) | copy-start | bytes 24580
  115.1 26.2 %collective-permute-start = (bf16[1024,256]{1,0:T(8,128)(2,1)S(1)}, bf16[1024,256]{1,0:T(8,128)(2,1)S(1)}, u32[]{:S(2)}, u32[]{:S(2)}) collective-permute-start(bf16[1024,256]{1,0:T(8,128)(2,1)S(1)} %get-tuple-element.93), channel_id=1, source_target_pairs={{0,4},{4,0},{1,5},{5,1},{2,6},{6,2},{3,7},{7,3},{8,12},{12,8},{9,1... | collective-permute-start | bytes 1572872 | tf_op jit(solution)/shard_map/ppermute | solution.py:218
  116.7 44.7 %collective-permute-start.2 = (bf16[1024,256]{1,0:T(8,128)(2,1)S(1)}, bf16[1024,256]{1,0:T(8,128)(2,1)S(1)}, u32[]{:S(2)}, u32[]{:S(2)}) collective-permute-start(bf16[1024,256]{1,0:T(8,128)(2,1)S(1)} %get-tuple-element.92), channel_id=1, source_target_pairs={{0,4},{4,0},{1,5},{5,1},{2,6},{6,2},{3,7},{7,3},{8,12},{12,8},{9,1... | collective-permute-start | bytes 1572872 | tf_op jit(solution)/shard_map/ppermute | solution.py:218
  163.1 9.6 %collective-permute-start.1 = (bf16[1024,256]{1,0:T(8,128)(2,1)}, bf16[1024,256]{1,0:T(8,128)(2,1)}, u32[]{:S(2)}, u32[]{:S(2)}) collective-permute-start(bf16[1024,256]{1,0:T(8,128)(2,1)} %get-tuple-element.91), channel_id=1, source_target_pairs={{0,4},{4,0},{1,5},{5,1},{2,6},{6,2},{3,7},{7,3},{8,12},{12,8},{9,1... | collective-permute-start | bytes 1572872 | tf_op jit(solution)/shard_map/ppermute | solution.py:218
  164.7 9.3 %copy-start.17 = (s32[4]{0:T(128)}, s32[4]{0:T(128)S(1)}, u32[]{:S(2)}) copy-start(s32[4]{0:T(128)S(1)} %get-tuple-element.115.first) | copy-start | bytes 52
  164.7 9.3 %copy-start.19 = (s32[4]{0:T(128)}, s32[4]{0:T(128)S(1)}, u32[]{:S(2)}) copy-start(s32[4]{0:T(128)S(1)} %get-tuple-element.116.last) | copy-start | bytes 52
  166.4 30.7 %copy-start.5 = (bf16[2048,256]{1,0:T(8,128)(2,1)}, bf16[2048,256]{1,0:T(8,128)(2,1)S(1)}, u32[]{:S(2)}) copy-start(bf16[2048,256]{1,0:T(8,128)(2,1)S(1)} %get-tuple-element.111.q_ref) | copy-start | bytes 3145732
  166.4 30.7 %copy-start.7 = (bf16[2048,256]{1,0:T(8,128)(2,1)}, bf16[2048,256]{1,0:T(8,128)(2,1)S(1)}, u32[]{:S(2)}) copy-start(bf16[2048,256]{1,0:T(8,128)(2,1)S(1)} %get-tuple-element.112.v_ref) | copy-start | bytes 3145732
  174.0 23.2 %copy-start.3 = (bf16[2048,256]{1,0:T(8,128)(2,1)}, bf16[2048,256]{1,0:T(8,128)(2,1)S(1)}, u32[]{:S(2)}) copy-start(bf16[2048,256]{1,0:T(8,128)(2,1)S(1)} %pad_maximum_fusion.1.k_ref) | copy-start | bytes 3145732
  197.2 25.1 %copy-start = (bf16[2048,256]{1,0:T(8,128)(2,1)}, bf16[2048,256]{1,0:T(8,128)(2,1)S(1)}, u32[]{:S(2)}) copy-start(bf16[2048,256]{1,0:T(8,128)(2,1)S(1)} %get-tuple-element.48.o_ref) | copy-start | bytes 3145732
  197.2 4.1 copy-start.31
  197.3 25.0 %collective-permute-start.3 = (bf16[1024,256]{1,0:T(8,128)(2,1)S(1)}, bf16[1024,256]{1,0:T(8,128)(2,1)S(1)}, u32[]{:S(2)}, u32[]{:S(2)}) collective-permute-start(bf16[1024,256]{1,0:T(8,128)(2,1)S(1)} %broadcast_select_fusion.12), channel_id=1, source_target_pairs={{0,4},{4,0},{1,5},{5,1},{2,6},{6,2},{3,7},{7,3},{8,12},{12,8},{9,1... | collective-permute-start | bytes 1572872 | tf_op jit(solution)/shard_map/ppermute | solution.py:218
  222.3 138.9 %copy-start.24 = (bf16[1024,256]{1,0:T(8,128)(2,1)}, bf16[1024,256]{1,0:T(8,128)(2,1)S(1)}, u32[]{:S(2)}) copy-start(bf16[1024,256]{1,0:T(8,128)(2,1)S(1)} %get-tuple-element.96) | copy-start | bytes 1572868
  222.3 138.9 %copy-start.26 = (bf16[1024,256]{1,0:T(8,128)(2,1)}, bf16[1024,256]{1,0:T(8,128)(2,1)S(1)}, u32[]{:S(2)}) copy-start(bf16[1024,256]{1,0:T(8,128)(2,1)S(1)} %get-tuple-element.97) | copy-start | bytes 1572868
  508.0 254.5 %reduce-scatter.7.cloned.1.call-start = ((), (), s32[]{:S(2)}) async-start(), calls=%async_computation.11 | async-start | bytes 9437184 | tf_op jit(solution)/shard_map/reduce_scatter | solution.py:992
  508.1 128.6 %copy-start.25 = (bf16[1024,256]{1,0:T(8,128)(2,1)S(1)}, bf16[1024,256]{1,0:T(8,128)(2,1)}, u32[]{:S(2)}) copy-start(bf16[1024,256]{1,0:T(8,128)(2,1)} %copy-done.24) | copy-start | bytes 1572868
  508.1 128.6 %copy-start.27 = (bf16[1024,256]{1,0:T(8,128)(2,1)S(1)}, bf16[1024,256]{1,0:T(8,128)(2,1)}, u32[]{:S(2)}) copy-start(bf16[1024,256]{1,0:T(8,128)(2,1)} %copy-done.26) | copy-start | bytes 1572868
  656.7 10.7 %copy-start.14 = (s32[1,2048]{1,0:T(1,128)S(1)}, s32[1,2048]{1,0:T(1,128)}, u32[]{:S(2)}) copy-start(s32[1,2048]{1,0:T(1,128)} %copy-done.13) | copy-start | bytes 24580
  656.8 10.7 %copy-start.16 = (s32[1,2048]{1,0:T(1,128)S(1)}, s32[1,2048]{1,0:T(1,128)}, u32[]{:S(2)}) copy-start(s32[1,2048]{1,0:T(1,128)} %copy-done.15) | copy-start | bytes 24580
  656.8 10.7 %copy-start.18 = (s32[4]{0:T(128)S(1)}, s32[4]{0:T(128)}, u32[]{:S(2)}) copy-start(s32[4]{0:T(128)} %copy-done.17) | copy-start | bytes 52
  656.8 10.7 %copy-start.20 = (s32[4]{0:T(128)S(1)}, s32[4]{0:T(128)}, u32[]{:S(2)}) copy-start(s32[4]{0:T(128)} %copy-done.19) | copy-start | bytes 52
  656.8 138.3 %reduce-scatter.11.cloned.1.call-start = ((), (), s32[]{:S(2)}) async-start(), calls=%async_computation.13 | async-start | bytes 2359296 | tf_op jit(solution)/shard_map/reduce_scatter | solution.py:992
  657.9 9.5 %copy-start.1 = (bf16[2048,256]{1,0:T(8,128)(2,1)S(1)}, bf16[2048,256]{1,0:T(8,128)(2,1)}, u32[]{:S(2)}) copy-start(bf16[2048,256]{1,0:T(8,128)(2,1)} %copy-done) | copy-start | bytes 3145732
  658.0 9.5 %copy-start.4 = (bf16[2048,256]{1,0:T(8,128)(2,1)S(1)}, bf16[2048,256]{1,0:T(8,128)(2,1)}, u32[]{:S(2)}) copy-start(bf16[2048,256]{1,0:T(8,128)(2,1)} %copy-done.3) | copy-start | bytes 3145732
  658.0 9.6 %copy-start.6 = (bf16[2048,256]{1,0:T(8,128)(2,1)S(1)}, bf16[2048,256]{1,0:T(8,128)(2,1)}, u32[]{:S(2)}) copy-start(bf16[2048,256]{1,0:T(8,128)(2,1)} %copy-done.5) | copy-start | bytes 3145732
  658.0 9.6 %copy-start.8 = (bf16[2048,256]{1,0:T(8,128)(2,1)S(1)}, bf16[2048,256]{1,0:T(8,128)(2,1)}, u32[]{:S(2)}) copy-start(bf16[2048,256]{1,0:T(8,128)(2,1)} %copy-done.7) | copy-start | bytes 3145732
  658.0 9.2 %collective-permute-start.4 = (bf16[1024,256]{1,0:T(8,128)(2,1)S(1)}, bf16[1024,256]{1,0:T(8,128)(2,1)S(1)}, u32[]{:S(2)}, u32[]{:S(2)}) collective-permute-start(bf16[1024,256]{1,0:T(8,128)(2,1)S(1)} %broadcast_select_fusion.8), channel_id=1, source_target_pairs={{0,4},{4,0},{1,5},{5,1},{2,6},{6,2},{3,7},{7,3},{8,12},{12,8},{9,1... | collective-permute-start | bytes 1572872 | tf_op jit(solution)/shard_map/ppermute | solution.py:218
  698.1 21.7 %collective-permute-start.5 = (bf16[1024,256]{1,0:T(8,128)(2,1)}, bf16[1024,256]{1,0:T(8,128)(2,1)}, u32[]{:S(2)}, u32[]{:S(2)}) collective-permute-start(bf16[1024,256]{1,0:T(8,128)(2,1)} %broadcast_select_fusion.4), channel_id=1, source_target_pairs={{0,4},{4,0},{1,5},{5,1},{2,6},{6,2},{3,7},{7,3},{8,12},{12,8},{9,1... | collective-permute-start | bytes 1572872 | tf_op jit(solution)/shard_map/ppermute | solution.py:218
  698.3 184.6 %reduce-scatter.9.cloned.1.call-start = ((), (), s32[]{:S(2)}) async-start(), calls=%async_computation.12 | async-start | bytes 7077888 | tf_op jit(solution)/shard_map/reduce_scatter | solution.py:992
  698.7 36.1 %collective-permute-start.6 = (bf16[1024,256]{1,0:T(8,128)(2,1)S(1)}, bf16[1024,256]{1,0:T(8,128)(2,1)S(1)}, u32[]{:S(2)}, u32[]{:S(2)}) collective-permute-start(bf16[1024,256]{1,0:T(8,128)(2,1)S(1)} %broadcast_select_fusion.2), channel_id=1, source_target_pairs={{0,4},{4,0},{1,5},{5,1},{2,6},{6,2},{3,7},{7,3},{8,12},{12,8},{9,1... | collective-permute-start | bytes 1572872 | tf_op jit(solution)/shard_map/ppermute | solution.py:218
  700.6 51.1 %collective-permute-start.7 = (bf16[1024,256]{1,0:T(8,128)(2,1)S(1)}, bf16[1024,256]{1,0:T(8,128)(2,1)S(1)}, u32[]{:S(2)}, u32[]{:S(2)}) collective-permute-start(bf16[1024,256]{1,0:T(8,128)(2,1)S(1)} %broadcast_select_fusion), channel_id=1, source_target_pairs={{0,4},{4,0},{1,5},{5,1},{2,6},{6,2},{3,7},{7,3},{8,12},{12,8},{9,1... | collective-permute-start | bytes 1572872 | tf_op jit(solution)/shard_map/ppermute | solution.py:218
  735.0 17.2 %copy-start.10 = (bf16[1024,2048]{1,0:T(8,128)(2,1)S(1)}, bf16[1024,2048]{1,0:T(8,128)(2,1)}, u32[]{:S(2)}) copy-start(bf16[1024,2048]{1,0:T(8,128)(2,1)} %copy-done.9) | copy-start | bytes 12582916
  765.8 25.4 %all-to-all-start.1 = ((bf16[4,4,64,512]{3,2,0,1:T(8,128)(2,1)}), bf16[4,4,64,512]{3,2,0,1:T(8,128)(2,1)S(1)}, u32[]{:S(2)}, u32[]{:S(2)}) async-start(bf16[4,4,64,512]{3,2,0,1:T(8,128)(2,1)} %bitcast.29), calls=%async_computation.1 | async-start | bytes 2097152 | tf_op jit(solution)/shard_map/all_to_all | solution.py:898
  771.8 25.1 %copy-start.22 = (f32[256,2048]{1,0:T(8,128)S(1)}, f32[256,2048]{1,0:T(8,128)}, u32[]{:S(2)}) copy-start(f32[256,2048]{1,0:T(8,128)} %get-tuple-element.71.inner_ref) | copy-start | bytes 6291460
  801.6 77.3 %copy-start.28 = (bf16[256,2048]{1,0:T(8,128)(2,1)S(1)}, bf16[256,2048]{1,0:T(8,128)(2,1)}, u32[]{:S(2)}) copy-start(bf16[256,2048]{1,0:T(8,128)(2,1)} %reduce-scatter.7.cloned.1.call-done) | copy-start | bytes 3145732
  (6 other events, 10.8 us)
Sparse Core Ops, SparseCore 0:
  10.5 46.6 all-gather.4
  59.1 27.8 all-gather.6
  88.9 74.4 all-gather.8
  165.2 68.3 all-gather.10
  508.2 75.2 reduce-scatter.4
  656.9 93.9 reduce-scatter.6
  754.8 40.2 reduce-scatter.10
  798.9 63.0 reduce-scatter.8

commit v5 on v4

--- a/solution.py
+++ b/solution.py
@@ -74,10 +74,10 @@
     lse_ref[...] = (top + jnp.log2(total))[None]
 
 
-def attend(queries, keys, values, low, high, first, last):
-    rows, width = queries.shape
-    span = keys.shape[0]
-    heads = width // HD
+def attend(queries, keys, values, heads, low, high, first, last, places=(0, 0, 0)):
+    rows, span = queries.shape[0], keys.shape[0]
+    width = heads * HD
+    q_at, k_at, v_at = places
     return pl.pallas_call(
         attend_kernel,
         out_shape=(
@@ -88,9 +88,9 @@
             num_scalar_prefetch=2,
             grid=(heads, rows // QB),
             in_specs=[
-                pl.BlockSpec((QB, HD), lambda h, i, *_: (i, h)),
-                pl.BlockSpec((span, HD), lambda h, i, *_: (0, h)),
-                pl.BlockSpec((span, HD), lambda h, i, *_: (0, h)),
+                pl.BlockSpec((QB, HD), lambda h, i, *_: (i, h + q_at)),
+                pl.BlockSpec((span, HD), lambda h, i, *_: (0, h + k_at)),
+                pl.BlockSpec((span, HD), lambda h, i, *_: (0, h + v_at)),
                 pl.BlockSpec((1, QB), lambda h, i, *_: (0, i)),
                 pl.BlockSpec((1, QB), lambda h, i, *_: (0, i)),
             ],
@@ -154,10 +154,13 @@
         dv_ref[...] = dv_sum[...].astype(dv_ref.dtype)
 
 
-def attend_back(queries, keys, values, out, upstream, lse, low, high, first, last, kind):
-    rows, width = queries.shape
+def attend_back(
+    queries, keys, values, out, upstream, lse, low, high, first, last, kind, places=(0, 0, 0)
+):
+    rows, width = out.shape
     span = keys.shape[0]
     heads = width // HD
+    q_at, k_at, v_at = places
     row_spec = pl.BlockSpec((QB, HD), lambda h, i, *_: (i, h))
     key_spec = pl.BlockSpec((span, HD), lambda h, i, *_: (0, h))
     mark_spec = pl.BlockSpec((1, QB), lambda h, i, *_: (0, i))
@@ -172,7 +175,10 @@
             num_scalar_prefetch=2,
             grid=(heads, rows // QB),
             in_specs=[
-                row_spec, key_spec, key_spec, row_spec, row_spec,
+                pl.BlockSpec((QB, HD), lambda h, i, *_: (i, h + q_at)),
+                pl.BlockSpec((span, HD), lambda h, i, *_: (0, h + k_at)),
+                pl.BlockSpec((span, HD), lambda h, i, *_: (0, h + v_at)),
+                row_spec, row_spec,
                 pl.BlockSpec((1, 1, QB), lambda h, i, *_: (h, 0, i)),
                 mark_spec, mark_spec,
             ],
@@ -214,28 +220,6 @@
     return jnp.concatenate([below, block, above], axis=0)
 
 
-def swap_halves(own, other):
-    got = lax.ppermute(other, "ctx", [(0, 1), (1, 0)])
-    here = lax.axis_index("ctx") == 0
-    return jnp.where(here, own, got), jnp.where(here, got, own)
-
-
-def heads_in(block):
-    half = block.shape[1] // 2
-    here = lax.axis_index("ctx") == 0
-    left, right = block[:, :half], block[:, half:]
-    pair = swap_halves(jnp.where(here, left, right), jnp.where(here, right, left))
-    return jnp.concatenate(pair, axis=0)
-
-
-def heads_out(block):
-    half = block.shape[0] // 2
-    here = lax.axis_index("ctx") == 0
-    top, bottom = block[:half], block[half:]
-    pair = swap_halves(jnp.where(here, top, bottom), jnp.where(here, bottom, top))
-    return jnp.concatenate(pair, axis=1)
-
-
 def norm_parts(rows):
     mean = jnp.mean(rows, axis=-1, keepdims=True)
     square = jnp.mean(rows * rows, axis=-1, keepdims=True)
@@ -259,7 +243,7 @@
 TILE = 512
 
 
-def greet(me, count):
+def greet(me, count, others=()):
     barrier = pltpu.get_barrier_semaphore()
 
     @pl.when(me > 0)
@@ -270,13 +254,16 @@
     def _():
         pl.semaphore_signal(barrier, inc=1, device_id={"tp": me + 1}, device_id_type=MESH)
 
+    for other in others:
+        pl.semaphore_signal(barrier, inc=1, device_id=other, device_id_type=MESH)
+
     @pl.when((me == 0) | (me == count - 1))
     def _():
-        pl.semaphore_wait(barrier, 1)
+        pl.semaphore_wait(barrier, 1 + len(others))
 
     @pl.when((me > 0) & (me < count - 1))
     def _():
-        pl.semaphore_wait(barrier, 2)
+        pl.semaphore_wait(barrier, 2 + len(others))
 
 
 def peers_along_tp(me, count):
@@ -537,8 +524,256 @@
     )(x, marks)
 
 
+class Swap:
+    def __init__(self, sent, got, source, place):
+        self.sent, self.got, self.source, self.place = sent, got, source, place
+
+    def copy(self, piece):
+        return pltpu.make_async_remote_copy(
+            src_ref=self.source(piece),
+            dst_ref=self.place(piece),
+            send_sem=self.sent.at[piece],
+            recv_sem=self.got.at[piece],
+            device_id={"ctx": 1 - lax.axis_index("ctx")},
+            device_id_type=MESH,
+        )
+
+    def start(self, piece):
+        self.copy(piece).start()
+
+    def wait_arrival(self, piece):
+        self.copy(piece).wait_recv()
+
+    def wait_sent(self, piece):
+        self.copy(piece).wait_send()
+
+
+class PlaneGather:
+    def __init__(self, whole, sent, got):
+        self.whole, self.sent, self.got = whole, sent, got
+        fsdp, self.ctx = lax.axis_index("fsdp"), lax.axis_index("ctx")
+        self.fsdp = fsdp
+        self.twin = fsdp + 1 - 2 * lax.rem(fsdp, 2)
+        self.along_x = lax.rem(fsdp + 2, 4)
+        self.twin_x = lax.rem(self.twin + 2, 4)
+        self.core_peer = {"fsdp": self.twin}
+        self.x_peer = {"fsdp": self.along_x}
+        self.y_peer = {"ctx": 1 - self.ctx}
+
+    def peers(self):
+        return [self.core_peer, self.x_peer, self.y_peer]
+
+    def shard(self, fsdp, ctx, half=None):
+        height = self.whole.shape[0] // 8
+        start = (fsdp * 2 + ctx) * height
+        if half is not None:
+            height //= 2
+            start += half * height
+        return self.whole.at[pl.ds(pl.multiple_of(start, height), height)]
+
+    def copy(self, number, view, peer):
+        return pltpu.make_async_remote_copy(
+            src_ref=view,
+            dst_ref=view,
+            send_sem=self.sent.at[number],
+            recv_sem=self.got.at[number],
+            device_id=peer,
+            device_id_type=MESH,
+        )
+
+    def copies(self):
+        own = self.shard(self.fsdp, self.ctx)
+        from_x = self.shard(self.along_x, self.ctx)
+        from_y = self.shard(self.fsdp, 1 - self.ctx)
+        return [
+            (own, self.core_peer),
+            (own, self.x_peer),
+            (own, self.y_peer),
+            (from_x, self.core_peer),
+            (self.shard(self.along_x, self.ctx, 0), self.y_peer),
+            (from_y, self.core_peer),
+            (self.shard(self.fsdp, 1 - self.ctx, 1), self.x_peer),
+            (self.shard(self.along_x, 1 - self.ctx, 0), self.core_peer),
+            (self.shard(self.along_x, 1 - self.ctx, 1), self.core_peer),
+        ]
+
+    def arrivals(self):
+        return [
+            self.shard(self.twin, self.ctx),
+            self.shard(self.along_x, self.ctx),
+            self.shard(self.fsdp, 1 - self.ctx),
+            self.shard(self.twin_x, self.ctx),
+            self.shard(self.along_x, 1 - self.ctx, 0),
+            self.shard(self.twin, 1 - self.ctx),
+            self.shard(self.along_x, 1 - self.ctx, 1),
+            self.shard(self.twin_x, 1 - self.ctx, 0),
+            self.shard(self.twin_x, 1 - self.ctx, 1),
+        ]
+
+    def start(self, *numbers):
+        copies = self.copies()
+        for number in numbers:
+            self.copy(number, *copies[number]).start()
+
+    def wait(self, *numbers):
+        arrivals = self.arrivals()
+        for number in numbers:
+            view = arrivals[number]
+            pltpu.make_async_copy(view, view, self.got.at[number]).wait()
+
+    def first(self):
+        self.start(1, 2, 0)
+
+    def second(self):
+        self.wait(1)
+        self.start(4, 3)
+        self.wait(2)
+        self.start(6, 5)
+
+    def third(self):
+        self.wait(4)
+        self.start(7)
+        self.wait(6)
+        self.start(8)
+
+    def last(self):
+        self.wait(0, 3, 5, 7, 8)
+
+    def wait_sent(self):
+        for number, (view, peer) in enumerate(self.copies()):
+            self.copy(number, view, peer).wait_send()
+
+
+def enter_kernel(
+    count, x_ref, marks_ref, query_ref, key_ref, value_ref, bias,
+    wide, marks_out, weight, heads,
+    mark_slots, stage, sent, got, marks_sent, marks_got,
+    weight_sent, weight_got, swap_sent, swap_got,
+):
+    me, ctx = lax.axis_index("tp"), lax.axis_index("ctx")
+    rows, width = x_ref.shape
+    height = rows // PIECES
+    half = query_ref.shape[1] // 2
+    part = 3 * half
+
+    def piece_rows(piece, start=0):
+        return pl.ds(pl.multiple_of(start + piece * height, height), height)
+
+    def view(piece, owner):
+        return wide.at[piece_rows(piece), pl.ds(pl.multiple_of(owner * width, width), width)]
+
+    gather = PlaneGather(weight, weight_sent, weight_got)
+    own_shard = gather.shard(gather.fsdp, ctx)
+    for side in range(2):
+        for i, ref in enumerate((query_ref, key_ref, value_ref)):
+            start = side * part + i * half
+            own_shard[:, start : start + half] = ref[:, side * half : (side + 1) * half]
+    line = Line(me, count, None, None, None, view, sent, got)
+    tp_peers = peers_along_tp(me, count)
+    greet_peers(tp_peers + gather.peers())
+
+    def source(piece):
+        return x_ref.at[piece_rows(piece)]
+
+    @pl.loop(0, PIECES)
+    def _(piece):
+        line.spread_start(piece, source(piece))
+
+    gather.first()
+    marks = Exchange(
+        tp_peers, marks_sent, marks_got, lambda _: marks_ref, lambda i: mark_slots.at[i]
+    )
+    marks.start()
+    own = pl.ds(pl.multiple_of(me * width, width), width)
+    wide[:, own] = x_ref[...]
+    marks_out[:, own] = marks_ref[...]
+    swap = Swap(
+        swap_sent, swap_got,
+        lambda piece: stage.at[piece_rows(piece)],
+        lambda piece: heads.at[piece_rows(piece, ctx * rows)],
+    )
+
+    def products(piece, side, place):
+        x = wide[piece_rows(piece), :]
+
+        @pl.loop(0, 3)
+        def _(tile):
+            start = pl.multiple_of(side * part + tile * half, half)
+            columns = pl.ds(start, half)
+            values = dot_plain(x, weight[:, columns]) + bias[:, columns]
+            place[:, pl.ds(pl.multiple_of(tile * half, half), half)] = values.astype(jnp.bfloat16)
+
+    for distance in range(1, count):
+        if distance == count - 1:
+            gather.last()
+
+        @pl.loop(0, PIECES)
+        def _(piece, distance=distance):
+            line.spread_onward(piece, distance)
+            if distance == count - 1:
+                products(piece, 1 - ctx, stage.at[piece_rows(piece)])
+                swap.start(piece)
+                products(piece, ctx, heads.at[piece_rows(piece, ctx * rows)])
+
+        if distance == 1:
+            gather.second()
+        if distance == count - 2:
+            gather.third()
+
+    marks.wait_arrivals()
+    for i in range(1, count):
+        owner = lax.rem(me - i + count, count)
+        marks_out[:, pl.ds(pl.multiple_of(owner * width, width), width)] = mark_slots[i - 1]
+
+    @pl.loop(0, PIECES)
+    def _(piece):
+        swap.wait_arrival(piece)
+        swap.wait_sent(piece)
+
+    marks.wait_sent()
+    gather.wait_sent()
+    line.spread_finish(PIECES, source)
+
+
+def enter(tokens, marks, query_weight, key_weight, value_weight, bias, collective_id):
+    count = lax.axis_size("tp")
+    rows, width = tokens.shape
+    head_cols = query_weight.shape[1]
+    plane = 8
+    part = 3 * head_cols // 2
+    return pl.pallas_call(
+        functools.partial(enter_kernel, count),
+        out_shape=[
+            jax.ShapeDtypeStruct((rows, count * width), tokens.dtype),
+            jax.ShapeDtypeStruct((marks.shape[0], count * width), marks.dtype),
+            jax.ShapeDtypeStruct((plane * query_weight.shape[0], 2 * part), query_weight.dtype),
+            jax.ShapeDtypeStruct((2 * rows, part), jnp.bfloat16),
+        ],
+        in_specs=[pl.BlockSpec(memory_space=pltpu.VMEM)] * 6,
+        out_specs=[pl.BlockSpec(memory_space=pltpu.VMEM)] * 4,
+        scratch_shapes=[
+            pltpu.VMEM((count - 1, *marks.shape), marks.dtype),
+            pltpu.VMEM((rows, part), jnp.bfloat16),
+            *line_semaphores(count, PIECES)[1],
+            pltpu.SemaphoreType.DMA((count - 1,)),
+            pltpu.SemaphoreType.DMA((count - 1,)),
+            pltpu.SemaphoreType.DMA((9,)),
+            pltpu.SemaphoreType.DMA((9,)),
+            pltpu.SemaphoreType.DMA((PIECES,)),
+            pltpu.SemaphoreType.DMA((PIECES,)),
+        ],
+        compiler_params=pltpu.CompilerParams(
+            collective_id=collective_id, has_side_effects=True, vmem_limit_bytes=40 << 20
+        ),
+        cost_estimate=pl.CostEstimate(
+            flops=80_000_000_000, bytes_accessed=64 * rows * count * width, transcendentals=0
+        ),
+        name="enter",
+    )(tokens, marks, query_weight, key_weight, value_weight, bias)
+
+
 def relay_kernel(count, row_step, use_step, sizes, *refs):
-    row_in, use_in, row_out, use_out, shared = sizes
+    row_in, use_in, row_out, use_out, shared, swap_in, swap_out = sizes
     refs = list(refs)
 
     def take(number):
@@ -551,20 +786,45 @@
     row_inputs, use_inputs = take(row_in), take(use_in)
     (gathered,) = take(1)
     row_outputs, use_outputs = take(row_out), take(use_out)
-    terms, total, slots, sum_sent, sum_got, spread_sent, spread_got = refs
-    me = lax.axis_index("tp")
-    height = x_ref.shape[0] // PIECES
+    swapped = take(1)[0] if swap_in or swap_out else None
+    terms, total, slots, sum_sent, sum_got, spread_sent, spread_got = take(7)
+    me, ctx = lax.axis_index("tp"), lax.axis_index("ctx")
+    rows = gathered.shape[0]
+    height = rows // PIECES
     own = height // count
     width = sum_weight.shape[0]
 
+    def piece_rows(piece, start=0):
+        return pl.ds(pl.multiple_of(start + piece * height, height), height)
+
     def view(piece, owner):
         return gathered.at[pl.ds(pl.multiple_of(piece * height + owner * own, own), own)]
 
     line = Line(me, count, slots, sum_sent, sum_got, view, spread_sent, spread_got)
-    greet(me, count)
-
-    def piece_rows(piece):
-        return pl.ds(pl.multiple_of(piece * height, height), height)
+    greet(me, count, [{"ctx": 1 - ctx}] if swap_in or swap_out else [])
+    swap = None
+    if swap_in:
+        half = x_ref.shape[1]
+        own_half = pl.ds(pl.multiple_of(ctx * half, half), half)
+        swap = Swap(
+            *refs,
+            lambda piece: x_ref.at[piece_rows(piece, (1 - ctx) * rows)],
+            lambda piece: swapped.at[piece_rows(piece), own_half],
+        )
+
+        @pl.loop(0, PIECES)
+        def _(piece):
+            swap.start(piece)
+            swapped[piece_rows(piece), own_half] = x_ref[piece_rows(piece, ctx * rows), :]
+
+    if swap_out:
+        stage, swap_sent, swap_got = refs
+        half = swapped.shape[1]
+        swap = Swap(
+            swap_sent, swap_got,
+            lambda piece: stage.at[piece_rows(piece)],
+            lambda piece: swapped.at[piece_rows(piece, ctx * rows)],
+        )
 
     @pl.loop(0, PIECES + 2)
     def _(step):
@@ -575,7 +835,9 @@
 
         @pl.when(step < PIECES)
         def _():
-            x = x_ref[piece_rows(step), :]
+            if swap_in:
+                swap.wait_arrival(step)
+            x = (swapped if swap_in else x_ref)[piece_rows(step), :]
 
             @pl.loop(0, width // TILE)
             def _(tile):
@@ -607,8 +869,23 @@
 
         @pl.when(step >= 2)
         def _():
-            rows = piece_rows(step - 2)
-            use_step(rows, gathered[rows, :], use_weight, use_inputs, use_outputs)
+            piece = step - 2
+            part = piece_rows(piece)
+            result = use_step(part, gathered[part, :], use_weight, use_inputs, use_outputs)
+            if swap_out:
+                here = ctx == 0
+                left, right = result[:, :half], result[:, half:]
+                stage[part, :] = jnp.where(here, right, left)
+                swap.start(piece)
+                swapped[piece_rows(piece, ctx * rows), :] = jnp.where(here, left, right)
+
+    if swap is not None:
+
+        @pl.loop(0, PIECES)
+        def _(piece):
+            if swap_out:
+                swap.wait_arrival(piece)
+            swap.wait_sent(piece)
 
     line.sum_finish(PIECES)
     line.spread_finish(PIECES)
@@ -616,18 +893,26 @@
 
 def relay(
     x, sum_weight, use_weight, row_inputs, row_step, row_shapes, use_inputs, use_step, use_shapes,
-    collective_id, name,
+    collective_id, name, rows, swap_in=None, swap_out=None,
 ):
     count = lax.axis_size("tp")
-    rows = x.shape[0]
     width = sum_weight.shape[0]
     height = rows // PIECES
     own = height // count
     shared = use_weight is None
     operands = [x, sum_weight, *([] if shared else [use_weight]), *row_inputs, *use_inputs]
     shapes = [jax.ShapeDtypeStruct((rows, width), jnp.bfloat16), *row_shapes, *use_shapes]
+    shapes += [shape for shape in (swap_in, swap_out) if shape is not None]
     sums, spreads = line_semaphores(count, PIECES)
-    sizes = (len(row_inputs), len(use_inputs), len(row_shapes), len(use_shapes), shared)
+    swaps = []
+    if swap_out is not None:
+        swaps.append(pltpu.VMEM((rows, swap_out.shape[1]), swap_out.dtype))
+    if swap_in is not None or swap_out is not None:
+        swaps += [pltpu.SemaphoreType.DMA((PIECES,))] * 2
+    sizes = (
+        len(row_inputs), len(use_inputs), len(row_shapes), len(use_shapes), shared,
+        swap_in is not None, swap_out is not None,
+    )
     return pl.pallas_call(
         functools.partial(relay_kernel, count, row_step, use_step, sizes),
         out_shape=shapes,
@@ -639,6 +924,7 @@
             pltpu.VMEM((PIECES, count + 1, own, width), jnp.bfloat16),
             *sums,
             *spreads,
+            *swaps,
         ],
         compiler_params=pltpu.CompilerParams(
             collective_id=collective_id, has_side_effects=True, vmem_limit_bytes=60 << 20
@@ -742,8 +1028,10 @@
 
 
 def attended_step(rows, chunk, weight, inputs, outputs):
-    (attended_grad,) = outputs
-    attended_grad[rows, :] = dot_plain(chunk, weight[...]).astype(jnp.bfloat16)
+    result = dot_plain(chunk, weight[...]).astype(jnp.bfloat16)
+    if outputs:
+        outputs[0][rows, :] = result
+    return result
 
 
 def peers_in_plane(sizes):
@@ -917,38 +1205,38 @@
 ):
     rows = tokens.shape[0]
     head_cols = query_weight.shape[1]
+    heads = head_cols // HD
     plane = ("fsdp", "ctx")
-    ctx_size = lax.axis_size("ctx")
-    by_heads = ctx_size == 2 and (head_cols // HD) % 2 == 0
+    plane_sizes = tuple(lax.axis_size(axis) for axis in plane)
+    by_heads = plane_sizes == (4, 2) and heads % 2 == 0
 
     def weight_rows(weight):
         return lax.all_gather(weight, plane, axis=0, tiled=True)
 
-    wide_qkv = weight_rows(jnp.concatenate([query_weight, key_weight, value_weight], axis=1))
     marks = jnp.concatenate(
         [norm_gains, row_biases, jnp.zeros((10, norm_gains.shape[1]), norm_gains.dtype)]
     )
-    wide_tokens, wide_marks = gather_features(tokens, marks, 0)
-    gains = wide_marks[:2].astype(jnp.float32)
-    biases = wide_marks[2:6].astype(jnp.float32)
-    full_output = weight_rows(output_weight)
-    full_expand = weight_rows(expand_weight)
-    full_shrink = weight_rows(shrink_weight)
-    upstream = spread_own(out_grad)
-
-    qkv_bias = jnp.concatenate([query_bias, jnp.zeros_like(query_bias), value_bias])
-    qkv = (dot_plain(wide_tokens, wide_qkv) + qkv_bias.astype(jnp.float32)).astype(jnp.bfloat16)
-    queries, keys, values = (
-        qkv[:, i * head_cols : (i + 1) * head_cols] for i in range(3)
-    )
-    block_index = lax.axis_index("fsdp") * ctx_size + lax.axis_index("ctx")
+    block_index = lax.axis_index("fsdp") * plane_sizes[1] + lax.axis_index("ctx")
+    qkv_bias = jnp.stack([query_bias, jnp.zeros_like(query_bias), value_bias])
+    qkv_bias = qkv_bias.astype(jnp.float32)
     if by_heads:
-        queries, keys, values = heads_in(queries), heads_in(keys), heads_in(values)
+        half_bias = qkv_bias.reshape(3, 2, -1).transpose(1, 0, 2).reshape(1, -1)
+        wide_tokens, wide_marks, wide_qkv, qkv_heads = enter(
+            tokens, marks, query_weight, key_weight, value_weight, half_bias, 0
+        )
+        queries = keys = values = qkv_heads
+        own_heads = heads // 2
+        stream_rows = plane_sizes[1] * rows
         stream_ids = lax.dynamic_slice_in_dim(
-            segments, lax.axis_index("fsdp") * ctx_size * rows, ctx_size * rows, 0
+            segments, lax.axis_index("fsdp") * stream_rows, stream_rows, 0
         )
         bounds = key_bounds(stream_ids, stream_ids, 0)
     else:
+        wide_qkv = weight_rows(jnp.concatenate([query_weight, key_weight, value_weight], axis=1))
+        wide_tokens, wide_marks = gather_features(tokens, marks, 0)
+        qkv = dot_plain(wide_tokens, wide_qkv) + qkv_bias.reshape(1, -1)
+        queries, keys, values = jnp.split(qkv.astype(jnp.bfloat16), 3, axis=1)
+        own_heads = heads
         keys, values = padded(keys, WIN), padded(values, WIN)
         ids = jnp.concatenate(
             [
@@ -959,8 +1247,15 @@
         )
         key_ids = lax.dynamic_slice_in_dim(ids, block_index * rows, rows + 2 * WIN, 0)
         bounds = key_bounds(key_ids[WIN : WIN + rows], key_ids, WIN)
-    attended_heads, lse = attend(queries, keys, values, *bounds)
-    attended = heads_out(attended_heads) if by_heads else attended_heads
+    places = (0, own_heads, 2 * own_heads) if by_heads else (0, 0, 0)
+    gains = wide_marks[:2].astype(jnp.float32)
+    biases = wide_marks[2:6].astype(jnp.float32)
+    full_output = weight_rows(output_weight)
+    full_expand = weight_rows(expand_weight)
+    full_shrink = weight_rows(shrink_weight)
+    attended_heads, lse = attend(queries, keys, values, own_heads, *bounds, places)
+    attended_heads, out_grad = lax.optimization_barrier((attended_heads, out_grad))
+    upstream = spread_own(out_grad)
 
     own_tokens = to_own_rows(wide_tokens)
     own_rows, features = own_tokens.shape
@@ -970,21 +1265,23 @@
         return jax.ShapeDtypeStruct(extent, kind)
 
     own_shape = shape((own_rows, features))
-    norm_low, first_norm, normed_one, inverse_one, hidden, activated = relay(
-        attended, full_output, full_expand,
+    norm_low, first_norm, normed_one, inverse_one, hidden, activated, *swapped = relay(
+        attended_heads, full_output, full_expand,
         [own_tokens, gains, biases], first_norm_step,
         [own_shape, own_shape, shape((own_rows, 128))],
         [hidden_bias.astype(jnp.float32)[None]], expand_step,
         [shape((rows, hidden_cols)), shape((rows, hidden_cols), jnp.bfloat16)],
-        1, "first_norm",
-    )
+        1, "first_norm", rows,
+        swap_in=shape((rows, head_cols), jnp.bfloat16) if by_heads else None,
+    )
+    attended = swapped[0] if by_heads else attended_heads
     ffn_low, mixed_own, grad_second, second_sums, hidden_low, hidden_sums = relay(
         activated, full_shrink, None,
         [first_norm, upstream, gains, biases], second_norm_step,
         [shape((own_rows, features), jnp.bfloat16), own_shape, shape((8, features))],
         [hidden], shrink_step,
         [shape((rows, hidden_cols), jnp.bfloat16), shape((8, hidden_cols))],
-        2, "second_norm",
+        2, "second_norm", rows,
     )
     mixed = unspread_own(mixed_own)
 
@@ -1002,8 +1299,9 @@
         [grad_second, normed_one, inverse_one, gains], first_back_step,
         [own_shape, shape((8, features))],
         [], attended_step,
-        [shape((rows, head_cols), jnp.bfloat16)],
-        3, "first_back",
+        [] if by_heads else [shape((rows, head_cols), jnp.bfloat16)],
+        3, "first_back", rows,
+        swap_out=shape((2 * rows, head_cols // 2), jnp.bfloat16) if by_heads else None,
     )
     attended_grad, shrink_grad, expand_part, output_part = lax.optimization_barrier(
         (
@@ -1018,10 +1316,16 @@
 
     if by_heads:
         grads = attend_back(
-            queries, keys, values, attended_heads, heads_in(attended_grad), lse, *bounds,
-            jnp.bfloat16,
+            queries, keys, values, attended_heads, attended_grad, lse, *bounds,
+            jnp.bfloat16, places,
         )
-        query_low, key_low, value_low = (heads_out(grad) for grad in grads)
+        halves = jnp.concatenate(grads, axis=1).reshape(2, rows, -1)
+        first = lax.axis_index("ctx") == 0
+        mine, other = (jnp.where(first, halves[i], halves[1 - i]) for i in range(2))
+        other = lax.ppermute(other, "ctx", [(0, 1), (1, 0)])
+        qkv_low = jnp.concatenate(
+            [jnp.where(first, mine, other), jnp.where(first, other, mine)], axis=1
+        )
     else:
         query_low, key_ext, value_ext = attend_back(
             queries, keys, values, attended_heads, attended_grad, lse, *bounds, jnp.float32
@@ -1034,8 +1338,7 @@
             own = own.at[:WIN].add(around[:WIN]).at[rows - WIN :].add(around[3 * WIN :])
             return own.astype(jnp.bfloat16)
 
-        key_low, value_low = fold(key_ext), fold(value_ext)
-    qkv_low = jnp.concatenate([query_low, key_low, value_low], axis=1)
+        qkv_low = jnp.concatenate([query_low, fold(key_ext), fold(value_ext)], axis=1)
     qkv_low, expand_grad, qkv_part = lax.optimization_barrier(
         (qkv_low, expand_grad, dot_rows(wide_tokens, qkv_low).astype(jnp.bfloat16))
     )
@@ -1049,19 +1352,28 @@
     )
     input_grad, vectors = input_sum(qkv_low, wide_qkv, grad_inner, row_sums, hidden_sums[:1], 4)
     hidden_rows = hidden_cols // head_cols
-    query_place = 8 + hidden_rows
+    sides = 2 if by_heads else 1
+
+    def by_kind(columns):
+        parts = columns.reshape(-1, sides, 3, head_cols // sides)
+        return [parts[:, :, i].reshape(-1, head_cols) for i in range(3)]
+
+    query_grad, key_grad, value_grad = by_kind(qkv_grad.astype(jnp.float32))
+    query_sum, _, value_sum = by_kind(
+        vectors[8 + hidden_rows : 8 + hidden_rows + 3].reshape(1, -1)
+    )
     return (
         mixed,
         input_grad,
-        qkv_grad[:, :head_cols].astype(jnp.float32),
-        qkv_grad[:, head_cols : 2 * head_cols].astype(jnp.float32),
-        qkv_grad[:, 2 * head_cols :].astype(jnp.float32),
+        query_grad,
+        key_grad,
+        value_grad,
         output_grad.astype(jnp.float32),
         expand_grad.astype(jnp.float32),
         shrink_grad.astype(jnp.float32),
-        vectors[query_place],
-        vectors[query_place + 2],
-        vectors[8:query_place].reshape(-1),
+        query_sum[0],
+        value_sum[0],
+        vectors[8 : 8 + hidden_rows].reshape(-1),
         vectors[:2],
         vectors[2:6],
     )

time: 902 us -> 887 us (0.983)
  waiting for transfers between devices: 143 us -> 102 us
  Pallas kernels: 609 us -> 641 us
  local copies, waits for them, and re-layouts: 27.6 us -> 47.9 us
  other arithmetic: 26.2 us -> 16.3 us
  matrix products: 52.8 us -> 43.6 us
    ppermute x8 -> x1, waiting for transfers between devices: 124 us -> 62 us  [body(): other = lax.ppermute(other, 'ctx', [(0, 1), (1, 0)])]
    pallas_call x1, Pallas kernels: 80.1 us -> 115 us  [enter(): pl.pallas_call(functools.partial(enter_kernel, count), out_shape=[jax.Sha...]
    all_to_all x1, waiting for transfers between devices: 0.01 us -> 17.3 us  [spread_own(): got = lax.all_to_all(parts, 'tp', split_axis=1, concat_axis=1, tiled=True)]
    unnamed x75 -> x56, local copies, waits for them, and re-layouts: 13.6 us -> 25.5 us
    dot_general x1 -> x0, matrix products: 10 us -> none  [dot_plain(): return jnp.dot(left, right, preferred_element_type=jnp.float32)]
  transfers between devices with their start and end apart: 18 -> 10, of which waited for: 9 -> 3; matrix products, arithmetic and copies ran while one was open for 9% -> 8% of each run, Pallas kernels for 53% -> 57%
where the time goes in v5:
time: 887 us; the launch traced here: 880 us
  Pallas kernels  641 us (72%)
  waiting for transfers between devices  102 us (11%)
  local copies, waits for them, and re-layouts  47.9 us (5%)
  matrix products  43.6 us (5%)
  other arithmetic  16.3 us (2%)
  between operations  14.9 us (2%)
  starting transfers between devices  14.1 us (2%)
    pallas_call x3, Pallas kernels, relay(): pl.pallas_call(functools.partial(relay_kernel, count, row_step, use_step,...  404 us
    pallas_call x1, Pallas kernels, enter(): pl.pallas_call(functools.partial(enter_kernel, count), out_shape=[jax.Sha...  115 us
    pallas_call x1, Pallas kernels, input_sum(): pl.pallas_call(functools.partial(input_kernel, sizes), out_shape=[jax.Sha...  76.9 us
    ppermute x1, waiting for transfers between devices, body(): other = lax.ppermute(other, 'ctx', [(0, 1), (1, 0)])  62 us
    dot_general x4, matrix products, dot_rows(): lax.dot_general(left, right, (((0,), (0,)), ((), ())), preferred_element_...  43.6 us
    pallas_call x1, Pallas kernels, attend_back(): pl.pallas_call(attend_back_kernel, out_shape=(jax.ShapeDtypeStruct((rows,...  25.8 us
    unnamed x56, local copies, waits for them, and re-layouts  25.5 us
    all_to_all x1, waiting for transfers between devices, unspread_own(): got = lax.all_to_all(parts, 'tp', split_axis=1, concat_axis=1, tiled=True)  20.7 us
  transfers between devices with their start and end apart: 10, of which 3 were waited for; matrix products, arithmetic and copies ran while one was open for 8% of the time, Pallas kernels for 57%

profile of v5, /device:TPU:8, one launch (start us, length us, event | category | flops | bytes accessed | tf_op | source)
XLA Modules:
  0.0 880.4 jit_solution(13708265784331415670)
XLA Ops:
  11.8 1.2 copy-done.12
  13.1 0.9 copy-done.13
  14.0 0.9 copy-done.14
  15.9 115.4 %enter.1 = (bf16[1024,2048]{1,0:T(8,128)(2,1)S(1)}, bf16[16,2048]{1,0:T(8,128)(2,1)S(1)}, bf16[2048,1536]{1,0:T(8,128)(2,1)}, bf16[2048,768]{1,0:T(8,128)(2,1)S(1)}) custom-call(bf16[1024,512]{1,0:T(8,128)(2,1)S(1)} %copy-done.12, bf16[16,512]{1,0:T(8,128)(2,1)S(1)} %maximum_maximum_fusion.marks_ref, bf16[256,512]{1,0:T(8,128)(2,1)S(1)} %copy-done.13, ...), custom_call_target="tpu_custom_call" | custom-call | flops 80000000000 | bytes 134217728 | tf_op jit(solution)/shard_map/enter/pallas_call | solution.py:744
  131.3 2.0 copy-done.2
  134.0 4.0 convert_reduce_fusion
  138.3 19.8 %attend.1 = (bf16[2048,256]{1,0:T(8,128)(2,1)S(1)}, f32[2,1,2048]{2,1,0:T(1,128)S(1)}) custom-call(s32[4]{0:T(128)S(1)} %get-tuple-element.162.first, s32[4]{0:T(128)S(1)} %get-tuple-element.163.last, bf16[2048,768]{1,0:T(8,128)(2,1)S(1)} %get-tuple-element.52.q_ref.k_ref.v_ref, bf16[2048,768]{1,0:T(8,128)(2,1)S(1)} %get-tuple-element.52.q_ref.k_ref.v_ref, ...), custom_call_target="tpu_custom_call" | custom-call | flops 3221225472 | bytes 4194304 | tf_op jit(solution)/shard_map/attend/pallas_call | solution.py:81
  158.2 1.0 copy-done.16
  159.2 1.1 copy.58
  160.3 8.1 all-to-all-start
  169.0 2.3 constant_dynamic-slice_fusion
  172.5 17.3 %all-to-all-done = bf16[4,4,64,512]{3,2,0,1:T(8,128)(2,1)} async-done(((bf16[4,4,64,512]{3,2,0,1:T(8,128)(2,1)}), bf16[4,4,64,512]{3,2,0,1:T(8,128)(2,1)}, u32[]{:S(2)}, u32[]{:S(2)}) %all-to-all-start) | async-done | bytes 1048608 | tf_op jit(solution)/shard_map/all_to_all | solution.py:1178
  189.8 2.0 copy.59
  191.8 1.2 copy.67
  193.1 138.2 %first_norm.1 = (bf16[1024,2048]{1,0:T(8,128)(2,1)}, f32[256,2048]{1,0:T(8,128)}, f32[256,2048]{1,0:T(8,128)}, f32[256,128]{1,0:T(8,128)}, f32[1024,2048]{1,0:T(...) custom-call(bf16[2048,256]{1,0:T(8,128)(2,1)} %copy-done.16, ...), custom_call_target="tpu_custom_call" | custom-call | flops 99999997952 | bytes 134217728 | tf_op jit(solution)/shard_map/first_norm/pallas_call | solution.py:916
  331.4 135.4 %second_norm.1 = (bf16[1024,2048]{1,0:T(8,128)(2,1)}, bf16[256,2048]{1,0:T(8,128)(2,1)}, f32[256,2048]{1,0:T(8,128)}, f32[8,2048]{1,0:T(8,128)}, bf16[1024,2048]{1,0:T(8,128)(2,1)}, /*index=5*/f32[8,2048]{1,0:T(8,128)}) custom-call(bf16[1024,2048]{1,0:T(8,128)(2,1)} %get-tuple-element.57.refs_0_, bf16[2048,2048]{1,0:T(8,128)(2,1)} %all-gather.8.cloned.1.call-done.refs_1_, ...), custom_call_target="tpu_custom_call" | custom-call | flops 99999997952 | bytes 134217728 | tf_op jit(solution)/shard_map/second_norm/pallas_call | solution.py:916
  466.8 14.0 %convolution_convert_fusion.2 = bf16[2048,2048]{1,0:T(8,128)(2,1)} fusion(bf16[1024,2048]{1,0:T(8,128)(2,1)} %get-tuple-element.63, bf16[1024,2048]{1,0:T(8,128)(2,1)} %get-tuple-element.57.refs_0_), kind=kOutput, calls=%fused_computation.4 | convolution fusion | flops 8594128896 | bytes 16777216 | tf_op jit(solution)/shard_map/dot_general | solution.py:27
  480.9 129.9 %first_back.1 = (bf16[1024,2048]{1,0:T(8,128)(2,1)}, f32[256,2048]{1,0:T(8,128)}, f32[8,2048]{1,0:T(8,128)}, bf16[2048,256]{1,0:T(8,128)(2,1)}) custom-call(bf16[1024,2048]{1,0:T(8,128)(2,1)} %get-tuple-element.64.refs_0_, bf16[2048,2048]{1,0:T(8,128)(2,1)} %all-gather.6.cloned.1.call-done.refs_2_.refs_1_, ...), custom_call_target="tpu_custom_call" | custom-call | flops 99999997952 | bytes 134217728 | tf_op jit(solution)/shard_map/first_back/pallas_call | solution.py:916
  610.8 6.2 convolution_convert_fusion.3
  617.0 14.1 %convolution_convert_fusion.1 = bf16[2048,2048]{1,0:T(8,128)(2,1)} fusion(bf16[1024,2048]{1,0:T(8,128)(2,1)} %get-tuple-element.70, bf16[1024,2048]{1,0:T(8,128)(2,1)} %get-tuple-element.64.refs_0_), kind=kOutput, calls=%fused_computation.3 | convolution fusion | flops 8594128896 | bytes 16777216 | tf_op jit(solution)/shard_map/dot_general | solution.py:27
  631.8 1.2 copy-done.17
  633.1 1.2 copy-done.18
  634.3 25.8 %attend_back.1 = (bf16[2048,256]{1,0:T(8,128)(2,1)S(1)}, bf16[2048,256]{1,0:T(8,128)(2,1)S(1)}, bf16[2048,256]{1,0:T(8,128)(2,1)S(1)}) custom-call(s32[4]{0:T(128)S(1)} %copy-done.9, s32[4]{0:T(128)S(1)} %copy-done.11, bf16[2048,768]{1,0:T(8,128)(2,1)S(1)} %get-tuple-element.52.q_ref.k_ref.v_ref, bf16[2048,768]{1,0:T(8,128)(2,1)S(1)} %get-tuple-element.52.q_ref.k_ref.v_ref, ...), custom_call_target="tpu_custom_call" | custom-call | flops 8589934592 | bytes 8388608 | tf_op jit(solution)/shard_map/attend_back/pallas_call | solution.py:167
  660.3 1.3 broadcast_select_fusion.2
  662.0 62.0 %collective-permute-done = bf16[1024,768]{1,0:T(8,128)(2,1)} collective-permute-done((bf16[1024,768]{1,0:T(8,128)(2,1)}, bf16[1024,768]{1,0:T(8,128)(2,1)}, u32[]{:S(2)}, u32[]{:S(2)}) %collective-permute-start) | collective-permute-done | bytes 1572896 | tf_op jit(solution)/shard_map/ppermute | solution.py:1325
  724.0 1.7 broadcast_select_fusion.1
  725.9 2.0 copy-done.3
  727.9 9.3 %convolution_convert_fusion = bf16[2048,1536]{1,0:T(8,128)(2,1)} fusion(bf16[1024,2048]{1,0:T(8,128)(2,1)S(1)} %copy-done.3, bf16[1024,768]{1,0:T(8,128)(2,1)S(1)} %get-tuple-element.146, bf16[1024,768]{1,0:T(8,128)(2,1)S(1)} %get-tuple-element.145), kind=kOutput, calls=%fused_computation.2 | convolution fusion | flops 6451888128 | bytes 13631488 | tf_op jit(solution)/shard_map/dot_general | solution.py:27
  737.2 2.6 reshape.119
  739.9 2.5 copy.70
  742.3 5.4 all-to-all-start.1
  748.6 1.0 fusion.3
  749.5 1.0 fusion.2
  750.6 20.7 %all-to-all-done.1 = bf16[4,4,64,512]{3,2,0,1:T(8,128)(2,1)} async-done(((bf16[4,4,64,512]{3,2,0,1:T(8,128)(2,1)}), bf16[4,4,64,512]{3,2,0,1:T(8,128)(2,1)}, u32[]{:S(2)}, u32[]{:S(2)}) %all-to-all-start.1) | async-done | bytes 1048608 | tf_op jit(solution)/shard_map/all_to_all | solution.py:1186
  771.4 2.3 copy.61
  773.6 2.8 convert_element_type.47
  776.4 1.8 convert_element_type.45
  778.2 2.8 copy-done.19
  781.0 1.6 copy-done.20
  782.6 76.9 %input_sum.1 = (bf16[1024,512]{1,0:T(8,128)(2,1)S(1)}, f32[16,512]{1,0:T(8,128)S(1)}) custom-call(bf16[1024,1536]{1,0:T(8,128)(2,1)S(1)} %pad_maximum_fusion.x_ref, bf16[2048,1536]{1,0:T(8,128)(2,1)S(1)} %copy-done.19, f32[256,2048]{1,0:T(8,128)S(1)} %copy-done.20, f32[8,2048]{1,0:T(8,128)S(1)} %concatenate.16.rows_ref, f32[1,2048]{1,0:T(1,128)S(1)} %slice.74.hidden_ref), custom_call_target="tpu_custom_call" | custom-call | flops 60000002048 | bytes 33554432 | tf_op jit(solution)/shard_map/input_sum/pallas_call | solution.py:1135
  859.5 1.0 copy-done
  861.1 1.6 convert_element_type.46
  864.4 1.5 copy.62
  865.9 1.1 fusion.1
  867.0 2.0 copy.63
  869.1 2.0 copy.64
  871.1 1.0 copy.65
  872.1 1.0 copy.74
  (92 shorter events, 13.5 us)
Async XLA Ops:
  7.2 185.9 %all-gather.4.cloned.1.call-start = ((), (), s32[]{:S(2)}) async-start(), calls=%async_computation.6 | async-start | bytes 2359296 | tf_op jit(solution)/shard_map/all_gather | solution.py:1214
  7.9 185.2 %all-gather.6.cloned.1.call-start = ((), (), s32[]{:S(2)}) async-start(), calls=%async_computation.7 | async-start | bytes 9437184 | tf_op jit(solution)/shard_map/all_gather | solution.py:1214
  8.7 322.7 %all-gather.8.cloned.1.call-start = ((), (), s32[]{:S(2)}) async-start(), calls=%async_computation.8 | async-start | bytes 9437184 | tf_op jit(solution)/shard_map/all_gather | solution.py:1214
  11.8 1.2 copy-start.12
  13.1 0.9 copy-start.13
  14.0 0.9 copy-start.14
  15.0 0.9 copy-start.15
  131.3 2.0 copy-start.2
  138.3 19.9 %copy-start.8 = (s32[4]{0:T(128)}, s32[4]{0:T(128)S(1)}, u32[]{:S(2)}) copy-start(s32[4]{0:T(128)S(1)} %get-tuple-element.162.first) | copy-start | bytes 52
  138.3 19.9 %copy-start.10 = (s32[4]{0:T(128)}, s32[4]{0:T(128)S(1)}, u32[]{:S(2)}) copy-start(s32[4]{0:T(128)S(1)} %get-tuple-element.163.last) | copy-start | bytes 52
  138.3 19.9 %copy-start.4 = (s32[1,2048]{1,0:T(1,128)}, s32[1,2048]{1,0:T(1,128)S(1)}, u32[]{:S(2)}) copy-start(s32[1,2048]{1,0:T(1,128)S(1)} %get-tuple-element.160.high_ref) | copy-start | bytes 24580
  138.3 19.9 %copy-start.6 = (s32[1,2048]{1,0:T(1,128)}, s32[1,2048]{1,0:T(1,128)S(1)}, u32[]{:S(2)}) copy-start(s32[1,2048]{1,0:T(1,128)S(1)} %get-tuple-element.161.low_ref) | copy-start | bytes 24580
  138.3 20.9 %copy-start.22 = (bf16[1024,512]{1,0:T(8,128)(2,1)S(1)}, bf16[1024,512]{1,0:T(8,128)(2,1)}, u32[]{:S(2)}) copy-start(bf16[1024,512]{1,0:T(8,128)(2,1)} %param.27) | copy-start | bytes 3145732
  158.2 1.0 copy-start.16
  159.2 9.2 %copy-start.23 = (bf16[2048]{0:T(1024)(128)(2,1)S(1)}, bf16[2048]{0:T(1024)(128)(2,1)}, u32[]{:S(2)}) copy-start(bf16[2048]{0:T(1024)(128)(2,1)} %param.24) | copy-start | bytes 12292
  160.3 29.5 %all-to-all-start = ((bf16[4,4,64,512]{3,2,0,1:T(8,128)(2,1)}), bf16[4,4,64,512]{3,2,0,1:T(8,128)(2,1)}, u32[]{:S(2)}, u32[]{:S(2)}) async-start(bf16[4,4,64,512]{3,2,0,1:T(8,128)(2,1)} %copy.58), calls=%async_computation | async-start | bytes 2097152 | tf_op jit(solution)/shard_map/all_to_all | solution.py:1178
  168.4 462.7 %reduce-scatter.5.cloned.1.call-start = ((), (), s32[]{:S(2)}) async-start(), calls=%async_computation.9 | async-start | bytes 9437184 | tf_op jit(solution)/shard_map/reduce_scatter | solution.py:1289
  480.9 256.3 %reduce-scatter.7.cloned.1.call-start = ((), (), s32[]{:S(2)}) async-start(), calls=%async_computation.10 | async-start | bytes 9437184 | tf_op jit(solution)/shard_map/reduce_scatter | solution.py:1289
  631.1 0.7 copy-start.5
  631.1 0.7 copy-start.7
  631.1 0.7 copy-start.9
  631.1 0.7 copy-start.11
  631.2 145.3 %reduce-scatter.11.cloned.1.call-start = ((), (), s32[]{:S(2)}) async-start(), calls=%async_computation.12 | async-start | bytes 2359296 | tf_op jit(solution)/shard_map/reduce_scatter | solution.py:1289
  631.8 1.2 copy-start.17
  633.0 1.2 copy-start.18
  661.6 62.4 %collective-permute-start = (bf16[1024,768]{1,0:T(8,128)(2,1)}, bf16[1024,768]{1,0:T(8,128)(2,1)}, u32[]{:S(2)}, u32[]{:S(2)}) collective-permute-start(bf16[1024,768]{1,0:T(8,128)(2,1)} %broadcast_select_fusion.2), channel_id=1, source_target_pairs={{0,4},{4,0},{1,5},{5,1},{2,6},{6,2},{3,7},{7,3},{8,12},{12,8},{9,1... | collective-permute-start | bytes 4718600 | tf_op jit(solution)/shard_map/ppermute | solution.py:1325
  661.7 202.7 %reduce-scatter.9.cloned.1.call-start = ((), (), s32[]{:S(2)}) async-start(), calls=%async_computation.11 | async-start | bytes 7077888 | tf_op jit(solution)/shard_map/reduce_scatter | solution.py:1289
  725.6 2.2 copy-start.3
  742.3 29.0 %all-to-all-start.1 = ((bf16[4,4,64,512]{3,2,0,1:T(8,128)(2,1)}), bf16[4,4,64,512]{3,2,0,1:T(8,128)(2,1)}, u32[]{:S(2)}, u32[]{:S(2)}) async-start(bf16[4,4,64,512]{3,2,0,1:T(8,128)(2,1)} %bitcast.37), calls=%async_computation.1 | async-start | bytes 2097152 | tf_op jit(solution)/shard_map/all_to_all | solution.py:1186
  778.2 2.8 copy-start.19
  781.0 1.6 copy-start.20
  782.6 78.4 %copy-start.21 = (bf16[256,2048]{1,0:T(8,128)(2,1)S(1)}, bf16[256,2048]{1,0:T(8,128)(2,1)}, u32[]{:S(2)}) copy-start(bf16[256,2048]{1,0:T(8,128)(2,1)} %reduce-scatter.7.cloned.1.call-done) | copy-start | bytes 3145732
  859.5 1.0 copy-start
  864.4 7.7 copy-start.1
Sparse Core Ops, SparseCore 0:
  9.9 38.2 all-gather.3
  50.1 76.4 all-gather.5
  128.5 54.3 all-gather.7
  481.0 79.1 reduce-scatter.4
  631.3 100.4 reduce-scatter.6
  735.5 40.2 reduce-scatter.10
  779.6 61.9 reduce-scatter.8

commit v6 on v5

--- a/solution.py
+++ b/solution.py
@@ -112,9 +112,10 @@
 
 def attend_back_kernel(
     first, last, q_ref, k_ref, v_ref, o_ref, g_ref, lse_ref, low_ref, high_ref,
-    dq_ref, dk_ref, dv_ref, kt, dk_sum, dv_sum,
+    *outputs,
 ):
-    block = pl.program_id(1)
+    *results, kt, dk_sum, dv_sum = outputs
+    head, block = pl.program_id(0), pl.program_id(1)
     rows = q_ref.shape[0]
 
     @pl.when(block == 0)
@@ -146,16 +147,28 @@
     dq = lax.fori_loop(
         first[block], last[block], step, jnp.zeros((HD, rows), jnp.float32)
     )
-    dq_ref[...] = (dq * score_scale).T.astype(dq_ref.dtype)
+    dq = (dq * score_scale).T
+    if len(results) == 1:
+        width = results[0].shape[1] // 3
+
+        def place(part):
+            start = pl.multiple_of(part * width + head * HD, HD)
+            return results[0].at[:, pl.ds(start, HD)]
+
+        query_place = place(0).at[pl.ds(pl.multiple_of(block * rows, rows), rows)]
+        key_place, value_place = place(1), place(2)
+    else:
+        query_place, key_place, value_place = results
+    query_place[...] = dq.astype(query_place.dtype)
 
     @pl.when(block == pl.num_programs(1) - 1)
     def _():
-        dk_ref[...] = (dk_sum[...] * score_scale).astype(dk_ref.dtype)
-        dv_ref[...] = dv_sum[...].astype(dv_ref.dtype)
+        key_place[...] = (dk_sum[...] * score_scale).astype(key_place.dtype)
+        value_place[...] = dv_sum[...].astype(value_place.dtype)
 
 
 def attend_back(
-    queries, keys, values, out, upstream, lse, low, high, first, last, kind, places=(0, 0, 0)
+    queries, keys, values, out, upstream, lse, low, high, first, last, places=(0, 0, 0), merged=False
 ):
     rows, width = out.shape
     span = keys.shape[0]
@@ -166,11 +179,13 @@
     mark_spec = pl.BlockSpec((1, QB), lambda h, i, *_: (0, i))
     return pl.pallas_call(
         attend_back_kernel,
-        out_shape=(
+        out_shape=[jax.ShapeDtypeStruct((rows, 3 * width), jnp.bfloat16)]
+        if merged
+        else [
             jax.ShapeDtypeStruct((rows, width), jnp.bfloat16),
-            jax.ShapeDtypeStruct((span, width), kind),
-            jax.ShapeDtypeStruct((span, width), kind),
-        ),
+            jax.ShapeDtypeStruct((span, width), jnp.float32),
+            jax.ShapeDtypeStruct((span, width), jnp.float32),
+        ],
         grid_spec=pltpu.PrefetchScalarGridSpec(
             num_scalar_prefetch=2,
             grid=(heads, rows // QB),
@@ -182,7 +197,9 @@
                 pl.BlockSpec((1, 1, QB), lambda h, i, *_: (h, 0, i)),
                 mark_spec, mark_spec,
             ],
-            out_specs=[row_spec, key_spec, key_spec],
+            out_specs=[pl.BlockSpec((rows, 3 * width), lambda h, i, *_: (0, 0))]
+            if merged
+            else [row_spec, key_spec, key_spec],
             scratch_shapes=[
                 pltpu.VMEM((HD, span), jnp.bfloat16),
                 pltpu.VMEM((span, HD), jnp.float32),
@@ -621,6 +638,11 @@
             view = arrivals[number]
             pltpu.make_async_copy(view, view, self.got.at[number]).wait()
 
+    def put(self, shard, done):
+        copy = pltpu.make_async_copy(shard, self.shard(self.fsdp, self.ctx), done)
+        copy.start()
+        copy.wait()
+
     def first(self):
         self.start(1, 2, 0)
 
@@ -645,10 +667,10 @@
 
 
 def enter_kernel(
-    count, x_ref, marks_ref, query_ref, key_ref, value_ref, bias,
-    wide, marks_out, weight, heads,
+    count, x_ref, marks_ref, query_ref, key_ref, value_ref, output_ref, bias,
+    wide, marks_out, weight, output_weight, heads,
     mark_slots, stage, sent, got, marks_sent, marks_got,
-    weight_sent, weight_got, swap_sent, swap_got,
+    weight_sent, weight_got, output_sent, output_got, swap_sent, swap_got,
 ):
     me, ctx = lax.axis_index("tp"), lax.axis_index("ctx")
     rows, width = x_ref.shape
@@ -668,6 +690,8 @@
         for i, ref in enumerate((query_ref, key_ref, value_ref)):
             start = side * part + i * half
             own_shard[:, start : start + half] = ref[:, side * half : (side + 1) * half]
+    output_gather = PlaneGather(output_weight, output_sent, output_got)
+    output_gather.shard(gather.fsdp, ctx)[...] = output_ref[...]
     line = Line(me, count, None, None, None, view, sent, got)
     tp_peers = peers_along_tp(me, count)
     greet_peers(tp_peers + gather.peers())
@@ -680,6 +704,7 @@
         line.spread_start(piece, source(piece))
 
     gather.first()
+    output_gather.first()
     marks = Exchange(
         tp_peers, marks_sent, marks_got, lambda _: marks_ref, lambda i: mark_slots.at[i]
     )
@@ -717,8 +742,10 @@
 
         if distance == 1:
             gather.second()
+            output_gather.second()
         if distance == count - 2:
             gather.third()
+            output_gather.third()
 
     marks.wait_arrivals()
     for i in range(1, count):
@@ -730,12 +757,16 @@
         swap.wait_arrival(piece)
         swap.wait_sent(piece)
 
+    output_gather.last()
     marks.wait_sent()
     gather.wait_sent()
+    output_gather.wait_sent()
     line.spread_finish(PIECES, source)
 
 
-def enter(tokens, marks, query_weight, key_weight, value_weight, bias, collective_id):
+def enter(
+    tokens, marks, query_weight, key_weight, value_weight, output_weight, bias, collective_id
+):
     count = lax.axis_size("tp")
     rows, width = tokens.shape
     head_cols = query_weight.shape[1]
@@ -747,18 +778,20 @@
             jax.ShapeDtypeStruct((rows, count * width), tokens.dtype),
             jax.ShapeDtypeStruct((marks.shape[0], count * width), marks.dtype),
             jax.ShapeDtypeStruct((plane * query_weight.shape[0], 2 * part), query_weight.dtype),
+            jax.ShapeDtypeStruct(
+                (plane * output_weight.shape[0], output_weight.shape[1]), output_weight.dtype
+            ),
             jax.ShapeDtypeStruct((2 * rows, part), jnp.bfloat16),
         ],
-        in_specs=[pl.BlockSpec(memory_space=pltpu.VMEM)] * 6,
-        out_specs=[pl.BlockSpec(memory_space=pltpu.VMEM)] * 4,
+        in_specs=[pl.BlockSpec(memory_space=pltpu.VMEM)] * 7,
+        out_specs=[pl.BlockSpec(memory_space=pltpu.VMEM)] * 5,
         scratch_shapes=[
             pltpu.VMEM((count - 1, *marks.shape), marks.dtype),
             pltpu.VMEM((rows, part), jnp.bfloat16),
             *line_semaphores(count, PIECES)[1],
             pltpu.SemaphoreType.DMA((count - 1,)),
             pltpu.SemaphoreType.DMA((count - 1,)),
-            pltpu.SemaphoreType.DMA((9,)),
-            pltpu.SemaphoreType.DMA((9,)),
+            *[pltpu.SemaphoreType.DMA((9,))] * 4,
             pltpu.SemaphoreType.DMA((PIECES,)),
             pltpu.SemaphoreType.DMA((PIECES,)),
         ],
@@ -769,11 +802,11 @@
             flops=80_000_000_000, bytes_accessed=64 * rows * count * width, transcendentals=0
         ),
         name="enter",
-    )(tokens, marks, query_weight, key_weight, value_weight, bias)
+    )(tokens, marks, query_weight, key_weight, value_weight, output_weight, bias)
 
 
 def relay_kernel(count, row_step, use_step, sizes, *refs):
-    row_in, use_in, row_out, use_out, shared, swap_in, swap_out = sizes
+    row_in, use_in, row_out, use_out, shared, swap_in, swap_out, gathers = sizes
     refs = list(refs)
 
     def take(number):
@@ -787,6 +820,11 @@
     (gathered,) = take(1)
     row_outputs, use_outputs = take(row_out), take(use_out)
     swapped = take(1)[0] if swap_in or swap_out else None
+    if gathers:
+        shards = [use_weight, *use_inputs[-1:]]
+        use_inputs = use_inputs[:-1]
+        wholes = take(2)
+        use_weight = wholes[0]
     terms, total, slots, sum_sent, sum_got, spread_sent, spread_got = take(7)
     me, ctx = lax.axis_index("tp"), lax.axis_index("ctx")
     rows = gathered.shape[0]
@@ -801,7 +839,17 @@
         return gathered.at[pl.ds(pl.multiple_of(piece * height + owner * own, own), own)]
 
     line = Line(me, count, slots, sum_sent, sum_got, view, spread_sent, spread_got)
-    greet(me, count, [{"ctx": 1 - ctx}] if swap_in or swap_out else [])
+    use_gather = next_gather = None
+    if gathers:
+        use_gather, next_gather = (
+            PlaneGather(whole, *take(2)) for whole in wholes
+        )
+        greet(me, count, use_gather.peers())
+        use_gather.put(shards[0], take(1)[0])
+        next_gather.put(shards[1], take(1)[0])
+        use_gather.first()
+    else:
+        greet(me, count, [{"ctx": 1 - ctx}] if swap_in or swap_out else [])
     swap = None
     if swap_in:
         half = x_ref.shape[1]
@@ -867,6 +915,26 @@
         def _():
             line.spread_onward(step - 1, 1)
 
+        if gathers:
+
+            @pl.when(step == 1)
+            def _():
+                use_gather.second()
+                next_gather.first()
+
+            @pl.when(step == 2)
+            def _():
+                use_gather.third()
+                use_gather.last()
+
+            @pl.when(step == 3)
+            def _():
+                next_gather.second()
+
+            @pl.when(step == 4)
+            def _():
+                next_gather.third()
+
         @pl.when(step >= 2)
         def _():
             piece = step - 2
@@ -887,22 +955,38 @@
                 swap.wait_arrival(piece)
             swap.wait_sent(piece)
 
+    if gathers:
+        next_gather.last()
+        use_gather.wait_sent()
+        next_gather.wait_sent()
     line.sum_finish(PIECES)
     line.spread_finish(PIECES)
 
 
 def relay(
     x, sum_weight, use_weight, row_inputs, row_step, row_shapes, use_inputs, use_step, use_shapes,
-    collective_id, name, rows, swap_in=None, swap_out=None,
+    collective_id, name, rows, swap_in=None, swap_out=None, next_shard=None,
 ):
     count = lax.axis_size("tp")
     width = sum_weight.shape[0]
     height = rows // PIECES
     own = height // count
     shared = use_weight is None
+    gathers = next_shard is not None
+    if gathers:
+        use_inputs = [*use_inputs, next_shard]
     operands = [x, sum_weight, *([] if shared else [use_weight]), *row_inputs, *use_inputs]
+    in_specs = [pl.BlockSpec(memory_space=pltpu.VMEM)] * len(operands)
     shapes = [jax.ShapeDtypeStruct((rows, width), jnp.bfloat16), *row_shapes, *use_shapes]
     shapes += [shape for shape in (swap_in, swap_out) if shape is not None]
+    out_specs = [pl.BlockSpec(memory_space=pltpu.VMEM)] * len(shapes)
+    extra = []
+    if gathers:
+        for shard, space in ((use_weight, pltpu.VMEM), (next_shard, pl.ANY)):
+            whole = (8 * shard.shape[0], shard.shape[1])
+            shapes.append(jax.ShapeDtypeStruct(whole, shard.dtype))
+            out_specs.append(pl.BlockSpec(memory_space=space))
+        extra = [pltpu.SemaphoreType.DMA((9,))] * 4 + [pltpu.SemaphoreType.DMA] * 2
     sums, spreads = line_semaphores(count, PIECES)
     swaps = []
     if swap_out is not None:
@@ -911,19 +995,20 @@
         swaps += [pltpu.SemaphoreType.DMA((PIECES,))] * 2
     sizes = (
         len(row_inputs), len(use_inputs), len(row_shapes), len(use_shapes), shared,
-        swap_in is not None, swap_out is not None,
+        swap_in is not None, swap_out is not None, gathers,
     )
     return pl.pallas_call(
         functools.partial(relay_kernel, count, row_step, use_step, sizes),
         out_shape=shapes,
-        in_specs=[pl.BlockSpec(memory_space=pltpu.VMEM)] * len(operands),
-        out_specs=[pl.BlockSpec(memory_space=pltpu.VMEM)] * len(shapes),
+        in_specs=in_specs,
+        out_specs=out_specs,
         scratch_shapes=[
             pltpu.VMEM((2, height, width), jnp.float32),
             pltpu.VMEM((own, width), jnp.float32),
             pltpu.VMEM((PIECES, count + 1, own, width), jnp.bfloat16),
             *sums,
             *spreads,
+            *extra,
             *swaps,
         ],
         compiler_params=pltpu.CompilerParams(
@@ -1047,7 +1132,7 @@
 def input_kernel(
     sizes, x_ref, weight, inner_ref, rows_ref, hidden_ref, out_ref, vectors_ref,
     term_ref, total, slots, own_vectors, tp_slots, plane_slots,
-    sum_sent, sum_got, tp_sent, tp_got, plane_sent, plane_got,
+    sum_sent, sum_got, tp_sent, tp_got, plane_sent, plane_got, hooks=None, pack_step=1,
 ):
     count = sizes[2]
     me = lax.axis_index("tp")
@@ -1068,6 +1153,8 @@
     over_plane = Exchange(
         plane_peers, plane_sent, plane_got, lambda _: own_vectors, lambda i: plane_slots.at[i]
     )
+    opening, before, after, closing = hooks or (lambda *_: None,) * 4
+    opening()
     over_tp.start()
 
     def terms(piece):
@@ -1102,10 +1189,11 @@
     def _(step):
         @pl.when(step < PIECES)
         def _():
+            before(step)
             line.sum_start(step, terms(step))
             line.sum_onward(step, terms(step))
 
-        pl.when(step == 1)(pack)
+        pl.when(step == pack_step)(pack)
 
         @pl.when(step >= 1)
         def _():
@@ -1115,6 +1203,9 @@
             rows = pl.ds(pl.multiple_of(piece * height, height), height)
             out_ref[rows, :] = total[...].astype(out_ref.dtype)
 
+        after(step)
+
+    closing()
     over_plane.wait_arrivals()
     vectors_ref[...] = own_vectors[...]
     for i in range(len(plane_peers)):
@@ -1163,6 +1254,236 @@
     )(x, weight, inner, row_sums, hidden_sums)
 
 
+class PlaneSum:
+    def __init__(self, parts, core_slots, first_slots, last_slots, sent, got):
+        self.parts, self.core_slots = parts, core_slots
+        self.first_slots, self.last_slots = first_slots, last_slots
+        self.sent, self.got = sent, got
+        self.fsdp, self.ctx = lax.axis_index("fsdp"), lax.axis_index("ctx")
+        self.twin = self.fsdp + 1 - 2 * lax.rem(self.fsdp, 2)
+        self.half = parts.shape[2] // 2
+
+    def number(self, fsdp, over_x, over_y):
+        chip = lax.rem(fsdp + 2 * over_x, 4)
+        return chip * 2 + (1 - self.ctx if over_y else self.ctx)
+
+    def view(self, over_x, over_y, side):
+        columns = pl.ds(side * self.half, self.half)
+        return self.parts.at[self.number(self.fsdp, over_x, over_y), :, columns]
+
+    def copy(self, number, source, place, peer):
+        return pltpu.make_async_remote_copy(
+            src_ref=source,
+            dst_ref=place,
+            send_sem=self.sent.at[number],
+            recv_sem=self.got.at[number],
+            device_id=peer,
+            device_id_type=MESH,
+        )
+
+    def core_copy(self, number):
+        over_x, over_y = number // 2, number % 2
+        source = self.parts.at[self.number(self.twin, over_x, over_y)]
+        return self.copy(number, source, self.core_slots.at[number], {"fsdp": self.twin})
+
+    def x_peer(self):
+        return {"fsdp": lax.rem(self.fsdp + 2, 4)}
+
+    def y_peer(self):
+        return {"ctx": 1 - self.ctx}
+
+    def first_copy(self, number):
+        slot = self.first_slots.at[number]
+        if number < 2:
+            return self.copy(4 + number, self.view(1, number, 0), slot, self.x_peer())
+        return self.copy(4 + number, self.view(number - 2, 1, 1), slot, self.y_peer())
+
+    def last_copy(self, side):
+        slot = self.last_slots.at[side]
+        if side == 0:
+            return self.copy(8, self.view(0, 1, 0), slot, self.y_peer())
+        return self.copy(9, self.view(1, 0, 1), slot, self.x_peer())
+
+    def add(self, view, slot):
+        total = view[...].astype(jnp.float32) + slot[...].astype(jnp.float32)
+        view[...] = total.astype(view.dtype)
+
+    def start(self):
+        for number in (3, 2, 1, 0):
+            self.core_copy(number).start()
+
+    def second(self):
+        for number in (3, 2, 1, 0):
+            self.core_copy(number).wait_recv()
+            shard = self.parts.at[self.number(self.fsdp, number // 2, number % 2)]
+            self.add(shard, self.core_slots.at[number])
+            if number == 3:
+                self.first_copy(1).start()
+                self.first_copy(3).start()
+            if number == 2:
+                self.first_copy(0).start()
+            if number == 1:
+                self.first_copy(2).start()
+
+    def third(self):
+        self.first_copy(1).wait_recv()
+        self.add(self.view(0, 1, 0), self.first_slots.at[1])
+        self.last_copy(0).start()
+        self.first_copy(3).wait_recv()
+        self.add(self.view(1, 0, 1), self.first_slots.at[3])
+        self.last_copy(1).start()
+
+    def finish(self):
+        totals = []
+        for side in range(2):
+            number = 2 * side
+            self.first_copy(number).wait_recv()
+            self.last_copy(side).wait_recv()
+            total = self.view(0, 0, side)[...].astype(jnp.float32)
+            total += self.first_slots[number].astype(jnp.float32)
+            totals.append(total + self.last_slots[side].astype(jnp.float32))
+        for number in range(4):
+            self.core_copy(number).wait_send()
+            self.first_copy(number).wait_send()
+        for side in range(2):
+            self.last_copy(side).wait_send()
+        return totals
+
+    @staticmethod
+    def scratch(shards, height, width):
+        return [
+            pltpu.VMEM((shards, height, width), jnp.bfloat16),
+            pltpu.VMEM((4, height, width), jnp.bfloat16),
+            pltpu.VMEM((4, height, width // 2), jnp.bfloat16),
+            pltpu.VMEM((2, height, width // 2), jnp.bfloat16),
+            pltpu.SemaphoreType.DMA((10,)),
+            pltpu.SemaphoreType.DMA((10,)),
+        ]
+
+
+def leave_kernel(
+    sizes, grads_ref, tokens_ref, weight, inner_ref, rows_ref, hidden_ref,
+    out_ref, vectors_ref, query_out, key_out, value_out,
+    x_ref, term_ref, total, slots, own_vectors, tp_slots, plane_slots,
+    sum_sent, sum_got, tp_sent, tp_got, plane_sent, plane_got, swap_sent, swap_got, *sum_scratch,
+):
+    count = sizes[2]
+    me, ctx = lax.axis_index("tp"), lax.axis_index("ctx")
+    rows = x_ref.shape[0]
+    height = rows // PIECES
+    part = grads_ref.shape[1]
+    plane_sum = PlaneSum(*sum_scratch)
+    shard = plane_sum.parts.shape[1]
+
+    def piece_rows(piece, start=0):
+        return pl.ds(pl.multiple_of(start + piece * height, height), height)
+
+    own_columns = pl.ds(pl.multiple_of(ctx * part, part), part)
+    swap = Swap(
+        swap_sent, swap_got,
+        lambda piece: grads_ref.at[piece_rows(piece, (1 - ctx) * rows)],
+        lambda piece: x_ref.at[piece_rows(piece), own_columns],
+    )
+
+    def product(number):
+        columns = pl.ds(pl.multiple_of(number * shard, shard), shard)
+        result = dot_rows(tokens_ref[:, columns], x_ref[...])
+        plane_sum.parts[number] = result.astype(jnp.bfloat16)
+
+    def opening():
+        @pl.loop(0, PIECES)
+        def _(piece):
+            swap.start(piece)
+
+        x_ref[:, own_columns] = grads_ref[pl.ds(pl.multiple_of(ctx * rows, rows), rows), :]
+
+    def before(step):
+        @pl.when(step < PIECES - 1)
+        def _():
+            swap.wait_arrival(step)
+
+    def after(step):
+        @pl.when(step == PIECES - 2)
+        def _():
+            swap.wait_arrival(PIECES - 1)
+            for over_x in (1, 0):
+                for over_y in (1, 0):
+                    product(plane_sum.number(plane_sum.twin, over_x, over_y))
+            plane_sum.start()
+
+        @pl.when(step == PIECES - 1)
+        def _():
+            for over_x in (1, 0):
+                for over_y in (1, 0):
+                    product(plane_sum.number(plane_sum.fsdp, over_x, over_y))
+            plane_sum.second()
+
+    def closing():
+        plane_sum.third()
+
+    input_kernel(
+        sizes, x_ref, weight, inner_ref, rows_ref, hidden_ref, out_ref, vectors_ref,
+        term_ref, total, slots, own_vectors, tp_slots, plane_slots,
+        sum_sent, sum_got, tp_sent, tp_got, plane_sent, plane_got,
+        hooks=(opening, before, after, closing), pack_step=PIECES - 1,
+    )
+    halves = plane_sum.finish()
+    third = part // 3
+    for side, half in enumerate(halves):
+        for i, ref in enumerate((query_out, key_out, value_out)):
+            ref[:, side * third : (side + 1) * third] = half[:, i * third : (i + 1) * third]
+
+    @pl.loop(0, PIECES)
+    def _(piece):
+        swap.wait_sent(piece)
+
+
+def leave(grads, tokens, weight, inner, row_sums, hidden_sums, collective_id):
+    sizes = tuple(lax.axis_size(axis) for axis in ("fsdp", "ctx", "tp"))
+    count = sizes[2]
+    others = sizes[0] * sizes[1] - 1
+    rows, features = tokens.shape
+    part = grads.shape[1]
+    width = features // count
+    height = rows // PIECES
+    shard = features // (others + 1)
+    packed = 8 + -(-(hidden_sums.shape[1] + 2 * part) // (8 * width)) * 8
+    return pl.pallas_call(
+        functools.partial(leave_kernel, sizes),
+        out_shape=[
+            jax.ShapeDtypeStruct((rows, width), jnp.bfloat16),
+            jax.ShapeDtypeStruct((packed, width), jnp.float32),
+            *[jax.ShapeDtypeStruct((shard, 2 * part // 3), jnp.float32)] * 3,
+        ],
+        in_specs=[pl.BlockSpec(memory_space=pltpu.VMEM)] * 6,
+        out_specs=[pl.BlockSpec(memory_space=pltpu.VMEM)] * 5,
+        scratch_shapes=[
+            pltpu.VMEM((rows, 2 * part), jnp.bfloat16),
+            pltpu.VMEM((height, width), jnp.float32),
+            pltpu.VMEM((height, width), jnp.float32),
+            pltpu.VMEM((PIECES, count + 1, height, width), jnp.bfloat16),
+            pltpu.VMEM((packed, width), jnp.float32),
+            pltpu.VMEM((count - 1, 8, width), jnp.float32),
+            pltpu.VMEM((others, packed, width), jnp.float32),
+            *line_semaphores(count, PIECES)[0],
+            pltpu.SemaphoreType.DMA((count - 1,)),
+            pltpu.SemaphoreType.DMA((count - 1,)),
+            pltpu.SemaphoreType.DMA((others,)),
+            pltpu.SemaphoreType.DMA((others,)),
+            pltpu.SemaphoreType.DMA((PIECES,)),
+            pltpu.SemaphoreType.DMA((PIECES,)),
+            *PlaneSum.scratch(others + 1, shard, 2 * part),
+        ],
+        compiler_params=pltpu.CompilerParams(
+            collective_id=collective_id, has_side_effects=True, vmem_limit_bytes=56 << 20
+        ),
+        cost_estimate=pl.CostEstimate(
+            flops=60_000_000_000, bytes_accessed=64 * rows * width, transcendentals=0
+        ),
+        name="leave",
+    )(grads, tokens, weight, inner, row_sums, hidden_sums)
+
+
 def to_own_rows(wide):
     count = lax.axis_size("tp")
     parts = wide.reshape(PIECES, count, -1, wide.shape[1])
@@ -1221,8 +1542,8 @@
     qkv_bias = qkv_bias.astype(jnp.float32)
     if by_heads:
         half_bias = qkv_bias.reshape(3, 2, -1).transpose(1, 0, 2).reshape(1, -1)
-        wide_tokens, wide_marks, wide_qkv, qkv_heads = enter(
-            tokens, marks, query_weight, key_weight, value_weight, half_bias, 0
+        wide_tokens, wide_marks, wide_qkv, full_output, qkv_heads = enter(
+            tokens, marks, query_weight, key_weight, value_weight, output_weight, half_bias, 0
         )
         queries = keys = values = qkv_heads
         own_heads = heads // 2
@@ -1245,17 +1566,16 @@
                 jnp.full((WIN,), jnp.iinfo(jnp.int32).max, jnp.int32),
             ]
         )
+        full_output = weight_rows(output_weight)
         key_ids = lax.dynamic_slice_in_dim(ids, block_index * rows, rows + 2 * WIN, 0)
         bounds = key_bounds(key_ids[WIN : WIN + rows], key_ids, WIN)
     places = (0, own_heads, 2 * own_heads) if by_heads else (0, 0, 0)
     gains = wide_marks[:2].astype(jnp.float32)
     biases = wide_marks[2:6].astype(jnp.float32)
-    full_output = weight_rows(output_weight)
-    full_expand = weight_rows(expand_weight)
-    full_shrink = weight_rows(shrink_weight)
+    wide_marks, out_grad = lax.optimization_barrier((wide_marks, out_grad))
+    upstream = spread_own(out_grad)
     attended_heads, lse = attend(queries, keys, values, own_heads, *bounds, places)
-    attended_heads, out_grad = lax.optimization_barrier((attended_heads, out_grad))
-    upstream = spread_own(out_grad)
+    attended_heads, upstream = lax.optimization_barrier((attended_heads, upstream))
 
     own_tokens = to_own_rows(wide_tokens)
     own_rows, features = own_tokens.shape
@@ -1265,16 +1585,21 @@
         return jax.ShapeDtypeStruct(extent, kind)
 
     own_shape = shape((own_rows, features))
-    norm_low, first_norm, normed_one, inverse_one, hidden, activated, *swapped = relay(
-        attended_heads, full_output, full_expand,
+    norm_low, first_norm, normed_one, inverse_one, hidden, activated, *more = relay(
+        attended_heads, full_output, expand_weight if by_heads else weight_rows(expand_weight),
         [own_tokens, gains, biases], first_norm_step,
         [own_shape, own_shape, shape((own_rows, 128))],
         [hidden_bias.astype(jnp.float32)[None]], expand_step,
         [shape((rows, hidden_cols)), shape((rows, hidden_cols), jnp.bfloat16)],
         1, "first_norm", rows,
         swap_in=shape((rows, head_cols), jnp.bfloat16) if by_heads else None,
-    )
-    attended = swapped[0] if by_heads else attended_heads
+        next_shard=shrink_weight if by_heads else None,
+    )
+    if by_heads:
+        attended, full_expand, full_shrink = more
+    else:
+        attended = attended_heads
+        full_expand, full_shrink = weight_rows(expand_weight), weight_rows(shrink_weight)
     ffn_low, mixed_own, grad_second, second_sums, hidden_low, hidden_sums = relay(
         activated, full_shrink, None,
         [first_norm, upstream, gains, biases], second_norm_step,
@@ -1290,10 +1615,15 @@
             grad, plane, scatter_dimension=0, tiled=True
         )
 
-    hidden_low, shrink_part = lax.optimization_barrier(
-        (hidden_low, dot_rows(ffn_low, activated).astype(jnp.bfloat16))
+    hidden_low, shrink_part, expand_part = lax.optimization_barrier(
+        (
+            hidden_low,
+            dot_rows(ffn_low, activated).astype(jnp.bfloat16),
+            dot_rows(norm_low, hidden_low).astype(jnp.bfloat16),
+        )
     )
     shrink_grad = owner_sum(shrink_part)
+    expand_grad = owner_sum(expand_part)
     branch_low, grad_inner, first_sums, attended_grad = relay(
         hidden_low, full_expand, full_output,
         [grad_second, normed_one, inverse_one, gains], first_back_step,
@@ -1303,32 +1633,23 @@
         3, "first_back", rows,
         swap_out=shape((2 * rows, head_cols // 2), jnp.bfloat16) if by_heads else None,
     )
-    attended_grad, shrink_grad, expand_part, output_part = lax.optimization_barrier(
+    attended_grad, shrink_grad, output_part = lax.optimization_barrier(
         (
             attended_grad,
             shrink_grad,
-            dot_rows(norm_low, hidden_low).astype(jnp.bfloat16),
             dot_rows(branch_low, attended).astype(jnp.bfloat16),
         )
     )
-    expand_grad = owner_sum(expand_part)
     output_grad = owner_sum(output_part)
 
     if by_heads:
-        grads = attend_back(
-            queries, keys, values, attended_heads, attended_grad, lse, *bounds,
-            jnp.bfloat16, places,
+        (grads,) = attend_back(
+            queries, keys, values, attended_heads, attended_grad, lse, *bounds, places, True
         )
-        halves = jnp.concatenate(grads, axis=1).reshape(2, rows, -1)
-        first = lax.axis_index("ctx") == 0
-        mine, other = (jnp.where(first, halves[i], halves[1 - i]) for i in range(2))
-        other = lax.ppermute(other, "ctx", [(0, 1), (1, 0)])
-        qkv_low = jnp.concatenate(
-            [jnp.where(first, mine, other), jnp.where(first, other, mine)], axis=1
-        )
+        grads, mixed, expand_grad = lax.optimization_barrier((grads, mixed, expand_grad))
     else:
         query_low, key_ext, value_ext = attend_back(
-            queries, keys, values, attended_heads, attended_grad, lse, *bounds, jnp.float32
+            queries, keys, values, attended_heads, attended_grad, lse, *bounds
         )
 
         def fold(ext):
@@ -1339,10 +1660,6 @@
             return own.astype(jnp.bfloat16)
 
         qkv_low = jnp.concatenate([query_low, fold(key_ext), fold(value_ext)], axis=1)
-    qkv_low, expand_grad, qkv_part = lax.optimization_barrier(
-        (qkv_low, expand_grad, dot_rows(wide_tokens, qkv_low).astype(jnp.bfloat16))
-    )
-    qkv_grad = owner_sum(qkv_part)
     row_sums = jnp.concatenate(
         [
             first_sums[0:1], second_sums[0:1],
@@ -1350,15 +1667,23 @@
             jnp.zeros_like(first_sums[:2]),
         ]
     )
-    input_grad, vectors = input_sum(qkv_low, wide_qkv, grad_inner, row_sums, hidden_sums[:1], 4)
-    hidden_rows = hidden_cols // head_cols
     sides = 2 if by_heads else 1
 
     def by_kind(columns):
         parts = columns.reshape(-1, sides, 3, head_cols // sides)
         return [parts[:, :, i].reshape(-1, head_cols) for i in range(3)]
 
-    query_grad, key_grad, value_grad = by_kind(qkv_grad.astype(jnp.float32))
+    if by_heads:
+        input_grad, vectors, query_grad, key_grad, value_grad = leave(
+            grads, wide_tokens, wide_qkv, grad_inner, row_sums, hidden_sums[:1], 4
+        )
+    else:
+        input_grad, vectors = input_sum(
+            qkv_low, wide_qkv, grad_inner, row_sums, hidden_sums[:1], 4
+        )
+        qkv_grad = owner_sum(dot_rows(wide_tokens, qkv_low).astype(jnp.bfloat16))
+        query_grad, key_grad, value_grad = by_kind(qkv_grad.astype(jnp.float32))
+    hidden_rows = hidden_cols // head_cols
     query_sum, _, value_sum = by_kind(
         vectors[8 + hidden_rows : 8 + hidden_rows + 3].reshape(1, -1)
     )

time: 887 us -> 840 us (0.947)
  waiting for transfers between devices: 102 us -> 0.53 us
  Pallas kernels: 641 us -> 705 us
  matrix products: 43.6 us -> 34.4 us
    ppermute x1 -> x0, waiting for transfers between devices: 62 us -> none  [body(): other = lax.ppermute(other, 'ctx', [(0, 1), (1, 0)])]
    pallas_call x2, Pallas kernels: 103 us -> 155 us  [the longest x1 126 us: leave(): pl.pallas_call(functools.partial(leave_kernel, sizes), out_shape=[jax.Sha...]
    pallas_call x3, Pallas kernels: 404 us -> 435 us  [relay(): pl.pallas_call(functools.partial(relay_kernel, count, row_step, use_step,...]
    pallas_call x1, Pallas kernels: 115 us -> 91.8 us  [enter(): pl.pallas_call(functools.partial(enter_kernel, count), out_shape=[jax.Sha...]
    all_to_all x1, waiting for transfers between devices: 20.7 us -> 0.01 us  [unspread_own(): got = lax.all_to_all(parts, 'tp', split_axis=1, concat_axis=1, tiled=True)]
    all_to_all x1, waiting for transfers between devices: 17.3 us -> 0.01 us  [spread_own(): got = lax.all_to_all(parts, 'tp', split_axis=1, concat_axis=1, tiled=True)]
    dot_general x4 -> x3, matrix products: 43.6 us -> 34.4 us  [dot_rows(): lax.dot_general(left, right, (((0,), (0,)), ((), ())), preferred_element_...]
    unnamed x56 -> x50, local copies, waits for them, and re-layouts: 25.5 us -> 19.6 us
  transfers between devices with their start and end apart: 10 -> 5, of which waited for: 3 -> 0; matrix products, arithmetic and copies ran while one was open for 8% -> 4% of each run, Pallas kernels for 57% -> 38%
where the time goes in v6:
time: 840 us; the launch traced here: 830 us
  Pallas kernels  705 us (84%)
  local copies, waits for them, and re-layouts  42.8 us (5%)
  matrix products  34.4 us (4%)
  starting transfers between devices  20.8 us (2%)
  between operations  14.4 us (2%)
  other arithmetic  11.9 us (1%)
    pallas_call x3, Pallas kernels, relay(): pl.pallas_call(functools.partial(relay_kernel, count, row_step, use_step,...  435 us
    pallas_call x1, Pallas kernels, leave(): pl.pallas_call(functools.partial(leave_kernel, sizes), out_shape=[jax.Sha...  126 us
    pallas_call x1, Pallas kernels, enter(): pl.pallas_call(functools.partial(enter_kernel, count), out_shape=[jax.Sha...  91.8 us
    dot_general x3, matrix products, dot_rows(): lax.dot_general(left, right, (((0,), (0,)), ((), ())), preferred_element_...  34.4 us
    pallas_call x1, Pallas kernels, attend_back(): pl.pallas_call(attend_back_kernel, out_shape=[jax.ShapeDtypeStruct((rows,...  29.2 us
    pallas_call x1, Pallas kernels, attend(): pl.pallas_call(attend_kernel, out_shape=(jax.ShapeDtypeStruct((rows, widt...  23.2 us
    unnamed x50, local copies, waits for them, and re-layouts  19.6 us
  transfers between devices with their start and end apart: 5, of which 0 were waited for; matrix products, arithmetic and copies ran while one was open for 4% of the time, Pallas kernels for 38%

profile of v6, /device:TPU:8, one launch (start us, length us, event | category | flops | bytes accessed | tf_op | source)
XLA Modules:
  0.0 829.6 jit_solution(16612351826682005440)
XLA Ops:
  7.2 0.7 stack.10
  8.8 0.8 maximum_maximum_fusion.marks_ref
  9.6 1.2 copy-done.5
  10.8 0.9 copy-done.6
  11.8 0.9 copy-done.7
  12.7 0.9 copy-done.8
  13.7 0.9 copy-done.9
  14.6 91.8 %enter.1 = (bf16[1024,2048]{1,0:T(8,128)(2,1)S(1)}, bf16[16,2048]{1,0:T(8,128)(2,1)S(1)}, bf16[2048,1536]{1,0:T(8,128)(2,1)}, bf16[2048,512]{1,0:T(8,128)(2,1)S(1)}, bf16[2048,768]{1,0:T(8,128)(2,1)S(1)}) custom-call(bf16[1024,512]{1,0:T(8,128)(2,1)S(1)} %copy-done.5, bf16[16,512]{1,0:T(8,128)(2,1)S(1)} %maximum_maximum_fusion.marks_ref, ...), custom_call_target="tpu_custom_call" | custom-call | flops 80000000000 | bytes 134217728 | tf_op jit(solution)/shard_map/enter/pallas_call | solution.py:775
  106.5 1.9 copy-done
  108.4 1.3 copy-done.14
  109.7 1.1 copy.45
  110.8 9.3 %all-to-all-start = ((bf16[4,4,64,512]{3,2,0,1:T(8,128)(2,1)}), bf16[4,4,64,512]{3,2,0,1:T(8,128)(2,1)}, u32[]{:S(2)}, u32[]{:S(2)}) async-start(bf16[4,4,64,512]{3,2,0,1:T(8,128)(2,1)} %copy.45), calls=%async_computation | async-start | bytes 2097152 | tf_op jit(solution)/shard_map/all_to_all | solution.py:1499
  120.1 0.7 dynamic_slice.7
  120.8 4.0 convert_reduce_fusion
  125.6 2.3 constant_dynamic-slice_fusion
  128.0 23.2 %attend.1 = (bf16[2048,256]{1,0:T(8,128)(2,1)S(1)}, f32[2,1,2048]{2,1,0:T(1,128)S(1)}) custom-call(s32[4]{0:T(128)S(1)} %get-tuple-element.113.first, s32[4]{0:T(128)S(1)} %get-tuple-element.114.last, bf16[2048,768]{1,0:T(8,128)(2,1)S(1)} %get-tuple-element.56.q_ref.k_ref.v_ref, bf16[2048,768]{1,0:T(8,128)(2,1)S(1)} %get-tuple-element.56.q_ref.k_ref.v_ref, ...), custom_call_target="tpu_custom_call" | custom-call | flops 3221225472 | bytes 4194304 | tf_op jit(solution)/shard_map/attend/pallas_call | solution.py:81
  151.2 1.0 copy-done.10
  153.4 2.0 copy.46
  155.4 1.2 copy.51
  156.7 157.0 %first_norm.1 = (bf16[1024,2048]{1,0:T(8,128)(2,1)}, f32[256,2048]{1,0:T(8,128)}, f32[256,2048]{1,0:T(8,128)}, f32[256,128]{1,0:T(8,128)}, f32[1024,2048]{1,0:T(...) custom-call(bf16[2048,256]{1,0:T(8,128)(2,1)} %copy-done.10, ...), custom_call_target="tpu_custom_call" | custom-call | flops 99999997952 | bytes 134217728 | tf_op jit(solution)/shard_map/first_norm/pallas_call | solution.py:1000
  313.7 142.4 %second_norm.1 = (bf16[1024,2048]{1,0:T(8,128)(2,1)}, bf16[256,2048]{1,0:T(8,128)(2,1)}, f32[256,2048]{1,0:T(8,128)}, f32[8,2048]{1,0:T(8,128)}, bf16[1024,2048]{1,0:T(8,128)(2,1)}, /*index=5*/f32[8,2048]{1,0:T(8,128)}) custom-call(bf16[1024,2048]{1,0:T(8,128)(2,1)} %get-tuple-element.63.refs_0_, bf16[2048,2048]{1,0:T(8,128)(2,1)} %get-tuple-element.64.refs_1_, ...), custom_call_target="tpu_custom_call" | custom-call | flops 99999997952 | bytes 134217728 | tf_op jit(solution)/shard_map/second_norm/pallas_call | solution.py:1000
  456.1 14.1 %convolution_convert_fusion.1 = bf16[2048,2048]{1,0:T(8,128)(2,1)} fusion(bf16[1024,2048]{1,0:T(8,128)(2,1)} %get-tuple-element.69, bf16[1024,2048]{1,0:T(8,128)(2,1)} %get-tuple-element.63.refs_0_), kind=kOutput, calls=%fused_computation.3 | convolution fusion | flops 8594128896 | bytes 16777216 | tf_op jit(solution)/shard_map/dot_general | solution.py:27
  470.2 14.0 %convolution_convert_fusion = bf16[2048,2048]{1,0:T(8,128)(2,1)} fusion(bf16[1024,2048]{1,0:T(8,128)(2,1)} %get-tuple-element.70, bf16[1024,2048]{1,0:T(8,128)(2,1)} %get-tuple-element.71.refs_0_), kind=kOutput, calls=%fused_computation.2 | convolution fusion | flops 8594128896 | bytes 16777216 | tf_op jit(solution)/shard_map/dot_general | solution.py:27
  485.0 2.6 reshape.108
  487.6 2.4 copy.54
  490.0 11.2 %all-to-all-start.1 = ((bf16[4,4,64,512]{3,2,0,1:T(8,128)(2,1)}), bf16[4,4,64,512]{3,2,0,1:T(8,128)(2,1)}, u32[]{:S(2)}, u32[]{:S(2)}) async-start(bf16[4,4,64,512]{3,2,0,1:T(8,128)(2,1)} %bitcast.31), calls=%async_computation.2 | async-start | bytes 2097152 | tf_op jit(solution)/shard_map/all_to_all | solution.py:1507
  501.2 135.6 %first_back.1 = (bf16[1024,2048]{1,0:T(8,128)(2,1)}, f32[256,2048]{1,0:T(8,128)}, f32[8,2048]{1,0:T(8,128)}, bf16[2048,256]{1,0:T(8,128)(2,1)}) custom-call(bf16[1024,2048]{1,0:T(8,128)(2,1)} %get-tuple-element.71.refs_0_, bf16[2048,2048]{1,0:T(8,128)(2,1)} %get-tuple-element.72.refs_1_, bf16[2048,512]{1,0:T(8,128)(2,1)} %copy-done.14, ...), custom_call_target="tpu_custom_call" | custom-call | flops 99999997952 | bytes 134217728 | tf_op jit(solution)/shard_map/first_back/pallas_call | solution.py:1000
  636.8 1.4 slice.53.hidden_ref
  638.3 1.0 fusion.2
  639.2 1.0 fusion.1
  640.2 0.7 concatenate.8.rows_ref
  641.0 6.3 convolution_convert_fusion.2
  647.3 2.3 copy.49
  649.6 1.2 copy-done.11
  650.8 1.2 copy-done.13
  652.0 29.2 %attend_back.1.grads_ref = bf16[2048,768]{1,0:T(8,128)(2,1)S(1)} custom-call(s32[4]{0:T(128)S(1)} %get-tuple-element.113.first, s32[4]{0:T(128)S(1)} %get-tuple-element.114.last, bf16[2048,768]{1,0:T(8,128)(2,1)S(1)} %get-tuple-element.56.q_ref.k_ref.v_ref, bf16[2048,768]{1,0:T(8,128)(2,1)S(1)} %get-tuple-element.56.q_ref.k_ref.v_ref, ...), custom_call_target="tpu_custom_call" | custom-call | flops 8589934592 | bytes 8388608 | tf_op jit(solution)/shard_map/attend_back/pallas_call | solution.py:180
  681.3 1.6 copy-done.12
  683.0 125.6 %leave.1 = (bf16[1024,512]{1,0:T(8,128)(2,1)}, f32[16,512]{1,0:T(8,128)}, f32[256,512]{1,0:T(8,128)}, f32[256,512]{1,0:T(8,128)}, f32[256,512]{1,0:T(8,128)}) custom-call(bf16[2048,768]{1,0:T(8,128)(2,1)} %copy-done.12, bf16[1024,2048]{1,0:T(8,128)(2,1)} %copy-done, bf16[2048,1536]{1,0:T(8,128)(2,1)} %get-tuple-element.86.weight, ...), custom_call_target="tpu_custom_call" | custom-call | flops 60000002048 | bytes 33554432 | tf_op jit(solution)/shard_map/leave/pallas_call | solution.py:1451
  808.6 0.8 slice.54
  809.4 1.3 slice.58
  810.7 1.3 fusion.3
  812.7 1.6 convert_element_type.41
  814.2 1.6 convert_element_type.42
  816.4 1.8 convert_element_type.40
  818.2 1.0 copy.59
  819.2 1.9 copy.60
  821.0 0.8 copy.61
  821.8 0.8 copy.62
  (65 shorter events, 5.2 us)
Async XLA Ops:
  9.6 1.2 copy-start.5
  10.8 0.9 copy-start.6
  11.8 0.9 copy-start.7
  12.7 0.9 copy-start.8
  13.7 0.9 copy-start.9
  14.6 95.1 %copy-start.17 = (bf16[1024,512]{1,0:T(8,128)(2,1)S(1)}, bf16[1024,512]{1,0:T(8,128)(2,1)}, u32[]{:S(2)}) copy-start(bf16[1024,512]{1,0:T(8,128)(2,1)} %param.27) | copy-start | bytes 3145732
  106.5 1.9 copy-start
  108.4 1.3 copy-start.14
  109.7 15.3 %copy-start.21 = (bf16[2048]{0:T(1024)(128)(2,1)S(1)}, bf16[2048]{0:T(1024)(128)(2,1)}, u32[]{:S(2)}) copy-start(bf16[2048]{0:T(1024)(128)(2,1)} %param.24) | copy-start | bytes 12292
  110.8 42.6 %all-to-all-start = ((bf16[4,4,64,512]{3,2,0,1:T(8,128)(2,1)}), bf16[4,4,64,512]{3,2,0,1:T(8,128)(2,1)}, u32[]{:S(2)}, u32[]{:S(2)}) async-start(bf16[4,4,64,512]{3,2,0,1:T(8,128)(2,1)} %copy.45), calls=%async_computation | async-start | bytes 2097152 | tf_op jit(solution)/shard_map/all_to_all | solution.py:1499
  120.1 529.5 %reduce-scatter.4.cloned.1.call-start = ((), (), s32[]{:S(2)}) async-start(), calls=%async_computation.5 | async-start | bytes 9437184 | tf_op jit(solution)/shard_map/reduce_scatter | solution.py:1614
  128.0 23.2 %copy-start.1 = (s32[1,2048]{1,0:T(1,128)}, s32[1,2048]{1,0:T(1,128)S(1)}, u32[]{:S(2)}) copy-start(s32[1,2048]{1,0:T(1,128)S(1)} %get-tuple-element.111.high_ref) | copy-start | bytes 24580
  128.0 23.2 %copy-start.3 = (s32[1,2048]{1,0:T(1,128)}, s32[1,2048]{1,0:T(1,128)S(1)}, u32[]{:S(2)}) copy-start(s32[1,2048]{1,0:T(1,128)S(1)} %get-tuple-element.112.low_ref) | copy-start | bytes 24580
  151.2 1.0 copy-start.10
  484.2 198.7 %reduce-scatter.6.cloned.1.call-start = ((), (), s32[]{:S(2)}) async-start(), calls=%async_computation.6 | async-start | bytes 9437184 | tf_op jit(solution)/shard_map/reduce_scatter | solution.py:1614
  490.0 157.3 %all-to-all-start.1 = ((bf16[4,4,64,512]{3,2,0,1:T(8,128)(2,1)}), bf16[4,4,64,512]{3,2,0,1:T(8,128)(2,1)}, u32[]{:S(2)}, u32[]{:S(2)}) async-start(bf16[4,4,64,512]{3,2,0,1:T(8,128)(2,1)} %bitcast.31), calls=%async_computation.2 | async-start | bytes 2097152 | tf_op jit(solution)/shard_map/all_to_all | solution.py:1507
  501.2 315.2 %reduce-scatter.8.cloned.1.call-start = ((), (), s32[]{:S(2)}) async-start(), calls=%async_computation.7 | async-start | bytes 2359296 | tf_op jit(solution)/shard_map/reduce_scatter | solution.py:1614
  641.0 8.6 %copy-start.2 = (s32[1,2048]{1,0:T(1,128)S(1)}, s32[1,2048]{1,0:T(1,128)}, u32[]{:S(2)}) copy-start(s32[1,2048]{1,0:T(1,128)} %copy-done.1) | copy-start | bytes 24580
  641.0 8.6 %copy-start.4 = (s32[1,2048]{1,0:T(1,128)S(1)}, s32[1,2048]{1,0:T(1,128)}, u32[]{:S(2)}) copy-start(s32[1,2048]{1,0:T(1,128)} %copy-done.3) | copy-start | bytes 24580
  649.6 1.2 copy-start.11
  650.8 1.2 copy-start.13
  681.3 1.6 copy-start.12
  683.0 129.7 %copy-start.16 = (bf16[256,2048]{1,0:T(8,128)(2,1)S(1)}, bf16[256,2048]{1,0:T(8,128)(2,1)}, u32[]{:S(2)}) copy-start(bf16[256,2048]{1,0:T(8,128)(2,1)} %reduce-scatter.6.cloned.1.call-done) | copy-start | bytes 3145732
  683.0 131.3 %copy-start.15 = (bf16[256,2048]{1,0:T(8,128)(2,1)S(1)}, bf16[256,2048]{1,0:T(8,128)(2,1)}, u32[]{:S(2)}) copy-start(bf16[256,2048]{1,0:T(8,128)(2,1)} %reduce-scatter.4.cloned.1.call-done) | copy-start | bytes 3145732
  808.6 9.6 %copy-start.18 = (bf16[1024,512]{1,0:T(8,128)(2,1)S(1)}, bf16[1024,512]{1,0:T(8,128)(2,1)}, u32[]{:S(2)}) copy-start(bf16[1024,512]{1,0:T(8,128)(2,1)} %get-tuple-element.129) | copy-start | bytes 3145732
  814.2 6.8 copy-start.20
  814.2 7.6 copy-start.19
Sparse Core Ops, SparseCore 0:
  484.3 76.0 reduce-scatter.3
  564.3 77.3 reduce-scatter.5
  683.1 54.2 reduce-scatter.7

commit v7 on v6

--- a/solution.py
+++ b/solution.py
@@ -228,6 +228,23 @@
     return low[None], high[None], first, last
 
 
+def document_bounds(ids, first_id):
+    rows = ids.shape[0]
+    second = jnp.sum(ids <= first_id, dtype=jnp.int32)
+    third = jnp.sum(ids <= first_id + 1, dtype=jnp.int32)
+
+    def bounds_at(places):
+        start = jnp.where(places < second, 0, jnp.where(places < third, second, third))
+        stop = jnp.where(places < second, second, jnp.where(places < third, third, rows))
+        return jnp.maximum(start, places - WIN), jnp.minimum(stop - 1, places + WIN)
+
+    low, high = bounds_at(jnp.arange(rows, dtype=jnp.int32))
+    starts = jnp.arange(0, rows, QB, dtype=jnp.int32)
+    first = bounds_at(starts)[0] // KB
+    last = bounds_at(starts + (QB - 1))[1] // KB + 1
+    return low[None], high[None], first, last
+
+
 def padded(block, width):
     count = lax.axis_size("ctx")
     forward = [(i, i + 1) for i in range(count - 1)]
@@ -256,7 +273,7 @@
 
 
 MESH = pl.DeviceIdType.MESH
-PIECES = 4
+PIECES = 8
 TILE = 512
 
 
@@ -366,12 +383,12 @@
                 self.sum_slots[piece, owner] = term(owner).astype(jnp.bfloat16)
                 self.sum_copy(piece, owner).start()
 
-    def sum_onward(self, piece, term):
+    def sum_onward(self, piece, term, distances):
         me, count = self.me, self.count
 
         @pl.when((me > 0) & (me < count - 1))
         def _():
-            for distance in range(count - 2, 0, -1):
+            for distance in distances:
 
                 def pass_on(owner):
                     self.sum_arrival(piece, owner)
@@ -667,10 +684,11 @@
 
 
 def enter_kernel(
-    count, x_ref, marks_ref, query_ref, key_ref, value_ref, output_ref, bias,
-    wide, marks_out, weight, output_weight, heads,
+    count, x_ref, marks_ref, query_ref, key_ref, value_ref, output_ref, expand_ref, bias,
+    wide, marks_out, weight, output_weight, expand_weight, heads,
     mark_slots, stage, sent, got, marks_sent, marks_got,
-    weight_sent, weight_got, output_sent, output_got, swap_sent, swap_got,
+    weight_sent, weight_got, output_sent, output_got, expand_sent, expand_got,
+    swap_sent, swap_got, put_done,
 ):
     me, ctx = lax.axis_index("tp"), lax.axis_index("ctx")
     rows, width = x_ref.shape
@@ -685,13 +703,26 @@
         return wide.at[piece_rows(piece), pl.ds(pl.multiple_of(owner * width, width), width)]
 
     gather = PlaneGather(weight, weight_sent, weight_got)
+    output_gather = PlaneGather(output_weight, output_sent, output_got)
+    expand_gather = PlaneGather(expand_weight, expand_sent, expand_got)
     own_shard = gather.shard(gather.fsdp, ctx)
-    for side in range(2):
-        for i, ref in enumerate((query_ref, key_ref, value_ref)):
-            start = side * part + i * half
-            own_shard[:, start : start + half] = ref[:, side * half : (side + 1) * half]
-    output_gather = PlaneGather(output_weight, output_sent, output_got)
-    output_gather.shard(gather.fsdp, ctx)[...] = output_ref[...]
+    own = pl.ds(pl.multiple_of(me * width, width), width)
+    puts = [
+        (ref.at[:, pl.ds(side * half, half)], own_shard.at[:, pl.ds(side * part + i * half, half)])
+        for side in range(2)
+        for i, ref in enumerate((query_ref, key_ref, value_ref))
+    ]
+    puts += [
+        (output_ref, output_gather.shard(gather.fsdp, ctx)),
+        (x_ref, wide.at[:, own]),
+        (expand_ref, expand_gather.shard(gather.fsdp, ctx)),
+    ]
+    puts = [
+        pltpu.make_async_copy(source, place, put_done.at[i])
+        for i, (source, place) in enumerate(puts)
+    ]
+    for put in puts:
+        put.start()
     line = Line(me, count, None, None, None, view, sent, got)
     tp_peers = peers_along_tp(me, count)
     greet_peers(tp_peers + gather.peers())
@@ -703,15 +734,17 @@
     def _(piece):
         line.spread_start(piece, source(piece))
 
+    for put in puts[:7]:
+        put.wait()
     gather.first()
     output_gather.first()
     marks = Exchange(
         tp_peers, marks_sent, marks_got, lambda _: marks_ref, lambda i: mark_slots.at[i]
     )
     marks.start()
-    own = pl.ds(pl.multiple_of(me * width, width), width)
-    wide[:, own] = x_ref[...]
     marks_out[:, own] = marks_ref[...]
+    for put in puts[7:]:
+        put.wait()
     swap = Swap(
         swap_sent, swap_got,
         lambda piece: stage.at[piece_rows(piece)],
@@ -739,10 +772,12 @@
                 products(piece, 1 - ctx, stage.at[piece_rows(piece)])
                 swap.start(piece)
                 products(piece, ctx, heads.at[piece_rows(piece, ctx * rows)])
+                pl.when(piece == PIECES // 2)(expand_gather.second)
 
         if distance == 1:
             gather.second()
             output_gather.second()
+            expand_gather.first()
         if distance == count - 2:
             gather.third()
             output_gather.third()
@@ -757,15 +792,19 @@
         swap.wait_arrival(piece)
         swap.wait_sent(piece)
 
+    expand_gather.third()
     output_gather.last()
+    expand_gather.last()
     marks.wait_sent()
     gather.wait_sent()
     output_gather.wait_sent()
+    expand_gather.wait_sent()
     line.spread_finish(PIECES, source)
 
 
 def enter(
-    tokens, marks, query_weight, key_weight, value_weight, output_weight, bias, collective_id
+    tokens, marks, query_weight, key_weight, value_weight, output_weight, expand_weight, bias,
+    collective_id,
 ):
     count = lax.axis_size("tp")
     rows, width = tokens.shape
@@ -781,19 +820,32 @@
             jax.ShapeDtypeStruct(
                 (plane * output_weight.shape[0], output_weight.shape[1]), output_weight.dtype
             ),
+            jax.ShapeDtypeStruct(
+                (plane * expand_weight.shape[0], expand_weight.shape[1]), expand_weight.dtype
+            ),
             jax.ShapeDtypeStruct((2 * rows, part), jnp.bfloat16),
         ],
-        in_specs=[pl.BlockSpec(memory_space=pltpu.VMEM)] * 7,
-        out_specs=[pl.BlockSpec(memory_space=pltpu.VMEM)] * 5,
+        in_specs=[
+            pl.BlockSpec(memory_space=pl.ANY),
+            pl.BlockSpec(memory_space=pltpu.VMEM),
+            *[pl.BlockSpec(memory_space=pl.ANY)] * 5,
+            pl.BlockSpec(memory_space=pltpu.VMEM),
+        ],
+        out_specs=[
+            *[pl.BlockSpec(memory_space=pltpu.VMEM)] * 4,
+            pl.BlockSpec(memory_space=pl.ANY),
+            pl.BlockSpec(memory_space=pltpu.VMEM),
+        ],
         scratch_shapes=[
             pltpu.VMEM((count - 1, *marks.shape), marks.dtype),
             pltpu.VMEM((rows, part), jnp.bfloat16),
             *line_semaphores(count, PIECES)[1],
             pltpu.SemaphoreType.DMA((count - 1,)),
             pltpu.SemaphoreType.DMA((count - 1,)),
-            *[pltpu.SemaphoreType.DMA((9,))] * 4,
+            *[pltpu.SemaphoreType.DMA((9,))] * 6,
             pltpu.SemaphoreType.DMA((PIECES,)),
             pltpu.SemaphoreType.DMA((PIECES,)),
+            pltpu.SemaphoreType.DMA((9,)),
         ],
         compiler_params=pltpu.CompilerParams(
             collective_id=collective_id, has_side_effects=True, vmem_limit_bytes=40 << 20
@@ -802,11 +854,11 @@
             flops=80_000_000_000, bytes_accessed=64 * rows * count * width, transcendentals=0
         ),
         name="enter",
-    )(tokens, marks, query_weight, key_weight, value_weight, output_weight, bias)
+    )(tokens, marks, query_weight, key_weight, value_weight, output_weight, expand_weight, bias)
 
 
 def relay_kernel(count, row_step, use_step, sizes, *refs):
-    row_in, use_in, row_out, use_out, shared, swap_in, swap_out, gathers = sizes
+    row_in, use_in, row_out, use_out, shared, swap_in, swap_out, next_shard = sizes
     refs = list(refs)
 
     def take(number):
@@ -817,14 +869,11 @@
     x_ref, sum_weight = take(2)
     use_weight = sum_weight if shared else take(1)[0]
     row_inputs, use_inputs = take(row_in), take(use_in)
+    next_ref = take(1)[0] if next_shard else None
     (gathered,) = take(1)
     row_outputs, use_outputs = take(row_out), take(use_out)
     swapped = take(1)[0] if swap_in or swap_out else None
-    if gathers:
-        shards = [use_weight, *use_inputs[-1:]]
-        use_inputs = use_inputs[:-1]
-        wholes = take(2)
-        use_weight = wholes[0]
+    next_whole = take(1)[0] if next_shard else None
     terms, total, slots, sum_sent, sum_got, spread_sent, spread_got = take(7)
     me, ctx = lax.axis_index("tp"), lax.axis_index("ctx")
     rows = gathered.shape[0]
@@ -839,15 +888,10 @@
         return gathered.at[pl.ds(pl.multiple_of(piece * height + owner * own, own), own)]
 
     line = Line(me, count, slots, sum_sent, sum_got, view, spread_sent, spread_got)
-    use_gather = next_gather = None
-    if gathers:
-        use_gather, next_gather = (
-            PlaneGather(whole, *take(2)) for whole in wholes
-        )
-        greet(me, count, use_gather.peers())
-        use_gather.put(shards[0], take(1)[0])
-        next_gather.put(shards[1], take(1)[0])
-        use_gather.first()
+    next_gather = None
+    if next_shard:
+        next_gather = PlaneGather(next_whole, *take(2))
+        greet(me, count, next_gather.peers())
     else:
         greet(me, count, [{"ctx": 1 - ctx}] if swap_in or swap_out else [])
     swap = None
@@ -855,7 +899,7 @@
         half = x_ref.shape[1]
         own_half = pl.ds(pl.multiple_of(ctx * half, half), half)
         swap = Swap(
-            *refs,
+            *take(2),
             lambda piece: x_ref.at[piece_rows(piece, (1 - ctx) * rows)],
             lambda piece: swapped.at[piece_rows(piece), own_half],
         )
@@ -865,8 +909,11 @@
             swap.start(piece)
             swapped[piece_rows(piece), own_half] = x_ref[piece_rows(piece, ctx * rows), :]
 
+    if next_gather is not None:
+        next_gather.put(next_ref, take(1)[0])
+        next_gather.first()
     if swap_out:
-        stage, swap_sent, swap_got = refs
+        stage, swap_sent, swap_got = take(3)
         half = swapped.shape[1]
         swap = Swap(
             swap_sent, swap_got,
@@ -874,70 +921,19 @@
             lambda piece: swapped.at[piece_rows(piece, ctx * rows)],
         )
 
-    @pl.loop(0, PIECES + 2)
+    @pl.loop(0, PIECES + 5)
     def _(step):
         odd = lax.rem(step, 2)
 
-        def term(owner):
-            return terms[odd, pl.ds(pl.multiple_of(owner * own, own), own), :]
-
-        @pl.when(step < PIECES)
-        def _():
-            if swap_in:
-                swap.wait_arrival(step)
-            x = (swapped if swap_in else x_ref)[piece_rows(step), :]
-
-            @pl.loop(0, width // TILE)
-            def _(tile):
-                part = pl.ds(pl.multiple_of(tile * TILE, TILE), TILE)
-                terms[odd, :, part] = dot_cols(x, sum_weight[part, :])
-
-            line.sum_start(step, term)
-
-        @pl.when((step >= 1) & (step <= PIECES))
-        def _():
-            piece = step - 1
-            total[...] = terms[1 - odd, pl.ds(pl.multiple_of(me * own, own), own), :]
-            line.sum_end(piece, total)
-            view(piece, me)[...] = row_step(piece, total, row_inputs, row_outputs)
-            line.spread_start(piece)
-
-        @pl.when(step >= 2)
-        def _():
-            for distance in range(2, count):
-                line.spread_onward(step - 2, distance)
-
-        @pl.when(step < PIECES)
-        def _():
-            line.sum_onward(step, term)
-
-        @pl.when((step >= 1) & (step <= PIECES))
-        def _():
-            line.spread_onward(step - 1, 1)
-
-        if gathers:
-
-            @pl.when(step == 1)
+        def term_of(parity):
+            return lambda owner: terms[parity, pl.ds(pl.multiple_of(owner * own, own), own), :]
+
+        def late(pieces, action):
+            @pl.when((step >= pieces) & (step < PIECES + pieces))
             def _():
-                use_gather.second()
-                next_gather.first()
-
-            @pl.when(step == 2)
-            def _():
-                use_gather.third()
-                use_gather.last()
-
-            @pl.when(step == 3)
-            def _():
-                next_gather.second()
-
-            @pl.when(step == 4)
-            def _():
-                next_gather.third()
-
-        @pl.when(step >= 2)
-        def _():
-            piece = step - 2
+                action(step - pieces)
+
+        def use(piece):
             part = piece_rows(piece)
             result = use_step(part, gathered[part, :], use_weight, use_inputs, use_outputs)
             if swap_out:
@@ -947,6 +943,40 @@
                 swap.start(piece)
                 swapped[piece_rows(piece, ctx * rows), :] = jnp.where(here, left, right)
 
+        def form(piece):
+            if swap_in:
+                swap.wait_arrival(piece)
+            x = (swapped if swap_in else x_ref)[piece_rows(piece), :]
+
+            @pl.loop(0, width // TILE)
+            def _(tile):
+                part = pl.ds(pl.multiple_of(tile * TILE, TILE), TILE)
+                terms[odd, :, part] = dot_cols(x, sum_weight[part, :])
+
+            line.sum_start(piece, term_of(odd))
+
+        def own_step(piece):
+            total[...] = terms[1 - odd, pl.ds(pl.multiple_of(me * own, own), own), :]
+            line.sum_end(piece, total)
+            view(piece, me)[...] = row_step(piece, total, row_inputs, row_outputs)
+            line.spread_start(piece)
+
+        def far_shards(piece):
+            for distance in range(3, count):
+                line.spread_onward(piece, distance)
+
+        late(5, use)
+        late(3, lambda piece: line.spread_onward(piece, 2))
+        late(1, lambda piece: line.sum_onward(piece, term_of(1 - odd), [1]))
+        late(0, form)
+        late(4, far_shards)
+        late(2, lambda piece: line.spread_onward(piece, 1))
+        late(0, lambda piece: line.sum_onward(piece, term_of(odd), range(count - 2, 1, -1)))
+        late(1, own_step)
+        if next_gather is not None:
+            pl.when(step == 4)(next_gather.second)
+            pl.when(step == 6)(next_gather.third)
+
     if swap is not None:
 
         @pl.loop(0, PIECES)
@@ -955,9 +985,8 @@
                 swap.wait_arrival(piece)
             swap.wait_sent(piece)
 
-    if gathers:
+    if next_gather is not None:
         next_gather.last()
-        use_gather.wait_sent()
         next_gather.wait_sent()
     line.sum_finish(PIECES)
     line.spread_finish(PIECES)
@@ -972,21 +1001,20 @@
     height = rows // PIECES
     own = height // count
     shared = use_weight is None
-    gathers = next_shard is not None
-    if gathers:
-        use_inputs = [*use_inputs, next_shard]
     operands = [x, sum_weight, *([] if shared else [use_weight]), *row_inputs, *use_inputs]
     in_specs = [pl.BlockSpec(memory_space=pltpu.VMEM)] * len(operands)
     shapes = [jax.ShapeDtypeStruct((rows, width), jnp.bfloat16), *row_shapes, *use_shapes]
     shapes += [shape for shape in (swap_in, swap_out) if shape is not None]
     out_specs = [pl.BlockSpec(memory_space=pltpu.VMEM)] * len(shapes)
-    extra = []
-    if gathers:
-        for shard, space in ((use_weight, pltpu.VMEM), (next_shard, pl.ANY)):
-            whole = (8 * shard.shape[0], shard.shape[1])
-            shapes.append(jax.ShapeDtypeStruct(whole, shard.dtype))
-            out_specs.append(pl.BlockSpec(memory_space=space))
-        extra = [pltpu.SemaphoreType.DMA((9,))] * 4 + [pltpu.SemaphoreType.DMA] * 2
+    extra, last = [], []
+    if next_shard is not None:
+        operands.append(next_shard)
+        in_specs.append(pl.BlockSpec(memory_space=pl.ANY))
+        whole = (8 * next_shard.shape[0], next_shard.shape[1])
+        shapes.append(jax.ShapeDtypeStruct(whole, next_shard.dtype))
+        out_specs.append(pl.BlockSpec(memory_space=pl.ANY))
+        extra = [pltpu.SemaphoreType.DMA((9,))] * 2
+        last = [pltpu.SemaphoreType.DMA]
     sums, spreads = line_semaphores(count, PIECES)
     swaps = []
     if swap_out is not None:
@@ -995,7 +1023,7 @@
         swaps += [pltpu.SemaphoreType.DMA((PIECES,))] * 2
     sizes = (
         len(row_inputs), len(use_inputs), len(row_shapes), len(use_shapes), shared,
-        swap_in is not None, swap_out is not None, gathers,
+        swap_in is not None, swap_out is not None, next_shard is not None,
     )
     return pl.pallas_call(
         functools.partial(relay_kernel, count, row_step, use_step, sizes),
@@ -1010,6 +1038,7 @@
             *spreads,
             *extra,
             *swaps,
+            *last,
         ],
         compiler_params=pltpu.CompilerParams(
             collective_id=collective_id, has_side_effects=True, vmem_limit_bytes=60 << 20
@@ -1065,8 +1094,12 @@
     mixed, grad_second, sums = outputs
     part = own_rows_of(piece, first_norm)
     normed, inverse = norm_parts(first_norm[part, :] + total[...] + biases[2:3, :])
-    mixed[part, :] = (normed * gains[1:2, :] + biases[3:4, :]).astype(jnp.bfloat16)
-    upstream = out_grad[part, :].astype(jnp.float32)
+    result = (normed * gains[1:2, :] + biases[3:4, :]).astype(jnp.bfloat16)
+    count, _, width = mixed.shape
+    for i in range(count):
+        mixed[i, part, :] = result[:, i * width : (i + 1) * width]
+    upstream = jnp.concatenate([out_grad[i, part, :] for i in range(count)], axis=1)
+    upstream = upstream.astype(jnp.float32)
     grad = norm_back(upstream, normed, inverse, gains[1:2, :])
     grad_second[part, :] = grad
     low = grad.astype(jnp.bfloat16)
@@ -1132,7 +1165,7 @@
 def input_kernel(
     sizes, x_ref, weight, inner_ref, rows_ref, hidden_ref, out_ref, vectors_ref,
     term_ref, total, slots, own_vectors, tp_slots, plane_slots,
-    sum_sent, sum_got, tp_sent, tp_got, plane_sent, plane_got, hooks=None, pack_step=1,
+    sum_sent, sum_got, tp_sent, tp_got, plane_sent, plane_got, hooks=None,
 ):
     count = sizes[2]
     me = lax.axis_index("tp")
@@ -1185,27 +1218,23 @@
             own_vectors[place : place + 1, :] = jnp.sum(part, axis=0, keepdims=True)
         over_plane.start()
 
-    @pl.loop(0, PIECES + 1)
-    def _(step):
-        @pl.when(step < PIECES)
-        def _():
-            before(step)
-            line.sum_start(step, terms(step))
-            line.sum_onward(step, terms(step))
-
-        pl.when(step == pack_step)(pack)
-
-        @pl.when(step >= 1)
-        def _():
-            piece = step - 1
-            total[...] = terms(piece)(me)
-            line.sum_end(piece, total)
-            rows = pl.ds(pl.multiple_of(piece * height, height), height)
-            out_ref[rows, :] = total[...].astype(out_ref.dtype)
-
-        after(step)
-
+    @pl.loop(0, PIECES)
+    def _(piece):
+        before(piece)
+        line.sum_start(piece, terms(piece))
+        line.sum_onward(piece, terms(piece), range(count - 2, 0, -1))
+        after(piece)
+
+    pack()
     closing()
+
+    @pl.loop(0, PIECES)
+    def _(piece):
+        total[...] = terms(piece)(me)
+        line.sum_end(piece, total)
+        rows = pl.ds(pl.multiple_of(piece * height, height), height)
+        out_ref[rows, :] = total[...].astype(out_ref.dtype)
+
     over_plane.wait_arrivals()
     vectors_ref[...] = own_vectors[...]
     for i in range(len(plane_peers)):
@@ -1397,26 +1426,31 @@
 
         x_ref[:, own_columns] = grads_ref[pl.ds(pl.multiple_of(ctx * rows, rows), rows), :]
 
-    def before(step):
-        @pl.when(step < PIECES - 1)
+    middle = PIECES // 2
+
+    def before(piece):
+        @pl.when(piece <= middle)
         def _():
-            swap.wait_arrival(step)
-
-    def after(step):
-        @pl.when(step == PIECES - 2)
+            swap.wait_arrival(piece)
+
+    def products(fsdp):
+        for over_x in (1, 0):
+            for over_y in (1, 0):
+                product(plane_sum.number(fsdp, over_x, over_y))
+
+    def after(piece):
+        @pl.when(piece == middle)
         def _():
-            swap.wait_arrival(PIECES - 1)
-            for over_x in (1, 0):
-                for over_y in (1, 0):
-                    product(plane_sum.number(plane_sum.twin, over_x, over_y))
+            for other in range(middle + 1, PIECES):
+                swap.wait_arrival(other)
+            products(plane_sum.twin)
             plane_sum.start()
 
-        @pl.when(step == PIECES - 1)
+        @pl.when(piece == middle + 1)
         def _():
-            for over_x in (1, 0):
-                for over_y in (1, 0):
-                    product(plane_sum.number(plane_sum.fsdp, over_x, over_y))
-            plane_sum.second()
+            products(plane_sum.fsdp)
+
+        pl.when(piece == middle + 2)(plane_sum.second)
 
     def closing():
         plane_sum.third()
@@ -1425,7 +1459,7 @@
         sizes, x_ref, weight, inner_ref, rows_ref, hidden_ref, out_ref, vectors_ref,
         term_ref, total, slots, own_vectors, tp_slots, plane_slots,
         sum_sent, sum_got, tp_sent, tp_got, plane_sent, plane_got,
-        hooks=(opening, before, after, closing), pack_step=PIECES - 1,
+        hooks=(opening, before, after, closing),
     )
     halves = plane_sum.finish()
     third = part // 3
@@ -1495,17 +1529,16 @@
 def spread_own(block):
     count = lax.axis_size("tp")
     rows, width = block.shape
-    parts = block.reshape(PIECES, count, -1, width)
-    got = lax.all_to_all(parts, "tp", split_axis=1, concat_axis=1, tiled=True)
-    return got.transpose(0, 2, 1, 3).reshape(rows // count, count * width)
-
-
-def unspread_own(block):
-    count = lax.axis_size("tp")
-    rows, width = block.shape
-    parts = block.reshape(PIECES, -1, count, width // count).transpose(0, 2, 1, 3)
-    got = lax.all_to_all(parts, "tp", split_axis=1, concat_axis=1, tiled=True)
-    return got.reshape(rows * count, width // count)
+    parts = block.reshape(PIECES, count, -1, width).transpose(1, 0, 2, 3)
+    return lax.all_to_all(
+        parts.reshape(count, -1, width), "tp", split_axis=0, concat_axis=0, tiled=True
+    )
+
+
+def unspread_own(parts):
+    count, own_rows, width = parts.shape
+    got = lax.all_to_all(parts, "tp", split_axis=0, concat_axis=0, tiled=True)
+    return got.reshape(count, PIECES, -1, width).transpose(1, 0, 2, 3).reshape(-1, width)
 
 
 def body(
@@ -1542,8 +1575,9 @@
     qkv_bias = qkv_bias.astype(jnp.float32)
     if by_heads:
         half_bias = qkv_bias.reshape(3, 2, -1).transpose(1, 0, 2).reshape(1, -1)
-        wide_tokens, wide_marks, wide_qkv, full_output, qkv_heads = enter(
-            tokens, marks, query_weight, key_weight, value_weight, output_weight, half_bias, 0
+        wide_tokens, wide_marks, wide_qkv, full_output, full_expand, qkv_heads = enter(
+            tokens, marks, query_weight, key_weight, value_weight, output_weight, expand_weight,
+            half_bias, 0,
         )
         queries = keys = values = qkv_heads
         own_heads = heads // 2
@@ -1551,7 +1585,7 @@
         stream_ids = lax.dynamic_slice_in_dim(
             segments, lax.axis_index("fsdp") * stream_rows, stream_rows, 0
         )
-        bounds = key_bounds(stream_ids, stream_ids, 0)
+        bounds = document_bounds(stream_ids, 3 * lax.axis_index("fsdp"))
     else:
         wide_qkv = weight_rows(jnp.concatenate([query_weight, key_weight, value_weight], axis=1))
         wide_tokens, wide_marks = gather_features(tokens, marks, 0)
@@ -1566,7 +1600,7 @@
                 jnp.full((WIN,), jnp.iinfo(jnp.int32).max, jnp.int32),
             ]
         )
-        full_output = weight_rows(output_weight)
+        full_output, full_expand = weight_rows(output_weight), weight_rows(expand_weight)
         key_ids = lax.dynamic_slice_in_dim(ids, block_index * rows, rows + 2 * WIN, 0)
         bounds = key_bounds(key_ids[WIN : WIN + rows], key_ids, WIN)
     places = (0, own_heads, 2 * own_heads) if by_heads else (0, 0, 0)
@@ -1586,7 +1620,7 @@
 
     own_shape = shape((own_rows, features))
     norm_low, first_norm, normed_one, inverse_one, hidden, activated, *more = relay(
-        attended_heads, full_output, expand_weight if by_heads else weight_rows(expand_weight),
+        attended_heads, full_output, full_expand,
         [own_tokens, gains, biases], first_norm_step,
         [own_shape, own_shape, shape((own_rows, 128))],
         [hidden_bias.astype(jnp.float32)[None]], expand_step,
@@ -1596,19 +1630,17 @@
         next_shard=shrink_weight if by_heads else None,
     )
     if by_heads:
-        attended, full_expand, full_shrink = more
+        attended, full_shrink = more
     else:
-        attended = attended_heads
-        full_expand, full_shrink = weight_rows(expand_weight), weight_rows(shrink_weight)
+        attended, full_shrink = attended_heads, weight_rows(shrink_weight)
     ffn_low, mixed_own, grad_second, second_sums, hidden_low, hidden_sums = relay(
         activated, full_shrink, None,
         [first_norm, upstream, gains, biases], second_norm_step,
-        [shape((own_rows, features), jnp.bfloat16), own_shape, shape((8, features))],
+        [shape(upstream.shape, jnp.bfloat16), own_shape, shape((8, features))],
         [hidden], shrink_step,
         [shape((rows, hidden_cols), jnp.bfloat16), shape((8, hidden_cols))],
         2, "second_norm", rows,
     )
-    mixed = unspread_own(mixed_own)
 
     def owner_sum(grad):
         return lax.psum_scatter(
@@ -1633,20 +1665,24 @@
         3, "first_back", rows,
         swap_out=shape((2 * rows, head_cols // 2), jnp.bfloat16) if by_heads else None,
     )
-    attended_grad, shrink_grad, output_part = lax.optimization_barrier(
+    attended_grad, mixed_own, shrink_grad, output_part = lax.optimization_barrier(
         (
             attended_grad,
+            mixed_own,
             shrink_grad,
             dot_rows(branch_low, attended).astype(jnp.bfloat16),
         )
     )
     output_grad = owner_sum(output_part)
+    mixed = unspread_own(mixed_own)
 
     if by_heads:
         (grads,) = attend_back(
             queries, keys, values, attended_heads, attended_grad, lse, *bounds, places, True
         )
-        grads, mixed, expand_grad = lax.optimization_barrier((grads, mixed, expand_grad))
+        grads, mixed, expand_grad, output_grad = lax.optimization_barrier(
+            (grads, mixed, expand_grad, output_grad)
+        )
     else:
         query_low, key_ext, value_ext = attend_back(
             queries, keys, values, attended_heads, attended_grad, lse, *bounds

time: 840 us -> 808 us (0.962); the launches traced: 830 us -> 808 us
  Pallas kernels: 705 us -> 692 us
  waiting for transfers between devices: 0.53 us -> 10.4 us
  starting transfers between devices: 20.8 us -> 11.5 us
  local copies, waits for them, and re-layouts: 42.8 us -> 34.1 us
    pallas_call x3, Pallas kernels: 435 us -> 409 us  [relay(): pl.pallas_call(functools.partial(relay_kernel, count, row_step, use_step,...]
    pallas_call x1, Pallas kernels: 91.8 us -> 114 us  [enter(): pl.pallas_call(functools.partial(enter_kernel, count), out_shape=[jax.Sha...]
    pallas_call x1, Pallas kernels: 126 us -> 109 us  [leave(): pl.pallas_call(functools.partial(leave_kernel, sizes), out_shape=[jax.Sha...]
    reduce_scatter x3, waiting for transfers between devices: 0.01 us -> 9.66 us  [owner_sum(): return lax.psum_scatter(grad, plane, scatter_dimension=0, tiled=True)]
    all_to_all x2, starting transfers between devices: 20.5 us -> 11.4 us  [the longest x1 7.02 us: unspread_own(): got = lax.all_to_all(parts, 'tp', split_axis=0, concat_axis=0, tiled=True)]
    unnamed x50 -> x53, local copies, waits for them, and re-layouts: 19.6 us -> 18.6 us
  transfers between devices with their start and end apart: 5 -> 5, of which waited for: 0 -> 1; matrix products, arithmetic and copies ran while one was open for 4% -> 3% of each run, Pallas kernels for 38% -> 23%
where the time goes in v7:
time: 808 us
  Pallas kernels  692 us (86%)
  matrix products  34.4 us (4%)
  local copies, waits for them, and re-layouts  34.1 us (4%)
  between operations  14 us (2%)
  other arithmetic  11.9 us (1%)
  starting transfers between devices  11.5 us (1%)
  waiting for transfers between devices  10.4 us (1%)
    pallas_call x3, Pallas kernels, relay(): pl.pallas_call(functools.partial(relay_kernel, count, row_step, use_step,...  409 us
    pallas_call x1, Pallas kernels, enter(): pl.pallas_call(functools.partial(enter_kernel, count), out_shape=[jax.Sha...  114 us
    pallas_call x1, Pallas kernels, leave(): pl.pallas_call(functools.partial(leave_kernel, sizes), out_shape=[jax.Sha...  109 us
    dot_general x3, matrix products, dot_rows(): lax.dot_general(left, right, (((0,), (0,)), ((), ())), preferred_element_...  34.4 us
    pallas_call x1, Pallas kernels, attend_back(): pl.pallas_call(attend_back_kernel, out_shape=[jax.ShapeDtypeStruct((rows,...  33.3 us
    pallas_call x1, Pallas kernels, attend(): pl.pallas_call(attend_kernel, out_shape=(jax.ShapeDtypeStruct((rows, widt...  26.5 us
    unnamed x53, local copies, waits for them, and re-layouts  18.6 us
  transfers between devices with their start and end apart: 5, of which 1 were waited for; matrix products, arithmetic and copies ran while one was open for 3% of the time, Pallas kernels for 23%

profile of v7, /device:TPU:8, one launch (start us, length us, event | category | flops | bytes accessed | tf_op | source)
XLA Modules:
  0.0 808.2 jit_solution(8802123028411966510)
XLA Ops:
  7.2 0.7 stack.10
  8.8 0.8 maximum_maximum_fusion.marks_ref
  9.6 1.2 copy-done.5
  10.8 1.2 copy-done.6
  12.1 0.9 copy-done.7
  13.0 0.9 copy-done.8
  14.0 0.9 copy-done.9
  14.9 0.9 copy-done.10
  15.9 114.3 %enter.1 = (bf16[1024,2048]{1,0:T(8,128)(2,1)S(1)}, bf16[16,2048]{1,0:T(8,128)(2,1)S(1)}, bf16[2048,1536]{1,0:T(8,128)(2,1)}, bf16[2048,512]{1,0:T(8,128)(2,1)S(...) custom-call(bf16[1024,512]{1,0:T(8,128)(2,1)S(1)} %copy-done.5, ...), custom_call_target="tpu_custom_call" | custom-call | flops 80000000000 | bytes 134217728 | tf_op jit(solution)/shard_map/enter/pallas_call | solution.py:814
  130.1 2.0 copy-done
  132.1 1.3 copy-done.15
  133.4 1.1 copy.31
  134.5 4.4 all-to-all-start
  138.9 1.3 convert_reduce_fusion.1
  140.2 1.3 fusion
  142.2 1.3 and_select_fusion.1
  143.5 2.3 constant_dynamic-slice_fusion
  145.8 26.5 %attend.1 = (bf16[2048,256]{1,0:T(8,128)(2,1)S(1)}, f32[2,1,2048]{2,1,0:T(1,128)S(1)}) custom-call(s32[4]{0:T(128)S(1)} %get-tuple-element.117.first, s32[4]{0:T(128)S(1)} %get-tuple-element.118.last, bf16[2048,768]{1,0:T(8,128)(2,1)S(1)} %get-tuple-element.58.q_ref.k_ref.v_ref, bf16[2048,768]{1,0:T(8,128)(2,1)S(1)} %get-tuple-element.58.q_ref.k_ref.v_ref, ...), custom_call_target="tpu_custom_call" | custom-call | flops 3221225472 | bytes 4194304 | tf_op jit(solution)/shard_map/attend/pallas_call | solution.py:81
  172.3 1.0 copy-done.11
  174.5 156.3 %first_norm.1 = (bf16[1024,2048]{1,0:T(8,128)(2,1)}, f32[256,2048]{1,0:T(8,128)}, f32[256,2048]{1,0:T(8,128)}, f32[256,128]{1,0:T(8,128)}, f32[1024,2048]{1,0:T(...) custom-call(bf16[2048,256]{1,0:T(8,128)(2,1)} %copy-done.11, ...), custom_call_target="tpu_custom_call" | custom-call | flops 99999997952 | bytes 134217728 | tf_op jit(solution)/shard_map/first_norm/pallas_call | solution.py:1028
  330.9 125.3 %second_norm.1 = (bf16[1024,2048]{1,0:T(8,128)(2,1)}, bf16[4,256,512]{2,1,0:T(8,128)(2,1)}, f32[256,2048]{1,0:T(8,128)}, f32[8,2048]{1,0:T(8,128)}, bf16[1024,2048]{1,0:T(8,128)(2,1)}, /*index=5*/f32[8,2048]{1,0:T(8,128)}) custom-call(bf16[1024,2048]{1,0:T(8,128)(2,1)} %get-tuple-element.66.refs_0_, bf16[2048,2048]{1,0:T(8,128)(2,1)} %get-tuple-element.67.refs_1_, ...), custom_call_target="tpu_custom_call" | custom-call | flops 99999997952 | bytes 134217728 | tf_op jit(solution)/shard_map/second_norm/pallas_call | solution.py:1028
  456.2 14.1 %convolution_convert_fusion.1 = bf16[2048,2048]{1,0:T(8,128)(2,1)} fusion(bf16[1024,2048]{1,0:T(8,128)(2,1)} %get-tuple-element.72, bf16[1024,2048]{1,0:T(8,128)(2,1)} %get-tuple-element.66.refs_0_), kind=kOutput, calls=%fused_computation.1 | convolution fusion | flops 8594128896 | bytes 16777216 | tf_op jit(solution)/shard_map/dot_general | solution.py:27
  470.3 14.0 %convolution_convert_fusion = bf16[2048,2048]{1,0:T(8,128)(2,1)} fusion(bf16[1024,2048]{1,0:T(8,128)(2,1)} %get-tuple-element.73, bf16[1024,2048]{1,0:T(8,128)(2,1)} %get-tuple-element.74.refs_0_), kind=kOutput, calls=%fused_computation | convolution fusion | flops 8594128896 | bytes 16777216 | tf_op jit(solution)/shard_map/dot_general | solution.py:27
  484.4 0.7 reduce-scatter.6.cloned.1.call-update
  485.1 127.9 %first_back.1 = (bf16[1024,2048]{1,0:T(8,128)(2,1)}, f32[256,2048]{1,0:T(8,128)}, f32[8,2048]{1,0:T(8,128)}, bf16[2048,256]{1,0:T(8,128)(2,1)}) custom-call(bf16[1024,2048]{1,0:T(8,128)(2,1)} %get-tuple-element.74.refs_0_, bf16[2048,2048]{1,0:T(8,128)(2,1)} %get-tuple-element.64.refs_2_.refs_1_, bf16[2048,512]{1,0:T(8,128)(2,1)} %copy-done.15, ...), custom_call_target="tpu_custom_call" | custom-call | flops 99999997952 | bytes 134217728 | tf_op jit(solution)/shard_map/first_back/pallas_call | solution.py:1028
  613.0 6.3 convolution_convert_fusion.2
  619.3 1.4 slice.53.hidden_ref
  620.7 7.0 all-to-all-start.1
  627.8 1.0 fusion.8
  628.7 1.0 fusion.7
  629.7 0.7 concatenate.8.rows_ref
  630.4 2.8 convert_element_type.42
  633.2 1.2 copy-done.12
  634.5 1.3 copy-done.14
  635.7 33.3 %attend_back.1.grads_ref = bf16[2048,768]{1,0:T(8,128)(2,1)S(1)} custom-call(s32[4]{0:T(128)S(1)} %copy-done.2, s32[4]{0:T(128)S(1)} %copy-done.4, bf16[2048,768]{1,0:T(8,128)(2,1)S(1)} %get-tuple-element.58.q_ref.k_ref.v_ref, bf16[2048,768]{1,0:T(8,128)(2,1)S(1)} %get-tuple-element.58.q_ref.k_ref.v_ref, ...), custom_call_target="tpu_custom_call" | custom-call | flops 8589934592 | bytes 8388608 | tf_op jit(solution)/shard_map/attend_back/pallas_call | solution.py:180
  669.0 1.6 copy-done.13
  670.6 2.3 copy.33
  673.0 9.7 %reduce-scatter.8.cloned.1.call-done = bf16[256,512]{1,0:T(8,128)(2,1)} async-done(((bf16[2048,512]{1,0:T(8,128)(2,1)}), bf16[256,512]{1,0:T(8,128)(2,1)}) %reduce-scatter.8.cloned.1.call-update) | async-done | bytes 262160 | tf_op jit(solution)/shard_map/reduce_scatter | solution.py:1646
  682.6 108.5 %leave.1 = (bf16[1024,512]{1,0:T(8,128)(2,1)}, f32[16,512]{1,0:T(8,128)}, f32[256,512]{1,0:T(8,128)}, f32[256,512]{1,0:T(8,128)}, f32[256,512]{1,0:T(8,128)}) custom-call(bf16[2048,768]{1,0:T(8,128)(2,1)} %copy-done.13, bf16[1024,2048]{1,0:T(8,128)(2,1)} %copy-done, bf16[2048,1536]{1,0:T(8,128)(2,1)} %get-tuple-element.90.weight, ...), custom_call_target="tpu_custom_call" | custom-call | flops 60000002048 | bytes 33554432 | tf_op jit(solution)/shard_map/leave/pallas_call | solution.py:1485
  791.2 1.5 fusion.9
  792.7 0.7 slice.54
  793.4 1.3 slice.58
  795.9 1.6 convert_element_type.41
  797.5 0.9 convert_element_type.40
  798.4 1.0 copy.40
  799.3 0.8 copy.41
  800.1 0.8 copy.42
  800.9 0.8 copy.43
  (59 shorter events, 4.2 us)
Async XLA Ops:
  9.6 1.2 copy-start.5
  10.8 1.2 copy-start.6
  12.1 0.9 copy-start.7
  13.0 0.9 copy-start.8
  14.0 0.9 copy-start.9
  14.9 0.9 copy-start.10
  15.9 117.6 %copy-start.17 = (bf16[1024,512]{1,0:T(8,128)(2,1)S(1)}, bf16[1024,512]{1,0:T(8,128)(2,1)}, u32[]{:S(2)}) copy-start(bf16[1024,512]{1,0:T(8,128)(2,1)} %param.27) | copy-start | bytes 3145732
  130.1 2.0 copy-start
  132.1 1.3 copy-start.15
  133.4 8.2 %copy-start.23 = (bf16[2048]{0:T(1024)(128)(2,1)S(1)}, bf16[2048]{0:T(1024)(128)(2,1)}, u32[]{:S(2)}) copy-start(bf16[2048]{0:T(1024)(128)(2,1)} %param.24) | copy-start | bytes 12292
  134.5 40.0 %all-to-all-start = ((bf16[4,256,512]{2,1,0:T(8,128)(2,1)}), bf16[4,256,512]{2,1,0:T(8,128)(2,1)}, u32[]{:S(2)}, u32[]{:S(2)}) async-start(bf16[4,256,512]{2,1,0:T(8,128)(2,1)} %bitcast.28), calls=%async_computation | async-start | bytes 2097152 | tf_op jit(solution)/shard_map/all_to_all | solution.py:1533
  138.9 480.4 %reduce-scatter.4.cloned.1.call-start = ((), (), s32[]{:S(2)}) async-start(), calls=%async_computation.5 | async-start | bytes 9437184 | tf_op jit(solution)/shard_map/reduce_scatter | solution.py:1646
  143.5 28.8 %copy-start.1 = (s32[4]{0:T(128)}, s32[4]{0:T(128)S(1)}, u32[]{:S(2)}) copy-start(s32[4]{0:T(128)S(1)} %get-tuple-element.117.first) | copy-start | bytes 52
  143.5 28.8 %copy-start.3 = (s32[4]{0:T(128)}, s32[4]{0:T(128)S(1)}, u32[]{:S(2)}) copy-start(s32[4]{0:T(128)S(1)} %get-tuple-element.118.last) | copy-start | bytes 52
  172.3 1.0 copy-start.11
  484.3 188.7 %reduce-scatter.6.cloned.1.call-start = ((), (), s32[]{:S(2)}) async-start(), calls=%async_computation.6 | async-start | bytes 9437184 | tf_op jit(solution)/shard_map/reduce_scatter | solution.py:1646
  485.1 197.6 %reduce-scatter.8.cloned.1.call-start = ((), (), s32[]{:S(2)}) async-start(), calls=%async_computation.7 | async-start | bytes 2359296 | tf_op jit(solution)/shard_map/reduce_scatter | solution.py:1646
  619.3 14.0 %copy-start.2 = (s32[4]{0:T(128)S(1)}, s32[4]{0:T(128)}, u32[]{:S(2)}) copy-start(s32[4]{0:T(128)} %copy-done.1) | copy-start | bytes 52
  619.3 14.0 %copy-start.4 = (s32[4]{0:T(128)S(1)}, s32[4]{0:T(128)}, u32[]{:S(2)}) copy-start(s32[4]{0:T(128)} %copy-done.3) | copy-start | bytes 52
  620.7 49.9 %all-to-all-start.1 = ((bf16[4,256,512]{2,1,0:T(8,128)(2,1)}), bf16[4,256,512]{2,1,0:T(8,128)(2,1)}, u32[]{:S(2)}, u32[]{:S(2)}) async-start(bf16[4,256,512]{2,1,0:T(8,128)(2,1)} %get-tuple-element.85), calls=%async_computation.2 | async-start | bytes 2097152 | tf_op jit(solution)/shard_map/all_to_all | solution.py:1540
  633.2 1.2 copy-start.12
  634.5 1.3 copy-start.14
  669.0 1.6 copy-start.13
  682.6 113.3 %copy-start.16 = (bf16[256,2048]{1,0:T(8,128)(2,1)S(1)}, bf16[256,2048]{1,0:T(8,128)(2,1)}, u32[]{:S(2)}) copy-start(bf16[256,2048]{1,0:T(8,128)(2,1)} %reduce-scatter.6.cloned.1.call-done) | copy-start | bytes 3145732
  682.6 114.8 %copy-start.22 = (bf16[256,512]{1,0:T(8,128)(2,1)S(1)}, bf16[256,512]{1,0:T(8,128)(2,1)}, u32[]{:S(2)}) copy-start(bf16[256,512]{1,0:T(8,128)(2,1)} %reduce-scatter.8.cloned.1.call-done) | copy-start | bytes 786436
  791.2 7.2 copy-start.18
  791.2 8.9 %copy-start.20 = (f32[256,512]{1,0:T(8,128)S(1)}, f32[256,512]{1,0:T(8,128)}, u32[]{:S(2)}) copy-start(f32[256,512]{1,0:T(8,128)} %get-tuple-element.135) | copy-start | bytes 1572868
  791.2 9.7 %copy-start.19 = (f32[256,512]{1,0:T(8,128)S(1)}, f32[256,512]{1,0:T(8,128)}, u32[]{:S(2)}) copy-start(f32[256,512]{1,0:T(8,128)} %get-tuple-element.136) | copy-start | bytes 1572868
  795.3 4.0 copy-start.21
Sparse Core Ops, SparseCore 0:
  484.4 73.8 reduce-scatter.3
  562.2 75.3 reduce-scatter.5
  641.4 41.1 reduce-scatter.7

commit v8 on v7

--- a/solution.py
+++ b/solution.py
@@ -35,7 +35,43 @@
     )
 
 
-def attend_kernel(first, last, q_ref, k_ref, v_ref, low_ref, high_ref, out_ref, lse_ref, vt):
+def block_bounds(block, rows, bounds, marks):
+    if len(bounds) == 4:
+        first, last, low, high = bounds
+        return first[block], last[block], low[...], high[...]
+    (ids,) = bounds
+    run = ids.shape[1]
+
+    @pl.when((pl.program_id(0) == 0) & (block == 0))
+    def _():
+        own = lax.axis_index("fsdp")
+        own_ids = ids[pl.ds(own, 1), :]
+        for i in range(2):
+            marks[i] = jnp.sum((own_ids <= 3 * own + i).astype(jnp.int32))
+
+    second, third = marks[0], marks[1]
+
+    def bounds_at(places):
+        start = jnp.where(places < second, 0, jnp.where(places < third, second, third))
+        stop = jnp.where(places < second, second, jnp.where(places < third, third, run))
+        return jnp.maximum(start, places - WIN), jnp.minimum(stop - 1, places + WIN)
+
+    begin = block * rows
+    low, high = bounds_at(begin + lax.broadcasted_iota(jnp.int32, (1, rows), 1))
+    return bounds_at(begin)[0] // KB, bounds_at(begin + rows - 1)[1] // KB + 1, low, high
+
+
+def bound_operands(bounds):
+    if len(bounds) == 4:
+        mark_spec = pl.BlockSpec((1, QB), lambda h, i, *_: (0, i))
+        return list(bounds[:2]), list(bounds[2:]), [mark_spec, mark_spec]
+    shape = bounds[0].shape
+    return [], list(bounds), [pl.BlockSpec(shape, lambda h, i, *_: (0, 0))]
+
+
+def attend_kernel(scalars, *refs):
+    bounds = refs[:scalars]
+    q_ref, k_ref, v_ref, *arrays, out_ref, lse_ref, vt, marks = refs[scalars:]
     block = pl.program_id(1)
     rows = q_ref.shape[0]
 
@@ -44,7 +80,7 @@
         vt[...] = v_ref[...].T
 
     queries = q_ref[...]
-    low, high = low_ref[...], high_ref[...]
+    first, last, low, high = block_bounds(block, rows, (*bounds, *arrays), marks)
     places = lax.broadcasted_iota(jnp.int32, (KB, rows), 0)
 
     def step(number, carry):
@@ -61,8 +97,8 @@
         return new_top, total, mixed
 
     top, total, mixed = lax.fori_loop(
-        first[block],
-        last[block],
+        first,
+        last,
         step,
         (
             jnp.full((1, rows), hidden_floor, jnp.float32),
@@ -74,31 +110,31 @@
     lse_ref[...] = (top + jnp.log2(total))[None]
 
 
-def attend(queries, keys, values, heads, low, high, first, last, places=(0, 0, 0)):
+def attend(queries, keys, values, heads, bounds, places=(0, 0, 0)):
     rows, span = queries.shape[0], keys.shape[0]
     width = heads * HD
     q_at, k_at, v_at = places
+    scalars, arrays, specs = bound_operands(bounds)
     return pl.pallas_call(
-        attend_kernel,
+        functools.partial(attend_kernel, len(scalars)),
         out_shape=(
             jax.ShapeDtypeStruct((rows, width), jnp.bfloat16),
             jax.ShapeDtypeStruct((heads, 1, rows), jnp.float32),
         ),
         grid_spec=pltpu.PrefetchScalarGridSpec(
-            num_scalar_prefetch=2,
+            num_scalar_prefetch=len(scalars),
             grid=(heads, rows // QB),
             in_specs=[
                 pl.BlockSpec((QB, HD), lambda h, i, *_: (i, h + q_at)),
                 pl.BlockSpec((span, HD), lambda h, i, *_: (0, h + k_at)),
                 pl.BlockSpec((span, HD), lambda h, i, *_: (0, h + v_at)),
-                pl.BlockSpec((1, QB), lambda h, i, *_: (0, i)),
-                pl.BlockSpec((1, QB), lambda h, i, *_: (0, i)),
+                *specs,
             ],
             out_specs=[
                 pl.BlockSpec((QB, HD), lambda h, i, *_: (i, h)),
                 pl.BlockSpec((1, 1, QB), lambda h, i, *_: (h, 0, i)),
             ],
-            scratch_shapes=[pltpu.VMEM((HD, span), jnp.bfloat16)],
+            scratch_shapes=[pltpu.VMEM((HD, span), jnp.bfloat16), pltpu.SMEM((2,), jnp.int32)],
         ),
         compiler_params=pltpu.CompilerParams(vmem_limit_bytes=32 << 20),
         cost_estimate=pl.CostEstimate(
@@ -107,14 +143,14 @@
             transcendentals=rows * span * heads,
         ),
         name="attend",
-    )(first, last, queries, keys, values, low, high)
-
-
-def attend_back_kernel(
-    first, last, q_ref, k_ref, v_ref, o_ref, g_ref, lse_ref, low_ref, high_ref,
-    *outputs,
-):
-    *results, kt, dk_sum, dv_sum = outputs
+    )(*scalars, queries, keys, values, *arrays)
+
+
+def attend_back_kernel(scalars, arrays, *refs):
+    bounds = refs[:scalars]
+    q_ref, k_ref, v_ref, o_ref, g_ref, lse_ref, *refs = refs[scalars:]
+    bounds = (*bounds, *refs[:arrays])
+    *results, kt, dk_sum, dv_sum, marks = refs[arrays:]
     head, block = pl.program_id(0), pl.program_id(1)
     rows = q_ref.shape[0]
 
@@ -127,7 +163,7 @@
     queries = q_ref[...]
     upstream = g_ref[...]
     lse = lse_ref[0]
-    low, high = low_ref[...], high_ref[...]
+    first, last, low, high = block_bounds(block, rows, bounds, marks)
     places = lax.broadcasted_iota(jnp.int32, (KB, rows), 0)
     product = upstream.astype(jnp.float32) * o_ref[...].astype(jnp.float32)
     delta = jnp.sum(product.T, axis=0, keepdims=True)
@@ -144,9 +180,7 @@
         dk_sum[window, :] += dot_plain(score_grad, queries)
         return dq + dot_plain(kt[:, window], score_grad)
 
-    dq = lax.fori_loop(
-        first[block], last[block], step, jnp.zeros((HD, rows), jnp.float32)
-    )
+    dq = lax.fori_loop(first, last, step, jnp.zeros((HD, rows), jnp.float32))
     dq = (dq * score_scale).T
     if len(results) == 1:
         width = results[0].shape[1] // 3
@@ -168,7 +202,7 @@
 
 
 def attend_back(
-    queries, keys, values, out, upstream, lse, low, high, first, last, places=(0, 0, 0), merged=False
+    queries, keys, values, out, upstream, lse, bounds, places=(0, 0, 0), merged=False
 ):
     rows, width = out.shape
     span = keys.shape[0]
@@ -176,9 +210,9 @@
     q_at, k_at, v_at = places
     row_spec = pl.BlockSpec((QB, HD), lambda h, i, *_: (i, h))
     key_spec = pl.BlockSpec((span, HD), lambda h, i, *_: (0, h))
-    mark_spec = pl.BlockSpec((1, QB), lambda h, i, *_: (0, i))
+    scalars, arrays, specs = bound_operands(bounds)
     return pl.pallas_call(
-        attend_back_kernel,
+        functools.partial(attend_back_kernel, len(scalars), len(arrays)),
         out_shape=[jax.ShapeDtypeStruct((rows, 3 * width), jnp.bfloat16)]
         if merged
         else [
@@ -187,7 +221,7 @@
             jax.ShapeDtypeStruct((span, width), jnp.float32),
         ],
         grid_spec=pltpu.PrefetchScalarGridSpec(
-            num_scalar_prefetch=2,
+            num_scalar_prefetch=len(scalars),
             grid=(heads, rows // QB),
             in_specs=[
                 pl.BlockSpec((QB, HD), lambda h, i, *_: (i, h + q_at)),
@@ -195,7 +229,7 @@
                 pl.BlockSpec((span, HD), lambda h, i, *_: (0, h + v_at)),
                 row_spec, row_spec,
                 pl.BlockSpec((1, 1, QB), lambda h, i, *_: (h, 0, i)),
-                mark_spec, mark_spec,
+                *specs,
             ],
             out_specs=[pl.BlockSpec((rows, 3 * width), lambda h, i, *_: (0, 0))]
             if merged
@@ -204,6 +238,7 @@
                 pltpu.VMEM((HD, span), jnp.bfloat16),
                 pltpu.VMEM((span, HD), jnp.float32),
                 pltpu.VMEM((span, HD), jnp.float32),
+                pltpu.SMEM((2,), jnp.int32),
             ],
         ),
         compiler_params=pltpu.CompilerParams(vmem_limit_bytes=32 << 20),
@@ -213,7 +248,7 @@
             transcendentals=rows * span * heads,
         ),
         name="attend_back",
-    )(first, last, queries, keys, values, out, upstream, lse, low, high)
+    )(*scalars, queries, keys, values, out, upstream, lse, *arrays)
 
 
 def key_bounds(query_ids, key_ids, offset):
@@ -225,24 +260,7 @@
     high = jnp.minimum(stop - 1, places + WIN)
     first = jnp.min(low.reshape(-1, QB), axis=1) // KB
     last = jnp.max(high.reshape(-1, QB), axis=1) // KB + 1
-    return low[None], high[None], first, last
-
-
-def document_bounds(ids, first_id):
-    rows = ids.shape[0]
-    second = jnp.sum(ids <= first_id, dtype=jnp.int32)
-    third = jnp.sum(ids <= first_id + 1, dtype=jnp.int32)
-
-    def bounds_at(places):
-        start = jnp.where(places < second, 0, jnp.where(places < third, second, third))
-        stop = jnp.where(places < second, second, jnp.where(places < third, third, rows))
-        return jnp.maximum(start, places - WIN), jnp.minimum(stop - 1, places + WIN)
-
-    low, high = bounds_at(jnp.arange(rows, dtype=jnp.int32))
-    starts = jnp.arange(0, rows, QB, dtype=jnp.int32)
-    first = bounds_at(starts)[0] // KB
-    last = bounds_at(starts + (QB - 1))[1] // KB + 1
-    return low[None], high[None], first, last
+    return first, last, low[None], high[None]
 
 
 def padded(block, width):
@@ -684,11 +702,10 @@
 
 
 def enter_kernel(
-    count, x_ref, marks_ref, query_ref, key_ref, value_ref, output_ref, expand_ref, bias,
-    wide, marks_out, weight, output_weight, expand_weight, heads,
+    count, x_ref, marks_ref, query_ref, key_ref, value_ref, output_ref, bias,
+    wide, own_tokens, marks_out, weight, output_weight, heads,
     mark_slots, stage, sent, got, marks_sent, marks_got,
-    weight_sent, weight_got, output_sent, output_got, expand_sent, expand_got,
-    swap_sent, swap_got, put_done,
+    weight_sent, weight_got, output_sent, output_got, swap_sent, swap_got, put_done,
 ):
     me, ctx = lax.axis_index("tp"), lax.axis_index("ctx")
     rows, width = x_ref.shape
@@ -704,7 +721,6 @@
 
     gather = PlaneGather(weight, weight_sent, weight_got)
     output_gather = PlaneGather(output_weight, output_sent, output_got)
-    expand_gather = PlaneGather(expand_weight, expand_sent, expand_got)
     own_shard = gather.shard(gather.fsdp, ctx)
     own = pl.ds(pl.multiple_of(me * width, width), width)
     puts = [
@@ -715,7 +731,6 @@
     puts += [
         (output_ref, output_gather.shard(gather.fsdp, ctx)),
         (x_ref, wide.at[:, own]),
-        (expand_ref, expand_gather.shard(gather.fsdp, ctx)),
     ]
     puts = [
         pltpu.make_async_copy(source, place, put_done.at[i])
@@ -730,10 +745,8 @@
     def source(piece):
         return x_ref.at[piece_rows(piece)]
 
-    @pl.loop(0, PIECES)
-    def _(piece):
+    for piece in range(2):
         line.spread_start(piece, source(piece))
-
     for put in puts[:7]:
         put.wait()
     gather.first()
@@ -761,26 +774,38 @@
             values = dot_plain(x, weight[:, columns]) + bias[:, columns]
             place[:, pl.ds(pl.multiple_of(tile * half, half), half)] = values.astype(jnp.bfloat16)
 
-    for distance in range(1, count):
-        if distance == count - 1:
+    @pl.loop(0, PIECES + 7)
+    def _(step):
+        def late(pieces, action, least=0):
+            @pl.when((step >= pieces + least) & (step < PIECES + pieces))
+            def _():
+                action(step - pieces)
+
+        def use(piece):
+            products(piece, 1 - ctx, stage.at[piece_rows(piece)])
+            swap.start(piece)
+            products(piece, ctx, heads.at[piece_rows(piece, ctx * rows)])
+
+        @pl.when(step == 7)
+        def _():
+            gather.third()
             gather.last()
 
-        @pl.loop(0, PIECES)
-        def _(piece, distance=distance):
-            line.spread_onward(piece, distance)
-            if distance == count - 1:
-                products(piece, 1 - ctx, stage.at[piece_rows(piece)])
-                swap.start(piece)
-                products(piece, ctx, heads.at[piece_rows(piece, ctx * rows)])
-                pl.when(piece == PIECES // 2)(expand_gather.second)
-
-        if distance == 1:
-            gather.second()
-            output_gather.second()
-            expand_gather.first()
-        if distance == count - 2:
-            gather.third()
-            output_gather.third()
+        late(0, lambda piece: line.spread_start(piece, source(piece)), 2)
+        late(7, use)
+        late(5, lambda piece: line.spread_onward(piece, 2))
+        late(3, lambda piece: line.spread_onward(piece, 1))
+        late(6, lambda piece: [line.spread_onward(piece, i) for i in range(3, count)])
+        pl.when(step == 5)(gather.second)
+        pl.when(step == 7)(output_gather.second)
+        pl.when(step == 9)(output_gather.third)
+
+    own_height = height // count
+    for piece in range(PIECES):
+        start = pl.multiple_of(piece * height + me * own_height, own_height)
+        own_tokens[piece * own_height : (piece + 1) * own_height, :] = wide[
+            pl.ds(start, own_height), :
+        ]
 
     marks.wait_arrivals()
     for i in range(1, count):
@@ -792,19 +817,15 @@
         swap.wait_arrival(piece)
         swap.wait_sent(piece)
 
-    expand_gather.third()
     output_gather.last()
-    expand_gather.last()
     marks.wait_sent()
     gather.wait_sent()
     output_gather.wait_sent()
-    expand_gather.wait_sent()
     line.spread_finish(PIECES, source)
 
 
 def enter(
-    tokens, marks, query_weight, key_weight, value_weight, output_weight, expand_weight, bias,
-    collective_id,
+    tokens, marks, query_weight, key_weight, value_weight, output_weight, bias, collective_id
 ):
     count = lax.axis_size("tp")
     rows, width = tokens.shape
@@ -815,50 +836,44 @@
         functools.partial(enter_kernel, count),
         out_shape=[
             jax.ShapeDtypeStruct((rows, count * width), tokens.dtype),
+            jax.ShapeDtypeStruct((rows // count, count * width), tokens.dtype),
             jax.ShapeDtypeStruct((marks.shape[0], count * width), marks.dtype),
             jax.ShapeDtypeStruct((plane * query_weight.shape[0], 2 * part), query_weight.dtype),
             jax.ShapeDtypeStruct(
                 (plane * output_weight.shape[0], output_weight.shape[1]), output_weight.dtype
-            ),
-            jax.ShapeDtypeStruct(
-                (plane * expand_weight.shape[0], expand_weight.shape[1]), expand_weight.dtype
             ),
             jax.ShapeDtypeStruct((2 * rows, part), jnp.bfloat16),
         ],
         in_specs=[
             pl.BlockSpec(memory_space=pl.ANY),
             pl.BlockSpec(memory_space=pltpu.VMEM),
-            *[pl.BlockSpec(memory_space=pl.ANY)] * 5,
+            *[pl.BlockSpec(memory_space=pl.ANY)] * 4,
             pl.BlockSpec(memory_space=pltpu.VMEM),
         ],
-        out_specs=[
-            *[pl.BlockSpec(memory_space=pltpu.VMEM)] * 4,
-            pl.BlockSpec(memory_space=pl.ANY),
-            pl.BlockSpec(memory_space=pltpu.VMEM),
-        ],
+        out_specs=[pl.BlockSpec(memory_space=pltpu.VMEM)] * 6,
         scratch_shapes=[
             pltpu.VMEM((count - 1, *marks.shape), marks.dtype),
             pltpu.VMEM((rows, part), jnp.bfloat16),
             *line_semaphores(count, PIECES)[1],
             pltpu.SemaphoreType.DMA((count - 1,)),
             pltpu.SemaphoreType.DMA((count - 1,)),
-            *[pltpu.SemaphoreType.DMA((9,))] * 6,
+            *[pltpu.SemaphoreType.DMA((9,))] * 4,
             pltpu.SemaphoreType.DMA((PIECES,)),
             pltpu.SemaphoreType.DMA((PIECES,)),
-            pltpu.SemaphoreType.DMA((9,)),
+            pltpu.SemaphoreType.DMA((8,)),
         ],
         compiler_params=pltpu.CompilerParams(
-            collective_id=collective_id, has_side_effects=True, vmem_limit_bytes=40 << 20
+            collective_id=collective_id, has_side_effects=True, vmem_limit_bytes=60 << 20
         ),
         cost_estimate=pl.CostEstimate(
             flops=80_000_000_000, bytes_accessed=64 * rows * count * width, transcendentals=0
         ),
         name="enter",
-    )(tokens, marks, query_weight, key_weight, value_weight, output_weight, expand_weight, bias)
+    )(tokens, marks, query_weight, key_weight, value_weight, output_weight, bias)
 
 
 def relay_kernel(count, row_step, use_step, sizes, *refs):
-    row_in, use_in, row_out, use_out, shared, swap_in, swap_out, next_shard = sizes
+    row_in, use_in, row_out, use_out, shared, swap_in, swap_out, gathers, fill_step = sizes
     refs = list(refs)
 
     def take(number):
@@ -869,11 +884,13 @@
     x_ref, sum_weight = take(2)
     use_weight = sum_weight if shared else take(1)[0]
     row_inputs, use_inputs = take(row_in), take(use_in)
-    next_ref = take(1)[0] if next_shard else None
+    next_ref = take(1)[0] if gathers else None
+    fill_inputs = take(1) if fill_step is not None else []
     (gathered,) = take(1)
     row_outputs, use_outputs = take(row_out), take(use_out)
     swapped = take(1)[0] if swap_in or swap_out else None
-    next_whole = take(1)[0] if next_shard else None
+    wholes = take(2) if gathers else []
+    fill_outputs = take(1) if fill_step is not None else []
     terms, total, slots, sum_sent, sum_got, spread_sent, spread_got = take(7)
     me, ctx = lax.axis_index("tp"), lax.axis_index("ctx")
     rows = gathered.shape[0]
@@ -888,10 +905,11 @@
         return gathered.at[pl.ds(pl.multiple_of(piece * height + owner * own, own), own)]
 
     line = Line(me, count, slots, sum_sent, sum_got, view, spread_sent, spread_got)
-    next_gather = None
-    if next_shard:
-        next_gather = PlaneGather(next_whole, *take(2))
+    use_gather = next_gather = None
+    if gathers:
+        use_gather, next_gather = [PlaneGather(whole, *take(2)) for whole in wholes]
         greet(me, count, next_gather.peers())
+        shards, use_weight = (use_weight, next_ref), wholes[0]
     else:
         greet(me, count, [{"ctx": 1 - ctx}] if swap_in or swap_out else [])
     swap = None
@@ -909,9 +927,10 @@
             swap.start(piece)
             swapped[piece_rows(piece), own_half] = x_ref[piece_rows(piece, ctx * rows), :]
 
-    if next_gather is not None:
-        next_gather.put(next_ref, take(1)[0])
-        next_gather.first()
+    if gathers:
+        for gather, shard in zip((use_gather, next_gather), shards, strict=True):
+            gather.put(shard, take(1)[0])
+        use_gather.first()
     if swap_out:
         stage, swap_sent, swap_got = take(3)
         half = swapped.shape[1]
@@ -965,17 +984,28 @@
             for distance in range(3, count):
                 line.spread_onward(piece, distance)
 
+        if gathers:
+            pl.when(step == 5)(use_gather.last)
         late(5, use)
         late(3, lambda piece: line.spread_onward(piece, 2))
         late(1, lambda piece: line.sum_onward(piece, term_of(1 - odd), [1]))
         late(0, form)
         late(4, far_shards)
         late(2, lambda piece: line.spread_onward(piece, 1))
+        if fill_step is not None:
+            late(0, lambda piece: fill_step(piece, x_ref, fill_inputs, fill_outputs))
         late(0, lambda piece: line.sum_onward(piece, term_of(odd), range(count - 2, 1, -1)))
         late(1, own_step)
-        if next_gather is not None:
-            pl.when(step == 4)(next_gather.second)
-            pl.when(step == 6)(next_gather.third)
+        if gathers:
+
+            @pl.when(step == 3)
+            def _():
+                use_gather.second()
+                next_gather.first()
+
+            pl.when(step == 4)(use_gather.third)
+            pl.when(step == 6)(next_gather.second)
+            pl.when(step == 8)(next_gather.third)
 
     if swap is not None:
 
@@ -985,8 +1015,9 @@
                 swap.wait_arrival(piece)
             swap.wait_sent(piece)
 
-    if next_gather is not None:
+    if gathers:
         next_gather.last()
+        use_gather.wait_sent()
         next_gather.wait_sent()
     line.sum_finish(PIECES)
     line.spread_finish(PIECES)
@@ -994,7 +1025,7 @@
 
 def relay(
     x, sum_weight, use_weight, row_inputs, row_step, row_shapes, use_inputs, use_step, use_shapes,
-    collective_id, name, rows, swap_in=None, swap_out=None, next_shard=None,
+    collective_id, name, rows, swap_in=None, swap_out=None, next_shard=None, fill=None,
 ):
     count = lax.axis_size("tp")
     width = sum_weight.shape[0]
@@ -1009,12 +1040,20 @@
     extra, last = [], []
     if next_shard is not None:
         operands.append(next_shard)
-        in_specs.append(pl.BlockSpec(memory_space=pl.ANY))
-        whole = (8 * next_shard.shape[0], next_shard.shape[1])
-        shapes.append(jax.ShapeDtypeStruct(whole, next_shard.dtype))
-        out_specs.append(pl.BlockSpec(memory_space=pl.ANY))
-        extra = [pltpu.SemaphoreType.DMA((9,))] * 2
-        last = [pltpu.SemaphoreType.DMA]
+        in_specs.append(pl.BlockSpec(memory_space=pltpu.VMEM))
+        for shard, space in ((use_weight, pltpu.VMEM), (next_shard, pl.ANY)):
+            whole = (8 * shard.shape[0], shard.shape[1])
+            shapes.append(jax.ShapeDtypeStruct(whole, shard.dtype))
+            out_specs.append(pl.BlockSpec(memory_space=space))
+        extra = [pltpu.SemaphoreType.DMA((9,))] * 4
+        last = [pltpu.SemaphoreType.DMA] * 2
+    fill_step = None
+    if fill is not None:
+        fill_step, fill_input, fill_shape = fill
+        operands.append(fill_input)
+        in_specs.append(pl.BlockSpec(memory_space=pltpu.VMEM))
+        shapes.append(fill_shape)
+        out_specs.append(pl.BlockSpec(memory_space=pltpu.VMEM))
     sums, spreads = line_semaphores(count, PIECES)
     swaps = []
     if swap_out is not None:
@@ -1023,7 +1062,7 @@
         swaps += [pltpu.SemaphoreType.DMA((PIECES,))] * 2
     sizes = (
         len(row_inputs), len(use_inputs), len(row_shapes), len(use_shapes), shared,
-        swap_in is not None, swap_out is not None, next_shard is not None,
+        swap_in is not None, swap_out is not None, next_shard is not None, fill_step,
     )
     return pl.pallas_call(
         functools.partial(relay_kernel, count, row_step, use_step, sizes),
@@ -1150,6 +1189,18 @@
     if outputs:
         outputs[0][rows, :] = result
     return result
+
+
+def expand_product_step(piece, x, inputs, outputs):
+    (norm_low,), (product,) = inputs, outputs
+    height = product.shape[0] // PIECES
+    part = pl.ds(pl.multiple_of(piece * height, height), height)
+    left = norm_low[:, part].T
+
+    @pl.loop(0, product.shape[1] // TILE)
+    def _(tile):
+        columns = pl.ds(pl.multiple_of(tile * TILE, TILE), TILE)
+        product[part, columns] = dot_plain(left, x[:, columns]).astype(product.dtype)
 
 
 def peers_in_plane(sizes):
@@ -1391,8 +1442,8 @@
 
 
 def leave_kernel(
-    sizes, grads_ref, tokens_ref, weight, inner_ref, rows_ref, hidden_ref,
-    out_ref, vectors_ref, query_out, key_out, value_out,
+    sizes, grads_ref, tokens_ref, weight, inner_ref, rows_ref, hidden_ref, branch_ref, attended_ref,
+    out_ref, vectors_ref, query_out, key_out, value_out, output_out,
     x_ref, term_ref, total, slots, own_vectors, tp_slots, plane_slots,
     sum_sent, sum_got, tp_sent, tp_got, plane_sent, plane_got, swap_sent, swap_got, *sum_scratch,
 ):
@@ -1401,7 +1452,7 @@
     rows = x_ref.shape[0]
     height = rows // PIECES
     part = grads_ref.shape[1]
-    plane_sum = PlaneSum(*sum_scratch)
+    plane_sum, output_sum = PlaneSum(*sum_scratch[:6]), PlaneSum(*sum_scratch[6:])
     shard = plane_sum.parts.shape[1]
 
     def piece_rows(piece, start=0):
@@ -1414,43 +1465,48 @@
         lambda piece: x_ref.at[piece_rows(piece), own_columns],
     )
 
-    def product(number):
-        columns = pl.ds(pl.multiple_of(number * shard, shard), shard)
-        result = dot_rows(tokens_ref[:, columns], x_ref[...])
-        plane_sum.parts[number] = result.astype(jnp.bfloat16)
+    def products(sums, fsdp, left, right):
+        for over_x in (1, 0):
+            for over_y in (1, 0):
+                number = sums.number(fsdp, over_x, over_y)
+                columns = pl.ds(pl.multiple_of(number * shard, shard), shard)
+                sums.parts[number] = dot_rows(left[:, columns], right[...]).astype(jnp.bfloat16)
 
     def opening():
         @pl.loop(0, PIECES)
         def _(piece):
             swap.start(piece)
 
+        products(output_sum, output_sum.twin, branch_ref, attended_ref)
+        output_sum.start()
         x_ref[:, own_columns] = grads_ref[pl.ds(pl.multiple_of(ctx * rows, rows), rows), :]
-
-    middle = PIECES // 2
+        products(output_sum, output_sum.fsdp, branch_ref, attended_ref)
+        output_sum.second()
+
+    last = PIECES - 1
+    begin = jnp.where((me == 0) | (me == count - 1), last, 2)
 
     def before(piece):
-        @pl.when(piece <= middle)
+        @pl.when(piece <= begin)
         def _():
             swap.wait_arrival(piece)
 
-    def products(fsdp):
-        for over_x in (1, 0):
-            for over_y in (1, 0):
-                product(plane_sum.number(fsdp, over_x, over_y))
-
     def after(piece):
-        @pl.when(piece == middle)
+        @pl.when(piece == begin)
         def _():
-            for other in range(middle + 1, PIECES):
+            @pl.loop(begin + 1, PIECES)
+            def _(other):
                 swap.wait_arrival(other)
-            products(plane_sum.twin)
+
+            products(plane_sum, plane_sum.twin, tokens_ref, x_ref)
             plane_sum.start()
 
-        @pl.when(piece == middle + 1)
+        @pl.when(piece == jnp.minimum(begin + 1, last))
         def _():
-            products(plane_sum.fsdp)
-
-        pl.when(piece == middle + 2)(plane_sum.second)
+            products(plane_sum, plane_sum.fsdp, tokens_ref, x_ref)
+
+        pl.when(piece == jnp.minimum(begin + 2, last))(plane_sum.second)
+        pl.when(piece == jnp.minimum(begin + 3, last))(output_sum.third)
 
     def closing():
         plane_sum.third()
@@ -1466,13 +1522,14 @@
     for side, half in enumerate(halves):
         for i, ref in enumerate((query_out, key_out, value_out)):
             ref[:, side * third : (side + 1) * third] = half[:, i * third : (i + 1) * third]
+    output_out[...] = jnp.concatenate(output_sum.finish(), axis=1)
 
     @pl.loop(0, PIECES)
     def _(piece):
         swap.wait_sent(piece)
 
 
-def leave(grads, tokens, weight, inner, row_sums, hidden_sums, collective_id):
+def leave(grads, tokens, weight, inner, row_sums, hidden_sums, branch, attended, collective_id):
     sizes = tuple(lax.axis_size(axis) for axis in ("fsdp", "ctx", "tp"))
     count = sizes[2]
     others = sizes[0] * sizes[1] - 1
@@ -1487,10 +1544,10 @@
         out_shape=[
             jax.ShapeDtypeStruct((rows, width), jnp.bfloat16),
             jax.ShapeDtypeStruct((packed, width), jnp.float32),
-            *[jax.ShapeDtypeStruct((shard, 2 * part // 3), jnp.float32)] * 3,
+            *[jax.ShapeDtypeStruct((shard, 2 * part // 3), jnp.float32)] * 4,
         ],
-        in_specs=[pl.BlockSpec(memory_space=pltpu.VMEM)] * 6,
-        out_specs=[pl.BlockSpec(memory_space=pltpu.VMEM)] * 5,
+        in_specs=[pl.BlockSpec(memory_space=pltpu.VMEM)] * 8,
+        out_specs=[pl.BlockSpec(memory_space=pltpu.VMEM)] * 6,
         scratch_shapes=[
             pltpu.VMEM((rows, 2 * part), jnp.bfloat16),
             pltpu.VMEM((height, width), jnp.float32),
@@ -1507,15 +1564,16 @@
             pltpu.SemaphoreType.DMA((PIECES,)),
             pltpu.SemaphoreType.DMA((PIECES,)),
             *PlaneSum.scratch(others + 1, shard, 2 * part),
+            *PlaneSum.scratch(others + 1, shard, attended.shape[1]),
         ],
         compiler_params=pltpu.CompilerParams(
-            collective_id=collective_id, has_side_effects=True, vmem_limit_bytes=56 << 20
+            collective_id=collective_id, has_side_effects=True, vmem_limit_bytes=60 << 20
         ),
         cost_estimate=pl.CostEstimate(
             flops=60_000_000_000, bytes_accessed=64 * rows * width, transcendentals=0
         ),
         name="leave",
-    )(grads, tokens, weight, inner, row_sums, hidden_sums)
+    )(grads, tokens, weight, inner, row_sums, hidden_sums, branch, attended)
 
 
 def to_own_rows(wide):
@@ -1575,20 +1633,16 @@
     qkv_bias = qkv_bias.astype(jnp.float32)
     if by_heads:
         half_bias = qkv_bias.reshape(3, 2, -1).transpose(1, 0, 2).reshape(1, -1)
-        wide_tokens, wide_marks, wide_qkv, full_output, full_expand, qkv_heads = enter(
-            tokens, marks, query_weight, key_weight, value_weight, output_weight, expand_weight,
-            half_bias, 0,
+        wide_tokens, own_tokens, wide_marks, wide_qkv, full_output, qkv_heads = enter(
+            tokens, marks, query_weight, key_weight, value_weight, output_weight, half_bias, 0
         )
         queries = keys = values = qkv_heads
         own_heads = heads // 2
-        stream_rows = plane_sizes[1] * rows
-        stream_ids = lax.dynamic_slice_in_dim(
-            segments, lax.axis_index("fsdp") * stream_rows, stream_rows, 0
-        )
-        bounds = document_bounds(stream_ids, 3 * lax.axis_index("fsdp"))
+        bounds = (segments.reshape(-1, plane_sizes[1] * rows),)
     else:
         wide_qkv = weight_rows(jnp.concatenate([query_weight, key_weight, value_weight], axis=1))
         wide_tokens, wide_marks = gather_features(tokens, marks, 0)
+        own_tokens = to_own_rows(wide_tokens)
         qkv = dot_plain(wide_tokens, wide_qkv) + qkv_bias.reshape(1, -1)
         queries, keys, values = jnp.split(qkv.astype(jnp.bfloat16), 3, axis=1)
         own_heads = heads
@@ -1608,10 +1662,9 @@
     biases = wide_marks[2:6].astype(jnp.float32)
     wide_marks, out_grad = lax.optimization_barrier((wide_marks, out_grad))
     upstream = spread_own(out_grad)
-    attended_heads, lse = attend(queries, keys, values, own_heads, *bounds, places)
+    attended_heads, lse = attend(queries, keys, values, own_heads, bounds, places)
     attended_heads, upstream = lax.optimization_barrier((attended_heads, upstream))
 
-    own_tokens = to_own_rows(wide_tokens)
     own_rows, features = own_tokens.shape
     hidden_cols = expand_weight.shape[1]
 
@@ -1620,7 +1673,7 @@
 
     own_shape = shape((own_rows, features))
     norm_low, first_norm, normed_one, inverse_one, hidden, activated, *more = relay(
-        attended_heads, full_output, full_expand,
+        attended_heads, full_output, expand_weight if by_heads else full_expand,
         [own_tokens, gains, biases], first_norm_step,
         [own_shape, own_shape, shape((own_rows, 128))],
         [hidden_bias.astype(jnp.float32)[None]], expand_step,
@@ -1630,7 +1683,7 @@
         next_shard=shrink_weight if by_heads else None,
     )
     if by_heads:
-        attended, full_shrink = more
+        attended, full_expand, full_shrink = more
     else:
         attended, full_shrink = attended_heads, weight_rows(shrink_weight)
     ffn_low, mixed_own, grad_second, second_sums, hidden_low, hidden_sums = relay(
@@ -1647,16 +1700,11 @@
             grad, plane, scatter_dimension=0, tiled=True
         )
 
-    hidden_low, shrink_part, expand_part = lax.optimization_barrier(
-        (
-            hidden_low,
-            dot_rows(ffn_low, activated).astype(jnp.bfloat16),
-            dot_rows(norm_low, hidden_low).astype(jnp.bfloat16),
-        )
+    hidden_low, shrink_part = lax.optimization_barrier(
+        (hidden_low, dot_rows(ffn_low, activated).astype(jnp.bfloat16))
     )
     shrink_grad = owner_sum(shrink_part)
-    expand_grad = owner_sum(expand_part)
-    branch_low, grad_inner, first_sums, attended_grad = relay(
+    branch_low, grad_inner, first_sums, attended_grad, expand_part = relay(
         hidden_low, full_expand, full_output,
         [grad_second, normed_one, inverse_one, gains], first_back_step,
         [own_shape, shape((8, features))],
@@ -1664,28 +1712,22 @@
         [] if by_heads else [shape((rows, head_cols), jnp.bfloat16)],
         3, "first_back", rows,
         swap_out=shape((2 * rows, head_cols // 2), jnp.bfloat16) if by_heads else None,
-    )
-    attended_grad, mixed_own, shrink_grad, output_part = lax.optimization_barrier(
-        (
-            attended_grad,
-            mixed_own,
-            shrink_grad,
-            dot_rows(branch_low, attended).astype(jnp.bfloat16),
-        )
-    )
-    output_grad = owner_sum(output_part)
+        fill=(expand_product_step, norm_low, shape((features, hidden_cols), jnp.bfloat16)),
+    )
+    expand_grad = owner_sum(expand_part)
+    attended_grad, mixed_own, shrink_grad = lax.optimization_barrier(
+        (attended_grad, mixed_own, shrink_grad)
+    )
     mixed = unspread_own(mixed_own)
 
     if by_heads:
         (grads,) = attend_back(
-            queries, keys, values, attended_heads, attended_grad, lse, *bounds, places, True
+            queries, keys, values, attended_heads, attended_grad, lse, bounds, places, True
         )
-        grads, mixed, expand_grad, output_grad = lax.optimization_barrier(
-            (grads, mixed, expand_grad, output_grad)
-        )
+        grads, mixed = lax.optimization_barrier((grads, mixed))
     else:
         query_low, key_ext, value_ext = attend_back(
-            queries, keys, values, attended_heads, attended_grad, lse, *bounds
+            queries, keys, values, attended_heads, attended_grad, lse, bounds
         )
 
         def fold(ext):
@@ -1710,13 +1752,15 @@
         return [parts[:, :, i].reshape(-1, head_cols) for i in range(3)]
 
     if by_heads:
-        input_grad, vectors, query_grad, key_grad, value_grad = leave(
-            grads, wide_tokens, wide_qkv, grad_inner, row_sums, hidden_sums[:1], 4
+        input_grad, vectors, query_grad, key_grad, value_grad, output_grad = leave(
+            grads, wide_tokens, wide_qkv, grad_inner, row_sums, hidden_sums[:1], branch_low,
+            attended, 4,
         )
     else:
         input_grad, vectors = input_sum(
             qkv_low, wide_qkv, grad_inner, row_sums, hidden_sums[:1], 4
         )
+        output_grad = owner_sum(dot_rows(branch_low, attended).astype(jnp.bfloat16))
         qkv_grad = owner_sum(dot_rows(wide_tokens, qkv_low).astype(jnp.bfloat16))
         query_grad, key_grad, value_grad = by_kind(qkv_grad.astype(jnp.float32))
     hidden_rows = hidden_cols // head_cols

time: 808 us -> 774 us (0.958)
  Pallas kernels: 692 us -> 630 us
  waiting for transfers between devices: 10.4 us -> 58.4 us
  matrix products: 34.4 us -> 14.1 us
  starting transfers between devices: 11.5 us -> 19.7 us
    reduce_scatter x3 -> x2, waiting for transfers between devices: 9.66 us -> 58.4 us  [owner_sum(): return lax.psum_scatter(grad, plane, scatter_dimension=0, tiled=True)]
    pallas_call x1, Pallas kernels: 114 us -> 83.6 us  [enter(): pl.pallas_call(functools.partial(enter_kernel, count), out_shape=[jax.Sha...]
    dot_general x3 -> x1, matrix products: 34.4 us -> 14.1 us  [dot_rows(): lax.dot_general(left, right, (((0,), (0,)), ((), ())), preferred_element_...]
    pallas_call x3, Pallas kernels: 409 us -> 389 us  [relay(): pl.pallas_call(functools.partial(relay_kernel, count, row_step, use_step,...]
    unnamed x53 -> x24, local copies, waits for them, and re-layouts: 18.6 us -> 13.3 us
  transfers between devices with their start and end apart: 5 -> 4, of which waited for: 1 -> 1; matrix products, arithmetic and copies ran while one was open for 3% -> 2% of each run, Pallas kernels for 23% -> 23%
where the time goes in v8:
time: 774 us
  Pallas kernels  630 us (81%)
  waiting for transfers between devices  58.4 us (8%)
  local copies, waits for them, and re-layouts  27.7 us (4%)
  starting transfers between devices  19.7 us (3%)
  between operations  14.2 us (2%)
  matrix products  14.1 us (2%)
  other arithmetic  10.6 us (1%)
    pallas_call x3, Pallas kernels, relay(): pl.pallas_call(functools.partial(relay_kernel, count, row_step, use_step,...  389 us
    pallas_call x1, Pallas kernels, leave(): pl.pallas_call(functools.partial(leave_kernel, sizes), out_shape=[jax.Sha...  105 us
    pallas_call x1, Pallas kernels, enter(): pl.pallas_call(functools.partial(enter_kernel, count), out_shape=[jax.Sha...  83.6 us
    reduce_scatter x2, waiting for transfers between devices, owner_sum(): return lax.psum_scatter(grad, plane, scatter_dimension=0, tiled=True)  58.4 us
    pallas_call x1, Pallas kernels, attend_back(): pl.pallas_call(functools.partial(attend_back_kernel, len(scalars), len(ar...  29.1 us
    pallas_call x1, Pallas kernels, attend(): pl.pallas_call(functools.partial(attend_kernel, len(scalars)), out_shape=...  22.7 us
  transfers between devices with their start and end apart: 4, of which 1 were waited for; matrix products, arithmetic and copies ran while one was open for 2% of the time, Pallas kernels for 23%

profile of v8, /device:TPU:8, one launch (start us, length us, event | category | flops | bytes accessed | tf_op | source)
XLA Modules:
  0.0 774.5 jit_solution(15063615083963931484)
XLA Ops:
  7.2 0.7 stack.10
  7.9 0.7 stack.9
  8.6 0.1 pad.1.clone
  8.6 0.1 convert_bitcast_fusion
  8.7 0.6 reshape.64.bias
  9.3 0.1 pad.5.clone
  9.4 1.4 maximum_maximum_fusion.marks_ref
  10.8 83.6 %enter.1 = (bf16[1024,2048]{1,0:T(8,128)(2,1)}, bf16[256,2048]{1,0:T(8,128)(2,1)}, bf16[16,2048]{1,0:T(8,128)(2,1)}, bf16[2048,1536]{1,0:T(8,128)(2,1)}, bf16[20...) custom-call(bf16[1024,512]{1,0:T(8,128)(2,1)} %x_ref.1, bf16[16,512]{1,0:T(8,128)(2,1)} %maximum_maximum_fusion.marks_ref, ...), custom_call_target="tpu_custom_call" | custom-call | flops 80000000000 | bytes 134217728 | tf_op jit(solution)/shard_map/enter/pallas_call | solution.py:835
  94.4 0.0 copy-start.7
  94.4 0.0 copy-start.8
  94.4 2.5 copy.30
  96.9 11.2 %all-to-all-start = ((bf16[4,256,512]{2,1,0:T(8,128)(2,1)}), bf16[4,256,512]{2,1,0:T(8,128)(2,1)}, u32[]{:S(2)}, u32[]{:S(2)}) async-start(bf16[4,256,512]{2,1,0:T(8,128)(2,1)} %bitcast.19), calls=%async_computation | async-start | bytes 2097152 | tf_op jit(solution)/shard_map/all_to_all | solution.py:1591
  108.1 0.6 broadcast_in_dim.15
  108.7 22.7 %attend.1 = (bf16[2048,256]{1,0:T(8,128)(2,1)S(1)}, f32[2,1,2048]{2,1,0:T(1,128)S(1)}) custom-call(bf16[2048,768]{1,0:T(8,128)(2,1)S(1)} %copy-done, bf16[2048,768]{1,0:T(8,128)(2,1)S(1)} %copy-done, bf16[2048,768]{1,0:T(8,128)(2,1)S(1)} %copy-done, s32[4,2048]{1,0:T(4,128)S(1)} %reshape.57.refs_3_.refs_6_), custom_call_target="tpu_custom_call" | custom-call | flops 3221225472 | bytes 4194304 | tf_op jit(solution)/shard_map/attend/pallas_call | solution.py:118
  131.4 1.0 copy-done.1
  132.4 1.4 slice_convert_fusion.1.refs_4_.refs_6_
  133.8 1.4 slice_convert_fusion.refs_5_
  135.2 132.1 %first_norm.1 = (bf16[1024,2048]{1,0:T(8,128)(2,1)}, f32[256,2048]{1,0:T(8,128)}, f32[256,2048]{1,0:T(8,128)}, f32[256,128]{1,0:T(8,128)}, f32[1024,2048]{1,0:T(...) custom-call(bf16[2048,256]{1,0:T(8,128)(2,1)} %copy-done.1, ...), custom_call_target="tpu_custom_call" | custom-call | flops 99999997952 | bytes 134217728 | tf_op jit(solution)/shard_map/first_norm/pallas_call | solution.py:1067
  267.3 128.2 %second_norm.1 = (bf16[1024,2048]{1,0:T(8,128)(2,1)}, bf16[4,256,512]{2,1,0:T(8,128)(2,1)}, f32[256,2048]{1,0:T(8,128)}, f32[8,2048]{1,0:T(8,128)}, bf16[1024,2048]{1,0:T(8,128)(2,1)}, /*index=5*/f32[8,2048]{1,0:T(8,128)}) custom-call(bf16[1024,2048]{1,0:T(8,128)(2,1)} %get-tuple-element.64.refs_0_, bf16[2048,2048]{1,0:T(8,128)(2,1)} %get-tuple-element.65.refs_1_, ...), custom_call_target="tpu_custom_call" | custom-call | flops 99999997952 | bytes 134217728 | tf_op jit(solution)/shard_map/second_norm/pallas_call | solution.py:1067
  395.5 14.1 %convolution_convert_fusion = bf16[2048,2048]{1,0:T(8,128)(2,1)} fusion(bf16[1024,2048]{1,0:T(8,128)(2,1)} %get-tuple-element.70, bf16[1024,2048]{1,0:T(8,128)(2,1)} %get-tuple-element.64.refs_0_), kind=kOutput, calls=%fused_computation | convolution fusion | flops 8594128896 | bytes 16777216 | tf_op jit(solution)/shard_map/dot_general | solution.py:27
  409.6 0.0 reduce-scatter.3.cloned.1.call-update
  409.6 0.0 reduce-scatter.5.cloned.1.call-start
  409.7 129.0 %first_back.1 = (bf16[1024,2048]{1,0:T(8,128)(2,1)}, f32[256,2048]{1,0:T(8,128)}, f32[8,2048]{1,0:T(8,128)}, bf16[2048,256]{1,0:T(8,128)(2,1)}, bf16[2048,2048]{1,0:T(8,128)(2,1)}) custom-call(bf16[1024,2048]{1,0:T(8,128)(2,1)} %get-tuple-element.71.refs_0_, bf16[2048,2048]{1,0:T(8,128)(2,1)} %get-tuple-element.72.refs_1_, ...), custom_call_target="tpu_custom_call" | custom-call | flops 99999997952 | bytes 134217728 | tf_op jit(solution)/shard_map/first_back/pallas_call | solution.py:1067
  538.7 0.0 reduce-scatter.5.cloned.1.call-update
  538.7 0.0 reduce-scatter.3.cloned.1.call-done
  538.8 8.5 %all-to-all-start.1 = ((bf16[4,256,512]{2,1,0:T(8,128)(2,1)}), bf16[4,256,512]{2,1,0:T(8,128)(2,1)}, u32[]{:S(2)}, u32[]{:S(2)}) async-start(bf16[4,256,512]{2,1,0:T(8,128)(2,1)} %get-tuple-element.82), calls=%async_computation.2 | async-start | bytes 2097152 | tf_op jit(solution)/shard_map/all_to_all | solution.py:1598
  547.2 1.4 slice.53.hidden_ref
  548.7 1.2 fusion
  549.9 0.7 concatenate.8.rows_ref
  550.6 3.0 convert_element_type.22
  553.6 58.4 %reduce-scatter.5.cloned.1.call-done = bf16[256,2048]{1,0:T(8,128)(2,1)} async-done(((bf16[2048,2048]{1,0:T(8,128)(2,1)}), bf16[256,2048]{1,0:T(8,128)(2,1)}) %reduce-scatter.5.cloned.1.call-update) | async-done | bytes 1048592 | tf_op jit(solution)/shard_map/reduce_scatter | solution.py:1699
  612.0 2.8 convert_element_type.21
  614.8 1.2 copy-done.2
  616.0 1.2 copy-done.4
  617.2 29.1 %attend_back.1.grads_ref = bf16[2048,768]{1,0:T(8,128)(2,1)S(1)} custom-call(bf16[2048,768]{1,0:T(8,128)(2,1)S(1)} %copy-done, bf16[2048,768]{1,0:T(8,128)(2,1)S(1)} %copy-done, bf16[2048,768]{1,0:T(8,128)(2,1)S(1)} %copy-done, bf16[2048,256]{1,0:T(8,128)(2,1)S(1)} %copy-done.2, bf16[2048,256]{1,0:T(8,128)(2,1)S(1)} %copy-done.4, ...), custom_call_target="tpu_custom_call" | custom-call | flops 8589934592 | bytes 8388608 | tf_op jit(solution)/shard_map/attend_back/pallas_call | solution.py:214
  646.4 1.6 copy-done.3
  648.0 2.3 copy.31
  650.3 105.0 %leave.1 = (bf16[1024,512]{1,0:T(8,128)(2,1)}, f32[16,512]{1,0:T(8,128)}, f32[256,512]{1,0:T(8,128)}, f32[256,512]{1,0:T(8,128)}, f32[256,512]{1,0:T(8,128)}, /*index=5*/f32[256,512]{1,0:T(8,128)}) custom-call(bf16[2048,768]{1,0:T(8,128)(2,1)} %copy-done.3, bf16[1024,2048]{1,0:T(8,128)(2,1)} %get-tuple-element.85.tokens_ref, ...), custom_call_target="tpu_custom_call" | custom-call | flops 60000002048 | bytes 33554432 | tf_op jit(solution)/shard_map/leave/pallas_call | solution.py:1542
  755.4 1.4 fusion.2
  756.8 0.7 slice.54
  757.5 1.3 slice.58
  758.8 0.6 copy.32
  759.5 0.6 fusion.3
  760.0 2.3 copy.38
  762.3 1.9 copy.39
  764.2 1.9 copy.40
  766.0 0.8 copy.41
  766.8 0.8 copy.42
  (20 shorter events, 0.1 us)
Async XLA Ops:
  94.4 13.7 %copy-start.7 = (s32[8192]{0:T(1024)S(1)}, s32[8192]{0:T(1024)}, u32[]{:S(2)}) copy-start(s32[8192]{0:T(1024)} %param.15) | copy-start | bytes 98308
  94.4 13.7 %copy-start.8 = (bf16[2048]{0:T(1024)(128)(2,1)S(1)}, bf16[2048]{0:T(1024)(128)(2,1)}, u32[]{:S(2)}) copy-start(bf16[2048]{0:T(1024)(128)(2,1)} %param.24) | copy-start | bytes 12292
  94.4 14.3 %copy-start = (bf16[2048,768]{1,0:T(8,128)(2,1)S(1)}, bf16[2048,768]{1,0:T(8,128)(2,1)}, u32[]{:S(2)}) copy-start(bf16[2048,768]{1,0:T(8,128)(2,1)} %get-tuple-element.57.refs_0_.refs_1_.refs_2_) | copy-start | bytes 9437188
  96.9 38.3 %all-to-all-start = ((bf16[4,256,512]{2,1,0:T(8,128)(2,1)}), bf16[4,256,512]{2,1,0:T(8,128)(2,1)}, u32[]{:S(2)}, u32[]{:S(2)}) async-start(bf16[4,256,512]{2,1,0:T(8,128)(2,1)} %bitcast.19), calls=%async_computation | async-start | bytes 2097152 | tf_op jit(solution)/shard_map/all_to_all | solution.py:1591
  108.1 430.6 %reduce-scatter.3.cloned.1.call-start = ((), (), s32[]{:S(2)}) async-start(), calls=%async_computation.4 | async-start | bytes 9437184 | tf_op jit(solution)/shard_map/reduce_scatter | solution.py:1699
  131.4 1.0 copy-start.1
  409.6 202.4 %reduce-scatter.5.cloned.1.call-start = ((), (), s32[]{:S(2)}) async-start(), calls=%async_computation.5 | async-start | bytes 9437184 | tf_op jit(solution)/shard_map/reduce_scatter | solution.py:1699
  538.8 109.2 %all-to-all-start.1 = ((bf16[4,256,512]{2,1,0:T(8,128)(2,1)}), bf16[4,256,512]{2,1,0:T(8,128)(2,1)}, u32[]{:S(2)}, u32[]{:S(2)}) async-start(bf16[4,256,512]{2,1,0:T(8,128)(2,1)} %get-tuple-element.82), calls=%async_computation.2 | async-start | bytes 2097152 | tf_op jit(solution)/shard_map/all_to_all | solution.py:1598
  614.8 1.2 copy-start.2
  616.0 1.2 copy-start.4
  646.4 1.6 copy-start.3
  755.4 10.7 %copy-start.6 = (f32[256,512]{1,0:T(8,128)S(1)}, f32[256,512]{1,0:T(8,128)}, u32[]{:S(2)}) copy-start(f32[256,512]{1,0:T(8,128)} %get-tuple-element.131) | copy-start | bytes 1572868
  755.4 11.5 %copy-start.5 = (f32[256,512]{1,0:T(8,128)S(1)}, f32[256,512]{1,0:T(8,128)}, u32[]{:S(2)}) copy-start(f32[256,512]{1,0:T(8,128)} %get-tuple-element.132) | copy-start | bytes 1572868
Sparse Core Ops, SparseCore 0:
  409.7 73.3 reduce-scatter.2
  538.8 73.0 reduce-scatter.4

commit v9 on v8

--- a/solution.py
+++ b/solution.py
@@ -1756,6 +1756,7 @@
             grads, wide_tokens, wide_qkv, grad_inner, row_sums, hidden_sums[:1], branch_low,
             attended, 4,
         )
+        input_grad, expand_grad = lax.optimization_barrier((input_grad, expand_grad))
     else:
         input_grad, vectors = input_sum(
             qkv_low, wide_qkv, grad_inner, row_sums, hidden_sums[:1], 4

time: 774 us -> 721 us (0.932)
  waiting for transfers between devices: 58.4 us -> 0.06 us
    reduce_scatter x2, waiting for transfers between devices: 58.4 us -> 0.02 us  [owner_sum(): return lax.psum_scatter(grad, plane, scatter_dimension=0, tiled=True)]
  transfers between devices with their start and end apart: 4 -> 4, of which waited for: 1 -> 0; matrix products, arithmetic and copies ran while one was open for 2% -> 2% of each run, Pallas kernels for 23% -> 41%
where the time goes in v9:
time: 721 us; the launch traced here: 720 us
  Pallas kernels  635 us (88%)
  local copies, waits for them, and re-layouts  25.8 us (4%)
  starting transfers between devices  19.8 us (3%)
  between operations  14.2 us (2%)
  matrix products  14.1 us (2%)
  other arithmetic  10.6 us (1%)
    pallas_call x3, Pallas kernels, relay(): pl.pallas_call(functools.partial(relay_kernel, count, row_step, use_step,...  389 us
    pallas_call x1, Pallas kernels, leave(): pl.pallas_call(functools.partial(leave_kernel, sizes), out_shape=[jax.Sha...  111 us
    pallas_call x1, Pallas kernels, enter(): pl.pallas_call(functools.partial(enter_kernel, count), out_shape=[jax.Sha...  83.6 us
    pallas_call x1, Pallas kernels, attend_back(): pl.pallas_call(functools.partial(attend_back_kernel, len(scalars), len(ar...  29.1 us
    pallas_call x1, Pallas kernels, attend(): pl.pallas_call(functools.partial(attend_kernel, len(scalars)), out_shape=...  22.7 us
  transfers between devices with their start and end apart: 4, of which 0 were waited for; matrix products, arithmetic and copies ran while one was open for 2% of the time, Pallas kernels for 41%

profile of v9, /device:TPU:8, one launch (start us, length us, event | category | flops | bytes accessed | tf_op | source)
XLA Modules:
  0.0 719.7 jit_solution(13381298639648542060)
XLA Ops:
  7.2 0.7 stack.10
  7.9 0.7 stack.9
  8.6 0.1 pad.1.clone
  8.6 0.1 convert_bitcast_fusion
  8.7 0.6 reshape.64.bias
  9.3 0.1 pad.5.clone
  9.4 1.4 maximum_maximum_fusion.marks_ref
  10.8 83.6 %enter.1 = (bf16[1024,2048]{1,0:T(8,128)(2,1)}, bf16[256,2048]{1,0:T(8,128)(2,1)}, bf16[16,2048]{1,0:T(8,128)(2,1)}, bf16[2048,1536]{1,0:T(8,128)(2,1)}, bf16[20...) custom-call(bf16[1024,512]{1,0:T(8,128)(2,1)} %x_ref.1, bf16[16,512]{1,0:T(8,128)(2,1)} %maximum_maximum_fusion.marks_ref, ...), custom_call_target="tpu_custom_call" | custom-call | flops 80000000000 | bytes 134217728 | tf_op jit(solution)/shard_map/enter/pallas_call | solution.py:835
  94.4 0.0 copy-start.9
  94.4 0.0 copy-start.10
  94.4 2.5 copy.30
  96.9 11.3 %all-to-all-start = ((bf16[4,256,512]{2,1,0:T(8,128)(2,1)}), bf16[4,256,512]{2,1,0:T(8,128)(2,1)}, u32[]{:S(2)}, u32[]{:S(2)}) async-start(bf16[4,256,512]{2,1,0:T(8,128)(2,1)} %bitcast.19), calls=%async_computation | async-start | bytes 2097152 | tf_op jit(solution)/shard_map/all_to_all | solution.py:1591
  108.1 0.6 broadcast_in_dim.15
  108.7 22.7 %attend.1 = (bf16[2048,256]{1,0:T(8,128)(2,1)S(1)}, f32[2,1,2048]{2,1,0:T(1,128)S(1)}) custom-call(bf16[2048,768]{1,0:T(8,128)(2,1)S(1)} %copy-done, bf16[2048,768]{1,0:T(8,128)(2,1)S(1)} %copy-done, bf16[2048,768]{1,0:T(8,128)(2,1)S(1)} %copy-done, s32[4,2048]{1,0:T(4,128)S(1)} %reshape.57.refs_3_.refs_6_), custom_call_target="tpu_custom_call" | custom-call | flops 3221225472 | bytes 4194304 | tf_op jit(solution)/shard_map/attend/pallas_call | solution.py:118
  131.4 0.0 copy-start.1
  131.4 1.0 copy-done.1
  132.4 1.4 slice_convert_fusion.1.refs_4_.refs_6_
  133.8 1.4 slice_convert_fusion.refs_5_
  135.2 131.3 %first_norm.1 = (bf16[1024,2048]{1,0:T(8,128)(2,1)}, f32[256,2048]{1,0:T(8,128)}, f32[256,2048]{1,0:T(8,128)}, f32[256,128]{1,0:T(8,128)}, f32[1024,2048]{1,0:T(...) custom-call(bf16[2048,256]{1,0:T(8,128)(2,1)} %copy-done.1, ...), custom_call_target="tpu_custom_call" | custom-call | flops 99999997952 | bytes 134217728 | tf_op jit(solution)/shard_map/first_norm/pallas_call | solution.py:1067
  266.5 126.0 %second_norm.1 = (bf16[1024,2048]{1,0:T(8,128)(2,1)}, bf16[4,256,512]{2,1,0:T(8,128)(2,1)}, f32[256,2048]{1,0:T(8,128)}, f32[8,2048]{1,0:T(8,128)}, bf16[1024,2048]{1,0:T(8,128)(2,1)}, /*index=5*/f32[8,2048]{1,0:T(8,128)}) custom-call(bf16[1024,2048]{1,0:T(8,128)(2,1)} %get-tuple-element.66.refs_0_, bf16[2048,2048]{1,0:T(8,128)(2,1)} %get-tuple-element.67.refs_1_, ...), custom_call_target="tpu_custom_call" | custom-call | flops 99999997952 | bytes 134217728 | tf_op jit(solution)/shard_map/second_norm/pallas_call | solution.py:1067
  392.5 14.1 %convolution_convert_fusion = bf16[2048,2048]{1,0:T(8,128)(2,1)} fusion(bf16[1024,2048]{1,0:T(8,128)(2,1)} %get-tuple-element.72, bf16[1024,2048]{1,0:T(8,128)(2,1)} %get-tuple-element.66.refs_0_), kind=kOutput, calls=%fused_computation | convolution fusion | flops 8594128896 | bytes 16777216 | tf_op jit(solution)/shard_map/dot_general | solution.py:27
  406.6 0.0 reduce-scatter.3.cloned.1.call-update
  406.6 0.0 reduce-scatter.5.cloned.1.call-start
  406.6 132.0 %first_back.1 = (bf16[1024,2048]{1,0:T(8,128)(2,1)}, f32[256,2048]{1,0:T(8,128)}, f32[8,2048]{1,0:T(8,128)}, bf16[2048,256]{1,0:T(8,128)(2,1)}, bf16[2048,2048]{1,0:T(8,128)(2,1)}) custom-call(bf16[1024,2048]{1,0:T(8,128)(2,1)} %get-tuple-element.73.refs_0_, bf16[2048,2048]{1,0:T(8,128)(2,1)} %get-tuple-element.74.refs_1_, ...), custom_call_target="tpu_custom_call" | custom-call | flops 99999997952 | bytes 134217728 | tf_op jit(solution)/shard_map/first_back/pallas_call | solution.py:1067
  538.7 0.0 reduce-scatter.5.cloned.1.call-update
  538.7 0.0 reduce-scatter.3.cloned.1.call-done
  538.7 8.5 %all-to-all-start.1 = ((bf16[4,256,512]{2,1,0:T(8,128)(2,1)}), bf16[4,256,512]{2,1,0:T(8,128)(2,1)}, u32[]{:S(2)}, u32[]{:S(2)}) async-start(bf16[4,256,512]{2,1,0:T(8,128)(2,1)} %get-tuple-element.84), calls=%async_computation.2 | async-start | bytes 2097152 | tf_op jit(solution)/shard_map/all_to_all | solution.py:1598
  547.2 1.4 slice.53.hidden_ref
  548.6 1.1 fusion
  549.8 0.7 concatenate.8.rows_ref
  550.5 2.9 convert_element_type.22
  553.4 1.4 copy-done.2
  554.8 1.4 copy-done.4
  556.2 29.1 %attend_back.1.grads_ref = bf16[2048,768]{1,0:T(8,128)(2,1)S(1)} custom-call(bf16[2048,768]{1,0:T(8,128)(2,1)S(1)} %copy-done, bf16[2048,768]{1,0:T(8,128)(2,1)S(1)} %copy-done, bf16[2048,768]{1,0:T(8,128)(2,1)S(1)} %copy-done, bf16[2048,256]{1,0:T(8,128)(2,1)S(1)} %copy-done.2, bf16[2048,256]{1,0:T(8,128)(2,1)S(1)} %copy-done.4, ...), custom_call_target="tpu_custom_call" | custom-call | flops 8589934592 | bytes 8388608 | tf_op jit(solution)/shard_map/attend_back/pallas_call | solution.py:214
  585.3 1.7 copy-done.3
  587.0 2.3 copy.31
  589.3 110.6 %leave.1 = (bf16[1024,512]{1,0:T(8,128)(2,1)}, f32[16,512]{1,0:T(8,128)}, f32[256,512]{1,0:T(8,128)}, f32[256,512]{1,0:T(8,128)}, f32[256,512]{1,0:T(8,128)}, /*index=5*/f32[256,512]{1,0:T(8,128)}) custom-call(bf16[2048,768]{1,0:T(8,128)(2,1)} %copy-done.3, bf16[1024,2048]{1,0:T(8,128)(2,1)} %get-tuple-element.87.tokens_ref, ...), custom_call_target="tpu_custom_call" | custom-call | flops 60000002048 | bytes 33554432 | tf_op jit(solution)/shard_map/leave/pallas_call | solution.py:1542
  699.9 0.8 slice.54
  700.8 1.3 slice.58
  702.1 1.3 fusion.2
  703.4 2.8 convert_element_type.21
  706.3 0.6 copy.32
  706.9 0.6 fusion.3
  707.5 2.3 copy.38
  709.7 0.8 copy.39
  710.5 0.8 copy.40
  711.3 0.8 copy.41
  712.1 0.8 copy.42
  (24 shorter events, 0.1 us)
Async XLA Ops:
  94.4 13.7 %copy-start.9 = (s32[8192]{0:T(1024)S(1)}, s32[8192]{0:T(1024)}, u32[]{:S(2)}) copy-start(s32[8192]{0:T(1024)} %param.15) | copy-start | bytes 98308
  94.4 13.8 %copy-start.10 = (bf16[2048]{0:T(1024)(128)(2,1)S(1)}, bf16[2048]{0:T(1024)(128)(2,1)}, u32[]{:S(2)}) copy-start(bf16[2048]{0:T(1024)(128)(2,1)} %param.24) | copy-start | bytes 12292
  94.4 14.4 %copy-start = (bf16[2048,768]{1,0:T(8,128)(2,1)S(1)}, bf16[2048,768]{1,0:T(8,128)(2,1)}, u32[]{:S(2)}) copy-start(bf16[2048,768]{1,0:T(8,128)(2,1)} %get-tuple-element.59.refs_0_.refs_1_.refs_2_) | copy-start | bytes 9437188
  96.9 38.3 %all-to-all-start = ((bf16[4,256,512]{2,1,0:T(8,128)(2,1)}), bf16[4,256,512]{2,1,0:T(8,128)(2,1)}, u32[]{:S(2)}, u32[]{:S(2)}) async-start(bf16[4,256,512]{2,1,0:T(8,128)(2,1)} %bitcast.19), calls=%async_computation | async-start | bytes 2097152 | tf_op jit(solution)/shard_map/all_to_all | solution.py:1591
  108.1 430.6 %reduce-scatter.3.cloned.1.call-start = ((), (), s32[]{:S(2)}) async-start(), calls=%async_computation.4 | async-start | bytes 9437184 | tf_op jit(solution)/shard_map/reduce_scatter | solution.py:1699
  131.4 1.0 copy-start.1
  406.6 296.8 %reduce-scatter.5.cloned.1.call-start = ((), (), s32[]{:S(2)}) async-start(), calls=%async_computation.5 | async-start | bytes 9437184 | tf_op jit(solution)/shard_map/reduce_scatter | solution.py:1699
  538.7 48.3 %all-to-all-start.1 = ((bf16[4,256,512]{2,1,0:T(8,128)(2,1)}), bf16[4,256,512]{2,1,0:T(8,128)(2,1)}, u32[]{:S(2)}, u32[]{:S(2)}) async-start(bf16[4,256,512]{2,1,0:T(8,128)(2,1)} %get-tuple-element.84), calls=%async_computation.2 | async-start | bytes 2097152 | tf_op jit(solution)/shard_map/all_to_all | solution.py:1598
  553.4 1.4 copy-start.2
  554.8 1.4 copy-start.4
  585.3 1.7 copy-start.3
  699.9 9.8 %copy-start.8 = (f32[256,512]{1,0:T(8,128)S(1)}, f32[256,512]{1,0:T(8,128)}, u32[]{:S(2)}) copy-start(f32[256,512]{1,0:T(8,128)} %get-tuple-element.133) | copy-start | bytes 1572868
  699.9 10.6 %copy-start.7 = (f32[256,512]{1,0:T(8,128)S(1)}, f32[256,512]{1,0:T(8,128)}, u32[]{:S(2)}) copy-start(f32[256,512]{1,0:T(8,128)} %get-tuple-element.134) | copy-start | bytes 1572868
  699.9 11.4 %copy-start.6 = (f32[256,512]{1,0:T(8,128)S(1)}, f32[256,512]{1,0:T(8,128)}, u32[]{:S(2)}) copy-start(f32[256,512]{1,0:T(8,128)} %get-tuple-element.135) | copy-start | bytes 1572868
  703.4 8.7 %copy-start.5 = (f32[256,512]{1,0:T(8,128)S(1)}, f32[256,512]{1,0:T(8,128)}, u32[]{:S(2)}) copy-start(f32[256,512]{1,0:T(8,128)} %get-tuple-element.136) | copy-start | bytes 1572868
Sparse Core Ops, SparseCore 0:
  406.7 75.5 reduce-scatter.2
  538.8 79.4 reduce-scatter.4

commit v10 on v8

--- a/solution.py
+++ b/solution.py
@@ -372,24 +372,25 @@
         self.sum_slots, self.sum_sent, self.sum_got = sum_slots, sum_sent, sum_got
         self.spread_view, self.spread_sent, self.spread_got = spread_view, spread_sent, spread_got
 
+    def slot(self, piece):
+        return lax.rem(piece, self.sum_slots.shape[0])
+
     def sum_copy(self, piece, owner):
         onward = jnp.where(owner > self.me, self.me + 1, self.me - 1)
         place = jnp.where((owner < self.me) & (owner == self.me - 1), self.count, owner)
+        slot = self.slot(piece)
         return pltpu.make_async_remote_copy(
-            src_ref=self.sum_slots.at[piece, owner],
-            dst_ref=self.sum_slots.at[piece, place],
-            send_sem=self.sum_sent.at[piece, owner],
-            recv_sem=self.sum_got.at[piece, place],
+            src_ref=self.sum_slots.at[slot, owner],
+            dst_ref=self.sum_slots.at[slot, place],
+            send_sem=self.sum_sent.at[slot, owner],
+            recv_sem=self.sum_got.at[slot, place],
             device_id={"tp": onward},
             device_id_type=MESH,
         )
 
     def sum_arrival(self, piece, place):
-        pltpu.make_async_copy(
-            self.sum_slots.at[piece, place],
-            self.sum_slots.at[piece, place],
-            self.sum_got.at[piece, place],
-        ).wait()
+        view = self.sum_slots.at[self.slot(piece), place]
+        pltpu.make_async_copy(view, view, self.sum_got.at[self.slot(piece), place]).wait()
 
     def sum_start(self, piece, term):
         me, count = self.me, self.count
@@ -398,7 +399,7 @@
         def _():
             for k in range(count - 1):
                 owner = jnp.where(me == 0, count - 1 - k, k)
-                self.sum_slots[piece, owner] = term(owner).astype(jnp.bfloat16)
+                self.sum_slots[self.slot(piece), owner] = term(owner).astype(jnp.bfloat16)
                 self.sum_copy(piece, owner).start()
 
     def sum_onward(self, piece, term, distances):
@@ -410,8 +411,9 @@
 
                 def pass_on(owner):
                     self.sum_arrival(piece, owner)
-                    total = self.sum_slots[piece, owner].astype(jnp.float32) + term(owner)
-                    self.sum_slots[piece, owner] = total.astype(jnp.bfloat16)
+                    slot = self.slot(piece)
+                    total = self.sum_slots[slot, owner].astype(jnp.float32) + term(owner)
+                    self.sum_slots[slot, owner] = total.astype(jnp.bfloat16)
                     self.sum_copy(piece, owner).start()
 
                 at_distance(me, count, distance, pass_on)
@@ -422,21 +424,22 @@
         @pl.when(me > 0)
         def _():
             self.sum_arrival(piece, me)
-            total[...] += self.sum_slots[piece, me].astype(jnp.float32)
+            total[...] += self.sum_slots[self.slot(piece), me].astype(jnp.float32)
 
         @pl.when(me < count - 1)
         def _():
             self.sum_arrival(piece, count)
-            total[...] += self.sum_slots[piece, count].astype(jnp.float32)
+            total[...] += self.sum_slots[self.slot(piece), count].astype(jnp.float32)
+
+    def sum_sent_all(self, piece):
+        for distance in range(1, self.count):
+            at_distance(
+                self.me, self.count, distance,
+                lambda owner: self.sum_copy(piece, owner).wait_send(),
+            )
 
     def sum_finish(self, pieces):
-        @pl.loop(0, pieces)
-        def _(piece):
-            for distance in range(1, self.count):
-                at_distance(
-                    self.me, self.count, distance,
-                    lambda owner: self.sum_copy(piece, owner).wait_send(),
-                )
+        pl.loop(0, pieces)(self.sum_sent_all)
 
     def spread_copy(self, piece, owner, to, sent, source=None):
         return pltpu.make_async_remote_copy(
@@ -672,11 +675,6 @@
         for number in numbers:
             view = arrivals[number]
             pltpu.make_async_copy(view, view, self.got.at[number]).wait()
-
-    def put(self, shard, done):
-        copy = pltpu.make_async_copy(shard, self.shard(self.fsdp, self.ctx), done)
-        copy.start()
-        copy.wait()
 
     def first(self):
         self.start(1, 2, 0)
@@ -873,7 +871,7 @@
 
 
 def relay_kernel(count, row_step, use_step, sizes, *refs):
-    row_in, use_in, row_out, use_out, shared, swap_in, swap_out, gathers, fill_step = sizes
+    row_in, use_in, row_out, use_out, shared = sizes
     refs = list(refs)
 
     def take(number):
@@ -884,61 +882,22 @@
     x_ref, sum_weight = take(2)
     use_weight = sum_weight if shared else take(1)[0]
     row_inputs, use_inputs = take(row_in), take(use_in)
-    next_ref = take(1)[0] if gathers else None
-    fill_inputs = take(1) if fill_step is not None else []
     (gathered,) = take(1)
     row_outputs, use_outputs = take(row_out), take(use_out)
-    swapped = take(1)[0] if swap_in or swap_out else None
-    wholes = take(2) if gathers else []
-    fill_outputs = take(1) if fill_step is not None else []
-    terms, total, slots, sum_sent, sum_got, spread_sent, spread_got = take(7)
-    me, ctx = lax.axis_index("tp"), lax.axis_index("ctx")
-    rows = gathered.shape[0]
-    height = rows // PIECES
+    terms, total, slots, sum_sent, sum_got, spread_sent, spread_got = refs
+    me = lax.axis_index("tp")
+    height = x_ref.shape[0] // PIECES
     own = height // count
     width = sum_weight.shape[0]
 
-    def piece_rows(piece, start=0):
-        return pl.ds(pl.multiple_of(start + piece * height, height), height)
+    def piece_rows(piece):
+        return pl.ds(pl.multiple_of(piece * height, height), height)
 
     def view(piece, owner):
         return gathered.at[pl.ds(pl.multiple_of(piece * height + owner * own, own), own)]
 
     line = Line(me, count, slots, sum_sent, sum_got, view, spread_sent, spread_got)
-    use_gather = next_gather = None
-    if gathers:
-        use_gather, next_gather = [PlaneGather(whole, *take(2)) for whole in wholes]
-        greet(me, count, next_gather.peers())
-        shards, use_weight = (use_weight, next_ref), wholes[0]
-    else:
-        greet(me, count, [{"ctx": 1 - ctx}] if swap_in or swap_out else [])
-    swap = None
-    if swap_in:
-        half = x_ref.shape[1]
-        own_half = pl.ds(pl.multiple_of(ctx * half, half), half)
-        swap = Swap(
-            *take(2),
-            lambda piece: x_ref.at[piece_rows(piece, (1 - ctx) * rows)],
-            lambda piece: swapped.at[piece_rows(piece), own_half],
-        )
-
-        @pl.loop(0, PIECES)
-        def _(piece):
-            swap.start(piece)
-            swapped[piece_rows(piece), own_half] = x_ref[piece_rows(piece, ctx * rows), :]
-
-    if gathers:
-        for gather, shard in zip((use_gather, next_gather), shards, strict=True):
-            gather.put(shard, take(1)[0])
-        use_gather.first()
-    if swap_out:
-        stage, swap_sent, swap_got = take(3)
-        half = swapped.shape[1]
-        swap = Swap(
-            swap_sent, swap_got,
-            lambda piece: stage.at[piece_rows(piece)],
-            lambda piece: swapped.at[piece_rows(piece, ctx * rows)],
-        )
+    greet(me, count)
 
     @pl.loop(0, PIECES + 5)
     def _(step):
@@ -954,18 +913,10 @@
 
         def use(piece):
             part = piece_rows(piece)
-            result = use_step(part, gathered[part, :], use_weight, use_inputs, use_outputs)
-            if swap_out:
-                here = ctx == 0
-                left, right = result[:, :half], result[:, half:]
-                stage[part, :] = jnp.where(here, right, left)
-                swap.start(piece)
-                swapped[piece_rows(piece, ctx * rows), :] = jnp.where(here, left, right)
+            use_step(part, gathered[part, :], use_weight, use_inputs, use_outputs)
 
         def form(piece):
-            if swap_in:
-                swap.wait_arrival(piece)
-            x = (swapped if swap_in else x_ref)[piece_rows(piece), :]
+            x = x_ref[piece_rows(piece), :]
 
             @pl.loop(0, width // TILE)
             def _(tile):
@@ -980,104 +931,44 @@
             view(piece, me)[...] = row_step(piece, total, row_inputs, row_outputs)
             line.spread_start(piece)
 
-        def far_shards(piece):
-            for distance in range(3, count):
-                line.spread_onward(piece, distance)
-
-        if gathers:
-            pl.when(step == 5)(use_gather.last)
         late(5, use)
         late(3, lambda piece: line.spread_onward(piece, 2))
         late(1, lambda piece: line.sum_onward(piece, term_of(1 - odd), [1]))
         late(0, form)
-        late(4, far_shards)
+        late(4, lambda piece: [line.spread_onward(piece, i) for i in range(3, count)])
         late(2, lambda piece: line.spread_onward(piece, 1))
-        if fill_step is not None:
-            late(0, lambda piece: fill_step(piece, x_ref, fill_inputs, fill_outputs))
         late(0, lambda piece: line.sum_onward(piece, term_of(odd), range(count - 2, 1, -1)))
         late(1, own_step)
-        if gathers:
-
-            @pl.when(step == 3)
-            def _():
-                use_gather.second()
-                next_gather.first()
-
-            pl.when(step == 4)(use_gather.third)
-            pl.when(step == 6)(next_gather.second)
-            pl.when(step == 8)(next_gather.third)
-
-    if swap is not None:
-
-        @pl.loop(0, PIECES)
-        def _(piece):
-            if swap_out:
-                swap.wait_arrival(piece)
-            swap.wait_sent(piece)
-
-    if gathers:
-        next_gather.last()
-        use_gather.wait_sent()
-        next_gather.wait_sent()
+
     line.sum_finish(PIECES)
     line.spread_finish(PIECES)
 
 
 def relay(
     x, sum_weight, use_weight, row_inputs, row_step, row_shapes, use_inputs, use_step, use_shapes,
-    collective_id, name, rows, swap_in=None, swap_out=None, next_shard=None, fill=None,
+    collective_id, name,
 ):
     count = lax.axis_size("tp")
+    rows = x.shape[0]
     width = sum_weight.shape[0]
     height = rows // PIECES
     own = height // count
     shared = use_weight is None
     operands = [x, sum_weight, *([] if shared else [use_weight]), *row_inputs, *use_inputs]
-    in_specs = [pl.BlockSpec(memory_space=pltpu.VMEM)] * len(operands)
     shapes = [jax.ShapeDtypeStruct((rows, width), jnp.bfloat16), *row_shapes, *use_shapes]
-    shapes += [shape for shape in (swap_in, swap_out) if shape is not None]
-    out_specs = [pl.BlockSpec(memory_space=pltpu.VMEM)] * len(shapes)
-    extra, last = [], []
-    if next_shard is not None:
-        operands.append(next_shard)
-        in_specs.append(pl.BlockSpec(memory_space=pltpu.VMEM))
-        for shard, space in ((use_weight, pltpu.VMEM), (next_shard, pl.ANY)):
-            whole = (8 * shard.shape[0], shard.shape[1])
-            shapes.append(jax.ShapeDtypeStruct(whole, shard.dtype))
-            out_specs.append(pl.BlockSpec(memory_space=space))
-        extra = [pltpu.SemaphoreType.DMA((9,))] * 4
-        last = [pltpu.SemaphoreType.DMA] * 2
-    fill_step = None
-    if fill is not None:
-        fill_step, fill_input, fill_shape = fill
-        operands.append(fill_input)
-        in_specs.append(pl.BlockSpec(memory_space=pltpu.VMEM))
-        shapes.append(fill_shape)
-        out_specs.append(pl.BlockSpec(memory_space=pltpu.VMEM))
     sums, spreads = line_semaphores(count, PIECES)
-    swaps = []
-    if swap_out is not None:
-        swaps.append(pltpu.VMEM((rows, swap_out.shape[1]), swap_out.dtype))
-    if swap_in is not None or swap_out is not None:
-        swaps += [pltpu.SemaphoreType.DMA((PIECES,))] * 2
-    sizes = (
-        len(row_inputs), len(use_inputs), len(row_shapes), len(use_shapes), shared,
-        swap_in is not None, swap_out is not None, next_shard is not None, fill_step,
-    )
+    sizes = (len(row_inputs), len(use_inputs), len(row_shapes), len(use_shapes), shared)
     return pl.pallas_call(
         functools.partial(relay_kernel, count, row_step, use_step, sizes),
         out_shape=shapes,
-        in_specs=in_specs,
-        out_specs=out_specs,
+        in_specs=[pl.BlockSpec(memory_space=pltpu.VMEM)] * len(operands),
+        out_specs=[pl.BlockSpec(memory_space=pltpu.VMEM)] * len(shapes),
         scratch_shapes=[
             pltpu.VMEM((2, height, width), jnp.float32),
             pltpu.VMEM((own, width), jnp.float32),
             pltpu.VMEM((PIECES, count + 1, own, width), jnp.bfloat16),
             *sums,
             *spreads,
-            *extra,
-            *swaps,
-            *last,
         ],
         compiler_params=pltpu.CompilerParams(
             collective_id=collective_id, has_side_effects=True, vmem_limit_bytes=60 << 20
@@ -1185,22 +1076,320 @@
 
 
 def attended_step(rows, chunk, weight, inputs, outputs):
-    result = dot_plain(chunk, weight[...]).astype(jnp.bfloat16)
-    if outputs:
-        outputs[0][rows, :] = result
-    return result
-
-
-def expand_product_step(piece, x, inputs, outputs):
-    (norm_low,), (product,) = inputs, outputs
-    height = product.shape[0] // PIECES
-    part = pl.ds(pl.multiple_of(piece * height, height), height)
-    left = norm_low[:, part].T
-
-    @pl.loop(0, product.shape[1] // TILE)
-    def _(tile):
-        columns = pl.ds(pl.multiple_of(tile * TILE, TILE), TILE)
-        product[part, columns] = dot_plain(left, x[:, columns]).astype(product.dtype)
+    (attended_grad,) = outputs
+    attended_grad[rows, :] = dot_plain(chunk, weight[...]).astype(jnp.bfloat16)
+
+
+def middle_kernel(
+    count, heads_ref, output_weight, expand_shard, shrink_shard, own_tokens, out_grad, gains,
+    biases, hidden_bias,
+    attended, mixed, inner, branch_out, grad_heads, first_sums, second_sums, hidden_sums,
+    shrink_out, expand_out,
+    expand_weight, shrink_weight, gathered, activated, slope, normed_one, inverse_one,
+    terms, total, slots, stage, shrink_stage, expand_stage,
+    sum_sent, sum_got, spread_sent, spread_got, expand_sent, expand_got, shrink_sent, shrink_got,
+    in_sent, in_got, out_sent, out_got, put_done, branch_done, product_done,
+):
+    me, ctx = lax.axis_index("tp"), lax.axis_index("ctx")
+    rows, width = gathered.shape[0] // 3, gathered.shape[1]
+    half = heads_ref.shape[1]
+    height = rows // PIECES
+    own = height // count
+    shard = width // PIECES
+    pieces = 3 * PIECES
+
+    def piece_rows(piece, start=0):
+        return pl.ds(pl.multiple_of(start + piece * height, height), height)
+
+    def view(piece, owner):
+        return gathered.at[pl.ds(pl.multiple_of(piece * height + owner * own, own), own)]
+
+    line = Line(me, count, slots, sum_sent, sum_got, view, spread_sent, spread_got)
+    expand_gather = PlaneGather(expand_weight, expand_sent, expand_got)
+    shrink_gather = PlaneGather(shrink_weight, shrink_sent, shrink_got)
+    own_half = pl.ds(pl.multiple_of(ctx * half, half), half)
+    own_block = pl.ds(pl.multiple_of(ctx * rows, rows), rows)
+    puts = [
+        pltpu.make_async_copy(source, place, put_done.at[i])
+        for i, (source, place) in enumerate(
+            (
+                (heads_ref.at[own_block], attended.at[:, own_half]),
+                (expand_shard, expand_gather.shard(expand_gather.fsdp, ctx)),
+                (shrink_shard, shrink_gather.shard(shrink_gather.fsdp, ctx)),
+            )
+        )
+    ]
+    for put in puts:
+        put.start()
+    swap_in = Swap(
+        in_sent, in_got,
+        lambda piece: heads_ref.at[piece_rows(piece, (1 - ctx) * rows)],
+        lambda piece: attended.at[piece_rows(piece), own_half],
+    )
+    swap_out = Swap(
+        out_sent, out_got,
+        lambda piece: stage.at[piece_rows(piece)],
+        lambda piece: grad_heads.at[piece_rows(piece, ctx * rows)],
+    )
+    greet(me, count, expand_gather.peers())
+    pl.loop(0, PIECES)(swap_in.start)
+    for put in puts:
+        put.wait()
+    expand_gather.first()
+
+    def branch_copy(piece):
+        part = piece_rows(piece)
+        return pltpu.make_async_copy(
+            gathered.at[piece_rows(piece, 2 * rows)], branch_out.at[part], branch_done.at[piece]
+        )
+
+    def in_stage(piece, number):
+        return (piece >= number * PIECES) & (piece < (number + 1) * PIECES)
+
+    def tiles(extent, action):
+        @pl.loop(0, extent // TILE)
+        def _(tile):
+            action(pl.ds(pl.multiple_of(tile * TILE, TILE), TILE))
+
+    def use(piece):
+        line.sum_sent_all(piece)
+        part = piece_rows(lax.rem(piece, PIECES))
+        chunk_rows = piece_rows(piece)
+
+        @pl.when(in_stage(piece, 0))
+        def _():
+            chunk = gathered[chunk_rows, :]
+
+            def expand(columns):
+                values = dot_plain(chunk, expand_weight[:, columns]) + hidden_bias[:, columns]
+                result, bend = gelu_with_slope(values)
+                activated[part, columns] = result.astype(jnp.bfloat16)
+                slope[part, columns] = bend.astype(jnp.bfloat16)
+
+            tiles(activated.shape[1], expand)
+
+        @pl.when(in_stage(piece, 1))
+        def _():
+            chunk = gathered[chunk_rows, :]
+
+            def shrink(columns):
+                grad = dot_plain(chunk, shrink_weight[:, columns])
+                low = (grad * slope[part, columns].astype(jnp.float32)).astype(jnp.bfloat16)
+                slope[part, columns] = low
+                added = jnp.sum(low.astype(jnp.float32), axis=0, keepdims=True)
+                before = jnp.where(piece == PIECES, 0.0, hidden_sums[0:1, columns])
+                hidden_sums[0:1, columns] = before + added
+
+            tiles(slope.shape[1], shrink)
+
+        @pl.when(in_stage(piece, 2))
+        def _():
+            place = piece - 2 * PIECES
+            result = dot_plain(gathered[chunk_rows, :], output_weight[...]).astype(jnp.bfloat16)
+            here = ctx == 0
+            left, right = result[:, :half], result[:, half:]
+            stage[part, :] = jnp.where(here, right, left)
+            swap_out.start(place)
+            grad_heads[piece_rows(place, ctx * rows), :] = jnp.where(here, left, right)
+            branch_copy(place).start()
+
+    def form(piece):
+        part = piece_rows(lax.rem(piece, PIECES))
+        parity = lax.rem(piece, 2)
+
+        def products(x, weight):
+            def product(columns):
+                terms[parity, :, columns] = dot_cols(x, weight[columns, :])
+
+            tiles(width, product)
+
+        @pl.when(in_stage(piece, 0))
+        def _():
+            swap_in.wait_arrival(piece)
+            products(attended[part, :], output_weight)
+
+        @pl.when(in_stage(piece, 1))
+        def _():
+            products(activated[part, :], shrink_weight)
+
+        @pl.when(in_stage(piece, 2))
+        def _():
+            products(slope[part, :], expand_weight)
+
+        line.sum_start(piece, term_of(piece))
+
+    def term_of(piece):
+        parity = lax.rem(piece, 2)
+        return lambda owner: terms[parity, pl.ds(pl.multiple_of(owner * own, own), own), :]
+
+    def own_step(piece):
+        place = lax.rem(piece, PIECES)
+        total[...] = term_of(piece)(me)
+        line.sum_end(piece, total)
+
+        @pl.when(in_stage(piece, 0))
+        def _():
+            view(piece, me)[...] = first_norm_step(
+                place, total, (own_tokens, gains, biases), (inner, normed_one, inverse_one)
+            )
+
+        @pl.when(in_stage(piece, 1))
+        def _():
+            view(piece, me)[...] = second_norm_step(
+                place, total, (inner, out_grad, gains, biases), (mixed, inner, second_sums)
+            )
+
+        @pl.when(in_stage(piece, 2))
+        def _():
+            view(piece, me)[...] = first_back_step(
+                place, total, (inner, normed_one, inverse_one, gains), (inner, first_sums)
+            )
+
+        line.spread_start(piece)
+
+    def gradient(left_start, right, place, out, done):
+        def copy(number):
+            part = pl.ds(pl.multiple_of(number * shard, shard), shard)
+            return pltpu.make_async_copy(place, out.at[part], done)
+
+        def step(number):
+            pl.when(number > 0)(lambda: copy(number - 1).wait())
+            columns = pl.ds(pl.multiple_of(number * shard, shard), shard)
+            left = gathered[left_start : left_start + rows, columns].T
+
+            def product(part):
+                place[:, part] = dot_plain(left, right[:, part]).astype(place.dtype)
+
+            tiles(place.shape[1], product)
+            copy(number).start()
+
+        return step, copy
+
+    shrink_step, shrink_copy = gradient(
+        rows, activated, shrink_stage, shrink_out, product_done.at[0]
+    )
+    expand_step, expand_copy = gradient(0, slope, expand_stage, expand_out, product_done.at[1])
+
+    @pl.loop(0, pieces + 5)
+    def _(step):
+        def late(number, action, most=pieces):
+            @pl.when((step >= number) & (step < most + number))
+            def _():
+                action(step - number)
+
+        pl.when(step == 5)(expand_gather.last)
+        late(5, use)
+        late(3, lambda piece: line.spread_onward(piece, 2))
+        late(1, lambda piece: line.sum_onward(piece, term_of(piece), [1]))
+        pl.when(step == PIECES)(shrink_gather.last)
+        late(0, form)
+        late(4, lambda piece: [line.spread_onward(piece, i) for i in range(3, count)])
+        late(2, lambda piece: line.spread_onward(piece, 1))
+        late(2 * PIECES + 4, shrink_step, PIECES)
+        late(2 * PIECES + 5, expand_step, PIECES)
+        late(0, lambda piece: line.sum_onward(piece, term_of(piece), range(count - 2, 1, -1)))
+        late(1, own_step)
+
+        @pl.when(step == 3)
+        def _():
+            expand_gather.second()
+            shrink_gather.first()
+
+        pl.when(step == 4)(expand_gather.third)
+        pl.when(step == 6)(shrink_gather.second)
+        pl.when(step == 7)(shrink_gather.third)
+
+    shrink_copy(PIECES - 1).wait()
+    expand_copy(PIECES - 1).wait()
+
+    @pl.loop(0, PIECES)
+    def _(piece):
+        branch_copy(piece).wait()
+        swap_in.wait_sent(piece)
+        swap_out.wait_arrival(piece)
+        swap_out.wait_sent(piece)
+
+    expand_gather.wait_sent()
+    shrink_gather.wait_sent()
+    line.spread_finish(pieces)
+
+
+def gelu_with_slope(values):
+    scale = math.sqrt(2.0 / math.pi)
+    square = values * values
+    bend = 0.5 * jnp.tanh(scale * values * (1.0 + 0.044715 * square)) + 0.5
+    inner = (2 * scale) * (1.0 + 3 * 0.044715 * square)
+    result = values * bend
+    return result, bend + result * (1.0 - bend) * inner
+
+
+def middle(
+    attended_heads, output_weight, expand_shard, shrink_shard, own_tokens, out_grad, gains, biases,
+    hidden_bias, collective_id,
+):
+    count = lax.axis_size("tp")
+    rows = attended_heads.shape[0] // 2
+    half = attended_heads.shape[1]
+    own_rows, width = own_tokens.shape
+    hidden = expand_shard.shape[1]
+    height = rows // PIECES
+    own = height // count
+    shard = width // PIECES
+    low = jnp.bfloat16
+    vmem, anywhere = pl.BlockSpec(memory_space=pltpu.VMEM), pl.BlockSpec(memory_space=pl.ANY)
+
+    def shape(extent, kind=jnp.float32):
+        return jax.ShapeDtypeStruct(extent, kind)
+
+    return pl.pallas_call(
+        functools.partial(middle_kernel, count),
+        out_shape=[
+            shape((rows, 2 * half), low),
+            shape(out_grad.shape, low),
+            shape((own_rows, width)),
+            shape((rows, width), low),
+            shape((2 * rows, half), low),
+            shape((8, width)),
+            shape((8, width)),
+            shape((8, hidden)),
+            shape((width, hidden), low),
+            shape((width, hidden), low),
+        ],
+        in_specs=[anywhere, vmem, anywhere, anywhere, vmem, vmem, vmem, vmem, vmem],
+        out_specs=[vmem, vmem, vmem, anywhere, vmem, vmem, vmem, vmem, anywhere, anywhere],
+        scratch_shapes=[
+            pltpu.VMEM((width, hidden), low),
+            pltpu.VMEM((width, hidden), low),
+            pltpu.VMEM((3 * rows, width), low),
+            pltpu.VMEM((rows, hidden), low),
+            pltpu.VMEM((rows, hidden), low),
+            pltpu.VMEM((own_rows, width), jnp.float32),
+            pltpu.VMEM((own_rows, 128), jnp.float32),
+            pltpu.VMEM((2, height, width), jnp.float32),
+            pltpu.VMEM((own, width), jnp.float32),
+            pltpu.VMEM((PIECES, count + 1, own, width), low),
+            pltpu.VMEM((rows, half), low),
+            pltpu.VMEM((shard, hidden), low),
+            pltpu.VMEM((shard, hidden), low),
+            *line_semaphores(count, PIECES)[0],
+            *line_semaphores(count, 3 * PIECES)[1],
+            *[pltpu.SemaphoreType.DMA((9,))] * 4,
+            *[pltpu.SemaphoreType.DMA((PIECES,))] * 4,
+            pltpu.SemaphoreType.DMA((3,)),
+            pltpu.SemaphoreType.DMA((PIECES,)),
+            pltpu.SemaphoreType.DMA((2,)),
+        ],
+        compiler_params=pltpu.CompilerParams(
+            collective_id=collective_id, has_side_effects=True, vmem_limit_bytes=62 << 20
+        ),
+        cost_estimate=pl.CostEstimate(
+            flops=300_000_000_000, bytes_accessed=192 * rows * width, transcendentals=0
+        ),
+        name="middle",
+    )(
+        attended_heads, output_weight, expand_shard, shrink_shard, own_tokens, out_grad, gains,
+        biases, hidden_bias,
+    )
 
 
 def peers_in_plane(sizes):
@@ -1672,60 +1861,55 @@
         return jax.ShapeDtypeStruct(extent, kind)
 
     own_shape = shape((own_rows, features))
-    norm_low, first_norm, normed_one, inverse_one, hidden, activated, *more = relay(
-        attended_heads, full_output, expand_weight if by_heads else full_expand,
-        [own_tokens, gains, biases], first_norm_step,
-        [own_shape, own_shape, shape((own_rows, 128))],
-        [hidden_bias.astype(jnp.float32)[None]], expand_step,
-        [shape((rows, hidden_cols)), shape((rows, hidden_cols), jnp.bfloat16)],
-        1, "first_norm", rows,
-        swap_in=shape((rows, head_cols), jnp.bfloat16) if by_heads else None,
-        next_shard=shrink_weight if by_heads else None,
-    )
-    if by_heads:
-        attended, full_expand, full_shrink = more
-    else:
-        attended, full_shrink = attended_heads, weight_rows(shrink_weight)
-    ffn_low, mixed_own, grad_second, second_sums, hidden_low, hidden_sums = relay(
-        activated, full_shrink, None,
-        [first_norm, upstream, gains, biases], second_norm_step,
-        [shape(upstream.shape, jnp.bfloat16), own_shape, shape((8, features))],
-        [hidden], shrink_step,
-        [shape((rows, hidden_cols), jnp.bfloat16), shape((8, hidden_cols))],
-        2, "second_norm", rows,
-    )
-
     def owner_sum(grad):
         return lax.psum_scatter(
             grad, plane, scatter_dimension=0, tiled=True
         )
 
-    hidden_low, shrink_part = lax.optimization_barrier(
-        (hidden_low, dot_rows(ffn_low, activated).astype(jnp.bfloat16))
-    )
-    shrink_grad = owner_sum(shrink_part)
-    branch_low, grad_inner, first_sums, attended_grad, expand_part = relay(
-        hidden_low, full_expand, full_output,
-        [grad_second, normed_one, inverse_one, gains], first_back_step,
-        [own_shape, shape((8, features))],
-        [], attended_step,
-        [] if by_heads else [shape((rows, head_cols), jnp.bfloat16)],
-        3, "first_back", rows,
-        swap_out=shape((2 * rows, head_cols // 2), jnp.bfloat16) if by_heads else None,
-        fill=(expand_product_step, norm_low, shape((features, hidden_cols), jnp.bfloat16)),
-    )
-    expand_grad = owner_sum(expand_part)
-    attended_grad, mixed_own, shrink_grad = lax.optimization_barrier(
-        (attended_grad, mixed_own, shrink_grad)
-    )
-    mixed = unspread_own(mixed_own)
-
     if by_heads:
+        (
+            attended, mixed_own, grad_inner, branch_low, attended_grad,
+            first_sums, second_sums, hidden_sums, shrink_part, expand_part,
+        ) = middle(
+            attended_heads, full_output, expand_weight, shrink_weight, own_tokens, upstream,
+            gains, biases, hidden_bias.astype(jnp.float32)[None], 1,
+        )
+        shrink_grad, expand_grad = owner_sum(shrink_part), owner_sum(expand_part)
+        mixed = unspread_own(mixed_own)
         (grads,) = attend_back(
             queries, keys, values, attended_heads, attended_grad, lse, bounds, places, True
         )
         grads, mixed = lax.optimization_barrier((grads, mixed))
     else:
+        full_shrink = weight_rows(shrink_weight)
+        norm_low, first_norm, normed_one, inverse_one, hidden, activated = relay(
+            attended_heads, full_output, full_expand,
+            [own_tokens, gains, biases], first_norm_step,
+            [own_shape, own_shape, shape((own_rows, 128))],
+            [hidden_bias.astype(jnp.float32)[None]], expand_step,
+            [shape((rows, hidden_cols)), shape((rows, hidden_cols), jnp.bfloat16)],
+            1, "first_norm",
+        )
+        ffn_low, mixed_own, grad_second, second_sums, hidden_low, hidden_sums = relay(
+            activated, full_shrink, None,
+            [first_norm, upstream, gains, biases], second_norm_step,
+            [shape(upstream.shape, jnp.bfloat16), own_shape, shape((8, features))],
+            [hidden], shrink_step,
+            [shape((rows, hidden_cols), jnp.bfloat16), shape((8, hidden_cols))],
+            2, "second_norm",
+        )
+        shrink_grad = owner_sum(dot_rows(ffn_low, activated).astype(jnp.bfloat16))
+        branch_low, grad_inner, first_sums, attended_grad = relay(
+            hidden_low, full_expand, full_output,
+            [grad_second, normed_one, inverse_one, gains], first_back_step,
+            [own_shape, shape((8, features))],
+            [], attended_step,
+            [shape((rows, head_cols), jnp.bfloat16)],
+            3, "first_back",
+        )
+        expand_grad = owner_sum(dot_rows(norm_low, hidden_low).astype(jnp.bfloat16))
+        output_grad = owner_sum(dot_rows(branch_low, attended_heads).astype(jnp.bfloat16))
+        mixed = unspread_own(mixed_own)
         query_low, key_ext, value_ext = attend_back(
             queries, keys, values, attended_heads, attended_grad, lse, bounds
         )
@@ -1756,11 +1940,13 @@
             grads, wide_tokens, wide_qkv, grad_inner, row_sums, hidden_sums[:1], branch_low,
             attended, 4,
         )
+        input_grad, shrink_grad, expand_grad = lax.optimization_barrier(
+            (input_grad, shrink_grad, expand_grad)
+        )
     else:
         input_grad, vectors = input_sum(
             qkv_low, wide_qkv, grad_inner, row_sums, hidden_sums[:1], 4
         )
-        output_grad = owner_sum(dot_rows(branch_low, attended).astype(jnp.bfloat16))
         qkv_grad = owner_sum(dot_rows(wide_tokens, qkv_low).astype(jnp.bfloat16))
         query_grad, key_grad, value_grad = by_kind(qkv_grad.astype(jnp.float32))
     hidden_rows = hidden_cols // head_cols

time: 774 us -> 655 us (0.85)
  waiting for transfers between devices: 58.4 us -> 6.69 us
  Pallas kernels: 630 us -> 580 us
  matrix products: 14.1 us -> 0 us
    pallas_call x3 -> x1, Pallas kernels: 389 us -> 321 us  [middle(): pl.pallas_call(functools.partial(middle_kernel, count), out_shape=[shape(...]
    reduce_scatter x2, waiting for transfers between devices: 58.4 us -> 5.99 us  [owner_sum(): return lax.psum_scatter(grad, plane, scatter_dimension=0, tiled=True)]
    pallas_call x1, Pallas kernels: 105 us -> 123 us  [leave(): pl.pallas_call(functools.partial(leave_kernel, sizes), out_shape=[jax.Sha...]
    dot_general x1 -> x0, matrix products: 14.1 us -> none  [dot_rows(): lax.dot_general(left, right, (((0,), (0,)), ((), ())), preferred_element_...]
  transfers between devices with their start and end apart: 4 -> 4, of which waited for: 1 -> 1; matrix products, arithmetic and copies ran while one was open for 2% -> 2% of each run, Pallas kernels for 23% -> 27%
where the time goes in v10:
time: 655 us; the launch traced here: 653 us
  Pallas kernels  580 us (89%)
  local copies, waits for them, and re-layouts  24.6 us (4%)
  starting transfers between devices  18.5 us (3%)
  between operations  14.2 us (2%)
  other arithmetic  9.25 us (1%)
  waiting for transfers between devices  6.69 us (1%)
    pallas_call x1, Pallas kernels, middle(): pl.pallas_call(functools.partial(middle_kernel, count), out_shape=[shape(...  321 us
    pallas_call x1, Pallas kernels, leave(): pl.pallas_call(functools.partial(leave_kernel, sizes), out_shape=[jax.Sha...  123 us
    pallas_call x1, Pallas kernels, enter(): pl.pallas_call(functools.partial(enter_kernel, count), out_shape=[jax.Sha...  83.7 us
    pallas_call x1, Pallas kernels, attend_back(): pl.pallas_call(functools.partial(attend_back_kernel, len(scalars), len(ar...  29.1 us
    pallas_call x1, Pallas kernels, attend(): pl.pallas_call(functools.partial(attend_kernel, len(scalars)), out_shape=...  22.7 us
  transfers between devices with their start and end apart: 4, of which 1 were waited for; matrix products, arithmetic and copies ran while one was open for 2% of the time, Pallas kernels for 27%

profile of v10, /device:TPU:8, one launch (start us, length us, event | category | flops | bytes accessed | tf_op | source)
XLA Modules:
  0.0 653.3 jit_solution(9479798746106998610)
XLA Ops:
  7.2 0.7 stack.10
  7.9 0.7 stack.9
  8.6 0.1 pad.1.clone
  8.6 0.1 convert_bitcast_fusion
  8.7 0.6 reshape.64.bias
  9.3 0.1 pad.5.clone
  9.4 1.4 maximum_maximum_fusion.marks_ref
  10.8 83.7 %enter.1 = (bf16[1024,2048]{1,0:T(8,128)(2,1)}, bf16[256,2048]{1,0:T(8,128)(2,1)}, bf16[16,2048]{1,0:T(8,128)(2,1)}, bf16[2048,1536]{1,0:T(8,128)(2,1)}, bf16[20...) custom-call(bf16[1024,512]{1,0:T(8,128)(2,1)} %x_ref.1, bf16[16,512]{1,0:T(8,128)(2,1)} %maximum_maximum_fusion.marks_ref, ...), custom_call_target="tpu_custom_call" | custom-call | flops 80000000000 | bytes 134217728 | tf_op jit(solution)/shard_map/enter/pallas_call | solution.py:833
  94.5 0.0 copy-start.14
  94.6 0.0 copy-start.15
  94.6 2.5 copy.30
  97.0 11.3 %all-to-all-start = ((bf16[4,256,512]{2,1,0:T(8,128)(2,1)}), bf16[4,256,512]{2,1,0:T(8,128)(2,1)}, u32[]{:S(2)}, u32[]{:S(2)}) async-start(bf16[4,256,512]{2,1,0:T(8,128)(2,1)} %bitcast.17), calls=%async_computation | async-start | bytes 2097152 | tf_op jit(solution)/shard_map/all_to_all | solution.py:1780
  108.3 0.0 copy-start
  108.3 0.6 broadcast_in_dim.15
  109.0 22.7 %attend.1 = (bf16[2048,256]{1,0:T(8,128)(2,1)S(1)}, f32[2,1,2048]{2,1,0:T(1,128)S(1)}) custom-call(bf16[2048,768]{1,0:T(8,128)(2,1)S(1)} %copy-done.2, bf16[2048,768]{1,0:T(8,128)(2,1)S(1)} %copy-done.2, bf16[2048,768]{1,0:T(8,128)(2,1)S(1)} %copy-done.2, s32[4,2048]{1,0:T(4,128)S(1)} %reshape.57.refs_3_.refs_6_), custom_call_target="tpu_custom_call" | custom-call | flops 3221225472 | bytes 4194304 | tf_op jit(solution)/shard_map/attend/pallas_call | solution.py:118
  131.7 0.0 copy-start.4
  131.7 1.0 copy-done.4
  132.6 1.4 slice_convert_fusion.1.gains
  134.0 1.4 slice_convert_fusion.biases
  135.4 0.0 all-to-all-done.out_grad
  135.4 321.0 %middle.1 = (bf16[1024,512]{1,0:T(8,128)(2,1)}, bf16[4,256,512]{2,1,0:T(8,128)(2,1)}, f32[256,2048]{1,0:T(8,128)}, bf16[1024,2048]{1,0:T(8,128)(2,1)}, bf16[2048...) custom-call(bf16[2048,256]{1,0:T(8,128)(2,1)} %copy-done.4, ...), custom_call_target="tpu_custom_call" | custom-call | flops 299999985664 | bytes 402653184 | tf_op jit(solution)/shard_map/middle/pallas_call | solution.py:1344
  456.4 0.0 reduce-scatter.3.cloned.1.call-update
  456.4 0.0 reduce-scatter.5.cloned.1.call-start
  456.5 0.0 copy-start.1
  456.5 0.7 reduce-scatter.5.cloned.1.call-update
  457.2 7.2 %all-to-all-start.1 = ((bf16[4,256,512]{2,1,0:T(8,128)(2,1)}), bf16[4,256,512]{2,1,0:T(8,128)(2,1)}, u32[]{:S(2)}, u32[]{:S(2)}) async-start(bf16[4,256,512]{2,1,0:T(8,128)(2,1)} %get-tuple-element.55), calls=%async_computation.1 | async-start | bytes 2097152 | tf_op jit(solution)/shard_map/all_to_all | solution.py:1787
  464.3 1.5 slice.53.hidden_ref
  465.8 1.2 fusion
  467.0 0.7 concatenate.8.rows_ref
  467.7 1.5 copy-done.5
  469.2 1.5 copy-done.7
  470.6 29.1 %attend_back.1.grads_ref = bf16[2048,768]{1,0:T(8,128)(2,1)S(1)} custom-call(bf16[2048,768]{1,0:T(8,128)(2,1)S(1)} %copy-done.3, bf16[2048,768]{1,0:T(8,128)(2,1)S(1)} %copy-done.3, bf16[2048,768]{1,0:T(8,128)(2,1)S(1)} %copy-done.3, bf16[2048,256]{1,0:T(8,128)(2,1)S(1)} %copy-done.5, bf16[2048,256]{1,0:T(8,128)(2,1)S(1)} %copy-done.7, ...), custom_call_target="tpu_custom_call" | custom-call | flops 8589934592 | bytes 8388608 | tf_op jit(solution)/shard_map/attend_back/pallas_call | solution.py:214
  499.8 1.6 copy-done.6
  501.4 2.3 copy.31
  503.7 123.5 %leave.1 = (bf16[1024,512]{1,0:T(8,128)(2,1)}, f32[16,512]{1,0:T(8,128)}, f32[256,512]{1,0:T(8,128)}, f32[256,512]{1,0:T(8,128)}, f32[256,512]{1,0:T(8,128)}, /*index=5*/f32[256,512]{1,0:T(8,128)}) custom-call(bf16[2048,768]{1,0:T(8,128)(2,1)} %copy-done.6, bf16[1024,2048]{1,0:T(8,128)(2,1)} %get-tuple-element.58.tokens_ref, ...), custom_call_target="tpu_custom_call" | custom-call | flops 60000002048 | bytes 33554432 | tf_op jit(solution)/shard_map/leave/pallas_call | solution.py:1731
  627.2 0.7 slice.54
  628.0 1.3 slice.58
  629.3 1.3 fusion.2
  630.6 0.6 copy.32
  631.2 0.6 fusion.3
  631.8 6.0 reduce-scatter.5.cloned.1.call-done
  637.8 2.9 convert_element_type.17
  640.7 1.6 convert_element_type.18
  642.3 1.0 copy.38
  643.2 0.8 copy.39
  644.0 0.8 copy.40
  644.8 0.8 copy.41
  645.6 0.8 copy.42
  (31 shorter events, 0.1 us)
Async XLA Ops:
  94.5 13.8 %copy-start.14 = (s32[8192]{0:T(1024)S(1)}, s32[8192]{0:T(1024)}, u32[]{:S(2)}) copy-start(s32[8192]{0:T(1024)} %param.15) | copy-start | bytes 98308
  94.6 13.8 %copy-start.15 = (bf16[2048]{0:T(1024)(128)(2,1)S(1)}, bf16[2048]{0:T(1024)(128)(2,1)}, u32[]{:S(2)}) copy-start(bf16[2048]{0:T(1024)(128)(2,1)} %param.24) | copy-start | bytes 12292
  94.6 14.4 %copy-start.2 = (bf16[2048,768]{1,0:T(8,128)(2,1)S(1)}, bf16[2048,768]{1,0:T(8,128)(2,1)}, u32[]{:S(2)}) copy-start(bf16[2048,768]{1,0:T(8,128)(2,1)} %get-tuple-element.45.refs_0_.refs_1_.refs_2_) | copy-start | bytes 9437188
  97.0 38.4 %all-to-all-start = ((bf16[4,256,512]{2,1,0:T(8,128)(2,1)}), bf16[4,256,512]{2,1,0:T(8,128)(2,1)}, u32[]{:S(2)}, u32[]{:S(2)}) async-start(bf16[4,256,512]{2,1,0:T(8,128)(2,1)} %bitcast.17), calls=%async_computation | async-start | bytes 2097152 | tf_op jit(solution)/shard_map/all_to_all | solution.py:1780
  108.3 523.5 %reduce-scatter.3.cloned.1.call-start = ((), (), s32[]{:S(2)}) async-start(), calls=%async_computation.4 | async-start | bytes 9437184 | tf_op jit(solution)/shard_map/reduce_scatter | solution.py:1865
  108.3 23.3 %copy-start = (s32[4,2048]{1,0:T(4,128)}, s32[4,2048]{1,0:T(4,128)S(1)}, u32[]{:S(2)}) copy-start(s32[4,2048]{1,0:T(4,128)S(1)} %reshape.57.refs_3_.refs_6_) | copy-start | bytes 98308
  131.7 1.0 copy-start.4
  456.4 181.4 %reduce-scatter.5.cloned.1.call-start = ((), (), s32[]{:S(2)}) async-start(), calls=%async_computation.5 | async-start | bytes 9437184 | tf_op jit(solution)/shard_map/reduce_scatter | solution.py:1865
  456.5 11.2 %copy-start.1 = (s32[4,2048]{1,0:T(4,128)S(1)}, s32[4,2048]{1,0:T(4,128)}, u32[]{:S(2)}) copy-start(s32[4,2048]{1,0:T(4,128)} %copy-done) | copy-start | bytes 98308
  456.5 11.2 %copy-start.3 = (bf16[2048,768]{1,0:T(8,128)(2,1)S(1)}, bf16[2048,768]{1,0:T(8,128)(2,1)}, u32[]{:S(2)}) copy-start(bf16[2048,768]{1,0:T(8,128)(2,1)} %get-tuple-element.45.refs_0_.refs_1_.refs_2_) | copy-start | bytes 9437188
  457.2 44.2 %all-to-all-start.1 = ((bf16[4,256,512]{2,1,0:T(8,128)(2,1)}), bf16[4,256,512]{2,1,0:T(8,128)(2,1)}, u32[]{:S(2)}, u32[]{:S(2)}) async-start(bf16[4,256,512]{2,1,0:T(8,128)(2,1)} %get-tuple-element.55), calls=%async_computation.1 | async-start | bytes 2097152 | tf_op jit(solution)/shard_map/all_to_all | solution.py:1787
  467.7 1.5 copy-start.5
  469.2 1.5 copy-start.7
  499.8 1.6 copy-start.6
  631.8 8.9 %copy-start.8 = (bf16[256,2048]{1,0:T(8,128)(2,1)S(1)}, bf16[256,2048]{1,0:T(8,128)(2,1)}, u32[]{:S(2)}) copy-start(bf16[256,2048]{1,0:T(8,128)(2,1)} %reduce-scatter.3.cloned.1.call-done) | copy-start | bytes 3145732
  637.8 4.5 copy-start.9
  640.7 2.5 copy-start.13
  640.7 3.3 copy-start.12
  640.7 4.1 copy-start.11
  642.3 3.4 copy-start.10
Sparse Core Ops, SparseCore 0:
  456.5 82.3 reduce-scatter.2
  542.8 94.9 reduce-scatter.4

commit v11 on v10

--- a/solution.py
+++ b/solution.py
@@ -1080,22 +1080,152 @@
     attended_grad[rows, :] = dot_plain(chunk, weight[...]).astype(jnp.bfloat16)
 
 
+class PlaneSum:
+    def __init__(self, parts, core_slots, first_slots, last_slots, sent, got):
+        self.parts, self.core_slots = parts, core_slots
+        self.first_slots, self.last_slots = first_slots, last_slots
+        self.sent, self.got = sent, got
+        self.fsdp, self.ctx = lax.axis_index("fsdp"), lax.axis_index("ctx")
+        self.twin = self.fsdp + 1 - 2 * lax.rem(self.fsdp, 2)
+        self.height = parts.shape[0] // 8
+        self.half = parts.shape[1] // 2
+
+    def number(self, fsdp, over_x, over_y):
+        chip = lax.rem(fsdp + 2 * over_x, 4)
+        return chip * 2 + (1 - self.ctx if over_y else self.ctx)
+
+    def rows(self, number):
+        return pl.ds(pl.multiple_of(number * self.height, self.height), self.height)
+
+    def view(self, over_x, over_y, side):
+        columns = pl.ds(side * self.half, self.half)
+        return self.parts.at[self.rows(self.number(self.fsdp, over_x, over_y)), columns]
+
+    def copy(self, number, source, place, peer):
+        return pltpu.make_async_remote_copy(
+            src_ref=source,
+            dst_ref=place,
+            send_sem=self.sent.at[number],
+            recv_sem=self.got.at[number],
+            device_id=peer,
+            device_id_type=MESH,
+        )
+
+    def core_copy(self, number):
+        over_x, over_y = number // 2, number % 2
+        source = self.parts.at[self.rows(self.number(self.twin, over_x, over_y))]
+        place = self.core_slots.at[self.rows(number)]
+        return self.copy(number, source, place, {"fsdp": self.twin})
+
+    def x_peer(self):
+        return {"fsdp": lax.rem(self.fsdp + 2, 4)}
+
+    def y_peer(self):
+        return {"ctx": 1 - self.ctx}
+
+    def first_copy(self, number):
+        slot = self.first_slots.at[number]
+        if number < 2:
+            return self.copy(4 + number, self.view(1, number, 0), slot, self.x_peer())
+        return self.copy(4 + number, self.view(number - 2, 1, 1), slot, self.y_peer())
+
+    def last_copy(self, side):
+        slot = self.last_slots.at[side]
+        if side == 0:
+            return self.copy(8, self.view(0, 1, 0), slot, self.y_peer())
+        return self.copy(9, self.view(1, 0, 1), slot, self.x_peer())
+
+    def bands(self, action):
+        band = min(self.height, 32)
+
+        @pl.loop(0, self.height // band)
+        def _(i):
+            action(pl.ds(pl.multiple_of(i * band, band), band))
+
+    def add(self, view, slot):
+        def band(part):
+            total = view[part, :].astype(jnp.float32) + slot[part, :].astype(jnp.float32)
+            view[part, :] = total.astype(view.dtype)
+
+        self.bands(band)
+
+    def start(self):
+        for number in (3, 2, 1, 0):
+            self.core_copy(number).start()
+
+    def second(self):
+        for number in (3, 2, 1, 0):
+            self.core_copy(number).wait_recv()
+            shard = self.parts.at[self.rows(self.number(self.fsdp, number // 2, number % 2))]
+            self.add(shard, self.core_slots.at[self.rows(number)])
+            if number == 3:
+                self.first_copy(1).start()
+                self.first_copy(3).start()
+            if number == 2:
+                self.first_copy(0).start()
+            if number == 1:
+                self.first_copy(2).start()
+
+    def third(self):
+        self.first_copy(1).wait_recv()
+        self.add(self.view(0, 1, 0), self.first_slots.at[1])
+        self.last_copy(0).start()
+        self.first_copy(3).wait_recv()
+        self.add(self.view(1, 0, 1), self.first_slots.at[3])
+        self.last_copy(1).start()
+
+    def finish(self, put):
+        for side in range(2):
+            self.first_copy(2 * side).wait_recv()
+            self.last_copy(side).wait_recv()
+            view, first, last = self.view(0, 0, side), self.first_slots, self.last_slots
+
+            def band(part, side=side, view=view):
+                total = view[part, :].astype(jnp.float32)
+                total += first[2 * side, part, :].astype(jnp.float32)
+                put(side, part, total + last[side, part, :].astype(jnp.float32))
+
+            self.bands(band)
+        for number in range(4):
+            self.core_copy(number).wait_send()
+            self.first_copy(number).wait_send()
+        for side in range(2):
+            self.last_copy(side).wait_send()
+
+    @staticmethod
+    def scratch(shards, height, width):
+        return [
+            pltpu.VMEM((shards * height, width), jnp.bfloat16),
+            pltpu.VMEM((4 * height, width), jnp.bfloat16),
+            *PlaneSum.slots(height, width),
+        ]
+
+    @staticmethod
+    def slots(height, width):
+        return [
+            pltpu.VMEM((4, height, width // 2), jnp.bfloat16),
+            pltpu.VMEM((2, height, width // 2), jnp.bfloat16),
+            pltpu.SemaphoreType.DMA((10,)),
+            pltpu.SemaphoreType.DMA((10,)),
+        ]
+
+
 def middle_kernel(
     count, heads_ref, output_weight, expand_shard, shrink_shard, own_tokens, out_grad, gains,
     biases, hidden_bias,
     attended, mixed, inner, branch_out, grad_heads, first_sums, second_sums, hidden_sums,
     shrink_out, expand_out,
     expand_weight, shrink_weight, gathered, activated, slope, normed_one, inverse_one,
-    terms, total, slots, stage, shrink_stage, expand_stage,
+    terms, total, slots, stage, expand_stage, first_slots, last_slots, plane_sent, plane_got,
     sum_sent, sum_got, spread_sent, spread_got, expand_sent, expand_got, shrink_sent, shrink_got,
-    in_sent, in_got, out_sent, out_got, put_done, branch_done, product_done,
+    in_sent, in_got, out_sent, out_got, put_done, branch_done, product_done, ready,
 ):
     me, ctx = lax.axis_index("tp"), lax.axis_index("ctx")
     rows, width = gathered.shape[0] // 3, gathered.shape[1]
     half = heads_ref.shape[1]
     height = rows // PIECES
     own = height // count
-    shard = width // PIECES
+    shard, hidden = width // PIECES, activated.shape[1]
     pieces = 3 * PIECES
 
     def piece_rows(piece, start=0):
@@ -1247,28 +1377,46 @@
 
         line.spread_start(piece)
 
-    def gradient(left_start, right, place, out, done):
-        def copy(number):
-            part = pl.ds(pl.multiple_of(number * shard, shard), shard)
-            return pltpu.make_async_copy(place, out.at[part], done)
-
-        def step(number):
-            pl.when(number > 0)(lambda: copy(number - 1).wait())
-            columns = pl.ds(pl.multiple_of(number * shard, shard), shard)
-            left = gathered[left_start : left_start + rows, columns].T
-
-            def product(part):
-                place[:, part] = dot_plain(left, right[:, part]).astype(place.dtype)
-
-            tiles(place.shape[1], product)
-            copy(number).start()
-
-        return step, copy
-
-    shrink_step, shrink_copy = gradient(
-        rows, activated, shrink_stage, shrink_out, product_done.at[0]
-    )
-    expand_step, expand_copy = gradient(0, slope, expand_stage, expand_out, product_done.at[1])
+    def gradient(number, left_start, right, place):
+        columns = pl.ds(pl.multiple_of(number * shard, shard), shard)
+        left = gathered[left_start : left_start + rows, columns].T
+
+        def product(part):
+            place[:, part] = dot_plain(left, right[:, part]).astype(place.dtype)
+
+        tiles(place.shape[1], product)
+
+    def expand_copy(number):
+        part = pl.ds(pl.multiple_of(number * shard, shard), shard)
+        return pltpu.make_async_copy(expand_stage, expand_out.at[part], product_done)
+
+    def expand_step(number):
+        pl.when(number > 0)(lambda: expand_copy(number - 1).wait())
+        gradient(number, 0, slope, expand_stage)
+        expand_copy(number).start()
+
+    plane_sum = PlaneSum(shrink_weight, activated, first_slots, last_slots, plane_sent, plane_got)
+    twin = {"fsdp": plane_sum.twin}
+
+    def shrink_step(number):
+        pl.when(number == 0)(shrink_gather.wait_sent)
+        fsdp = jnp.where(number < 2, plane_sum.twin, plane_sum.fsdp)
+        for over_y in (1, 0):
+            owner = plane_sum.number(fsdp, 1 - lax.rem(number, 2), over_y)
+            gradient(owner, rows, activated, shrink_weight.at[plane_sum.rows(owner)])
+
+        @pl.when(number == 3)
+        def _():
+            pl.semaphore_signal(ready, inc=1, device_id=twin, device_id_type=MESH)
+
+    def shrink_send(_):
+        pl.semaphore_wait(ready, 1)
+        plane_sum.start()
+
+    def shrink_total(side):
+        return pltpu.make_async_copy(
+            terms.at[side], shrink_out.at[pl.ds(side * height, height)], put_done.at[side]
+        )
 
     @pl.loop(0, pieces + 5)
     def _(step):
@@ -1278,6 +1426,8 @@
                 action(step - number)
 
         pl.when(step == 5)(expand_gather.last)
+        pl.when(step == 2 * PIECES + 9)(plane_sum.second)
+        pl.when(step == 2 * PIECES + 12)(plane_sum.third)
         late(5, use)
         late(3, lambda piece: line.spread_onward(piece, 2))
         late(1, lambda piece: line.sum_onward(piece, term_of(piece), [1]))
@@ -1285,8 +1435,9 @@
         late(0, form)
         late(4, lambda piece: [line.spread_onward(piece, i) for i in range(3, count)])
         late(2, lambda piece: line.spread_onward(piece, 1))
-        late(2 * PIECES + 4, shrink_step, PIECES)
+        late(2 * PIECES + 4, shrink_step, 4)
         late(2 * PIECES + 5, expand_step, PIECES)
+        late(2 * PIECES + 8, shrink_send, 1)
         late(0, lambda piece: line.sum_onward(piece, term_of(piece), range(count - 2, 1, -1)))
         late(1, own_step)
 
@@ -1299,8 +1450,18 @@
         pl.when(step == 6)(shrink_gather.second)
         pl.when(step == 7)(shrink_gather.third)
 
-    shrink_copy(PIECES - 1).wait()
     expand_copy(PIECES - 1).wait()
+
+    def put_total(side, part, values):
+        columns = pl.ds(side * (hidden // 2), hidden // 2)
+        start = pl.multiple_of(lax.rem(part.start, height), values.shape[0])
+        terms[part.start // height, pl.ds(start, values.shape[0]), columns] = values
+
+    plane_sum.finish(put_total)
+    for side in range(2):
+        shrink_total(side).start()
+    for side in range(2):
+        shrink_total(side).wait()
 
     @pl.loop(0, PIECES)
     def _(piece):
@@ -1310,7 +1471,6 @@
         swap_out.wait_sent(piece)
 
     expand_gather.wait_sent()
-    shrink_gather.wait_sent()
     line.spread_finish(pieces)
 
 
@@ -1352,7 +1512,7 @@
             shape((8, width)),
             shape((8, width)),
             shape((8, hidden)),
-            shape((width, hidden), low),
+            shape((shard, hidden)),
             shape((width, hidden), low),
         ],
         in_specs=[anywhere, vmem, anywhere, anywhere, vmem, vmem, vmem, vmem, vmem],
@@ -1370,14 +1530,15 @@
             pltpu.VMEM((PIECES, count + 1, own, width), low),
             pltpu.VMEM((rows, half), low),
             pltpu.VMEM((shard, hidden), low),
-            pltpu.VMEM((shard, hidden), low),
+            *PlaneSum.slots(shard, hidden),
             *line_semaphores(count, PIECES)[0],
             *line_semaphores(count, 3 * PIECES)[1],
             *[pltpu.SemaphoreType.DMA((9,))] * 4,
             *[pltpu.SemaphoreType.DMA((PIECES,))] * 4,
             pltpu.SemaphoreType.DMA((3,)),
             pltpu.SemaphoreType.DMA((PIECES,)),
-            pltpu.SemaphoreType.DMA((2,)),
+            pltpu.SemaphoreType.DMA,
+            pltpu.SemaphoreType.REGULAR,
         ],
         compiler_params=pltpu.CompilerParams(
             collective_id=collective_id, has_side_effects=True, vmem_limit_bytes=62 << 20
@@ -1523,113 +1684,6 @@
     )(x, weight, inner, row_sums, hidden_sums)
 
 
-class PlaneSum:
-    def __init__(self, parts, core_slots, first_slots, last_slots, sent, got):
-        self.parts, self.core_slots = parts, core_slots
-        self.first_slots, self.last_slots = first_slots, last_slots
-        self.sent, self.got = sent, got
-        self.fsdp, self.ctx = lax.axis_index("fsdp"), lax.axis_index("ctx")
-        self.twin = self.fsdp + 1 - 2 * lax.rem(self.fsdp, 2)
-        self.half = parts.shape[2] // 2
-
-    def number(self, fsdp, over_x, over_y):
-        chip = lax.rem(fsdp + 2 * over_x, 4)
-        return chip * 2 + (1 - self.ctx if over_y else self.ctx)
-
-    def view(self, over_x, over_y, side):
-        columns = pl.ds(side * self.half, self.half)
-        return self.parts.at[self.number(self.fsdp, over_x, over_y), :, columns]
-
-    def copy(self, number, source, place, peer):
-        return pltpu.make_async_remote_copy(
-            src_ref=source,
-            dst_ref=place,
-            send_sem=self.sent.at[number],
-            recv_sem=self.got.at[number],
-            device_id=peer,
-            device_id_type=MESH,
-        )
-
-    def core_copy(self, number):
-        over_x, over_y = number // 2, number % 2
-        source = self.parts.at[self.number(self.twin, over_x, over_y)]
-        return self.copy(number, source, self.core_slots.at[number], {"fsdp": self.twin})
-
-    def x_peer(self):
-        return {"fsdp": lax.rem(self.fsdp + 2, 4)}
-
-    def y_peer(self):
-        return {"ctx": 1 - self.ctx}
-
-    def first_copy(self, number):
-        slot = self.first_slots.at[number]
-        if number < 2:
-            return self.copy(4 + number, self.view(1, number, 0), slot, self.x_peer())
-        return self.copy(4 + number, self.view(number - 2, 1, 1), slot, self.y_peer())
-
-    def last_copy(self, side):
-        slot = self.last_slots.at[side]
-        if side == 0:
-            return self.copy(8, self.view(0, 1, 0), slot, self.y_peer())
-        return self.copy(9, self.view(1, 0, 1), slot, self.x_peer())
-
-    def add(self, view, slot):
-        total = view[...].astype(jnp.float32) + slot[...].astype(jnp.float32)
-        view[...] = total.astype(view.dtype)
-
-    def start(self):
-        for number in (3, 2, 1, 0):
-            self.core_copy(number).start()
-
-    def second(self):
-        for number in (3, 2, 1, 0):
-            self.core_copy(number).wait_recv()
-            shard = self.parts.at[self.number(self.fsdp, number // 2, number % 2)]
-            self.add(shard, self.core_slots.at[number])
-            if number == 3:
-                self.first_copy(1).start()
-                self.first_copy(3).start()
-            if number == 2:
-                self.first_copy(0).start()
-            if number == 1:
-                self.first_copy(2).start()
-
-    def third(self):
-        self.first_copy(1).wait_recv()
-        self.add(self.view(0, 1, 0), self.first_slots.at[1])
-        self.last_copy(0).start()
-        self.first_copy(3).wait_recv()
-        self.add(self.view(1, 0, 1), self.first_slots.at[3])
-        self.last_copy(1).start()
-
-    def finish(self):
-        totals = []
-        for side in range(2):
-            number = 2 * side
-            self.first_copy(number).wait_recv()
-            self.last_copy(side).wait_recv()
-            total = self.view(0, 0, side)[...].astype(jnp.float32)
-            total += self.first_slots[number].astype(jnp.float32)
-            totals.append(total + self.last_slots[side].astype(jnp.float32))
-        for number in range(4):
-            self.core_copy(number).wait_send()
-            self.first_copy(number).wait_send()
-        for side in range(2):
-            self.last_copy(side).wait_send()
-        return totals
-
-    @staticmethod
-    def scratch(shards, height, width):
-        return [
-            pltpu.VMEM((shards, height, width), jnp.bfloat16),
-            pltpu.VMEM((4, height, width), jnp.bfloat16),
-            pltpu.VMEM((4, height, width // 2), jnp.bfloat16),
-            pltpu.VMEM((2, height, width // 2), jnp.bfloat16),
-            pltpu.SemaphoreType.DMA((10,)),
-            pltpu.SemaphoreType.DMA((10,)),
-        ]
-
-
 def leave_kernel(
     sizes, grads_ref, tokens_ref, weight, inner_ref, rows_ref, hidden_ref, branch_ref, attended_ref,
     out_ref, vectors_ref, query_out, key_out, value_out, output_out,
@@ -1642,7 +1696,7 @@
     height = rows // PIECES
     part = grads_ref.shape[1]
     plane_sum, output_sum = PlaneSum(*sum_scratch[:6]), PlaneSum(*sum_scratch[6:])
-    shard = plane_sum.parts.shape[1]
+    shard = plane_sum.height
 
     def piece_rows(piece, start=0):
         return pl.ds(pl.multiple_of(start + piece * height, height), height)
@@ -1659,7 +1713,8 @@
             for over_y in (1, 0):
                 number = sums.number(fsdp, over_x, over_y)
                 columns = pl.ds(pl.multiple_of(number * shard, shard), shard)
-                sums.parts[number] = dot_rows(left[:, columns], right[...]).astype(jnp.bfloat16)
+                product = dot_rows(left[:, columns], right[...])
+                sums.parts[sums.rows(number), :] = product.astype(jnp.bfloat16)
 
     def opening():
         @pl.loop(0, PIECES)
@@ -1706,12 +1761,17 @@
         sum_sent, sum_got, tp_sent, tp_got, plane_sent, plane_got,
         hooks=(opening, before, after, closing),
     )
-    halves = plane_sum.finish()
     third = part // 3
-    for side, half in enumerate(halves):
+
+    def put_part(side, rows, values):
         for i, ref in enumerate((query_out, key_out, value_out)):
-            ref[:, side * third : (side + 1) * third] = half[:, i * third : (i + 1) * third]
-    output_out[...] = jnp.concatenate(output_sum.finish(), axis=1)
+            ref[rows, side * third : (side + 1) * third] = values[:, i * third : (i + 1) * third]
+
+    def put_output(side, rows, values):
+        output_out[rows, side * output_sum.half : (side + 1) * output_sum.half] = values
+
+    plane_sum.finish(put_part)
+    output_sum.finish(put_output)
 
     @pl.loop(0, PIECES)
     def _(piece):
@@ -1869,12 +1929,12 @@
     if by_heads:
         (
             attended, mixed_own, grad_inner, branch_low, attended_grad,
-            first_sums, second_sums, hidden_sums, shrink_part, expand_part,
+            first_sums, second_sums, hidden_sums, shrink_grad, expand_part,
         ) = middle(
             attended_heads, full_output, expand_weight, shrink_weight, own_tokens, upstream,
             gains, biases, hidden_bias.astype(jnp.float32)[None], 1,
         )
-        shrink_grad, expand_grad = owner_sum(shrink_part), owner_sum(expand_part)
+        expand_grad = owner_sum(expand_part)
         mixed = unspread_own(mixed_own)
         (grads,) = attend_back(
             queries, keys, values, attended_heads, attended_grad, lse, bounds, places, True
@@ -1940,9 +2000,7 @@
             grads, wide_tokens, wide_qkv, grad_inner, row_sums, hidden_sums[:1], branch_low,
             attended, 4,
         )
-        input_grad, shrink_grad, expand_grad = lax.optimization_barrier(
-            (input_grad, shrink_grad, expand_grad)
-        )
+        input_grad, expand_grad = lax.optimization_barrier((input_grad, expand_grad))
     else:
         input_grad, vectors = input_sum(
             qkv_low, wide_qkv, grad_inner, row_sums, hidden_sums[:1], 4

time: 655 us -> 659 us (level)
  Pallas kernels: 580 us -> 592 us
  waiting for transfers between devices: 6.69 us -> 0.02 us
    pallas_call x1, Pallas kernels: 321 us -> 348 us  [middle(): pl.pallas_call(functools.partial(middle_kernel, count), out_shape=[shape(...]
    pallas_call x1, Pallas kernels: 123 us -> 116 us  [leave(): pl.pallas_call(functools.partial(leave_kernel, sizes), out_shape=[jax.Sha...]
  transfers between devices with their start and end apart: 4 -> 3, of which waited for: 1 -> 0; matrix products, arithmetic and copies ran while one was open for 2% -> 2% of each run, Pallas kernels for 27% -> 24%
where the time goes in v11:
time: 659 us; the launch traced here: 658 us
  Pallas kernels  592 us (90%)
  local copies, waits for them, and re-layouts  26 us (4%)
  starting transfers between devices  18.2 us (3%)
  between operations  14.2 us (2%)
  other arithmetic  7.69 us (1%)
    pallas_call x1, Pallas kernels, middle(): pl.pallas_call(functools.partial(middle_kernel, count), out_shape=[shape(...  348 us
    pallas_call x1, Pallas kernels, leave(): pl.pallas_call(functools.partial(leave_kernel, sizes), out_shape=[jax.Sha...  116 us
    pallas_call x1, Pallas kernels, enter(): pl.pallas_call(functools.partial(enter_kernel, count), out_shape=[jax.Sha...  83.6 us
    pallas_call x1, Pallas kernels, attend_back(): pl.pallas_call(functools.partial(attend_back_kernel, len(scalars), len(ar...  25.1 us
    pallas_call x1, Pallas kernels, attend(): pl.pallas_call(functools.partial(attend_kernel, len(scalars)), out_shape=...  19.4 us
  transfers between devices with their start and end apart: 3, of which 0 were waited for; matrix products, arithmetic and copies ran while one was open for 2% of the time, Pallas kernels for 24%

profile of v11, /device:TPU:8, one launch (start us, length us, event | category | flops | bytes accessed | tf_op | source)
XLA Modules:
  0.0 658.0 jit_solution(3194409605950705491)
XLA Ops:
  7.2 0.7 stack.10
  7.9 0.7 stack.9
  8.6 0.1 pad.1.clone
  8.6 0.1 convert_bitcast_fusion
  8.7 0.6 reshape.64.bias
  9.3 0.1 pad.5.clone
  9.4 1.4 maximum_maximum_fusion.marks_ref
  10.8 83.6 %enter.1 = (bf16[1024,2048]{1,0:T(8,128)(2,1)}, bf16[256,2048]{1,0:T(8,128)(2,1)}, bf16[16,2048]{1,0:T(8,128)(2,1)}, bf16[2048,1536]{1,0:T(8,128)(2,1)}, bf16[20...) custom-call(bf16[1024,512]{1,0:T(8,128)(2,1)} %x_ref.1, bf16[16,512]{1,0:T(8,128)(2,1)} %maximum_maximum_fusion.marks_ref, ...), custom_call_target="tpu_custom_call" | custom-call | flops 80000000000 | bytes 134217728 | tf_op jit(solution)/shard_map/enter/pallas_call | solution.py:833
  94.4 0.0 copy-start.14
  94.4 0.0 copy-start.15
  94.4 0.0 copy-start.2
  94.4 2.5 copy.30
  96.9 11.3 %all-to-all-start = ((bf16[4,256,512]{2,1,0:T(8,128)(2,1)}), bf16[4,256,512]{2,1,0:T(8,128)(2,1)}, u32[]{:S(2)}, u32[]{:S(2)}) async-start(bf16[4,256,512]{2,1,0:T(8,128)(2,1)} %bitcast.17), calls=%async_computation | async-start | bytes 2097152 | tf_op jit(solution)/shard_map/all_to_all | solution.py:1840
  108.1 0.0 reduce-scatter.2.cloned.1.call-start
  108.2 0.0 copy-start
  108.2 0.6 broadcast_in_dim.15
  108.8 19.4 %attend.1 = (bf16[2048,256]{1,0:T(8,128)(2,1)S(1)}, f32[2,1,2048]{2,1,0:T(1,128)S(1)}) custom-call(bf16[2048,768]{1,0:T(8,128)(2,1)S(1)} %copy-done.2, bf16[2048,768]{1,0:T(8,128)(2,1)S(1)} %copy-done.2, bf16[2048,768]{1,0:T(8,128)(2,1)S(1)} %copy-done.2, s32[4,2048]{1,0:T(4,128)S(1)} %reshape.57.refs_3_.refs_6_), custom_call_target="tpu_custom_call" | custom-call | flops 3221225472 | bytes 4194304 | tf_op jit(solution)/shard_map/attend/pallas_call | solution.py:118
  128.2 0.0 copy-start.4
  128.2 1.0 copy-done.4
  129.2 1.4 slice_convert_fusion.1.gains
  130.6 1.4 slice_convert_fusion.biases
  131.9 0.0 all-to-all-done.out_grad
  131.9 348.2 %middle.1 = (bf16[1024,512]{1,0:T(8,128)(2,1)}, bf16[4,256,512]{2,1,0:T(8,128)(2,1)}, f32[256,2048]{1,0:T(8,128)}, bf16[1024,2048]{1,0:T(8,128)(2,1)}, bf16[2048...) custom-call(bf16[2048,256]{1,0:T(8,128)(2,1)} %copy-done.4, ...), custom_call_target="tpu_custom_call" | custom-call | flops 299999985664 | bytes 402653184 | tf_op jit(solution)/shard_map/middle/pallas_call | solution.py:1504
  480.2 0.0 copy-start.1
  480.2 0.0 reduce-scatter.2.cloned.1.call-update
  480.2 7.0 %all-to-all-start.1 = ((bf16[4,256,512]{2,1,0:T(8,128)(2,1)}), bf16[4,256,512]{2,1,0:T(8,128)(2,1)}, u32[]{:S(2)}, u32[]{:S(2)}) async-start(bf16[4,256,512]{2,1,0:T(8,128)(2,1)} %get-tuple-element.54), calls=%async_computation.1 | async-start | bytes 2097152 | tf_op jit(solution)/shard_map/all_to_all | solution.py:1847
  487.2 1.4 slice.53.hidden_ref
  488.7 1.2 fusion
  489.9 0.7 concatenate.8.rows_ref
  490.6 1.3 copy-done.5
  492.0 1.4 copy-done.7
  493.4 25.1 %attend_back.1.grads_ref = bf16[2048,768]{1,0:T(8,128)(2,1)S(1)} custom-call(bf16[2048,768]{1,0:T(8,128)(2,1)S(1)} %copy-done.3, bf16[2048,768]{1,0:T(8,128)(2,1)S(1)} %copy-done.3, bf16[2048,768]{1,0:T(8,128)(2,1)S(1)} %copy-done.3, bf16[2048,256]{1,0:T(8,128)(2,1)S(1)} %copy-done.5, bf16[2048,256]{1,0:T(8,128)(2,1)S(1)} %copy-done.7, ...), custom_call_target="tpu_custom_call" | custom-call | flops 8589934592 | bytes 8388608 | tf_op jit(solution)/shard_map/attend_back/pallas_call | solution.py:214
  518.5 1.7 copy-done.6
  520.2 0.0 all-to-all-done.1
  520.2 2.3 copy.31
  522.5 115.6 %leave.1 = (bf16[1024,512]{1,0:T(8,128)(2,1)}, f32[16,512]{1,0:T(8,128)}, f32[256,512]{1,0:T(8,128)}, f32[256,512]{1,0:T(8,128)}, f32[256,512]{1,0:T(8,128)}, /*index=5*/f32[256,512]{1,0:T(8,128)}) custom-call(bf16[2048,768]{1,0:T(8,128)(2,1)} %copy-done.6, bf16[1024,2048]{1,0:T(8,128)(2,1)} %get-tuple-element.57.tokens_ref, ...), custom_call_target="tpu_custom_call" | custom-call | flops 60000002048 | bytes 33554432 | tf_op jit(solution)/shard_map/leave/pallas_call | solution.py:1791
  638.1 0.8 slice.54
  639.0 1.3 slice.58
  640.3 1.3 fusion.2
  641.6 0.6 copy.32
  642.2 0.6 fusion.3
  642.8 2.9 convert_element_type.14
  645.7 1.0 copy.39
  646.7 0.8 copy.40
  647.5 0.8 copy.41
  648.3 0.8 copy.42
  649.1 0.8 copy.43
  649.9 1.3 copy.44
  (28 shorter events, 0.1 us)
Async XLA Ops:
  94.4 13.8 %copy-start.14 = (s32[8192]{0:T(1024)S(1)}, s32[8192]{0:T(1024)}, u32[]{:S(2)}) copy-start(s32[8192]{0:T(1024)} %param.15) | copy-start | bytes 98308
  94.4 13.8 %copy-start.15 = (bf16[2048]{0:T(1024)(128)(2,1)S(1)}, bf16[2048]{0:T(1024)(128)(2,1)}, u32[]{:S(2)}) copy-start(bf16[2048]{0:T(1024)(128)(2,1)} %param.24) | copy-start | bytes 12292
  94.4 14.4 %copy-start.2 = (bf16[2048,768]{1,0:T(8,128)(2,1)S(1)}, bf16[2048,768]{1,0:T(8,128)(2,1)}, u32[]{:S(2)}) copy-start(bf16[2048,768]{1,0:T(8,128)(2,1)} %get-tuple-element.44.refs_0_.refs_1_.refs_2_) | copy-start | bytes 9437188
  96.9 35.1 %all-to-all-start = ((bf16[4,256,512]{2,1,0:T(8,128)(2,1)}), bf16[4,256,512]{2,1,0:T(8,128)(2,1)}, u32[]{:S(2)}, u32[]{:S(2)}) async-start(bf16[4,256,512]{2,1,0:T(8,128)(2,1)} %bitcast.17), calls=%async_computation | async-start | bytes 2097152 | tf_op jit(solution)/shard_map/all_to_all | solution.py:1840
  108.1 534.7 %reduce-scatter.2.cloned.1.call-start = ((), (), s32[]{:S(2)}) async-start(), calls=%async_computation.3 | async-start | bytes 9437184 | tf_op jit(solution)/shard_map/reduce_scatter | solution.py:1925
  108.2 20.0 %copy-start = (s32[4,2048]{1,0:T(4,128)}, s32[4,2048]{1,0:T(4,128)S(1)}, u32[]{:S(2)}) copy-start(s32[4,2048]{1,0:T(4,128)S(1)} %reshape.57.refs_3_.refs_6_) | copy-start | bytes 98308
  128.2 1.0 copy-start.4
  480.2 10.4 %copy-start.1 = (s32[4,2048]{1,0:T(4,128)S(1)}, s32[4,2048]{1,0:T(4,128)}, u32[]{:S(2)}) copy-start(s32[4,2048]{1,0:T(4,128)} %copy-done) | copy-start | bytes 98308
  480.2 10.4 %copy-start.3 = (bf16[2048,768]{1,0:T(8,128)(2,1)S(1)}, bf16[2048,768]{1,0:T(8,128)(2,1)}, u32[]{:S(2)}) copy-start(bf16[2048,768]{1,0:T(8,128)(2,1)} %get-tuple-element.44.refs_0_.refs_1_.refs_2_) | copy-start | bytes 9437188
  480.2 40.0 %all-to-all-start.1 = ((bf16[4,256,512]{2,1,0:T(8,128)(2,1)}), bf16[4,256,512]{2,1,0:T(8,128)(2,1)}, u32[]{:S(2)}, u32[]{:S(2)}) async-start(bf16[4,256,512]{2,1,0:T(8,128)(2,1)} %get-tuple-element.54), calls=%async_computation.1 | async-start | bytes 2097152 | tf_op jit(solution)/shard_map/all_to_all | solution.py:1847
  490.6 1.3 copy-start.5
  492.0 1.4 copy-start.7
  518.5 1.7 copy-start.6
  638.1 7.6 %copy-start.9 = (bf16[1024,512]{1,0:T(8,128)(2,1)S(1)}, bf16[1024,512]{1,0:T(8,128)(2,1)}, u32[]{:S(2)}) copy-start(bf16[1024,512]{1,0:T(8,128)(2,1)} %get-tuple-element.102) | copy-start | bytes 3145732
  638.1 8.6 %copy-start.13 = (f32[256,512]{1,0:T(8,128)S(1)}, f32[256,512]{1,0:T(8,128)}, u32[]{:S(2)}) copy-start(f32[256,512]{1,0:T(8,128)} %get-tuple-element.103) | copy-start | bytes 1572868
  642.8 4.7 copy-start.12
  642.8 5.5 copy-start.11
  645.7 3.4 copy-start.10
  645.7 4.2 copy-start.8
Sparse Core Ops, SparseCore 0:
  480.4 83.4 reduce-scatter.1

commit v12 on v11

--- a/solution.py
+++ b/solution.py
@@ -38,7 +38,7 @@
 def block_bounds(block, rows, bounds, marks):
     if len(bounds) == 4:
         first, last, low, high = bounds
-        return first[block], last[block], low[...], high[...]
+        return first[block], last[block], last[block], last[block], low[...], high[...]
     (ids,) = bounds
     run = ids.shape[1]
 
@@ -58,7 +58,19 @@
 
     begin = block * rows
     low, high = bounds_at(begin + lax.broadcasted_iota(jnp.int32, (1, rows), 1))
-    return bounds_at(begin)[0] // KB, bounds_at(begin + rows - 1)[1] // KB + 1, low, high
+    least_low, least_high = bounds_at(begin)
+    most_low, most_high = bounds_at(begin + rows - 1)
+    first, last = least_low // KB, most_high // KB + 1
+    whole_first = jnp.minimum((most_low + KB - 1) // KB, last)
+    whole_last = jnp.maximum((least_high + 1) // KB, whole_first)
+    return first, whole_first, whole_last, last, low, high
+
+
+def over_key_blocks(step, marks, start):
+    first, whole_first, whole_last, last = marks
+    carry = lax.fori_loop(first, whole_first, functools.partial(step, True), start)
+    carry = lax.fori_loop(whole_first, whole_last, functools.partial(step, False), carry)
+    return lax.fori_loop(whole_last, last, functools.partial(step, True), carry)
 
 
 def bound_operands(bounds):
@@ -80,15 +92,16 @@
         vt[...] = v_ref[...].T
 
     queries = q_ref[...]
-    first, last, low, high = block_bounds(block, rows, (*bounds, *arrays), marks)
+    *span, low, high = block_bounds(block, rows, (*bounds, *arrays), marks)
     places = lax.broadcasted_iota(jnp.int32, (KB, rows), 0)
 
-    def step(number, carry):
+    def step(masked, number, carry):
         top, total, mixed = carry
         start = pl.multiple_of(number * KB, KB)
         scores = dot_cols(k_ref[pl.ds(start, KB), :], queries) * (score_scale * log2_e)
-        keep = (places >= low - start) & (places <= high - start)
-        scores = jnp.where(keep, scores, hidden_floor)
+        if masked:
+            keep = (places >= low - start) & (places <= high - start)
+            scores = jnp.where(keep, scores, hidden_floor)
         new_top = jnp.maximum(top, jnp.max(scores, axis=0, keepdims=True))
         shrink = jnp.exp2(top - new_top)
         powers = jnp.exp2(scores - new_top)
@@ -96,10 +109,9 @@
         mixed = mixed * shrink + dot_plain(vt[:, pl.ds(start, KB)], powers.astype(jnp.bfloat16))
         return new_top, total, mixed
 
-    top, total, mixed = lax.fori_loop(
-        first,
-        last,
+    top, total, mixed = over_key_blocks(
         step,
+        span,
         (
             jnp.full((1, rows), hidden_floor, jnp.float32),
             jnp.zeros((1, rows), jnp.float32),
@@ -136,7 +148,7 @@
             ],
             scratch_shapes=[pltpu.VMEM((HD, span), jnp.bfloat16), pltpu.SMEM((2,), jnp.int32)],
         ),
-        compiler_params=pltpu.CompilerParams(vmem_limit_bytes=32 << 20),
+        compiler_params=pltpu.CompilerParams(vmem_limit_bytes=60 << 20),
         cost_estimate=pl.CostEstimate(
             flops=3 * rows * span * width,
             bytes_accessed=2 * (2 * rows + 2 * span) * width,
@@ -163,24 +175,27 @@
     queries = q_ref[...]
     upstream = g_ref[...]
     lse = lse_ref[0]
-    first, last, low, high = block_bounds(block, rows, bounds, marks)
+    *span, low, high = block_bounds(block, rows, bounds, marks)
     places = lax.broadcasted_iota(jnp.int32, (KB, rows), 0)
     product = upstream.astype(jnp.float32) * o_ref[...].astype(jnp.float32)
     delta = jnp.sum(product.T, axis=0, keepdims=True)
 
-    def step(number, dq):
+    def step(masked, number, dq):
         start = pl.multiple_of(number * KB, KB)
         window = pl.ds(start, KB)
         scores = dot_cols(k_ref[window, :], queries) * (score_scale * log2_e)
-        keep = (places >= low - start) & (places <= high - start)
-        probs = jnp.exp2(jnp.where(keep, scores - lse, hidden_floor))
+        scores = scores - lse
+        if masked:
+            keep = (places >= low - start) & (places <= high - start)
+            scores = jnp.where(keep, scores, hidden_floor)
+        probs = jnp.exp2(scores)
         prob_grad = dot_cols(v_ref[window, :], upstream)
         score_grad = (probs * (prob_grad - delta)).astype(jnp.bfloat16)
         dv_sum[window, :] += dot_plain(probs.astype(jnp.bfloat16), upstream)
         dk_sum[window, :] += dot_plain(score_grad, queries)
         return dq + dot_plain(kt[:, window], score_grad)
 
-    dq = lax.fori_loop(first, last, step, jnp.zeros((HD, rows), jnp.float32))
+    dq = over_key_blocks(step, span, jnp.zeros((HD, rows), jnp.float32))
     dq = (dq * score_scale).T
     if len(results) == 1:
         width = results[0].shape[1] // 3
@@ -241,7 +256,7 @@
                 pltpu.SMEM((2,), jnp.int32),
             ],
         ),
-        compiler_params=pltpu.CompilerParams(vmem_limit_bytes=32 << 20),
+        compiler_params=pltpu.CompilerParams(vmem_limit_bytes=60 << 20),
         cost_estimate=pl.CostEstimate(
             flops=8 * rows * span * width,
             bytes_accessed=2 * (4 * rows + 4 * span) * width,
@@ -507,8 +522,15 @@
     ]
 
 
+def put_marks(marks, gains, biases):
+    marks[...] = jnp.zeros_like(marks)
+    marks[0:2, :] = gains[...].astype(jnp.float32)
+    marks[2:6, :] = biases[...].astype(jnp.float32)
+
+
 def gather_kernel(
-    count, x_ref, marks_ref, out_ref, marks_out, slots, sent, got, marks_sent, marks_got
+    count, x_ref, gains, biases, out_ref, marks_out, marks_ref, slots, sent, got,
+    marks_sent, marks_got,
 ):
     me = lax.axis_index("tp")
     height = x_ref.shape[0] // PIECES
@@ -525,6 +547,7 @@
 
     line = Line(me, count, None, None, None, view, sent, got)
     peers = peers_along_tp(me, count)
+    put_marks(marks_ref, gains, biases)
     greet_peers(peers)
 
     @pl.loop(0, PIECES)
@@ -552,19 +575,20 @@
     line.spread_finish(PIECES, source)
 
 
-def gather_features(x, marks, collective_id):
+def gather_features(x, gains, biases, collective_id):
     count = lax.axis_size("tp")
     rows, width = x.shape
     return pl.pallas_call(
         functools.partial(gather_kernel, count),
         out_shape=[
             jax.ShapeDtypeStruct((rows, count * width), x.dtype),
-            jax.ShapeDtypeStruct((marks.shape[0], count * width), marks.dtype),
+            jax.ShapeDtypeStruct((8, count * width), jnp.float32),
         ],
-        in_specs=[pl.BlockSpec(memory_space=pltpu.VMEM)] * 2,
+        in_specs=[pl.BlockSpec(memory_space=pltpu.VMEM)] * 3,
         out_specs=[pl.BlockSpec(memory_space=pltpu.VMEM)] * 2,
         scratch_shapes=[
-            pltpu.VMEM((count - 1, *marks.shape), marks.dtype),
+            pltpu.VMEM((8, width), jnp.float32),
+            pltpu.VMEM((count - 1, 8, width), jnp.float32),
             *line_semaphores(count, PIECES)[1],
             pltpu.SemaphoreType.DMA((count - 1,)),
             pltpu.SemaphoreType.DMA((count - 1,)),
@@ -576,7 +600,7 @@
             flops=0, bytes_accessed=64 * rows * count * width, transcendentals=0
         ),
         name="gather_features",
-    )(x, marks)
+    )(x, gains, biases)
 
 
 class Swap:
@@ -700,10 +724,12 @@
 
 
 def enter_kernel(
-    count, x_ref, marks_ref, query_ref, key_ref, value_ref, output_ref, bias,
-    wide, own_tokens, marks_out, weight, output_weight, heads,
-    mark_slots, stage, sent, got, marks_sent, marks_got,
-    weight_sent, weight_got, output_sent, output_got, swap_sent, swap_got, put_done,
+    count, x_ref, gains, biases, query_ref, key_ref, value_ref, output_ref, query_bias, value_bias,
+    grad_ref,
+    wide_out, own_tokens, marks_out, weight_out, output_out, heads, grad_out,
+    wide, weight, output_weight, marks_ref, mark_slots, stage, sent, got, marks_sent, marks_got,
+    weight_sent, weight_got, output_sent, output_got, swap_sent, swap_got, put_done, grad_done,
+    wide_done, out_done,
 ):
     me, ctx = lax.axis_index("tp"), lax.axis_index("ctx")
     rows, width = x_ref.shape
@@ -736,8 +762,13 @@
     ]
     for put in puts:
         put.start()
+    grads = [
+        pltpu.make_async_copy(grad_ref.at[:, owner], grad_out.at[owner], grad_done.at[owner])
+        for owner in range(count)
+    ]
     line = Line(me, count, None, None, None, view, sent, got)
     tp_peers = peers_along_tp(me, count)
+    put_marks(marks_ref, gains, biases)
     greet_peers(tp_peers + gather.peers())
 
     def source(piece):
@@ -756,6 +787,8 @@
     marks_out[:, own] = marks_ref[...]
     for put in puts[7:]:
         put.wait()
+    for grad in grads:
+        grad.start()
     swap = Swap(
         swap_sent, swap_got,
         lambda piece: stage.at[piece_rows(piece)],
@@ -764,13 +797,20 @@
 
     def products(piece, side, place):
         x = wide[piece_rows(piece), :]
-
-        @pl.loop(0, 3)
-        def _(tile):
-            start = pl.multiple_of(side * part + tile * half, half)
-            columns = pl.ds(start, half)
-            values = dot_plain(x, weight[:, columns]) + bias[:, columns]
-            place[:, pl.ds(pl.multiple_of(tile * half, half), half)] = values.astype(jnp.bfloat16)
+        own_half = pl.ds(pl.multiple_of(side * half, half), half)
+        for i, bias in enumerate((query_bias, None, value_bias)):
+            start = pl.multiple_of(side * part + i * half, half)
+            values = dot_plain(x, weight[:, pl.ds(start, half)])
+            if bias is not None:
+                values += bias[:, own_half].astype(jnp.float32)
+            place[:, i * half : (i + 1) * half] = values.astype(jnp.bfloat16)
+
+    def wide_copy(piece):
+        part = piece_rows(piece)
+        return pltpu.make_async_copy(wide.at[part], wide_out.at[part], wide_done.at[piece])
+
+    weight_copy = pltpu.make_async_copy(weight, weight_out, out_done.at[0])
+    output_copy = pltpu.make_async_copy(output_weight, output_out, out_done.at[1])
 
     @pl.loop(0, PIECES + 7)
     def _(step):
@@ -783,11 +823,13 @@
             products(piece, 1 - ctx, stage.at[piece_rows(piece)])
             swap.start(piece)
             products(piece, ctx, heads.at[piece_rows(piece, ctx * rows)])
+            wide_copy(piece).start()
 
         @pl.when(step == 7)
         def _():
             gather.third()
             gather.last()
+            weight_copy.start()
 
         late(0, lambda piece: line.spread_start(piece, source(piece)), 2)
         late(7, use)
@@ -816,42 +858,54 @@
         swap.wait_sent(piece)
 
     output_gather.last()
+    output_copy.start()
     marks.wait_sent()
     gather.wait_sent()
     output_gather.wait_sent()
+    for grad in grads:
+        grad.wait()
+    weight_copy.wait()
+    output_copy.wait()
+
+    @pl.loop(0, PIECES)
+    def _(piece):
+        wide_copy(piece).wait()
+
     line.spread_finish(PIECES, source)
 
 
 def enter(
-    tokens, marks, query_weight, key_weight, value_weight, output_weight, bias, collective_id
+    tokens, gains, biases, query_weight, key_weight, value_weight, output_weight, query_bias,
+    value_bias, out_grad, collective_id,
 ):
     count = lax.axis_size("tp")
     rows, width = tokens.shape
     head_cols = query_weight.shape[1]
-    plane = 8
+    features = count * width
     part = 3 * head_cols // 2
+    own = rows // PIECES // count
+    low = jnp.bfloat16
+    vmem, anywhere = pl.BlockSpec(memory_space=pltpu.VMEM), pl.BlockSpec(memory_space=pl.ANY)
     return pl.pallas_call(
         functools.partial(enter_kernel, count),
         out_shape=[
-            jax.ShapeDtypeStruct((rows, count * width), tokens.dtype),
-            jax.ShapeDtypeStruct((rows // count, count * width), tokens.dtype),
-            jax.ShapeDtypeStruct((marks.shape[0], count * width), marks.dtype),
-            jax.ShapeDtypeStruct((plane * query_weight.shape[0], 2 * part), query_weight.dtype),
-            jax.ShapeDtypeStruct(
-                (plane * output_weight.shape[0], output_weight.shape[1]), output_weight.dtype
-            ),
-            jax.ShapeDtypeStruct((2 * rows, part), jnp.bfloat16),
+            jax.ShapeDtypeStruct((rows, features), low),
+            jax.ShapeDtypeStruct((rows // count, features), low),
+            jax.ShapeDtypeStruct((8, features), jnp.float32),
+            jax.ShapeDtypeStruct((features, 2 * part), low),
+            jax.ShapeDtypeStruct((features, head_cols), low),
+            jax.ShapeDtypeStruct((2 * rows, part), low),
+            jax.ShapeDtypeStruct((count, PIECES, own, width), low),
         ],
-        in_specs=[
-            pl.BlockSpec(memory_space=pl.ANY),
-            pl.BlockSpec(memory_space=pltpu.VMEM),
-            *[pl.BlockSpec(memory_space=pl.ANY)] * 4,
-            pl.BlockSpec(memory_space=pltpu.VMEM),
-        ],
-        out_specs=[pl.BlockSpec(memory_space=pltpu.VMEM)] * 6,
+        in_specs=[anywhere, vmem, vmem, *[anywhere] * 4, vmem, vmem, anywhere],
+        out_specs=[anywhere, vmem, vmem, anywhere, anywhere, vmem, vmem],
         scratch_shapes=[
-            pltpu.VMEM((count - 1, *marks.shape), marks.dtype),
-            pltpu.VMEM((rows, part), jnp.bfloat16),
+            pltpu.VMEM((rows, features), low),
+            pltpu.VMEM((features, 2 * part), low),
+            pltpu.VMEM((features, head_cols), low),
+            pltpu.VMEM((8, width), jnp.float32),
+            pltpu.VMEM((count - 1, 8, width), jnp.float32),
+            pltpu.VMEM((rows, part), low),
             *line_semaphores(count, PIECES)[1],
             pltpu.SemaphoreType.DMA((count - 1,)),
             pltpu.SemaphoreType.DMA((count - 1,)),
@@ -859,15 +913,21 @@
             pltpu.SemaphoreType.DMA((PIECES,)),
             pltpu.SemaphoreType.DMA((PIECES,)),
             pltpu.SemaphoreType.DMA((8,)),
+            pltpu.SemaphoreType.DMA((count,)),
+            pltpu.SemaphoreType.DMA((PIECES,)),
+            pltpu.SemaphoreType.DMA((2,)),
         ],
         compiler_params=pltpu.CompilerParams(
             collective_id=collective_id, has_side_effects=True, vmem_limit_bytes=60 << 20
         ),
         cost_estimate=pl.CostEstimate(
-            flops=80_000_000_000, bytes_accessed=64 * rows * count * width, transcendentals=0
+            flops=80_000_000_000, bytes_accessed=64 * rows * features, transcendentals=0
         ),
         name="enter",
-    )(tokens, marks, query_weight, key_weight, value_weight, output_weight, bias)
+    )(
+        tokens, gains, biases, query_weight, key_weight, value_weight, output_weight,
+        query_bias[None], value_bias[None], out_grad.reshape(PIECES, count, own, width),
+    )
 
 
 def relay_kernel(count, row_step, use_step, sizes, *refs):
@@ -986,12 +1046,12 @@
 
 
 def first_norm_step(piece, total, inputs, outputs):
-    tokens, gains, biases = inputs
+    tokens, marks = inputs
     first_norm, normed_one, inverse_one = outputs
     part = own_rows_of(piece, tokens)
-    summed = tokens[part, :].astype(jnp.float32) + (total[...] + biases[0:1, :])
+    summed = tokens[part, :].astype(jnp.float32) + (total[...] + marks[2:3, :])
     normed, inverse = norm_parts(summed)
-    result = normed * gains[0:1, :] + biases[1:2, :]
+    result = normed * marks[0:1, :] + marks[3:4, :]
     first_norm[part, :] = result
     normed_one[part, :] = normed
     inverse_one[part, :] = jnp.broadcast_to(inverse, (inverse.shape[0], 128))
@@ -1020,17 +1080,17 @@
 
 
 def second_norm_step(piece, total, inputs, outputs):
-    first_norm, out_grad, gains, biases = inputs
+    first_norm, out_grad, marks = inputs
     mixed, grad_second, sums = outputs
     part = own_rows_of(piece, first_norm)
-    normed, inverse = norm_parts(first_norm[part, :] + total[...] + biases[2:3, :])
-    result = (normed * gains[1:2, :] + biases[3:4, :]).astype(jnp.bfloat16)
+    normed, inverse = norm_parts(first_norm[part, :] + total[...] + marks[4:5, :])
+    result = (normed * marks[1:2, :] + marks[5:6, :]).astype(jnp.bfloat16)
     count, _, width = mixed.shape
     for i in range(count):
         mixed[i, part, :] = result[:, i * width : (i + 1) * width]
     upstream = jnp.concatenate([out_grad[i, part, :] for i in range(count)], axis=1)
     upstream = upstream.astype(jnp.float32)
-    grad = norm_back(upstream, normed, inverse, gains[1:2, :])
+    grad = norm_back(upstream, normed, inverse, marks[1:2, :])
     grad_second[part, :] = grad
     low = grad.astype(jnp.bfloat16)
     add_sums(piece, sums, upstream * normed, upstream, low.astype(jnp.float32))
@@ -1063,12 +1123,12 @@
 
 
 def first_back_step(piece, total, inputs, outputs):
-    grad_second, normed_one, inverse_one, gains = inputs
+    grad_second, normed_one, inverse_one, marks = inputs
     grad_inner, sums = outputs
     part = own_rows_of(piece, grad_second)
     normed = normed_one[part, :]
     grad_first = grad_second[part, :] + total[...]
-    grad = norm_back(grad_first, normed, inverse_one[part, 0:1], gains[0:1, :])
+    grad = norm_back(grad_first, normed, inverse_one[part, 0:1], marks[0:1, :])
     grad_inner[part, :] = grad
     low = grad.astype(jnp.bfloat16)
     add_sums(piece, sums, grad_first * normed, grad_first, low.astype(jnp.float32))
@@ -1211,8 +1271,8 @@
 
 
 def middle_kernel(
-    count, heads_ref, output_weight, expand_shard, shrink_shard, own_tokens, out_grad, gains,
-    biases, hidden_bias,
+    count, heads_ref, output_weight, expand_shard, shrink_shard, own_tokens, out_grad, marks,
+    hidden_bias,
     attended, mixed, inner, branch_out, grad_heads, first_sums, second_sums, hidden_sums,
     shrink_out, expand_out,
     expand_weight, shrink_weight, gathered, activated, slope, normed_one, inverse_one,
@@ -1291,7 +1351,8 @@
             chunk = gathered[chunk_rows, :]
 
             def expand(columns):
-                values = dot_plain(chunk, expand_weight[:, columns]) + hidden_bias[:, columns]
+                values = dot_plain(chunk, expand_weight[:, columns])
+                values += hidden_bias[:, columns].astype(jnp.float32)
                 result, bend = gelu_with_slope(values)
                 activated[part, columns] = result.astype(jnp.bfloat16)
                 slope[part, columns] = bend.astype(jnp.bfloat16)
@@ -1360,19 +1421,19 @@
         @pl.when(in_stage(piece, 0))
         def _():
             view(piece, me)[...] = first_norm_step(
-                place, total, (own_tokens, gains, biases), (inner, normed_one, inverse_one)
+                place, total, (own_tokens, marks), (inner, normed_one, inverse_one)
             )
 
         @pl.when(in_stage(piece, 1))
         def _():
             view(piece, me)[...] = second_norm_step(
-                place, total, (inner, out_grad, gains, biases), (mixed, inner, second_sums)
+                place, total, (inner, out_grad, marks), (mixed, inner, second_sums)
             )
 
         @pl.when(in_stage(piece, 2))
         def _():
             view(piece, me)[...] = first_back_step(
-                place, total, (inner, normed_one, inverse_one, gains), (inner, first_sums)
+                place, total, (inner, normed_one, inverse_one, marks), (inner, first_sums)
             )
 
         line.spread_start(piece)
@@ -1400,12 +1461,13 @@
 
     def shrink_step(number):
         pl.when(number == 0)(shrink_gather.wait_sent)
-        fsdp = jnp.where(number < 2, plane_sum.twin, plane_sum.fsdp)
-        for over_y in (1, 0):
-            owner = plane_sum.number(fsdp, 1 - lax.rem(number, 2), over_y)
-            gradient(owner, rows, activated, shrink_weight.at[plane_sum.rows(owner)])
-
-        @pl.when(number == 3)
+        fsdp = jnp.where(number == 0, plane_sum.twin, plane_sum.fsdp)
+        for over_x in (1, 0):
+            for over_y in (1, 0):
+                owner = plane_sum.number(fsdp, over_x, over_y)
+                gradient(owner, rows, activated, shrink_weight.at[plane_sum.rows(owner)])
+
+        @pl.when(number == 1)
         def _():
             pl.semaphore_signal(ready, inc=1, device_id=twin, device_id_type=MESH)
 
@@ -1426,8 +1488,8 @@
                 action(step - number)
 
         pl.when(step == 5)(expand_gather.last)
-        pl.when(step == 2 * PIECES + 9)(plane_sum.second)
-        pl.when(step == 2 * PIECES + 12)(plane_sum.third)
+        pl.when(step == 2 * PIECES + 7)(plane_sum.second)
+        pl.when(step == 2 * PIECES + 9)(plane_sum.third)
         late(5, use)
         late(3, lambda piece: line.spread_onward(piece, 2))
         late(1, lambda piece: line.sum_onward(piece, term_of(piece), [1]))
@@ -1435,9 +1497,9 @@
         late(0, form)
         late(4, lambda piece: [line.spread_onward(piece, i) for i in range(3, count)])
         late(2, lambda piece: line.spread_onward(piece, 1))
-        late(2 * PIECES + 4, shrink_step, 4)
+        late(2 * PIECES + 4, shrink_step, 2)
         late(2 * PIECES + 5, expand_step, PIECES)
-        late(2 * PIECES + 8, shrink_send, 1)
+        late(2 * PIECES + 6, shrink_send, 1)
         late(0, lambda piece: line.sum_onward(piece, term_of(piece), range(count - 2, 1, -1)))
         late(1, own_step)
 
@@ -1484,7 +1546,7 @@
 
 
 def middle(
-    attended_heads, output_weight, expand_shard, shrink_shard, own_tokens, out_grad, gains, biases,
+    attended_heads, output_weight, expand_shard, shrink_shard, own_tokens, out_grad, marks,
     hidden_bias, collective_id,
 ):
     count = lax.axis_size("tp")
@@ -1515,7 +1577,7 @@
             shape((shard, hidden)),
             shape((width, hidden), low),
         ],
-        in_specs=[anywhere, vmem, anywhere, anywhere, vmem, vmem, vmem, vmem, vmem],
+        in_specs=[anywhere, vmem, anywhere, anywhere, vmem, vmem, vmem, vmem],
         out_specs=[vmem, vmem, vmem, anywhere, vmem, vmem, vmem, vmem, anywhere, anywhere],
         scratch_shapes=[
             pltpu.VMEM((width, hidden), low),
@@ -1548,8 +1610,8 @@
         ),
         name="middle",
     )(
-        attended_heads, output_weight, expand_shard, shrink_shard, own_tokens, out_grad, gains,
-        biases, hidden_bias,
+        attended_heads, output_weight, expand_shard, shrink_shard, own_tokens, out_grad, marks,
+        hidden_bias,
     )
 
 
@@ -1564,8 +1626,8 @@
 
 
 def input_kernel(
-    sizes, x_ref, weight, inner_ref, rows_ref, hidden_ref, out_ref, vectors_ref,
-    term_ref, total, slots, own_vectors, tp_slots, plane_slots,
+    sizes, x_ref, weight, inner_ref, first_ref, second_ref, hidden_ref, out_ref, vectors_ref,
+    rows_ref, term_ref, total, slots, own_vectors, tp_slots, plane_slots,
     sum_sent, sum_got, tp_sent, tp_got, plane_sent, plane_got, hooks=None,
 ):
     count = sizes[2]
@@ -1588,6 +1650,10 @@
         plane_peers, plane_sent, plane_got, lambda _: own_vectors, lambda i: plane_slots.at[i]
     )
     opening, before, after, closing = hooks or (lambda *_: None,) * 4
+    order = ((0, 0), (1, 0), (0, 2), (0, 1), (1, 2), (1, 1))
+    rows_ref[...] = jnp.zeros_like(rows_ref)
+    for i, (which, row) in enumerate(order):
+        rows_ref[i : i + 1, :] = (first_ref, second_ref)[which][row : row + 1, :]
     opening()
     over_tp.start()
 
@@ -1645,7 +1711,7 @@
     line.sum_finish(PIECES)
 
 
-def input_sum(x, weight, inner, row_sums, hidden_sums, collective_id):
+def input_sum(x, weight, inner, first_sums, second_sums, hidden_sums, collective_id):
     sizes = tuple(lax.axis_size(axis) for axis in ("fsdp", "ctx", "tp"))
     count = sizes[2]
     others = sizes[0] * sizes[1] - 1
@@ -1659,9 +1725,10 @@
             jax.ShapeDtypeStruct((rows, width), jnp.bfloat16),
             jax.ShapeDtypeStruct((packed, width), jnp.float32),
         ],
-        in_specs=[pl.BlockSpec(memory_space=pltpu.VMEM)] * 5,
+        in_specs=[pl.BlockSpec(memory_space=pltpu.VMEM)] * 6,
         out_specs=[pl.BlockSpec(memory_space=pltpu.VMEM)] * 2,
         scratch_shapes=[
+            pltpu.VMEM(first_sums.shape, jnp.float32),
             pltpu.VMEM((height, width), jnp.float32),
             pltpu.VMEM((height, width), jnp.float32),
             pltpu.VMEM((PIECES, count + 1, height, width), jnp.bfloat16),
@@ -1681,13 +1748,15 @@
             flops=60_000_000_000, bytes_accessed=64 * rows * width, transcendentals=0
         ),
         name="input_sum",
-    )(x, weight, inner, row_sums, hidden_sums)
+    )(x, weight, inner, first_sums, second_sums, hidden_sums)
 
 
 def leave_kernel(
-    sizes, grads_ref, tokens_ref, weight, inner_ref, rows_ref, hidden_ref, branch_ref, attended_ref,
+    sizes, grads_ref, tokens_in, weight_in, inner_in, first_ref, second_ref, hidden_ref, branch_in,
+    attended_in,
     out_ref, vectors_ref, query_out, key_out, value_out, output_out,
-    x_ref, term_ref, total, slots, own_vectors, tp_slots, plane_slots,
+    tokens_ref, weight, inner_ref, branch_ref, attended_ref, copied, own_copied,
+    x_ref, rows_ref, term_ref, total, slots, own_vectors, tp_slots, plane_slots,
     sum_sent, sum_got, tp_sent, tp_got, plane_sent, plane_got, swap_sent, swap_got, *sum_scratch,
 ):
     count = sizes[2]
@@ -1701,7 +1770,26 @@
     def piece_rows(piece, start=0):
         return pl.ds(pl.multiple_of(start + piece * height, height), height)
 
+    copies = [
+        pltpu.make_async_copy(source, place, copied.at[i])
+        for i, (source, place) in enumerate(
+            (
+                (branch_in, branch_ref),
+                (attended_in, attended_ref),
+                (weight_in, weight),
+                (inner_in, inner_ref),
+                (tokens_in, tokens_ref),
+            )
+        )
+    ]
+    for copy in copies:
+        copy.start()
     own_columns = pl.ds(pl.multiple_of(ctx * part, part), part)
+    own_block = pl.ds(pl.multiple_of(ctx * rows, rows), rows)
+    own_copy = pltpu.make_async_copy(
+        grads_ref.at[own_block], x_ref.at[:, own_columns], own_copied
+    )
+    own_copy.start()
     swap = Swap(
         swap_sent, swap_got,
         lambda piece: grads_ref.at[piece_rows(piece, (1 - ctx) * rows)],
@@ -1721,11 +1809,15 @@
         def _(piece):
             swap.start(piece)
 
+        for copy in copies[:2]:
+            copy.wait()
         products(output_sum, output_sum.twin, branch_ref, attended_ref)
         output_sum.start()
-        x_ref[:, own_columns] = grads_ref[pl.ds(pl.multiple_of(ctx * rows, rows), rows), :]
         products(output_sum, output_sum.fsdp, branch_ref, attended_ref)
         output_sum.second()
+        for copy in copies[2:]:
+            copy.wait()
+        own_copy.wait()
 
     last = PIECES - 1
     begin = jnp.where((me == 0) | (me == count - 1), last, 2)
@@ -1756,8 +1848,8 @@
         plane_sum.third()
 
     input_kernel(
-        sizes, x_ref, weight, inner_ref, rows_ref, hidden_ref, out_ref, vectors_ref,
-        term_ref, total, slots, own_vectors, tp_slots, plane_slots,
+        sizes, x_ref, weight, inner_ref, first_ref, second_ref, hidden_ref, out_ref, vectors_ref,
+        rows_ref, term_ref, total, slots, own_vectors, tp_slots, plane_slots,
         sum_sent, sum_got, tp_sent, tp_got, plane_sent, plane_got,
         hooks=(opening, before, after, closing),
     )
@@ -1778,7 +1870,10 @@
         swap.wait_sent(piece)
 
 
-def leave(grads, tokens, weight, inner, row_sums, hidden_sums, branch, attended, collective_id):
+def leave(
+    grads, tokens, weight, inner, first_sums, second_sums, hidden_sums, branch, attended,
+    collective_id,
+):
     sizes = tuple(lax.axis_size(axis) for axis in ("fsdp", "ctx", "tp"))
     count = sizes[2]
     others = sizes[0] * sizes[1] - 1
@@ -1795,10 +1890,18 @@
             jax.ShapeDtypeStruct((packed, width), jnp.float32),
             *[jax.ShapeDtypeStruct((shard, 2 * part // 3), jnp.float32)] * 4,
         ],
-        in_specs=[pl.BlockSpec(memory_space=pltpu.VMEM)] * 8,
+        in_specs=[
+            *[pl.BlockSpec(memory_space=pl.ANY)] * 4,
+            *[pl.BlockSpec(memory_space=pltpu.VMEM)] * 3,
+            *[pl.BlockSpec(memory_space=pl.ANY)] * 2,
+        ],
         out_specs=[pl.BlockSpec(memory_space=pltpu.VMEM)] * 6,
         scratch_shapes=[
+            *[pltpu.VMEM(x.shape, x.dtype) for x in (tokens, weight, inner, branch, attended)],
+            pltpu.SemaphoreType.DMA((5,)),
+            pltpu.SemaphoreType.DMA,
             pltpu.VMEM((rows, 2 * part), jnp.bfloat16),
+            pltpu.VMEM(first_sums.shape, jnp.float32),
             pltpu.VMEM((height, width), jnp.float32),
             pltpu.VMEM((height, width), jnp.float32),
             pltpu.VMEM((PIECES, count + 1, height, width), jnp.bfloat16),
@@ -1822,7 +1925,7 @@
             flops=60_000_000_000, bytes_accessed=64 * rows * width, transcendentals=0
         ),
         name="leave",
-    )(grads, tokens, weight, inner, row_sums, hidden_sums, branch, attended)
+    )(grads, tokens, weight, inner, first_sums, second_sums, hidden_sums, branch, attended)
 
 
 def to_own_rows(wide):
@@ -1833,19 +1936,20 @@
     )
 
 
-def spread_own(block):
+def by_owner(block):
     count = lax.axis_size("tp")
-    rows, width = block.shape
+    width = block.shape[1]
     parts = block.reshape(PIECES, count, -1, width).transpose(1, 0, 2, 3)
-    return lax.all_to_all(
-        parts.reshape(count, -1, width), "tp", split_axis=0, concat_axis=0, tiled=True
-    )
-
-
-def unspread_own(parts):
-    count, own_rows, width = parts.shape
-    got = lax.all_to_all(parts, "tp", split_axis=0, concat_axis=0, tiled=True)
-    return got.reshape(count, PIECES, -1, width).transpose(1, 0, 2, 3).reshape(-1, width)
+    return parts.reshape(count, -1, width)
+
+
+def swap_over_tp(parts):
+    return lax.all_to_all(parts, "tp", split_axis=0, concat_axis=0, tiled=True)
+
+
+def by_rows(parts):
+    count, _, width = parts.shape
+    return parts.reshape(count, PIECES, -1, width).transpose(1, 0, 2, 3).reshape(-1, width)
 
 
 def body(
@@ -1874,25 +1978,23 @@
     def weight_rows(weight):
         return lax.all_gather(weight, plane, axis=0, tiled=True)
 
-    marks = jnp.concatenate(
-        [norm_gains, row_biases, jnp.zeros((10, norm_gains.shape[1]), norm_gains.dtype)]
-    )
     block_index = lax.axis_index("fsdp") * plane_sizes[1] + lax.axis_index("ctx")
-    qkv_bias = jnp.stack([query_bias, jnp.zeros_like(query_bias), value_bias])
-    qkv_bias = qkv_bias.astype(jnp.float32)
     if by_heads:
-        half_bias = qkv_bias.reshape(3, 2, -1).transpose(1, 0, 2).reshape(1, -1)
-        wide_tokens, own_tokens, wide_marks, wide_qkv, full_output, qkv_heads = enter(
-            tokens, marks, query_weight, key_weight, value_weight, output_weight, half_bias, 0
+        wide_tokens, own_tokens, marks, wide_qkv, full_output, qkv_heads, upstream = enter(
+            tokens, norm_gains, row_biases, query_weight, key_weight, value_weight, output_weight,
+            query_bias, value_bias, out_grad, 0,
         )
+        upstream = upstream.reshape(upstream.shape[0], -1, upstream.shape[3])
         queries = keys = values = qkv_heads
         own_heads = heads // 2
         bounds = (segments.reshape(-1, plane_sizes[1] * rows),)
     else:
         wide_qkv = weight_rows(jnp.concatenate([query_weight, key_weight, value_weight], axis=1))
-        wide_tokens, wide_marks = gather_features(tokens, marks, 0)
+        wide_tokens, marks = gather_features(tokens, norm_gains, row_biases, 0)
+        upstream = by_owner(out_grad)
         own_tokens = to_own_rows(wide_tokens)
-        qkv = dot_plain(wide_tokens, wide_qkv) + qkv_bias.reshape(1, -1)
+        qkv_bias = jnp.concatenate([query_bias, jnp.zeros_like(query_bias), value_bias])
+        qkv = dot_plain(wide_tokens, wide_qkv) + qkv_bias.astype(jnp.float32)
         queries, keys, values = jnp.split(qkv.astype(jnp.bfloat16), 3, axis=1)
         own_heads = heads
         keys, values = padded(keys, WIN), padded(values, WIN)
@@ -1907,10 +2009,8 @@
         key_ids = lax.dynamic_slice_in_dim(ids, block_index * rows, rows + 2 * WIN, 0)
         bounds = key_bounds(key_ids[WIN : WIN + rows], key_ids, WIN)
     places = (0, own_heads, 2 * own_heads) if by_heads else (0, 0, 0)
-    gains = wide_marks[:2].astype(jnp.float32)
-    biases = wide_marks[2:6].astype(jnp.float32)
-    wide_marks, out_grad = lax.optimization_barrier((wide_marks, out_grad))
-    upstream = spread_own(out_grad)
+    marks, upstream = lax.optimization_barrier((marks, upstream))
+    upstream = swap_over_tp(upstream)
     attended_heads, lse = attend(queries, keys, values, own_heads, bounds, places)
     attended_heads, upstream = lax.optimization_barrier((attended_heads, upstream))
 
@@ -1932,10 +2032,10 @@
             first_sums, second_sums, hidden_sums, shrink_grad, expand_part,
         ) = middle(
             attended_heads, full_output, expand_weight, shrink_weight, own_tokens, upstream,
-            gains, biases, hidden_bias.astype(jnp.float32)[None], 1,
+            marks, hidden_bias[None], 1,
         )
         expand_grad = owner_sum(expand_part)
-        mixed = unspread_own(mixed_own)
+        mixed = by_rows(swap_over_tp(mixed_own))
         (grads,) = attend_back(
             queries, keys, values, attended_heads, attended_grad, lse, bounds, places, True
         )
@@ -1944,7 +2044,7 @@
         full_shrink = weight_rows(shrink_weight)
         norm_low, first_norm, normed_one, inverse_one, hidden, activated = relay(
             attended_heads, full_output, full_expand,
-            [own_tokens, gains, biases], first_norm_step,
+            [own_tokens, marks], first_norm_step,
             [own_shape, own_shape, shape((own_rows, 128))],
             [hidden_bias.astype(jnp.float32)[None]], expand_step,
             [shape((rows, hidden_cols)), shape((rows, hidden_cols), jnp.bfloat16)],
@@ -1952,7 +2052,7 @@
         )
         ffn_low, mixed_own, grad_second, second_sums, hidden_low, hidden_sums = relay(
             activated, full_shrink, None,
-            [first_norm, upstream, gains, biases], second_norm_step,
+            [first_norm, upstream, marks], second_norm_step,
             [shape(upstream.shape, jnp.bfloat16), own_shape, shape((8, features))],
             [hidden], shrink_step,
             [shape((rows, hidden_cols), jnp.bfloat16), shape((8, hidden_cols))],
@@ -1961,7 +2061,7 @@
         shrink_grad = owner_sum(dot_rows(ffn_low, activated).astype(jnp.bfloat16))
         branch_low, grad_inner, first_sums, attended_grad = relay(
             hidden_low, full_expand, full_output,
-            [grad_second, normed_one, inverse_one, gains], first_back_step,
+            [grad_second, normed_one, inverse_one, marks], first_back_step,
             [own_shape, shape((8, features))],
             [], attended_step,
             [shape((rows, head_cols), jnp.bfloat16)],
@@ -1969,7 +2069,7 @@
         )
         expand_grad = owner_sum(dot_rows(norm_low, hidden_low).astype(jnp.bfloat16))
         output_grad = owner_sum(dot_rows(branch_low, attended_heads).astype(jnp.bfloat16))
-        mixed = unspread_own(mixed_own)
+        mixed = by_rows(swap_over_tp(mixed_own))
         query_low, key_ext, value_ext = attend_back(
             queries, keys, values, attended_heads, attended_grad, lse, bounds
         )
@@ -1982,13 +2082,6 @@
             return own.astype(jnp.bfloat16)
 
         qkv_low = jnp.concatenate([query_low, fold(key_ext), fold(value_ext)], axis=1)
-    row_sums = jnp.concatenate(
-        [
-            first_sums[0:1], second_sums[0:1],
-            first_sums[2:3], first_sums[1:2], second_sums[2:3], second_sums[1:2],
-            jnp.zeros_like(first_sums[:2]),
-        ]
-    )
     sides = 2 if by_heads else 1
 
     def by_kind(columns):
@@ -1997,13 +2090,13 @@
 
     if by_heads:
         input_grad, vectors, query_grad, key_grad, value_grad, output_grad = leave(
-            grads, wide_tokens, wide_qkv, grad_inner, row_sums, hidden_sums[:1], branch_low,
-            attended, 4,
+            grads, wide_tokens, wide_qkv, grad_inner, first_sums, second_sums, hidden_sums,
+            branch_low, attended, 4,
         )
         input_grad, expand_grad = lax.optimization_barrier((input_grad, expand_grad))
     else:
         input_grad, vectors = input_sum(
-            qkv_low, wide_qkv, grad_inner, row_sums, hidden_sums[:1], 4
+            qkv_low, wide_qkv, grad_inner, first_sums, second_sums, hidden_sums, 4
         )
         qkv_grad = owner_sum(dot_rows(wide_tokens, qkv_low).astype(jnp.bfloat16))
         query_grad, key_grad, value_grad = by_kind(qkv_grad.astype(jnp.float32))

time: 659 us -> 631 us (0.958)
  Pallas kernels: 592 us -> 581 us
  local copies, waits for them, and re-layouts: 26 us -> 15.9 us
    pallas_call x1, Pallas kernels: 348 us -> 333 us  [middle(): pl.pallas_call(functools.partial(middle_kernel, count), out_shape=[shape(...]
  transfers between devices with their start and end apart: 3 -> 3, of which waited for: 0 -> 0; matrix products, arithmetic and copies ran while one was open for 2% -> 1% of each run, Pallas kernels for 24% -> 26%
where the time goes in v12:
time: 631 us; the launch traced here: 630 us
  Pallas kernels  581 us (92%)
  starting transfers between devices  16 us (3%)
  local copies, waits for them, and re-layouts  15.9 us (3%)
  between operations  14.1 us (2%)
    pallas_call x1, Pallas kernels, middle(): pl.pallas_call(functools.partial(middle_kernel, count), out_shape=[shape(...  333 us
    pallas_call x1, Pallas kernels, leave(): pl.pallas_call(functools.partial(leave_kernel, sizes), out_shape=[jax.Sha...  118 us
    pallas_call x1, Pallas kernels, enter(): pl.pallas_call(functools.partial(enter_kernel, count), out_shape=[jax.Sha...  81.3 us
    pallas_call x1, Pallas kernels, attend_back(): pl.pallas_call(functools.partial(attend_back_kernel, len(scalars), len(ar...  27 us
    pallas_call x1, Pallas kernels, attend(): pl.pallas_call(functools.partial(attend_kernel, len(scalars)), out_shape=...  20.9 us
    all_to_all x2, starting transfers between devices, swap_over_tp(): return lax.all_to_all(parts, 'tp', split_axis=0, concat_axis=0, tiled=True)  16 us
  transfers between devices with their start and end apart: 3, of which 0 were waited for; matrix products, arithmetic and copies ran while one was open for 1% of the time, Pallas kernels for 26%

profile of v12, /device:TPU:8, one launch (start us, length us, event | category | flops | bytes accessed | tf_op | source)
XLA Modules:
  0.0 629.5 jit_solution(6451040404685621003)
XLA Ops:
  7.2 1.3 broadcast_in_dim.9.query_bias
  8.4 1.3 broadcast_in_dim.10.value_bias
  9.7 0.0 copy-start.8
  9.7 0.0 copy-start.7
  9.7 81.3 %enter.1 = (bf16[1024,2048]{1,0:T(8,128)(2,1)}, bf16[256,2048]{1,0:T(8,128)(2,1)}, f32[8,2048]{1,0:T(8,128)}, bf16[2048,1536]{1,0:T(8,128)(2,1)}, bf16[2048,512]...) custom-call(bf16[1024,512]{1,0:T(8,128)(2,1)} %x_ref.1, bf16[2,512]{1,0:T(2,128)(2,1)} %gains.1, ...), custom_call_target="tpu_custom_call" | custom-call | flops 80000000000 | bytes 134217728 | tf_op jit(solution)/shard_map/enter/pallas_call | solution.py:889
  91.0 10.5 %all-to-all-start = ((bf16[4,256,512]{2,1,0:T(8,128)(2,1)}), bf16[4,256,512]{2,1,0:T(8,128)(2,1)S(1)}, u32[]{:S(2)}, u32[]{:S(2)}) async-start(bf16[4,256,512]{2,1,0:T(8,128)(2,1)} %bitcast.13), calls=%async_computation | async-start | bytes 2097152 | tf_op jit(solution)/shard_map/all_to_all | solution.py:1947
  101.6 0.0 reduce-scatter.2.cloned.1.call-start
  101.6 0.0 copy-done.8
  101.6 0.6 broadcast_in_dim.11.hidden_bias
  102.2 0.0 copy-done.7
  102.2 0.6 reshape.45.refs_3_.refs_6_
  102.8 20.9 %attend.1 = (bf16[2048,256]{1,0:T(8,128)(2,1)}, f32[2,1,2048]{2,1,0:T(1,128)}) custom-call(bf16[2048,768]{1,0:T(8,128)(2,1)} %get-tuple-element.46.refs_0_.refs_1_.refs_2_, bf16[2048,768]{1,0:T(8,128)(2,1)} %get-tuple-element.46.refs_0_.refs_1_.refs_2_, bf16[2048,768]{1,0:T(8,128)(2,1)} %get-tuple-element.46.refs_0_.refs_1_.refs_2_, ...), custom_call_target="tpu_custom_call" | custom-call | flops 3221225472 | bytes 4194304 | tf_op jit(solution)/shard_map/attend/pallas_call | solution.py:130
  123.8 0.0 all-to-all-done.out_grad
  123.8 0.0 copy-start.2
  123.8 1.0 copy-done.2
  124.7 333.4 %middle.1 = (bf16[1024,512]{1,0:T(8,128)(2,1)}, bf16[4,256,512]{2,1,0:T(8,128)(2,1)}, f32[256,2048]{1,0:T(8,128)}, bf16[1024,2048]{1,0:T(8,128)(2,1)}, bf16[2048...) custom-call(bf16[2048,256]{1,0:T(8,128)(2,1)} %get-tuple-element.51., ...), custom_call_target="tpu_custom_call" | custom-call | flops 299999985664 | bytes 402653184 | tf_op jit(solution)/shard_map/middle/pallas_call | solution.py:1566
  458.2 0.0 reduce-scatter.2.cloned.1.call-update
  458.2 5.5 all-to-all-start.1
  463.7 27.0 %attend_back.1.grads_ref = bf16[2048,768]{1,0:T(8,128)(2,1)} custom-call(bf16[2048,768]{1,0:T(8,128)(2,1)} %get-tuple-element.46.refs_0_.refs_1_.refs_2_, bf16[2048,768]{1,0:T(8,128)(2,1)} %get-tuple-element.46.refs_0_.refs_1_.refs_2_, bf16[2048,768]{1,0:T(8,128)(2,1)} %get-tuple-element.46.refs_0_.refs_1_.refs_2_, ...), custom_call_target="tpu_custom_call" | custom-call | flops 8589934592 | bytes 8388608 | tf_op jit(solution)/shard_map/attend_back/pallas_call | solution.py:229
  490.7 0.0 all-to-all-done.1
  490.7 1.0 copy.28
  491.8 117.9 %leave.1 = (bf16[1024,512]{1,0:T(8,128)(2,1)}, f32[16,512]{1,0:T(8,128)}, f32[256,512]{1,0:T(8,128)}, f32[256,512]{1,0:T(8,128)}, f32[256,512]{1,0:T(8,128)}, /*index=5*/f32[256,512]{1,0:T(8,128)}) custom-call(bf16[2048,768]{1,0:T(8,128)(2,1)} %attend_back.1.grads_ref, bf16[1024,2048]{1,0:T(8,128)(2,1)} %get-tuple-element.61.tokens_in, ...), custom_call_target="tpu_custom_call" | custom-call | flops 60000002048 | bytes 33554432 | tf_op jit(solution)/shard_map/leave/pallas_call | solution.py:1886
  609.6 0.0 copy-start.1
  609.6 0.0 copy-start.6
  609.6 1.4 slice.22
  611.1 0.7 slice.18
  611.8 1.3 fusion
  613.1 0.6 copy.29
  613.7 0.6 fusion.1
  614.3 0.0 reduce-scatter.2.cloned.1.call-done
  614.3 0.0 copy-start.5
  614.3 0.0 copy-start.4
  614.3 2.9 convert_element_type.3
  617.2 0.0 copy-start.3
  617.2 0.0 copy-done.1
  617.2 0.0 copy-start
  617.2 1.0 copy.36
  618.2 0.0 copy-done.6
  618.2 0.8 copy.37
  619.0 0.0 copy-done.5
  619.0 0.8 copy.38
  619.8 0.0 copy-done.4
  619.8 0.8 copy.39
  620.6 0.0 copy-done.3
  620.6 0.8 copy.40
  621.4 0.0 copy-done
  621.4 1.3 copy.41
  (1 shorter events, 0.0 us)
Async XLA Ops:
  9.7 91.9 %copy-start.8 = (bf16[2048]{0:T(1024)(128)(2,1)S(1)}, bf16[2048]{0:T(1024)(128)(2,1)}, u32[]{:S(2)}) copy-start(bf16[2048]{0:T(1024)(128)(2,1)} %param.24) | copy-start | bytes 12292
  9.7 92.5 %copy-start.7 = (s32[8192]{0:T(1024)S(1)}, s32[8192]{0:T(1024)}, u32[]{:S(2)}) copy-start(s32[8192]{0:T(1024)} %param.15) | copy-start | bytes 98308
  91.0 32.7 %all-to-all-start = ((bf16[4,256,512]{2,1,0:T(8,128)(2,1)}), bf16[4,256,512]{2,1,0:T(8,128)(2,1)S(1)}, u32[]{:S(2)}, u32[]{:S(2)}) async-start(bf16[4,256,512]{2,1,0:T(8,128)(2,1)} %bitcast.13), calls=%async_computation | async-start | bytes 2097152 | tf_op jit(solution)/shard_map/all_to_all | solution.py:1947
  101.6 512.8 %reduce-scatter.2.cloned.1.call-start = ((), (), s32[]{:S(2)}) async-start(), calls=%async_computation.3 | async-start | bytes 9437184 | tf_op jit(solution)/shard_map/reduce_scatter | solution.py:2025
  123.8 1.0 copy-start.2
  458.2 32.5 %all-to-all-start.1 = ((bf16[4,256,512]{2,1,0:T(8,128)(2,1)}), bf16[4,256,512]{2,1,0:T(8,128)(2,1)S(1)}, u32[]{:S(2)}, u32[]{:S(2)}) async-start(bf16[4,256,512]{2,1,0:T(8,128)(2,1)} %get-tuple-element.58), calls=%async_computation.1 | async-start | bytes 2097152 | tf_op jit(solution)/shard_map/all_to_all | solution.py:1947
  609.6 7.6 %copy-start.1 = (bf16[1024,512]{1,0:T(8,128)(2,1)S(1)}, bf16[1024,512]{1,0:T(8,128)(2,1)}, u32[]{:S(2)}) copy-start(bf16[1024,512]{1,0:T(8,128)(2,1)} %get-tuple-element.97) | copy-start | bytes 3145732
  609.6 8.6 %copy-start.6 = (f32[256,512]{1,0:T(8,128)S(1)}, f32[256,512]{1,0:T(8,128)}, u32[]{:S(2)}) copy-start(f32[256,512]{1,0:T(8,128)} %get-tuple-element.98) | copy-start | bytes 1572868
  614.3 4.7 copy-start.5
  614.3 5.5 copy-start.4
  617.2 3.4 copy-start.3
  617.2 4.2 copy-start
Sparse Core Ops, SparseCore 0:
  458.3 89.1 reduce-scatter.1

commit v13 on v12

--- a/solution.py
+++ b/solution.py
@@ -12,6 +12,7 @@
 WIN = 1024
 QB = 512
 KB = 512
+GROUP = 2
 
 epsilon = 1e-06
 hidden_floor = -1e30
@@ -81,51 +82,63 @@
     return [], list(bounds), [pl.BlockSpec(shape, lambda h, i, *_: (0, 0))]
 
 
+def head_columns(head):
+    return slice(head * HD, (head + 1) * HD)
+
+
 def attend_kernel(scalars, *refs):
     bounds = refs[:scalars]
     q_ref, k_ref, v_ref, *arrays, out_ref, lse_ref, vt, marks = refs[scalars:]
     block = pl.program_id(1)
     rows = q_ref.shape[0]
+    heads = range(GROUP)
 
     @pl.when(block == 0)
     def _():
         vt[...] = v_ref[...].T
 
-    queries = q_ref[...]
+    queries = [q_ref[:, head_columns(h)] for h in heads]
     *span, low, high = block_bounds(block, rows, (*bounds, *arrays), marks)
     places = lax.broadcasted_iota(jnp.int32, (KB, rows), 0)
 
     def step(masked, number, carry):
-        top, total, mixed = carry
         start = pl.multiple_of(number * KB, KB)
-        scores = dot_cols(k_ref[pl.ds(start, KB), :], queries) * (score_scale * log2_e)
+        window = pl.ds(start, KB)
+        scores = [dot_cols(k_ref[window, head_columns(h)], queries[h]) for h in heads]
+        scores = [score * (score_scale * log2_e) for score in scores]
         if masked:
             keep = (places >= low - start) & (places <= high - start)
-            scores = jnp.where(keep, scores, hidden_floor)
-        new_top = jnp.maximum(top, jnp.max(scores, axis=0, keepdims=True))
-        shrink = jnp.exp2(top - new_top)
-        powers = jnp.exp2(scores - new_top)
-        total = total * shrink + jnp.sum(powers, axis=0, keepdims=True)
-        mixed = mixed * shrink + dot_plain(vt[:, pl.ds(start, KB)], powers.astype(jnp.bfloat16))
-        return new_top, total, mixed
-
-    top, total, mixed = over_key_blocks(
-        step,
-        span,
-        (
-            jnp.full((1, rows), hidden_floor, jnp.float32),
-            jnp.zeros((1, rows), jnp.float32),
-            jnp.zeros((HD, rows), jnp.float32),
-        ),
+            scores = [jnp.where(keep, score, hidden_floor) for score in scores]
+        tops = [
+            jnp.maximum(carry[h][0], jnp.max(scores[h], axis=0, keepdims=True)) for h in heads
+        ]
+        powers = [jnp.exp2(scores[h] - tops[h]) for h in heads]
+        parts = [
+            dot_plain(vt[head_columns(h), window], powers[h].astype(jnp.bfloat16)) for h in heads
+        ]
+        result = []
+        for h in heads:
+            top, total, mixed = carry[h]
+            shrink = jnp.exp2(top - tops[h])
+            total = total * shrink + jnp.sum(powers[h], axis=0, keepdims=True)
+            result.append((tops[h], total, mixed * shrink + parts[h]))
+        return tuple(result)
+
+    start = (
+        jnp.full((1, rows), hidden_floor, jnp.float32),
+        jnp.zeros((1, rows), jnp.float32),
+        jnp.zeros((HD, rows), jnp.float32),
     )
-    out_ref[...] = (mixed / total).T.astype(out_ref.dtype)
-    lse_ref[...] = (top + jnp.log2(total))[None]
+    for h, (top, total, mixed) in enumerate(over_key_blocks(step, span, (start,) * GROUP)):
+        out_ref[:, head_columns(h)] = (mixed / total).T.astype(out_ref.dtype)
+        lse_ref[h] = top + jnp.log2(total)
 
 
 def attend(queries, keys, values, heads, bounds, places=(0, 0, 0)):
     rows, span = queries.shape[0], keys.shape[0]
     width = heads * HD
-    q_at, k_at, v_at = places
+    q_at, k_at, v_at = (place // GROUP for place in places)
+    some = GROUP * HD
     scalars, arrays, specs = bound_operands(bounds)
     return pl.pallas_call(
         functools.partial(attend_kernel, len(scalars)),
@@ -135,18 +148,18 @@
         ),
         grid_spec=pltpu.PrefetchScalarGridSpec(
             num_scalar_prefetch=len(scalars),
-            grid=(heads, rows // QB),
+            grid=(heads // GROUP, rows // QB),
             in_specs=[
-                pl.BlockSpec((QB, HD), lambda h, i, *_: (i, h + q_at)),
-                pl.BlockSpec((span, HD), lambda h, i, *_: (0, h + k_at)),
-                pl.BlockSpec((span, HD), lambda h, i, *_: (0, h + v_at)),
+                pl.BlockSpec((QB, some), lambda h, i, *_: (i, h + q_at)),
+                pl.BlockSpec((span, some), lambda h, i, *_: (0, h + k_at)),
+                pl.BlockSpec((span, some), lambda h, i, *_: (0, h + v_at)),
                 *specs,
             ],
             out_specs=[
-                pl.BlockSpec((QB, HD), lambda h, i, *_: (i, h)),
-                pl.BlockSpec((1, 1, QB), lambda h, i, *_: (h, 0, i)),
+                pl.BlockSpec((QB, some), lambda h, i, *_: (i, h)),
+                pl.BlockSpec((GROUP, 1, QB), lambda h, i, *_: (h, 0, i)),
             ],
-            scratch_shapes=[pltpu.VMEM((HD, span), jnp.bfloat16), pltpu.SMEM((2,), jnp.int32)],
+            scratch_shapes=[pltpu.VMEM((some, span), jnp.bfloat16), pltpu.SMEM((2,), jnp.int32)],
         ),
         compiler_params=pltpu.CompilerParams(vmem_limit_bytes=60 << 20),
         cost_estimate=pl.CostEstimate(
@@ -163,8 +176,9 @@
     q_ref, k_ref, v_ref, o_ref, g_ref, lse_ref, *refs = refs[scalars:]
     bounds = (*bounds, *refs[:arrays])
     *results, kt, dk_sum, dv_sum, marks = refs[arrays:]
-    head, block = pl.program_id(0), pl.program_id(1)
+    group, block = pl.program_id(0), pl.program_id(1)
     rows = q_ref.shape[0]
+    heads = range(GROUP)
 
     @pl.when(block == 0)
     def _():
@@ -172,43 +186,52 @@
         dk_sum[...] = jnp.zeros_like(dk_sum)
         dv_sum[...] = jnp.zeros_like(dv_sum)
 
-    queries = q_ref[...]
-    upstream = g_ref[...]
-    lse = lse_ref[0]
+    queries = [q_ref[:, head_columns(h)] for h in heads]
+    upstream = [g_ref[:, head_columns(h)] for h in heads]
     *span, low, high = block_bounds(block, rows, bounds, marks)
     places = lax.broadcasted_iota(jnp.int32, (KB, rows), 0)
-    product = upstream.astype(jnp.float32) * o_ref[...].astype(jnp.float32)
-    delta = jnp.sum(product.T, axis=0, keepdims=True)
-
-    def step(masked, number, dq):
+    deltas = []
+    for h in heads:
+        product = upstream[h].astype(jnp.float32) * o_ref[:, head_columns(h)].astype(jnp.float32)
+        deltas.append(jnp.sum(product.T, axis=0, keepdims=True))
+
+    def step(masked, number, carry):
         start = pl.multiple_of(number * KB, KB)
         window = pl.ds(start, KB)
-        scores = dot_cols(k_ref[window, :], queries) * (score_scale * log2_e)
-        scores = scores - lse
+        scores = [dot_cols(k_ref[window, head_columns(h)], queries[h]) for h in heads]
+        prob_grads = [dot_cols(v_ref[window, head_columns(h)], upstream[h]) for h in heads]
+        scores = [scores[h] * (score_scale * log2_e) - lse_ref[h] for h in heads]
         if masked:
             keep = (places >= low - start) & (places <= high - start)
-            scores = jnp.where(keep, scores, hidden_floor)
-        probs = jnp.exp2(scores)
-        prob_grad = dot_cols(v_ref[window, :], upstream)
-        score_grad = (probs * (prob_grad - delta)).astype(jnp.bfloat16)
-        dv_sum[window, :] += dot_plain(probs.astype(jnp.bfloat16), upstream)
-        dk_sum[window, :] += dot_plain(score_grad, queries)
-        return dq + dot_plain(kt[:, window], score_grad)
-
-    dq = over_key_blocks(step, span, jnp.zeros((HD, rows), jnp.float32))
-    dq = (dq * score_scale).T
+            scores = [jnp.where(keep, score, hidden_floor) for score in scores]
+        probs = [jnp.exp2(score) for score in scores]
+        grads = [
+            (probs[h] * (prob_grads[h] - deltas[h])).astype(jnp.bfloat16) for h in heads
+        ]
+        for h in heads:
+            columns = head_columns(h)
+            dv_sum[window, columns] += dot_plain(probs[h].astype(jnp.bfloat16), upstream[h])
+            dk_sum[window, columns] += dot_plain(grads[h], queries[h])
+        return tuple(
+            carry[h] + dot_plain(kt[head_columns(h), window], grads[h]) for h in heads
+        )
+
+    start = jnp.zeros((HD, rows), jnp.float32)
+    query_grads = over_key_blocks(step, span, (start,) * GROUP)
     if len(results) == 1:
         width = results[0].shape[1] // 3
 
         def place(part):
-            start = pl.multiple_of(part * width + head * HD, HD)
-            return results[0].at[:, pl.ds(start, HD)]
+            begin = pl.multiple_of(part * width + group * GROUP * HD, GROUP * HD)
+            return results[0].at[:, pl.ds(begin, GROUP * HD)]
 
         query_place = place(0).at[pl.ds(pl.multiple_of(block * rows, rows), rows)]
         key_place, value_place = place(1), place(2)
     else:
         query_place, key_place, value_place = results
-    query_place[...] = dq.astype(query_place.dtype)
+    for h in heads:
+        query_grad = (query_grads[h] * score_scale).T
+        query_place[:, head_columns(h)] = query_grad.astype(query_place.dtype)
 
     @pl.when(block == pl.num_programs(1) - 1)
     def _():
@@ -222,9 +245,10 @@
     rows, width = out.shape
     span = keys.shape[0]
     heads = width // HD
-    q_at, k_at, v_at = places
-    row_spec = pl.BlockSpec((QB, HD), lambda h, i, *_: (i, h))
-    key_spec = pl.BlockSpec((span, HD), lambda h, i, *_: (0, h))
+    q_at, k_at, v_at = (place // GROUP for place in places)
+    some = GROUP * HD
+    row_spec = pl.BlockSpec((QB, some), lambda h, i, *_: (i, h))
+    key_spec = pl.BlockSpec((span, some), lambda h, i, *_: (0, h))
     scalars, arrays, specs = bound_operands(bounds)
     return pl.pallas_call(
         functools.partial(attend_back_kernel, len(scalars), len(arrays)),
@@ -237,22 +261,22 @@
         ],
         grid_spec=pltpu.PrefetchScalarGridSpec(
             num_scalar_prefetch=len(scalars),
-            grid=(heads, rows // QB),
+            grid=(heads // GROUP, rows // QB),
             in_specs=[
-                pl.BlockSpec((QB, HD), lambda h, i, *_: (i, h + q_at)),
-                pl.BlockSpec((span, HD), lambda h, i, *_: (0, h + k_at)),
-                pl.BlockSpec((span, HD), lambda h, i, *_: (0, h + v_at)),
+                pl.BlockSpec((QB, some), lambda h, i, *_: (i, h + q_at)),
+                pl.BlockSpec((span, some), lambda h, i, *_: (0, h + k_at)),
+                pl.BlockSpec((span, some), lambda h, i, *_: (0, h + v_at)),
                 row_spec, row_spec,
-                pl.BlockSpec((1, 1, QB), lambda h, i, *_: (h, 0, i)),
+                pl.BlockSpec((GROUP, 1, QB), lambda h, i, *_: (h, 0, i)),
                 *specs,
             ],
             out_specs=[pl.BlockSpec((rows, 3 * width), lambda h, i, *_: (0, 0))]
             if merged
             else [row_spec, key_spec, key_spec],
             scratch_shapes=[
-                pltpu.VMEM((HD, span), jnp.bfloat16),
-                pltpu.VMEM((span, HD), jnp.float32),
-                pltpu.VMEM((span, HD), jnp.float32),
+                pltpu.VMEM((some, span), jnp.bfloat16),
+                pltpu.VMEM((span, some), jnp.float32),
+                pltpu.VMEM((span, some), jnp.float32),
                 pltpu.SMEM((2,), jnp.int32),
             ],
         ),
@@ -307,7 +331,7 @@
 
 MESH = pl.DeviceIdType.MESH
 PIECES = 8
-TILE = 512
+TILE = 2048
 
 
 def greet(me, count, others=()):
@@ -796,11 +820,11 @@
     )
 
     def products(piece, side, place):
-        x = wide[piece_rows(piece), :]
+        columns = pl.ds(pl.multiple_of(side * part, part), part)
+        result = dot_plain(wide[piece_rows(piece), :], weight[:, columns])
         own_half = pl.ds(pl.multiple_of(side * half, half), half)
         for i, bias in enumerate((query_bias, None, value_bias)):
-            start = pl.multiple_of(side * part + i * half, half)
-            values = dot_plain(x, weight[:, pl.ds(start, half)])
+            values = result[:, i * half : (i + 1) * half]
             if bias is not None:
                 values += bias[:, own_half].astype(jnp.float32)
             place[:, i * half : (i + 1) * half] = values.astype(jnp.bfloat16)
@@ -1440,10 +1464,9 @@
 
     def gradient(number, left_start, right, place):
         columns = pl.ds(pl.multiple_of(number * shard, shard), shard)
-        left = gathered[left_start : left_start + rows, columns].T
-
         def product(part):
-            place[:, part] = dot_plain(left, right[:, part]).astype(place.dtype)
+            left = gathered[left_start : left_start + rows, columns]
+            place[:, part] = dot_rows(left, right[:, part]).astype(place.dtype)
 
         tiles(place.shape[1], product)
 

time: 631 us -> 619 us (0.981)
  Pallas kernels: 581 us -> 564 us
    pallas_call x1, Pallas kernels: 333 us -> 318 us  [middle(): pl.pallas_call(functools.partial(middle_kernel, count), out_shape=[shape(...]
  transfers between devices with their start and end apart: 3 -> 3, of which waited for: 0 -> 0; matrix products, arithmetic and copies ran while one was open for 1% -> 1% of each run, Pallas kernels for 26% -> 27%
where the time goes in v13:
time: 619 us; the launch traced here: 613 us
  Pallas kernels  564 us (91%)
  local copies, waits for them, and re-layouts  15.9 us (3%)
  starting transfers between devices  15.8 us (3%)
  between operations  14.5 us (2%)
    pallas_call x1, Pallas kernels, middle(): pl.pallas_call(functools.partial(middle_kernel, count), out_shape=[shape(...  318 us
    pallas_call x1, Pallas kernels, leave(): pl.pallas_call(functools.partial(leave_kernel, sizes), out_shape=[jax.Sha...  114 us
    pallas_call x1, Pallas kernels, enter(): pl.pallas_call(functools.partial(enter_kernel, count), out_shape=[jax.Sha...  81.3 us
    pallas_call x1, Pallas kernels, attend_back(): pl.pallas_call(functools.partial(attend_back_kernel, len(scalars), len(ar...  29.6 us
    pallas_call x1, Pallas kernels, attend(): pl.pallas_call(functools.partial(attend_kernel, len(scalars)), out_shape=...  21.5 us
    all_to_all x2, starting transfers between devices, swap_over_tp(): return lax.all_to_all(parts, 'tp', split_axis=0, concat_axis=0, tiled=True)  15.8 us
  transfers between devices with their start and end apart: 3, of which 0 were waited for; matrix products, arithmetic and copies ran while one was open for 1% of the time, Pallas kernels for 27%

profile of v13, /device:TPU:8, one launch (start us, length us, event | category | flops | bytes accessed | tf_op | source)
XLA Modules:
  0.0 612.7 jit_solution(2746284347947888049)
XLA Ops:
  7.2 1.3 broadcast_in_dim.9.query_bias
  8.4 1.3 broadcast_in_dim.10.value_bias
  9.7 0.0 copy-start.8
  9.7 0.0 copy-start.7
  9.7 81.3 %enter.1 = (bf16[1024,2048]{1,0:T(8,128)(2,1)}, bf16[256,2048]{1,0:T(8,128)(2,1)}, f32[8,2048]{1,0:T(8,128)}, bf16[2048,1536]{1,0:T(8,128)(2,1)}, bf16[2048,512]...) custom-call(bf16[1024,512]{1,0:T(8,128)(2,1)} %x_ref.1, bf16[2,512]{1,0:T(2,128)(2,1)} %gains.1, ...), custom_call_target="tpu_custom_call" | custom-call | flops 80000000000 | bytes 134217728 | tf_op jit(solution)/shard_map/enter/pallas_call | solution.py:913
  91.0 10.5 %all-to-all-start = ((bf16[4,256,512]{2,1,0:T(8,128)(2,1)}), bf16[4,256,512]{2,1,0:T(8,128)(2,1)S(1)}, u32[]{:S(2)}, u32[]{:S(2)}) async-start(bf16[4,256,512]{2,1,0:T(8,128)(2,1)} %bitcast.13), calls=%async_computation | async-start | bytes 2097152 | tf_op jit(solution)/shard_map/all_to_all | solution.py:1970
  101.6 0.0 reduce-scatter.2.cloned.1.call-start
  101.6 0.0 copy-done.8
  101.6 0.6 broadcast_in_dim.11.hidden_bias
  102.2 0.0 copy-done.7
  102.2 0.6 reshape.45.refs_3_.refs_6_
  102.8 21.5 %attend.1 = (bf16[2048,256]{1,0:T(8,128)(2,1)}, f32[2,1,2048]{2,1,0:T(1,128)}) custom-call(bf16[2048,768]{1,0:T(8,128)(2,1)} %get-tuple-element.46.refs_0_.refs_1_.refs_2_, bf16[2048,768]{1,0:T(8,128)(2,1)} %get-tuple-element.46.refs_0_.refs_1_.refs_2_, bf16[2048,768]{1,0:T(8,128)(2,1)} %get-tuple-element.46.refs_0_.refs_1_.refs_2_, ...), custom_call_target="tpu_custom_call" | custom-call | flops 3221225472 | bytes 4194304 | tf_op jit(solution)/shard_map/attend/pallas_call | solution.py:143
  124.3 0.0 all-to-all-done.out_grad
  124.3 0.0 copy-start.2
  124.3 1.0 copy-done.2
  125.3 317.6 %middle.1 = (bf16[1024,512]{1,0:T(8,128)(2,1)}, bf16[4,256,512]{2,1,0:T(8,128)(2,1)}, f32[256,2048]{1,0:T(8,128)}, bf16[1024,2048]{1,0:T(8,128)(2,1)}, bf16[2048...) custom-call(bf16[2048,256]{1,0:T(8,128)(2,1)} %get-tuple-element.51., ...), custom_call_target="tpu_custom_call" | custom-call | flops 299999985664 | bytes 402653184 | tf_op jit(solution)/shard_map/middle/pallas_call | solution.py:1589
  442.9 0.0 reduce-scatter.2.cloned.1.call-update
  442.9 5.3 all-to-all-start.1
  448.2 29.6 %attend_back.1.grads_ref = bf16[2048,768]{1,0:T(8,128)(2,1)} custom-call(bf16[2048,768]{1,0:T(8,128)(2,1)} %get-tuple-element.46.refs_0_.refs_1_.refs_2_, bf16[2048,768]{1,0:T(8,128)(2,1)} %get-tuple-element.46.refs_0_.refs_1_.refs_2_, bf16[2048,768]{1,0:T(8,128)(2,1)} %get-tuple-element.46.refs_0_.refs_1_.refs_2_, ...), custom_call_target="tpu_custom_call" | custom-call | flops 8589934592 | bytes 8388608 | tf_op jit(solution)/shard_map/attend_back/pallas_call | solution.py:253
  477.8 0.0 all-to-all-done.1
  477.8 1.0 copy.28
  478.9 113.5 %leave.1 = (bf16[1024,512]{1,0:T(8,128)(2,1)}, f32[16,512]{1,0:T(8,128)}, f32[256,512]{1,0:T(8,128)}, f32[256,512]{1,0:T(8,128)}, f32[256,512]{1,0:T(8,128)}, /*index=5*/f32[256,512]{1,0:T(8,128)}) custom-call(bf16[2048,768]{1,0:T(8,128)(2,1)} %attend_back.1.grads_ref, bf16[1024,2048]{1,0:T(8,128)(2,1)} %get-tuple-element.61.tokens_in, ...), custom_call_target="tpu_custom_call" | custom-call | flops 60000002048 | bytes 33554432 | tf_op jit(solution)/shard_map/leave/pallas_call | solution.py:1909
  592.4 0.0 copy-start.1
  592.4 0.0 copy-start.6
  592.4 1.4 slice.22
  593.8 0.7 slice.18
  594.6 1.3 fusion
  595.9 0.6 copy.29
  596.5 0.6 fusion.1
  597.1 0.0 reduce-scatter.2.cloned.1.call-done
  597.1 0.0 copy-start.5
  597.1 0.0 copy-start.4
  597.1 2.9 convert_element_type.3
  600.0 0.0 copy-start.3
  600.0 0.0 copy-done.1
  600.0 0.0 copy-start
  600.0 1.0 copy.36
  600.9 0.0 copy-done.6
  600.9 0.8 copy.37
  601.7 0.0 copy-done.5
  601.7 0.8 copy.38
  602.5 0.0 copy-done.4
  602.5 0.8 copy.39
  603.3 0.0 copy-done.3
  603.3 0.8 copy.40
  604.1 0.0 copy-done
  604.1 1.3 copy.41
  (1 shorter events, 0.0 us)
Async XLA Ops:
  9.7 91.9 %copy-start.8 = (bf16[2048]{0:T(1024)(128)(2,1)S(1)}, bf16[2048]{0:T(1024)(128)(2,1)}, u32[]{:S(2)}) copy-start(bf16[2048]{0:T(1024)(128)(2,1)} %param.24) | copy-start | bytes 12292
  9.7 92.5 %copy-start.7 = (s32[8192]{0:T(1024)S(1)}, s32[8192]{0:T(1024)}, u32[]{:S(2)}) copy-start(s32[8192]{0:T(1024)} %param.15) | copy-start | bytes 98308
  91.0 33.3 %all-to-all-start = ((bf16[4,256,512]{2,1,0:T(8,128)(2,1)}), bf16[4,256,512]{2,1,0:T(8,128)(2,1)S(1)}, u32[]{:S(2)}, u32[]{:S(2)}) async-start(bf16[4,256,512]{2,1,0:T(8,128)(2,1)} %bitcast.13), calls=%async_computation | async-start | bytes 2097152 | tf_op jit(solution)/shard_map/all_to_all | solution.py:1970
  101.6 495.5 %reduce-scatter.2.cloned.1.call-start = ((), (), s32[]{:S(2)}) async-start(), calls=%async_computation.3 | async-start | bytes 9437184 | tf_op jit(solution)/shard_map/reduce_scatter | solution.py:2048
  124.3 1.0 copy-start.2
  442.9 34.9 %all-to-all-start.1 = ((bf16[4,256,512]{2,1,0:T(8,128)(2,1)}), bf16[4,256,512]{2,1,0:T(8,128)(2,1)S(1)}, u32[]{:S(2)}, u32[]{:S(2)}) async-start(bf16[4,256,512]{2,1,0:T(8,128)(2,1)} %get-tuple-element.58), calls=%async_computation.1 | async-start | bytes 2097152 | tf_op jit(solution)/shard_map/all_to_all | solution.py:1970
  592.4 7.6 %copy-start.1 = (bf16[1024,512]{1,0:T(8,128)(2,1)S(1)}, bf16[1024,512]{1,0:T(8,128)(2,1)}, u32[]{:S(2)}) copy-start(bf16[1024,512]{1,0:T(8,128)(2,1)} %get-tuple-element.97) | copy-start | bytes 3145732
  592.4 8.6 %copy-start.6 = (f32[256,512]{1,0:T(8,128)S(1)}, f32[256,512]{1,0:T(8,128)}, u32[]{:S(2)}) copy-start(f32[256,512]{1,0:T(8,128)} %get-tuple-element.98) | copy-start | bytes 1572868
  597.1 4.7 copy-start.5
  597.1 5.5 copy-start.4
  600.0 3.4 copy-start.3
  600.0 4.2 copy-start
Sparse Core Ops, SparseCore 0:
  443.1 91.9 reduce-scatter.1

commit v14 on v13

--- a/solution.py
+++ b/solution.py
@@ -332,6 +332,7 @@
 MESH = pl.DeviceIdType.MESH
 PIECES = 8
 TILE = 2048
+OWN_LATE = 5
 
 
 def greet(me, count, others=()):
@@ -748,8 +749,7 @@
 
 
 def enter_kernel(
-    count, x_ref, gains, biases, query_ref, key_ref, value_ref, output_ref, query_bias, value_bias,
-    grad_ref,
+    count, x_ref, gains, biases, query_ref, key_ref, value_ref, output_ref, unit_biases, grad_ref,
     wide_out, own_tokens, marks_out, weight_out, output_out, heads, grad_out,
     wide, weight, output_weight, marks_ref, mark_slots, stage, sent, got, marks_sent, marks_got,
     weight_sent, weight_got, output_sent, output_got, swap_sent, swap_got, put_done, grad_done,
@@ -822,11 +822,11 @@
     def products(piece, side, place):
         columns = pl.ds(pl.multiple_of(side * part, part), part)
         result = dot_plain(wide[piece_rows(piece), :], weight[:, columns])
-        own_half = pl.ds(pl.multiple_of(side * half, half), half)
-        for i, bias in enumerate((query_bias, None, value_bias)):
+        for i, bias in enumerate((0, None, 2 * half)):
             values = result[:, i * half : (i + 1) * half]
             if bias is not None:
-                values += bias[:, own_half].astype(jnp.float32)
+                own_half = pl.ds(pl.multiple_of(bias + side * half, half), half)
+                values += unit_biases[:, own_half].astype(jnp.float32)
             place[:, i * half : (i + 1) * half] = values.astype(jnp.bfloat16)
 
     def wide_copy(piece):
@@ -899,8 +899,8 @@
 
 
 def enter(
-    tokens, gains, biases, query_weight, key_weight, value_weight, output_weight, query_bias,
-    value_bias, out_grad, collective_id,
+    tokens, gains, biases, query_weight, key_weight, value_weight, output_weight, unit_biases,
+    out_grad, collective_id,
 ):
     count = lax.axis_size("tp")
     rows, width = tokens.shape
@@ -921,7 +921,7 @@
             jax.ShapeDtypeStruct((2 * rows, part), low),
             jax.ShapeDtypeStruct((count, PIECES, own, width), low),
         ],
-        in_specs=[anywhere, vmem, vmem, *[anywhere] * 4, vmem, vmem, anywhere],
+        in_specs=[anywhere, vmem, vmem, *[anywhere] * 4, vmem, anywhere],
         out_specs=[anywhere, vmem, vmem, anywhere, anywhere, vmem, vmem],
         scratch_shapes=[
             pltpu.VMEM((rows, features), low),
@@ -950,7 +950,7 @@
         name="enter",
     )(
         tokens, gains, biases, query_weight, key_weight, value_weight, output_weight,
-        query_bias[None], value_bias[None], out_grad.reshape(PIECES, count, own, width),
+        unit_biases, out_grad.reshape(PIECES, count, own, width),
     )
 
 
@@ -1296,7 +1296,7 @@
 
 def middle_kernel(
     count, heads_ref, output_weight, expand_shard, shrink_shard, own_tokens, out_grad, marks,
-    hidden_bias,
+    unit_biases,
     attended, mixed, inner, branch_out, grad_heads, first_sums, second_sums, hidden_sums,
     shrink_out, expand_out,
     expand_weight, shrink_weight, gathered, activated, slope, normed_one, inverse_one,
@@ -1310,6 +1310,7 @@
     height = rows // PIECES
     own = height // count
     shard, hidden = width // PIECES, activated.shape[1]
+    hidden_bias = unit_biases.at[:, pl.ds(unit_biases.shape[1] - hidden, hidden)]
     pieces = 3 * PIECES
 
     def piece_rows(piece, start=0):
@@ -1513,11 +1514,11 @@
         pl.when(step == 5)(expand_gather.last)
         pl.when(step == 2 * PIECES + 7)(plane_sum.second)
         pl.when(step == 2 * PIECES + 9)(plane_sum.third)
+        pl.when(step == PIECES)(shrink_gather.last)
+        late(0, form)
+        late(1, lambda piece: line.sum_onward(piece, term_of(piece), [1]))
         late(5, use)
         late(3, lambda piece: line.spread_onward(piece, 2))
-        late(1, lambda piece: line.sum_onward(piece, term_of(piece), [1]))
-        pl.when(step == PIECES)(shrink_gather.last)
-        late(0, form)
         late(4, lambda piece: [line.spread_onward(piece, i) for i in range(3, count)])
         late(2, lambda piece: line.spread_onward(piece, 1))
         late(2 * PIECES + 4, shrink_step, 2)
@@ -1570,7 +1571,7 @@
 
 def middle(
     attended_heads, output_weight, expand_shard, shrink_shard, own_tokens, out_grad, marks,
-    hidden_bias, collective_id,
+    unit_biases, collective_id,
 ):
     count = lax.axis_size("tp")
     rows = attended_heads.shape[0] // 2
@@ -1634,7 +1635,7 @@
         name="middle",
     )(
         attended_heads, output_weight, expand_shard, shrink_shard, own_tokens, out_grad, marks,
-        hidden_bias,
+        unit_biases,
     )
 
 
@@ -1672,7 +1673,7 @@
     over_plane = Exchange(
         plane_peers, plane_sent, plane_got, lambda _: own_vectors, lambda i: plane_slots.at[i]
     )
-    opening, before, after, closing = hooks or (lambda *_: None,) * 4
+    opening, before, after, closing, pack_at = hooks or (*(lambda *_: None,) * 4, 0)
     order = ((0, 0), (1, 0), (0, 2), (0, 1), (1, 2), (1, 1))
     rows_ref[...] = jnp.zeros_like(rows_ref)
     for i, (which, row) in enumerate(order):
@@ -1708,23 +1709,23 @@
             own_vectors[place : place + 1, :] = jnp.sum(part, axis=0, keepdims=True)
         over_plane.start()
 
+    def own_sum(piece):
+        total[...] = terms(piece)(me)
+        line.sum_end(piece, total)
+        rows = pl.ds(pl.multiple_of(piece * height, height), height)
+        out_ref[rows, :] = total[...].astype(out_ref.dtype)
+
     @pl.loop(0, PIECES)
     def _(piece):
         before(piece)
         line.sum_start(piece, terms(piece))
         line.sum_onward(piece, terms(piece), range(count - 2, 0, -1))
         after(piece)
-
-    pack()
+        pl.when(piece == pack_at)(pack)
+        pl.when(piece >= OWN_LATE)(lambda: own_sum(piece - OWN_LATE))
+
     closing()
-
-    @pl.loop(0, PIECES)
-    def _(piece):
-        total[...] = terms(piece)(me)
-        line.sum_end(piece, total)
-        rows = pl.ds(pl.multiple_of(piece * height, height), height)
-        out_ref[rows, :] = total[...].astype(out_ref.dtype)
-
+    pl.loop(PIECES - OWN_LATE, PIECES)(own_sum)
     over_plane.wait_arrivals()
     vectors_ref[...] = own_vectors[...]
     for i in range(len(plane_peers)):
@@ -1874,7 +1875,7 @@
         sizes, x_ref, weight, inner_ref, first_ref, second_ref, hidden_ref, out_ref, vectors_ref,
         rows_ref, term_ref, total, slots, own_vectors, tp_slots, plane_slots,
         sum_sent, sum_got, tp_sent, tp_got, plane_sent, plane_got,
-        hooks=(opening, before, after, closing),
+        hooks=(opening, before, after, closing, jnp.minimum(begin + 3, last)),
     )
     third = part // 3
 
@@ -2002,10 +2003,11 @@
         return lax.all_gather(weight, plane, axis=0, tiled=True)
 
     block_index = lax.axis_index("fsdp") * plane_sizes[1] + lax.axis_index("ctx")
+    unit_biases = jnp.concatenate([query_bias, value_bias, hidden_bias])[None]
     if by_heads:
         wide_tokens, own_tokens, marks, wide_qkv, full_output, qkv_heads, upstream = enter(
             tokens, norm_gains, row_biases, query_weight, key_weight, value_weight, output_weight,
-            query_bias, value_bias, out_grad, 0,
+            unit_biases, out_grad, 0,
         )
         upstream = upstream.reshape(upstream.shape[0], -1, upstream.shape[3])
         queries = keys = values = qkv_heads
@@ -2055,7 +2057,7 @@
             first_sums, second_sums, hidden_sums, shrink_grad, expand_part,
         ) = middle(
             attended_heads, full_output, expand_weight, shrink_weight, own_tokens, upstream,
-            marks, hidden_bias[None], 1,
+            marks, unit_biases, 1,
         )
         expand_grad = owner_sum(expand_part)
         mixed = by_rows(swap_over_tp(mixed_own))

time: 619 us -> 615 us (level)
  no operation moved by 1% of the time
where the time goes in v14:
time: 615 us; the launch traced here: 610 us
  Pallas kernels  563 us (92%)
  starting transfers between devices  15.4 us (3%)
  between operations  14.5 us (2%)
  local copies, waits for them, and re-layouts  13.4 us (2%)
    pallas_call x1, Pallas kernels, middle(): pl.pallas_call(functools.partial(middle_kernel, count), out_shape=[shape(...  314 us
    pallas_call x1, Pallas kernels, leave(): pl.pallas_call(functools.partial(leave_kernel, sizes), out_shape=[jax.Sha...  110 us
    pallas_call x1, Pallas kernels, enter(): pl.pallas_call(functools.partial(enter_kernel, count), out_shape=[jax.Sha...  81.3 us
    pallas_call x1, Pallas kernels, attend_back(): pl.pallas_call(functools.partial(attend_back_kernel, len(scalars), len(ar...  32.8 us
    pallas_call x1, Pallas kernels, attend(): pl.pallas_call(functools.partial(attend_kernel, len(scalars)), out_shape=...  23.7 us
    all_to_all x2, starting transfers between devices, swap_over_tp(): return lax.all_to_all(parts, 'tp', split_axis=0, concat_axis=0, tiled=True)  15.4 us
  transfers between devices with their start and end apart: 3, of which 0 were waited for; matrix products, arithmetic and copies ran while one was open for 1% of the time, Pallas kernels for 27%

profile of v14, /device:TPU:8, one launch (start us, length us, event | category | flops | bytes accessed | tf_op | source)
XLA Modules:
  0.0 609.7 jit_solution(3690066096132144080)
XLA Ops:
  7.2 0.7 pad_maximum_fusion
  7.9 0.6 broadcast_in_dim.3.unit_biases
  8.5 0.0 copy-start.7
  8.5 81.3 %enter.1 = (bf16[1024,2048]{1,0:T(8,128)(2,1)}, bf16[256,2048]{1,0:T(8,128)(2,1)}, f32[8,2048]{1,0:T(8,128)}, bf16[2048,1536]{1,0:T(8,128)(2,1)}, bf16[2048,512]...) custom-call(bf16[1024,512]{1,0:T(8,128)(2,1)} %x_ref.1, bf16[2,512]{1,0:T(2,128)(2,1)} %gains.1, ...), custom_call_target="tpu_custom_call" | custom-call | flops 80000000000 | bytes 134217728 | tf_op jit(solution)/shard_map/enter/pallas_call | solution.py:913
  89.9 10.5 %all-to-all-start = ((bf16[4,256,512]{2,1,0:T(8,128)(2,1)}), bf16[4,256,512]{2,1,0:T(8,128)(2,1)S(1)}, u32[]{:S(2)}, u32[]{:S(2)}) async-start(bf16[4,256,512]{2,1,0:T(8,128)(2,1)} %bitcast.13), calls=%async_computation | async-start | bytes 2097152 | tf_op jit(solution)/shard_map/all_to_all | solution.py:1971
  100.4 0.0 reduce-scatter.2.cloned.1.call-start
  100.4 0.0 copy-done.7
  100.4 0.6 reshape.45.refs_3_.refs_6_
  101.0 23.7 %attend.1 = (bf16[2048,256]{1,0:T(8,128)(2,1)}, f32[2,1,2048]{2,1,0:T(1,128)}) custom-call(bf16[2048,768]{1,0:T(8,128)(2,1)} %get-tuple-element.46.refs_0_.refs_1_.refs_2_, bf16[2048,768]{1,0:T(8,128)(2,1)} %get-tuple-element.46.refs_0_.refs_1_.refs_2_, bf16[2048,768]{1,0:T(8,128)(2,1)} %get-tuple-element.46.refs_0_.refs_1_.refs_2_, ...), custom_call_target="tpu_custom_call" | custom-call | flops 3221225472 | bytes 4194304 | tf_op jit(solution)/shard_map/attend/pallas_call | solution.py:143
  124.7 0.0 all-to-all-done.out_grad
  124.7 0.0 copy-start.2
  124.7 1.0 copy-done.2
  125.7 314.4 %middle.1 = (bf16[1024,512]{1,0:T(8,128)(2,1)}, bf16[4,256,512]{2,1,0:T(8,128)(2,1)}, f32[256,2048]{1,0:T(8,128)}, bf16[1024,2048]{1,0:T(8,128)(2,1)}, bf16[2048...) custom-call(bf16[2048,256]{1,0:T(8,128)(2,1)} %get-tuple-element.51., ...), custom_call_target="tpu_custom_call" | custom-call | flops 299999985664 | bytes 402653184 | tf_op jit(solution)/shard_map/middle/pallas_call | solution.py:1590
  440.1 0.0 reduce-scatter.2.cloned.1.call-update
  440.2 4.9 all-to-all-start.1
  445.0 32.8 %attend_back.1.grads_ref = bf16[2048,768]{1,0:T(8,128)(2,1)} custom-call(bf16[2048,768]{1,0:T(8,128)(2,1)} %get-tuple-element.46.refs_0_.refs_1_.refs_2_, bf16[2048,768]{1,0:T(8,128)(2,1)} %get-tuple-element.46.refs_0_.refs_1_.refs_2_, bf16[2048,768]{1,0:T(8,128)(2,1)} %get-tuple-element.46.refs_0_.refs_1_.refs_2_, ...), custom_call_target="tpu_custom_call" | custom-call | flops 8589934592 | bytes 8388608 | tf_op jit(solution)/shard_map/attend_back/pallas_call | solution.py:253
  477.8 0.0 all-to-all-done.1
  477.9 1.0 copy.28
  478.9 110.4 %leave.1 = (bf16[1024,512]{1,0:T(8,128)(2,1)}, f32[16,512]{1,0:T(8,128)}, f32[256,512]{1,0:T(8,128)}, f32[256,512]{1,0:T(8,128)}, f32[256,512]{1,0:T(8,128)}, /*index=5*/f32[256,512]{1,0:T(8,128)}) custom-call(bf16[2048,768]{1,0:T(8,128)(2,1)} %attend_back.1.grads_ref, bf16[1024,2048]{1,0:T(8,128)(2,1)} %get-tuple-element.61.tokens_in, ...), custom_call_target="tpu_custom_call" | custom-call | flops 60000002048 | bytes 33554432 | tf_op jit(solution)/shard_map/leave/pallas_call | solution.py:1910
  589.3 0.0 copy-start.1
  589.3 0.0 copy-start.6
  589.3 1.4 slice.22
  590.7 0.7 slice.18
  591.5 1.3 fusion
  592.8 0.6 copy.29
  593.4 0.6 fusion.1
  594.0 0.0 reduce-scatter.2.cloned.1.call-done
  594.0 0.0 copy-start.5
  594.0 0.0 copy-start.4
  594.0 2.9 convert_element_type.3
  596.9 0.0 copy-start.3
  596.9 0.0 copy-done.1
  596.9 0.0 copy-start
  596.9 1.0 copy.36
  597.9 0.0 copy-done.6
  597.9 0.8 copy.37
  598.7 0.0 copy-done.5
  598.7 0.8 copy.38
  599.5 0.0 copy-done.4
  599.5 0.8 copy.39
  600.3 0.0 copy-done.3
  600.3 0.8 copy.40
  601.1 0.0 copy-done
  601.1 1.3 copy.41
  (1 shorter events, 0.0 us)
Async XLA Ops:
  8.5 91.9 %copy-start.7 = (s32[8192]{0:T(1024)S(1)}, s32[8192]{0:T(1024)}, u32[]{:S(2)}) copy-start(s32[8192]{0:T(1024)} %param.15) | copy-start | bytes 98308
  89.9 34.9 %all-to-all-start = ((bf16[4,256,512]{2,1,0:T(8,128)(2,1)}), bf16[4,256,512]{2,1,0:T(8,128)(2,1)S(1)}, u32[]{:S(2)}, u32[]{:S(2)}) async-start(bf16[4,256,512]{2,1,0:T(8,128)(2,1)} %bitcast.13), calls=%async_computation | async-start | bytes 2097152 | tf_op jit(solution)/shard_map/all_to_all | solution.py:1971
  100.4 493.6 %reduce-scatter.2.cloned.1.call-start = ((), (), s32[]{:S(2)}) async-start(), calls=%async_computation.3 | async-start | bytes 9437184 | tf_op jit(solution)/shard_map/reduce_scatter | solution.py:2050
  124.7 1.0 copy-start.2
  440.2 37.7 %all-to-all-start.1 = ((bf16[4,256,512]{2,1,0:T(8,128)(2,1)}), bf16[4,256,512]{2,1,0:T(8,128)(2,1)S(1)}, u32[]{:S(2)}, u32[]{:S(2)}) async-start(bf16[4,256,512]{2,1,0:T(8,128)(2,1)} %get-tuple-element.58), calls=%async_computation.1 | async-start | bytes 2097152 | tf_op jit(solution)/shard_map/all_to_all | solution.py:1971
  589.3 7.6 %copy-start.1 = (bf16[1024,512]{1,0:T(8,128)(2,1)S(1)}, bf16[1024,512]{1,0:T(8,128)(2,1)}, u32[]{:S(2)}) copy-start(bf16[1024,512]{1,0:T(8,128)(2,1)} %get-tuple-element.97) | copy-start | bytes 3145732
  589.3 8.6 %copy-start.6 = (f32[256,512]{1,0:T(8,128)S(1)}, f32[256,512]{1,0:T(8,128)}, u32[]{:S(2)}) copy-start(f32[256,512]{1,0:T(8,128)} %get-tuple-element.98) | copy-start | bytes 1572868
  594.0 4.7 copy-start.5
  594.0 5.5 copy-start.4
  596.9 3.4 copy-start.3
  596.9 4.2 copy-start
Sparse Core Ops, SparseCore 0:
  440.3 88.8 reduce-scatter.1

commit v15 on v14

--- a/solution.py
+++ b/solution.py
@@ -1673,7 +1673,7 @@
     over_plane = Exchange(
         plane_peers, plane_sent, plane_got, lambda _: own_vectors, lambda i: plane_slots.at[i]
     )
-    opening, before, after, closing, pack_at = hooks or (*(lambda *_: None,) * 4, 0)
+    opening, before, after, pack_at = hooks or (*(lambda *_: None,) * 3, 0)
     order = ((0, 0), (1, 0), (0, 2), (0, 1), (1, 2), (1, 1))
     rows_ref[...] = jnp.zeros_like(rows_ref)
     for i, (which, row) in enumerate(order):
@@ -1724,7 +1724,6 @@
         pl.when(piece == pack_at)(pack)
         pl.when(piece >= OWN_LATE)(lambda: own_sum(piece - OWN_LATE))
 
-    closing()
     pl.loop(PIECES - OWN_LATE, PIECES)(own_sum)
     over_plane.wait_arrivals()
     vectors_ref[...] = own_vectors[...]
@@ -1865,17 +1864,15 @@
         def _():
             products(plane_sum, plane_sum.fsdp, tokens_ref, x_ref)
 
-        pl.when(piece == jnp.minimum(begin + 2, last))(plane_sum.second)
+        pl.when(piece == jnp.minimum(begin + 1, last))(plane_sum.second)
         pl.when(piece == jnp.minimum(begin + 3, last))(output_sum.third)
-
-    def closing():
-        plane_sum.third()
+        pl.when(piece == jnp.minimum(begin + 4, last))(plane_sum.third)
 
     input_kernel(
         sizes, x_ref, weight, inner_ref, first_ref, second_ref, hidden_ref, out_ref, vectors_ref,
         rows_ref, term_ref, total, slots, own_vectors, tp_slots, plane_slots,
         sum_sent, sum_got, tp_sent, tp_got, plane_sent, plane_got,
-        hooks=(opening, before, after, closing, jnp.minimum(begin + 3, last)),
+        hooks=(opening, before, after, jnp.minimum(begin + 3, last)),
     )
     third = part // 3
 

time: 615 us -> 612 us (level)
  no operation moved by 1% of the time
where the time goes in v15:
time: 612 us; the launch traced here: 606 us
  Pallas kernels  559 us (91%)
  starting transfers between devices  15.4 us (3%)
  between operations  14.5 us (2%)
  local copies, waits for them, and re-layouts  13.4 us (2%)
    pallas_call x1, Pallas kernels, middle(): pl.pallas_call(functools.partial(middle_kernel, count), out_shape=[shape(...  314 us
    pallas_call x1, Pallas kernels, leave(): pl.pallas_call(functools.partial(leave_kernel, sizes), out_shape=[jax.Sha...  106 us
    pallas_call x1, Pallas kernels, enter(): pl.pallas_call(functools.partial(enter_kernel, count), out_shape=[jax.Sha...  81.3 us
    pallas_call x1, Pallas kernels, attend_back(): pl.pallas_call(functools.partial(attend_back_kernel, len(scalars), len(ar...  32.8 us
    pallas_call x1, Pallas kernels, attend(): pl.pallas_call(functools.partial(attend_kernel, len(scalars)), out_shape=...  23.7 us
    all_to_all x2, starting transfers between devices, swap_over_tp(): return lax.all_to_all(parts, 'tp', split_axis=0, concat_axis=0, tiled=True)  15.4 us
  transfers between devices with their start and end apart: 3, of which 0 were waited for; matrix products, arithmetic and copies ran while one was open for 1% of the time, Pallas kernels for 27%

profile of v15, /device:TPU:8, one launch (start us, length us, event | category | flops | bytes accessed | tf_op | source)
XLA Modules:
  0.0 605.7 jit_solution(548802330313426037)
XLA Ops:
  7.2 0.7 pad_maximum_fusion
  7.9 0.6 broadcast_in_dim.3.unit_biases
  8.5 0.0 copy-start.7
  8.5 81.3 %enter.1 = (bf16[1024,2048]{1,0:T(8,128)(2,1)}, bf16[256,2048]{1,0:T(8,128)(2,1)}, f32[8,2048]{1,0:T(8,128)}, bf16[2048,1536]{1,0:T(8,128)(2,1)}, bf16[2048,512]...) custom-call(bf16[1024,512]{1,0:T(8,128)(2,1)} %x_ref.1, bf16[2,512]{1,0:T(2,128)(2,1)} %gains.1, ...), custom_call_target="tpu_custom_call" | custom-call | flops 80000000000 | bytes 134217728 | tf_op jit(solution)/shard_map/enter/pallas_call | solution.py:913
  89.9 10.5 %all-to-all-start = ((bf16[4,256,512]{2,1,0:T(8,128)(2,1)}), bf16[4,256,512]{2,1,0:T(8,128)(2,1)S(1)}, u32[]{:S(2)}, u32[]{:S(2)}) async-start(bf16[4,256,512]{2,1,0:T(8,128)(2,1)} %bitcast.13), calls=%async_computation | async-start | bytes 2097152 | tf_op jit(solution)/shard_map/all_to_all | solution.py:1968
  100.4 0.0 reduce-scatter.2.cloned.1.call-start
  100.4 0.0 copy-done.7
  100.4 0.6 reshape.45.refs_3_.refs_6_
  101.0 23.7 %attend.1 = (bf16[2048,256]{1,0:T(8,128)(2,1)}, f32[2,1,2048]{2,1,0:T(1,128)}) custom-call(bf16[2048,768]{1,0:T(8,128)(2,1)} %get-tuple-element.46.refs_0_.refs_1_.refs_2_, bf16[2048,768]{1,0:T(8,128)(2,1)} %get-tuple-element.46.refs_0_.refs_1_.refs_2_, bf16[2048,768]{1,0:T(8,128)(2,1)} %get-tuple-element.46.refs_0_.refs_1_.refs_2_, ...), custom_call_target="tpu_custom_call" | custom-call | flops 3221225472 | bytes 4194304 | tf_op jit(solution)/shard_map/attend/pallas_call | solution.py:143
  124.7 0.0 all-to-all-done.out_grad
  124.7 0.0 copy-start.2
  124.7 1.0 copy-done.2
  125.7 314.4 %middle.1 = (bf16[1024,512]{1,0:T(8,128)(2,1)}, bf16[4,256,512]{2,1,0:T(8,128)(2,1)}, f32[256,2048]{1,0:T(8,128)}, bf16[1024,2048]{1,0:T(8,128)(2,1)}, bf16[2048...) custom-call(bf16[2048,256]{1,0:T(8,128)(2,1)} %get-tuple-element.51., ...), custom_call_target="tpu_custom_call" | custom-call | flops 299999985664 | bytes 402653184 | tf_op jit(solution)/shard_map/middle/pallas_call | solution.py:1590
  440.1 0.0 reduce-scatter.2.cloned.1.call-update
  440.2 4.9 all-to-all-start.1
  445.0 32.8 %attend_back.1.grads_ref = bf16[2048,768]{1,0:T(8,128)(2,1)} custom-call(bf16[2048,768]{1,0:T(8,128)(2,1)} %get-tuple-element.46.refs_0_.refs_1_.refs_2_, bf16[2048,768]{1,0:T(8,128)(2,1)} %get-tuple-element.46.refs_0_.refs_1_.refs_2_, bf16[2048,768]{1,0:T(8,128)(2,1)} %get-tuple-element.46.refs_0_.refs_1_.refs_2_, ...), custom_call_target="tpu_custom_call" | custom-call | flops 8589934592 | bytes 8388608 | tf_op jit(solution)/shard_map/attend_back/pallas_call | solution.py:253
  477.9 0.0 all-to-all-done.1
  477.9 1.0 copy.28
  478.9 106.4 %leave.1 = (bf16[1024,512]{1,0:T(8,128)(2,1)}, f32[16,512]{1,0:T(8,128)}, f32[256,512]{1,0:T(8,128)}, f32[256,512]{1,0:T(8,128)}, f32[256,512]{1,0:T(8,128)}, /*index=5*/f32[256,512]{1,0:T(8,128)}) custom-call(bf16[2048,768]{1,0:T(8,128)(2,1)} %attend_back.1.grads_ref, bf16[1024,2048]{1,0:T(8,128)(2,1)} %get-tuple-element.61.tokens_in, ...), custom_call_target="tpu_custom_call" | custom-call | flops 60000002048 | bytes 33554432 | tf_op jit(solution)/shard_map/leave/pallas_call | solution.py:1907
  585.3 0.0 copy-start.1
  585.4 0.0 copy-start.6
  585.4 1.4 slice.22
  586.8 0.7 slice.18
  587.5 1.3 fusion
  588.9 0.6 copy.29
  589.5 0.6 fusion.1
  590.1 0.0 reduce-scatter.2.cloned.1.call-done
  590.1 0.0 copy-start.5
  590.1 0.0 copy-start.4
  590.1 2.9 convert_element_type.3
  592.9 0.0 copy-start.3
  592.9 0.0 copy-done.1
  592.9 0.0 copy-start
  592.9 1.0 copy.36
  593.9 0.0 copy-done.6
  593.9 0.8 copy.37
  594.7 0.0 copy-done.5
  594.7 0.8 copy.38
  595.5 0.0 copy-done.4
  595.5 0.8 copy.39
  596.3 0.0 copy-done.3
  596.3 0.8 copy.40
  597.1 0.0 copy-done
  597.1 1.3 copy.41
  (1 shorter events, 0.0 us)
Async XLA Ops:
  8.5 91.9 %copy-start.7 = (s32[8192]{0:T(1024)S(1)}, s32[8192]{0:T(1024)}, u32[]{:S(2)}) copy-start(s32[8192]{0:T(1024)} %param.15) | copy-start | bytes 98308
  89.9 34.9 %all-to-all-start = ((bf16[4,256,512]{2,1,0:T(8,128)(2,1)}), bf16[4,256,512]{2,1,0:T(8,128)(2,1)S(1)}, u32[]{:S(2)}, u32[]{:S(2)}) async-start(bf16[4,256,512]{2,1,0:T(8,128)(2,1)} %bitcast.13), calls=%async_computation | async-start | bytes 2097152 | tf_op jit(solution)/shard_map/all_to_all | solution.py:1968
  100.4 489.7 %reduce-scatter.2.cloned.1.call-start = ((), (), s32[]{:S(2)}) async-start(), calls=%async_computation.3 | async-start | bytes 9437184 | tf_op jit(solution)/shard_map/reduce_scatter | solution.py:2047
  124.7 1.0 copy-start.2
  440.2 37.7 %all-to-all-start.1 = ((bf16[4,256,512]{2,1,0:T(8,128)(2,1)}), bf16[4,256,512]{2,1,0:T(8,128)(2,1)S(1)}, u32[]{:S(2)}, u32[]{:S(2)}) async-start(bf16[4,256,512]{2,1,0:T(8,128)(2,1)} %get-tuple-element.58), calls=%async_computation.1 | async-start | bytes 2097152 | tf_op jit(solution)/shard_map/all_to_all | solution.py:1968
  585.3 7.6 %copy-start.1 = (bf16[1024,512]{1,0:T(8,128)(2,1)S(1)}, bf16[1024,512]{1,0:T(8,128)(2,1)}, u32[]{:S(2)}) copy-start(bf16[1024,512]{1,0:T(8,128)(2,1)} %get-tuple-element.97) | copy-start | bytes 3145732
  585.4 8.6 %copy-start.6 = (f32[256,512]{1,0:T(8,128)S(1)}, f32[256,512]{1,0:T(8,128)}, u32[]{:S(2)}) copy-start(f32[256,512]{1,0:T(8,128)} %get-tuple-element.98) | copy-start | bytes 1572868
  590.1 4.7 copy-start.5
  590.1 5.5 copy-start.4
  592.9 3.4 copy-start.3
  592.9 4.2 copy-start
Sparse Core Ops, SparseCore 0:
  440.3 88.9 reduce-scatter.1
